TPU v7x, 256 devices: a whole 4x4x8 slice. The times are simulated.
256 devices in a mesh: blk: 64 (over z, x_lo, y), grp: 4 (over x_hi, core).
Axes of the slice: x: 4 (x_hi: 2, x_lo: 2; x = x_hi * 2 + x_lo), y: 4, z: 8, core: 2. Of those that a mesh axis runs over, the one named last changes fastest.
Arguments:
- queries: bfloat16 [49152, 1024], P('blk'), may hold values from -18 to 18
- passages: bfloat16 [393216, 1024], P(('blk', 'grp')), may hold values from -18 to 18
- loss_grad: float32 [49152], P('blk'), may hold values from -40 to 40
- teacher_logits: float32 [8, 49152], P(None, 'blk'), may hold values from -8 to 410
- passage_ids: int32 [8, 49152], P(None, 'blk'), may hold values from 0 to 393215, as said below
Outputs:
- query_grad: bfloat16 [49152, 1024], P(('blk', 'grp'))
- passage_grad: bfloat16 [393216, 1024], P(('blk', 'grp'))
Inputs may be any that keep to these rules, and one draw needn't show every extreme that they name: passage_ids[0, i] names a passage of block i // 768, and every passage_ids[k, i] names a passage of block i // 768 or of block (i // 768 - 1) mod 64, where passage j lies in block j // 6144.
All inputs are finite; a program needn't handle non-finite values.
Results may differ from a plain program's by a relative error of at most 0.015.
Values may be sent and summed in bfloat16 or wider, within the bound.
No kernel may reach another device: no remote copies, remote signals or barrier semaphores. Data moves between devices by JAX's collectives and lax.ppermute only.
A program may use at most 128 MiB of HBM per device.

v0:
```python
import math

import jax
import jax.numpy as jnp
from jax import lax
from jax.sharding import PartitionSpec as P


def shifted(x, axis, by):
    devices = lax.axis_size(axis)
    return lax.ppermute(x, axis, [(i, (i + by) % devices) for i in range(devices)])


def contract(left_rows, right_rows):
    return lax.dot_general(
        left_rows, right_rows, (((1,), (1,)), ((), ())), preferred_element_type=jnp.float32
    )


def grad_product(grads, rows):
    return lax.dot_general(
        grads, rows, (((0,), (0,)), ((), ())), preferred_element_type=jnp.float32
    )


def combine_stats(earlier, later):
    joint_top = jnp.maximum(earlier[0], later[0])
    joint_total = earlier[1] * jnp.exp(earlier[0] - joint_top) + later[1] * jnp.exp(
        later[0] - joint_top
    )
    return (joint_top, joint_total)


def tile_stats(scores):
    tile_top = jnp.max(scores, axis=1)
    tile_total = jnp.sum(jnp.exp(scores - tile_top[:, None]), axis=1)
    return (tile_top, tile_total)


def merge_rows(row_top, row_total):
    whole_top = lax.pmax(row_top, "grp")
    whole_total = lax.psum(row_total * jnp.exp(row_top - whole_top), "grp")
    return (whole_top, whole_total)


def tile_grad(scores, row_lse, query_coef, weighted, labels, first_col):
    columns = first_col + lax.broadcasted_iota(jnp.int32, (1, scores.shape[1]), 1)
    target = jnp.zeros(scores.shape, jnp.float32)
    for cand_slot in range(labels.shape[0]):
        target = target + jnp.where(
            labels[cand_slot][:, None] == columns, weighted[cand_slot][:, None], 0.0
        )
    return (query_coef[:, None] * jnp.exp(scores - row_lse[:, None]) - target).astype(jnp.bfloat16)


def per_device(queries, passages, loss_grad, teacher_logits, passage_ids):
    score_scale = 3.0 / math.sqrt(queries.shape[1])
    blocks = lax.axis_size("blk")
    groups = lax.axis_size("grp")
    blk_index = lax.axis_index("blk")
    grp_index = lax.axis_index("grp")
    pass_rows = passages.shape[0]
    own_first = (blk_index * groups + grp_index) * pass_rows
    query_coef = score_scale * loss_grad
    weighted = query_coef[None, :] * jax.nn.softmax(teacher_logits, axis=0)
    own_scores = score_scale * contract(queries, passages)
    own_top, own_total = tile_stats(own_scores)
    neighbour = shifted(passages, "blk", 1)
    prev_first = ((blk_index - 1 + blocks) % blocks * groups + grp_index) * pass_rows
    prev_scores = score_scale * contract(queries, neighbour)
    row_top, row_total = combine_stats((own_top, own_total), tile_stats(prev_scores))
    row_top, row_total = merge_rows(row_top, row_total)
    row_lse = row_top + jnp.log(row_total)
    own_grad = tile_grad(own_scores, row_lse, query_coef, weighted, passage_ids, own_first)
    prev_grad = tile_grad(prev_scores, row_lse, query_coef, weighted, passage_ids, prev_first)
    query_sum = lax.psum_scatter(
        (
            jnp.dot(own_grad, passages, preferred_element_type=jnp.float32)
            + jnp.dot(prev_grad, neighbour, preferred_element_type=jnp.float32)
        ).astype(jnp.bfloat16),
        "grp",
        scatter_dimension=0,
        tiled=True,
    )
    returned = shifted(grad_product(prev_grad, queries).astype(jnp.bfloat16), "blk", -1)
    passage_sum = grad_product(own_grad, queries) + returned.astype(jnp.float32)
    return (query_sum, passage_sum.astype(jnp.bfloat16))


def solution(mesh):
    in_specs = (P("blk", None), P(("blk", "grp"), None), P("blk"), P(None, "blk"), P(None, "blk"))
    out_specs = (P(("blk", "grp"), None), P(("blk", "grp"), None))
    return jax.shard_map(
        per_device, mesh=mesh, in_specs=in_specs, out_specs=out_specs, check_vma=False
    )
```

profile of v0, /device:TPU:1, one launch (start us, length us, event | category | flops | bytes accessed | tf_op | source)
XLA Modules:
  0.0 214.0 jit_solution(5553744066355227684)
XLA Ops:
  7.2 0.0 copy-start
  7.2 0.0 reduce-scatter.2.cloned.1.call-start
  7.2 2.2 %collective-permute-start = (bf16[1536,1024]{1,0:T(8,128)(2,1)}, bf16[1536,1024]{1,0:T(8,128)(2,1)}, u32[]{:S(2)}, u32[]{:S(2)}) collective-permute-start(bf16[1536,1024]{1,0:T(8,128)(2,1)} %param.6), channel_id=1, source_target_pairs={{0,4},{4,8},{8,12},{12,16},{16,20},{20,24},{24,28},{28,32},{32,36}... | collective-permute-start | bytes 9437192 | tf_op jit(solution)/shard_map/ppermute | solution.py:11
  9.4 0.7 reduce_max.29
  10.2 0.8 fusion
  11.0 0.7 broadcast_multiply_fusion
  11.7 0.8 divide_multiply_fusion
  12.4 0.1 slice_reduce_fusion.7
  12.5 1.1 slice_reduce_fusion.15
  13.6 0.0 copy-done
  13.6 4.6 %multiply_reduce_fusion.1 = (f32[768]{0:T(1024)S(1)}, f32[768,1536]{1,0:T(8,128)S(1)}) fusion(bf16[768,1024]{1,0:T(8,128)(2,1)S(1)} %copy-done, bf16[1536,1024]{1,0:T(8,128)(2,1)} %param.6), kind=kOutput, calls=%fused_computation.6 | convolution fusion | flops 2418277632 | bytes 9440256 | tf_op jit(solution)/shard_map/dot_general | solution.py:15
  18.2 0.0 copy-start.1
  18.2 0.9 exponential_reduce_fusion.1
  19.1 66.1 %collective-permute-done = bf16[1536,1024]{1,0:T(8,128)(2,1)} collective-permute-done((bf16[1536,1024]{1,0:T(8,128)(2,1)}, bf16[1536,1024]{1,0:T(8,128)(2,1)}, u32[]{:S(2)}, u32[]{:S(2)}) %collective-permute-start) | collective-permute-done | bytes 3145760 | tf_op jit(solution)/shard_map/ppermute | solution.py:11
  85.2 4.6 %multiply_reduce_fusion = (f32[768]{0:T(1024)S(1)}, f32[768,1536]{1,0:T(8,128)S(1)}) fusion(bf16[768,1024]{1,0:T(8,128)(2,1)S(1)} %copy-done, bf16[1536,1024]{1,0:T(8,128)(2,1)} %collective-permute-done), kind=kOutput, calls=%fused_computation.5 | convolution fusion | flops 2418277632 | bytes 9440256 | tf_op jit(solution)/shard_map/dot_general | solution.py:15
  89.8 0.0 copy-done.1
  89.8 0.0 copy-start.3
  89.9 2.1 %copy-done.3 = f32[768,1536]{1,0:T(8,128)} copy-done((f32[768,1536]{1,0:T(8,128)}, f32[768,1536]{1,0:T(8,128)S(1)}, u32[]{:S(2)}) %copy-start.3) | copy-done | bytes 4718616
  92.0 0.9 exponential_reduce_fusion
  92.9 7.8 %pmax.7 = f32[768]{0:T(1024)S(1)} all-reduce(f32[768]{0:T(1024)S(1)} %max.1), channel_id=1, replica_groups=mesh['blk'=64,'grp'=4] {'grp'}, use_global_device_ids=true, to_apply=%region_2.0 | all-reduce | flops 768 | bytes 6144 | tf_op jit(solution)/shard_map/pmax | solution.py:41
  100.7 8.8 %psum.7 = f32[768]{0:T(1024)S(1)} all-reduce(f32[768]{0:T(1024)S(1)} %exponential_multiply_fusion), channel_id=1, replica_groups=mesh['blk'=64,'grp'=4] {'grp'}, use_global_device_ids=true, to_apply=%region_5.6 | all-reduce | flops 768 | bytes 6144 | tf_op jit(solution)/shard_map/psum | solution.py:42
  109.5 0.0 copy-start.2
  109.5 7.8 %subtract_convert_fusion = bf16[768,1536]{1,0:T(8,128)(2,1)S(1)} fusion(f32[768,1536]{1,0:T(8,128)} %copy-done.3, s32[1536]{0:T(1024)S(1)} %iota_add_fusion, f32[768]{0:T(1024)S(1)} %get-tuple-element.11, f32[768]{0:T(1024)S(1)} %get-tuple-element.12, f32[768]{0:T(1024)S(1)} %get-tuple-element.13, f32[768]{0:T(1024)S(1)} %get-tuple-element.14, ...), kind=kLoop, calls=%fused_computation.1 | loop fusion | flops 33030144 | bytes 7139328 | tf_op jit(solution)/shard_map/convert_element_type | solution.py:53
  117.3 0.0 copy-done.2
  117.3 0.0 copy-start.5
  117.3 5.2 %subtract_convert_fusion.1 = bf16[768,1536]{1,0:T(8,128)(2,1)S(1)} fusion(f32[768,1536]{1,0:T(8,128)S(1)} %copy-done.2, f32[768]{0:T(1024)S(1)} %get-tuple-element.11, f32[768]{0:T(1024)S(1)} %get-tuple-element.12, f32[768]{0:T(1024)S(1)} %get-tuple-element.13, f32[768]{0:T(1024)S(1)} %get-tuple-element.14, f32[768]{0:T(1024)S(1)} %get-tuple-element.15, ...), kind=kLoop, calls=%fused_computation.2 | loop fusion | flops 33030144 | bytes 7139328 | tf_op jit(solution)/shard_map/convert_element_type | solution.py:53
  122.6 0.0 copy-start.4
  122.6 1.4 copy-done.4
  124.0 0.0 copy-done.5
  124.0 2.6 %fusion.1 = f32[768,1024]{1,0:T(8,128)S(1)} fusion(bf16[768,1536]{1,0:T(8,128)(2,1)S(1)} %subtract_convert_fusion.1, bf16[1536,1024]{1,0:T(8,128)(2,1)S(1)} %copy-done.5), kind=kOutput, calls=%fused_computation.33 | convolution fusion | flops 2415919104 | bytes 8650752 | tf_op jit(solution)/shard_map/dot_general | solution.py:78
  126.6 4.0 %convolution_convert_fusion = bf16[1536,1024]{1,0:T(8,128)(2,1)} fusion(bf16[768,1536]{1,0:T(8,128)(2,1)S(1)} %subtract_convert_fusion, bf16[768,1024]{1,0:T(8,128)(2,1)S(1)} %copy-done), kind=kOutput, calls=%fused_computation.7 | convolution fusion | flops 2417491968 | bytes 7077888 | tf_op jit(solution)/shard_map/dot_general | solution.py:21
  130.7 0.5 collective-permute-start.1
  131.2 5.7 %add_convert_fusion.1 = bf16[768,1024]{1,0:T(8,128)(2,1)} fusion(f32[768,1024]{1,0:T(8,128)S(1)} %fusion.1, bf16[768,1536]{1,0:T(8,128)(2,1)S(1)} %subtract_convert_fusion, bf16[1536,1024]{1,0:T(8,128)(2,1)} %collective-permute-done), kind=kOutput, calls=%fused_computation.8 | convolution fusion | flops 2417491968 | bytes 10223616 | tf_op jit(solution)/shard_map/dot_general | solution.py:79
  136.9 0.0 reduce-scatter.2.cloned.1.call-update
  137.0 62.1 %collective-permute-done.1 = bf16[1536,1024]{1,0:T(8,128)(2,1)} collective-permute-done((bf16[1536,1024]{1,0:T(8,128)(2,1)}, bf16[1536,1024]{1,0:T(8,128)(2,1)}, u32[]{:S(2)}, u32[]{:S(2)}) %collective-permute-start.1) | collective-permute-done | bytes 3145760 | tf_op jit(solution)/shard_map/ppermute | solution.py:11
  199.1 6.2 %add_convert_fusion = bf16[1536,1024]{1,0:T(8,128)(2,1)} fusion(bf16[1536,1024]{1,0:T(8,128)(2,1)} %collective-permute-done.1, bf16[768,1536]{1,0:T(8,128)(2,1)} %copy-done.4, bf16[768,1024]{1,0:T(8,128)(2,1)S(1)} %copy-done), kind=kOutput, calls=%fused_computation | convolution fusion | flops 2420637696 | bytes 10223616 | tf_op jit(solution)/shard_map/dot_general | solution.py:21
  205.3 1.9 reduce-scatter.2.cloned.1.call-done
  (5 shorter events, 0.0 us)
Async XLA Ops:
  7.2 6.4 %copy-start = (bf16[768,1024]{1,0:T(8,128)(2,1)S(1)}, bf16[768,1024]{1,0:T(8,128)(2,1)}, u32[]{:S(2)}) copy-start(bf16[768,1024]{1,0:T(8,128)(2,1)} %param.5) | copy-start | bytes 4718596
  7.2 200.0 %reduce-scatter.2.cloned.1.call-start = ((), (), s32[]{:S(2)}) async-start(), calls=%async_computation.1 | async-start | bytes 1966080 | tf_op jit(solution)/shard_map/reduce_scatter | solution.py:76
  7.2 78.0 %collective-permute-start = (bf16[1536,1024]{1,0:T(8,128)(2,1)}, bf16[1536,1024]{1,0:T(8,128)(2,1)}, u32[]{:S(2)}, u32[]{:S(2)}) collective-permute-start(bf16[1536,1024]{1,0:T(8,128)(2,1)} %param.6), channel_id=1, source_target_pairs={{0,4},{4,8},{8,12},{12,16},{16,20},{20,24},{24,28},{28,32},{32,36}... | collective-permute-start | bytes 9437192 | tf_op jit(solution)/shard_map/ppermute | solution.py:11
  18.2 71.6 %copy-start.1 = (f32[768,1536]{1,0:T(8,128)}, f32[768,1536]{1,0:T(8,128)S(1)}, u32[]{:S(2)}) copy-start(f32[768,1536]{1,0:T(8,128)S(1)} %get-tuple-element.19) | copy-start | bytes 14155780
  89.8 2.2 %copy-start.3 = (f32[768,1536]{1,0:T(8,128)}, f32[768,1536]{1,0:T(8,128)S(1)}, u32[]{:S(2)}) copy-start(f32[768,1536]{1,0:T(8,128)S(1)} %get-tuple-element.21) | copy-start | bytes 14155780
  109.5 7.9 %copy-start.2 = (f32[768,1536]{1,0:T(8,128)S(1)}, f32[768,1536]{1,0:T(8,128)}, u32[]{:S(2)}) copy-start(f32[768,1536]{1,0:T(8,128)} %copy-done.1) | copy-start | bytes 14155780
  117.3 6.7 %copy-start.5 = (bf16[1536,1024]{1,0:T(8,128)(2,1)S(1)}, bf16[1536,1024]{1,0:T(8,128)(2,1)}, u32[]{:S(2)}) copy-start(bf16[1536,1024]{1,0:T(8,128)(2,1)} %param.6) | copy-start | bytes 9437188
  122.6 1.4 copy-start.4
  130.7 68.4 %collective-permute-start.1 = (bf16[1536,1024]{1,0:T(8,128)(2,1)}, bf16[1536,1024]{1,0:T(8,128)(2,1)}, u32[]{:S(2)}, u32[]{:S(2)}) collective-permute-start(bf16[1536,1024]{1,0:T(8,128)(2,1)} %convolution_convert_fusion), channel_id=1, source_target_pairs={{0,252},{4,0},{8,4},{12,8},{16,12},{20,16},{24,20},{28,24},{32,28}... | collective-permute-start | bytes 9437192 | tf_op jit(solution)/shard_map/ppermute | solution.py:11
Sparse Core Ops, SparseCore 0:
  137.1 70.0 reduce-scatter.1
where the time goes:
time: 217 us; the launch traced here: 214 us
  waiting for transfers between devices  130 us (60%)
  matrix products  27.8 us (13%)
  other arithmetic  17.8 us (8%)
  blocking collectives  16.5 us (8%)
  between operations  14.2 us (7%)
  local copies, waits for them, and re-layouts  4.78 us (2%)
  starting transfers between devices  2.77 us (1%)
    ppermute x2, waiting for transfers between devices, shifted(): lax.ppermute(x, axis, [(i, (i + by) % devices) for i in range(devices)])  128 us
    convert_element_type x2, other arithmetic, tile_grad(): (query_coef[:, None] * jnp.exp(scores - row_lse[:, None]) - target).astyp...  13.1 us
    dot_general x2, matrix products, grad_product(): lax.dot_general(grads, rows, (((0,), (0,)), ((), ())), preferred_element_...  10.2 us
    dot_general x2, matrix products, contract(): lax.dot_general(left_rows, right_rows, (((1,), (1,)), ((), ())), preferre...  9.21 us
    psum x1, blocking collectives, merge_rows(): whole_total = lax.psum(row_total * jnp.exp(row_top - whole_top), 'grp')  8.78 us
    pmax x1, blocking collectives, merge_rows(): whole_top = lax.pmax(row_top, 'grp')  7.76 us
    dot_general x1, matrix products, per_device(): jnp.dot(prev_grad, neighbour, preferred_element_type=jnp.float32)  5.73 us
  transfers between devices with their start and end apart: 3, of which 3 were waited for; matrix products, arithmetic and copies ran while one was open for 10% of the time, Pallas kernels for 0%

commit v1 on v0

v1 whole, which is shorter than its diff:
```python
import functools
import math

import jax
import jax.numpy as jnp
from jax import lax
from jax.experimental import pallas as pl
from jax.experimental.pallas import tpu as pltpu
from jax.sharding import PartitionSpec as P

AXES = ("blk", "grp")
LANE = 128
LOG2E = 1.4426950408889634
IN_VMEM = pl.BlockSpec(memory_space=pltpu.VMEM)
TILE = 256
ROWS = 64


def shape(dims, dtype):
    return jax.ShapeDtypeStruct(dims, dtype)


def eye(rows, cols):
    return (
        lax.broadcasted_iota(jnp.int32, (rows, cols), 0)
        == lax.broadcasted_iota(jnp.int32, (rows, cols), 1)
    )


def lanes_of(column, out, row, quarter):
    for at in range(0, quarter, LANE):
        width = min(LANE, quarter - at)
        piece = jnp.broadcast_to(column[at : at + width], (width, LANE))
        out[row : row + 1, at : at + LANE] = jnp.sum(
            jnp.where(eye(width, LANE), piece, 0.0), axis=0, keepdims=True
        )


def column_of(line, quarter):
    parts = []
    for at in range(0, quarter, LANE):
        width = min(LANE, quarter - at)
        piece = jnp.broadcast_to(line[:, at : at + LANE], (width, LANE))
        parts.append(jnp.sum(jnp.where(eye(width, LANE), piece, 0.0), axis=1, keepdims=True))
    return jnp.concatenate(parts, axis=0)


def fill_scores(scale, rows_ref, pass_ref, scores_ref, top_ref):
    top_ref[...] = jnp.full(top_ref.shape, -jnp.inf, jnp.float32)

    def step(tile, carry):
        at = pl.multiple_of(tile * TILE, TILE)
        scores = scale * lax.dot_general(
            rows_ref[...],
            pass_ref[pl.ds(at, TILE), :],
            (((1,), (1,)), ((), ())),
            preferred_element_type=jnp.float32,
        )
        scores_ref[:, pl.ds(at, TILE)] = scores
        best = top_ref[...]
        for lane in range(0, TILE, LANE):
            best = jnp.maximum(best, scores[:, lane : lane + LANE])
        top_ref[...] = best
        return carry

    lax.fori_loop(0, pass_ref.shape[0] // TILE, step, 0)


def exponentials(scores_ref, top_ref, total_ref, floor_ref=None):
    width = scores_ref.shape[1]

    def step(block, carry):
        rows = pl.ds(pl.multiple_of(block * ROWS, ROWS), ROWS)
        top = jnp.max(top_ref[rows, :], axis=1, keepdims=True)
        if floor_ref is not None:
            top = jnp.maximum(top, floor_ref[rows, :1])
        total = jnp.zeros((ROWS, LANE), jnp.float32)
        for at in range(0, width, LANE):
            value = jnp.exp2(scores_ref[rows, at : at + LANE] - top)
            scores_ref[rows, at : at + LANE] = value
            total = total + value
        top_ref[rows, :] = jnp.broadcast_to(top, (ROWS, LANE))
        total_ref[rows, :] = jnp.broadcast_to(
            jnp.sum(total, axis=1, keepdims=True), (ROWS, LANE)
        )
        return carry

    lax.fori_loop(0, scores_ref.shape[0] // ROWS, step, 0)


def own_kernel(scale, q_ref, p_ref, exp_ref, stat_ref, slot_ref, top_ref, total_ref):
    quarter = q_ref.shape[0] // 4
    group = lax.axis_index("grp")
    for slot in range(4):
        first = pl.multiple_of((group ^ slot) * quarter, quarter)
        slot_ref[slot * quarter : (slot + 1) * quarter, :] = q_ref[pl.ds(first, quarter), :]
    fill_scores(scale, slot_ref, p_ref, exp_ref, top_ref)
    exponentials(exp_ref, top_ref, total_ref)
    stat_ref[...] = jnp.zeros(stat_ref.shape, jnp.float32)
    for slot in range(4):
        rows = slice(slot * quarter, (slot + 1) * quarter)
        lanes_of(top_ref[rows, :1], stat_ref, slot, quarter)
        lanes_of(total_ref[rows, :1], stat_ref, 4 + slot, quarter)


def next_kernel(scale, slots, mine_ref, other_ref, p_ref, before_ref, *rest):
    known_ref = rest[0] if len(rest) == 7 else None
    exp_ref, stat_ref, rows_ref, top_ref, total_ref, floor_ref = rest[-6:]
    quarter = mine_ref.shape[0]
    rows_ref[:quarter, :] = mine_ref[...]
    rows_ref[quarter:, :] = other_ref[...]
    fill_scores(scale, rows_ref, p_ref, exp_ref, top_ref)
    for place, slot in enumerate(slots):
        floor_ref[place * quarter : (place + 1) * quarter, :] = jnp.broadcast_to(
            column_of(before_ref[slot : slot + 1, :], quarter), (quarter, LANE)
        )
    exponentials(exp_ref, top_ref, total_ref, floor_ref)
    if known_ref is None:
        stat_ref[...] = jnp.zeros(stat_ref.shape, jnp.float32)
    else:
        stat_ref[...] = known_ref[...]
    for place, slot in enumerate(slots):
        rows = slice(place * quarter, (place + 1) * quarter)
        lanes_of(top_ref[rows, :1], stat_ref, slot, quarter)
        lanes_of(total_ref[rows, :1], stat_ref, 4 + slot, quarter)
        stat_ref[4 + slot : 5 + slot, :] += before_ref[4 + slot : 5 + slot, :] * jnp.exp2(
            before_ref[slot : slot + 1, :] - stat_ref[slot : slot + 1, :]
        )


def target_kernel(quarter, pack_ref, target_ref):
    width = target_ref.shape[1]
    group = lax.axis_index("grp")
    steps = quarter // 32
    lane = lax.broadcasted_iota(jnp.int32, (32, LANE), 1).astype(jnp.float32)

    def step(block, carry):
        slot, inner = block // steps, block % steps
        source = pl.multiple_of((group ^ slot) * quarter + inner * 32, 32)
        pack = pack_ref[pl.ds(source, 32), :]
        ids = [jnp.broadcast_to(pack[:, k : k + 1], (32, LANE)) for k in range(8)]
        weights = [jnp.broadcast_to(pack[:, 8 + k : 9 + k], (32, LANE)) for k in range(8)]
        rows = pl.ds(pl.multiple_of(block * 32, 32), 32)
        for at in range(0, width, LANE):
            column = lane + float(at)
            value = jnp.zeros((32, LANE), jnp.float32)
            for k in range(8):
                value = jnp.where(ids[k] == column, weights[k], value)
            target_ref[rows, at : at + LANE] = value
        return carry

    lax.fori_loop(0, 4 * steps, step, 0)


def merge_stats(stat_ref, cross_ref, core_ref, both_ref, whole_ref):
    for slot in range(4):
        pairs = []
        for ref, turn in ((stat_ref, 0), (core_ref, 1), (cross_ref, 2), (both_ref, 3)):
            at = slot ^ turn
            pairs.append((ref[at : at + 1, :], ref[4 + at : 5 + at, :]))
        top = functools.reduce(jnp.maximum, [pair[0] for pair in pairs])
        total = sum(pair[1] * jnp.exp2(pair[0] - top) for pair in pairs)
        whole_ref[slot : slot + 1, :] = top
        whole_ref[4 + slot : 5 + slot, :] = total


def grad_kernel(slots, first_row, merge, *refs):
    if merge:
        exp_ref, target_ref, pack_ref, p_ref, stat_ref, cross_ref, core_ref, both_ref = refs[:8]
        grad_ref, mine_ref, other_ref, whole_ref, factor_ref = refs[8:]
        merge_stats(stat_ref, cross_ref, core_ref, both_ref, whole_ref)
    else:
        exp_ref, target_ref, pack_ref, p_ref, stat_ref, whole_ref = refs[:6]
        grad_ref, mine_ref, other_ref, factor_ref = refs[6:]
    quarter = mine_ref.shape[0]
    width = grad_ref.shape[1]
    group = lax.axis_index("grp")
    for place, slot in enumerate(slots):
        line = jnp.exp2(stat_ref[slot : slot + 1, :] - whole_ref[slot : slot + 1, :])
        line = line / whole_ref[4 + slot : 5 + slot, :]
        source = pl.multiple_of((group ^ slot) * quarter, quarter)
        factor = column_of(line, quarter) * pack_ref[pl.ds(source, quarter), 16:17]
        factor_ref[place * quarter : (place + 1) * quarter, :] = jnp.broadcast_to(
            factor, (quarter, LANE)
        )

    offset = first_row[0], first_row[1]

    def step(block, carry):
        at = pl.multiple_of(block * 32, 32)
        rows = pl.ds(at, 32)
        exp_rows = pl.ds(pl.multiple_of(at + offset[0], 32), 32)
        target_rows = pl.ds(pl.multiple_of(at + offset[1], 32), 32)
        factor = factor_ref[rows, :]
        for lane in range(0, width, LANE):
            grad_ref[rows, lane : lane + LANE] = (
                factor * exp_ref[exp_rows, lane : lane + LANE]
                - target_ref[target_rows, lane : lane + LANE]
            ).astype(jnp.bfloat16)
        return carry

    lax.fori_loop(0, grad_ref.shape[0] // 32, step, 0)
    for at in range(0, p_ref.shape[1], TILE):
        part = jnp.dot(
            grad_ref[...], p_ref[:, at : at + TILE], preferred_element_type=jnp.float32
        ).astype(jnp.bfloat16)
        mine_ref[:, at : at + TILE] = part[:quarter]
        other_ref[:, at : at + TILE] = part[quarter:]


def passage_kernel(count, *refs):
    grads, rows, out_ref = refs[:count], refs[count : 2 * count], refs[2 * count]

    def step(tile, carry):
        at = pl.multiple_of(tile * TILE, TILE)
        total = None
        for grad_ref, rows_ref in zip(grads, rows):
            part = lax.dot_general(
                grad_ref[:, pl.ds(at, TILE)],
                rows_ref[...],
                (((0,), (0,)), ((), ())),
                preferred_element_type=jnp.float32,
            )
            total = part if total is None else total + part
        out_ref[pl.ds(at, TILE), :] = total.astype(jnp.bfloat16)
        return carry

    lax.fori_loop(0, out_ref.shape[0] // TILE, step, 0)


def call(kernel, outs, ins, scratch=(), flops=0, name=None):
    size = sum(math.prod(o.shape) * o.dtype.itemsize for o in list(outs) + list(ins))
    return pl.pallas_call(
        kernel,
        out_shape=tuple(outs),
        in_specs=[IN_VMEM] * len(ins),
        out_specs=(IN_VMEM,) * len(outs),
        scratch_shapes=list(scratch),
        compiler_params=pltpu.CompilerParams(vmem_limit_bytes=16 * 2**20),
        cost_estimate=pl.CostEstimate(
            flops=int(flops), bytes_accessed=int(size), transcendentals=0
        ),
        name=name,
    )(*ins)


def per_device(queries, passages, loss_grad, teacher_logits, passage_ids):
    rows, depth = queries.shape
    width = passages.shape[0]
    quarter, half = rows // 4, rows // 2
    blocks, groups = lax.axis_size("blk"), lax.axis_size("grp")
    blk_index, grp_index = lax.axis_index("blk"), lax.axis_index("grp")
    f32, bf16 = jnp.float32, jnp.bfloat16
    score_scale = 3.0 / math.sqrt(depth)

    def along(by):
        return [
            (b * groups + g, (b + by) % blocks * groups + g)
            for b in range(blocks)
            for g in range(groups)
        ]

    def across(turn):
        return [
            (b * groups + g, b * groups + (g ^ turn))
            for b in range(blocks)
            for g in range(groups)
        ]

    def move(x, pairs):
        return lax.ppermute(x, AXES, pairs)

    def quarter_rows(slot):
        first = (grp_index ^ slot) * quarter
        return lax.dynamic_slice_in_dim(queries, first, quarter, 0)

    a_mine = move(quarter_rows(0), along(-1))
    b_mine = move(quarter_rows(2), along(-1))

    coef = score_scale * loss_grad
    weighted = coef[None, :] * jax.nn.softmax(teacher_logits, axis=0)
    same = passage_ids[:, None, :] == passage_ids[None, :, :]
    weighted = jnp.sum(jnp.where(same, weighted[None], 0.0), axis=1)

    def packed(block):
        first = (block * groups + grp_index) * width
        return jnp.concatenate(
            [
                (passage_ids - first).astype(f32),
                weighted,
                jnp.broadcast_to(coef[None, :], (8, rows)),
            ]
        )

    pack_next = move(packed((blk_index - 1 + blocks) % blocks), along(-1)).T
    pack_own = packed(blk_index).T

    a_other = move(a_mine, across(1))
    b_other = move(b_mine, across(1))

    scale = score_scale * LOG2E
    stat = shape((8, 2 * LANE), f32)
    exp_own, stat_own, q_slots = call(
        functools.partial(own_kernel, scale),
        [shape((rows, width), f32), stat, shape((rows, depth), bf16)],
        [queries, passages],
        [pltpu.VMEM((rows, LANE), f32)] * 2,
        flops=2 * rows * width * depth,
        name="own_scores",
    )
    stat_before = move(stat_own, along(-1))
    (target_own,) = call(
        functools.partial(target_kernel, quarter), [shape((rows, width), f32)], [pack_own],
        flops=rows * width * 1500, name="own_target",
    )
    (target_next,) = call(
        functools.partial(target_kernel, quarter), [shape((rows, width), f32)], [pack_next],
        flops=rows * width * 1500, name="next_target",
    )

    def next_scores(slots, mine, other, known, name):
        return call(
            functools.partial(next_kernel, scale, slots),
            [shape((half, width), f32), stat, shape((half, depth), bf16)],
            [mine, other, passages, stat_before] + known,
            [pltpu.VMEM((half, LANE), f32)] * 3,
            flops=2 * half * width * depth,
            name=name,
        )

    exp_a, stat_a, q_a = next_scores((0, 1), a_mine, a_other, [], "next_scores_a")
    exp_b, stat_next, q_b = next_scores((2, 3), b_mine, b_other, [stat_a], "next_scores_b")

    cross, core, both = (move(stat_next, across(turn)) for turn in (2, 1, 3))

    def grads(slots, offsets, exps, target, pack, stats, merge, name):
        outs = [shape((half, width), bf16)] + [shape((quarter, depth), bf16)] * 2
        return call(
            functools.partial(grad_kernel, slots, offsets, merge),
            outs + ([stat] if merge else []),
            [exps, target, pack, passages] + stats,
            [pltpu.VMEM((half, LANE), f32)],
            flops=2 * half * width * depth,
            name=name,
        )

    g_b, nb_mine, nb_other, whole_next = grads(
        (2, 3), (0, half), exp_b, target_next, pack_next, [stat_next, cross, core, both], True,
        "next_grad_b",
    )
    whole_own = move(whole_next, along(1))
    nb = (nb_mine.astype(f32) + move(nb_other, across(1)).astype(f32)).astype(bf16)
    nb_in = move(nb, across(2))
    g_a, na_mine, na_other = grads(
        (0, 1), (0, 0), exp_a, target_next, pack_next, [stat_next, whole_next], False,
        "next_grad_a",
    )
    na_in = move(na_other, across(1))
    g_ob, ob_mine, ob_other = grads(
        (2, 3), (half, half), exp_own, target_own, pack_own, [stat_own, whole_own], False,
        "own_grad_b",
    )
    ob = (ob_mine.astype(f32) + move(ob_other, across(1)).astype(f32)).astype(bf16)
    ob_in = move(ob, across(2))
    g_oa, oa_mine, oa_other = grads(
        (0, 1), (0, 0), exp_own, target_own, pack_own, [stat_own, whole_own], False,
        "own_grad_a",
    )
    oa_in = move(oa_other, across(1))
    sent = (na_mine.astype(f32) + na_in.astype(f32) + nb_in.astype(f32)).astype(bf16)
    came = move(sent, along(1))
    (passage_grad,) = call(
        functools.partial(passage_kernel, 4),
        [shape((width, depth), bf16)],
        [g_b, g_a, g_ob, g_oa, q_b, q_a, q_slots[half:], q_slots[:half]],
        flops=4 * rows * width * depth,
        name="passage_grad",
    )
    query_grad = (
        oa_mine.astype(f32) + oa_in.astype(f32) + ob_in.astype(f32) + came.astype(f32)
    ).astype(bf16)
    return query_grad, passage_grad


def solution(mesh):
    in_specs = (P("blk", None), P(("blk", "grp"), None), P("blk"), P(None, "blk"), P(None, "blk"))
    out_specs = (P(("blk", "grp"), None), P(("blk", "grp"), None))
    return jax.shard_map(
        per_device, mesh=mesh, in_specs=in_specs, out_specs=out_specs, check_vma=False
    )
```

time: 217 us -> 127 us (0.59)
  waiting for transfers between devices: 130 us -> 17.8 us
  Pallas kernels: 0 us -> 53.1 us
  matrix products: 27.8 us -> 0 us
  starting transfers between devices: 2.77 us -> 27.7 us
  blocking collectives: 16.5 us -> 0 us
  local copies, waits for them, and re-layouts: 4.78 us -> 18.3 us
  between operations: 14.2 us -> 1.01 us
  other arithmetic: 17.8 us -> 8.17 us
    ppermute x2 -> x17, waiting for transfers between devices: 128 us -> 17.8 us  [move(): return lax.ppermute(x, AXES, pairs)]
    pallas_call x0 -> x10, Pallas kernels: none -> 53.1 us  [call(): pl.pallas_call(kernel, out_shape=tuple(outs), in_specs=[IN_VMEM] * len(in...]
    dot_general x6 -> x0, matrix products: 27.8 us -> none  [the longest x2 10.2 us: grad_product(): lax.dot_general(grads, rows, (((0,), (0,)), ((), ())), preferred_element_...]
    ppermute x2 -> x17, starting transfers between devices: 2.74 us -> 27.7 us  [move(): return lax.ppermute(x, AXES, pairs)]
    convert_element_type x2 -> x5, other arithmetic: 13.1 us -> 3.18 us  [the longest x1 1.1 us: per_device(): (nb_mine.astype(f32) + move(nb_other, across(1)).astype(f32)).astype(bf16)]
    unnamed x12 -> x54, local copies, waits for them, and re-layouts: 3.61 us -> 12.5 us
    psum x1 -> x0, blocking collectives: 8.78 us -> none  [merge_rows(): whole_total = lax.psum(row_total * jnp.exp(row_top - whole_top), 'grp')]
    pmax x1 -> x0, blocking collectives: 7.76 us -> none  [merge_rows(): whole_top = lax.pmax(row_top, 'grp')]
  transfers between devices with their start and end apart: 3 -> 17, of which waited for: 3 -> 4; matrix products, arithmetic and copies ran while one was open for 10% -> 9% of each run, Pallas kernels for 0% -> 40%
where the time goes in v1:
time: 127 us; the launch traced here: 126 us
  Pallas kernels  53.1 us (42%)
  starting transfers between devices  27.7 us (22%)
  local copies, waits for them, and re-layouts  18.3 us (14%)
  waiting for transfers between devices  17.8 us (14%)
  other arithmetic  8.17 us (6%)
    pallas_call x10, Pallas kernels, call(): pl.pallas_call(kernel, out_shape=tuple(outs), in_specs=[IN_VMEM] * len(in...  53.1 us
    ppermute x17, starting transfers between devices, move(): return lax.ppermute(x, AXES, pairs)  27.7 us
    ppermute x17, waiting for transfers between devices, move(): return lax.ppermute(x, AXES, pairs)  17.8 us
    unnamed x54, local copies, waits for them, and re-layouts  12.5 us
    concatenate x2, local copies, waits for them, and re-layouts, packed(): jnp.concatenate([(passage_ids - first).astype(f32), weighted, jnp.broadca...  2.84 us
  transfers between devices with their start and end apart: 17, of which 4 were waited for; matrix products, arithmetic and copies ran while one was open for 9% of the time, Pallas kernels for 40%

profile of v1, /device:TPU:1, one launch (start us, length us, event | category | flops | bytes accessed | tf_op | source)
XLA Modules:
  0.0 126.0 jit_solution(15399245817161775969)
XLA Ops:
  0.7 2.2 %constant_dynamic-slice_fusion = (bf16[192,1024]{1,0:T(8,128)(2,1)}, bf16[192,1024]{1,0:T(8,128)(2,1)}) fusion(bf16[768,1024]{1,0:T(8,128)(2,1)} %q_ref.1, s32[]{:T(128)S(6)} %select_n.19, s32[]{:T(128)S(6)} %select_n.18), kind=kLoop, calls=%fused_computation.15 | loop fusion | bytes 1572872 | tf_op jit(solution)/shard_map/dynamic_slice | solution.py:275
  2.8 9.8 %collective-permute-start = (bf16[192,1024]{1,0:T(8,128)(2,1)}, bf16[192,1024]{1,0:T(8,128)(2,1)S(1)}, u32[]{:S(2)}, u32[]{:S(2)}) collective-permute-start(bf16[192,1024]{1,0:T(8,128)(2,1)} %get-tuple-element.49), channel_id=1, source_target_pairs={{0,252},{1,253},{2,254},{3,255},{4,0},{5,1},{6,2},{7,3},{8,4},{9,5... | collective-permute-start | bytes 1179656 | tf_op jit(solution)/shard_map/ppermute | solution.py:271
  12.6 1.9 %copy-done = bf16[1536,1024]{1,0:T(8,128)(2,1)S(1)} copy-done((bf16[1536,1024]{1,0:T(8,128)(2,1)S(1)}, bf16[1536,1024]{1,0:T(8,128)(2,1)}, u32[]{:S(2)}) %copy-start) | copy-done | bytes 3145752
  14.5 6.6 %own_scores.1 = (f32[768,1536]{1,0:T(8,128)S(1)}, f32[8,256]{1,0:T(8,128)S(1)}, bf16[768,1024]{1,0:T(8,128)(2,1)S(1)}) custom-call(bf16[768,1024]{1,0:T(8,128)(2,1)S(1)} %copy-done.11, bf16[1536,1024]{1,0:T(8,128)(2,1)S(1)} %copy-done), custom_call_target="tpu_custom_call" | custom-call | flops 2415919104 | bytes 11018240 | tf_op jit(solution)/shard_map/own_scores/pallas_call | solution.py:233
  21.1 2.1 %copy-done.2 = f32[768,1536]{1,0:T(8,128)} copy-done((f32[768,1536]{1,0:T(8,128)}, f32[768,1536]{1,0:T(8,128)S(1)}, u32[]{:S(2)}) %copy-start.2) | copy-done | bytes 4718616
  23.3 1.1 copy-done.7
  24.4 0.5 collective-permute-start.2
  24.9 0.2 collective-permute-start.3
  25.1 0.6 broadcast_multiply_fusion
  25.6 1.3 %reduce_max.9 = f32[768]{0:T(1024)} reduce(f32[8,768]{1,0:T(8,128)} %param.8, f32[]{:T(128)} %constant.35.clone.1), dimensions={0}, to_apply=%region_0.0 | reduce | flops 5376 | bytes 27652 | tf_op jit(solution)/shard_map/reduce_max | solution.py:281
  27.0 0.8 fusion
  27.7 0.7 subtract_convert_fusion.1
  28.5 0.0 collective-permute-done.mine_ref
  28.5 1.6 %collective-permute-start.1 = (bf16[192,1024]{1,0:T(8,128)(2,1)S(1)}, bf16[192,1024]{1,0:T(8,128)(2,1)}, u32[]{:S(2)}, u32[]{:S(2)}) collective-permute-start(bf16[192,1024]{1,0:T(8,128)(2,1)S(1)} %collective-permute-done.mine_ref), channel_id=1, source_target_pairs={{0,1},{1,0},{2,3},{3,2},{4,5},{5,4},{6,7},{7,6},{8,9},{9,8},{10,11... | collective-permute-start | bytes 1179656 | tf_op jit(solution)/shard_map/ppermute | solution.py:271
  30.1 4.6 %collective-permute-done.3.mine_ref = bf16[192,1024]{1,0:T(8,128)(2,1)} collective-permute-done((bf16[192,1024]{1,0:T(8,128)(2,1)}, bf16[192,1024]{1,0:T(8,128)(2,1)}, u32[]{:S(2)}, u32[]{:S(2)}) %collective-permute-start.3) | collective-permute-done | bytes 393248 | tf_op jit(solution)/shard_map/ppermute | solution.py:271
  34.8 2.1 %collective-permute-start.4 = (bf16[192,1024]{1,0:T(8,128)(2,1)}, bf16[192,1024]{1,0:T(8,128)(2,1)}, u32[]{:S(2)}, u32[]{:S(2)}) collective-permute-start(bf16[192,1024]{1,0:T(8,128)(2,1)} %collective-permute-done.3.mine_ref), channel_id=1, source_target_pairs={{0,1},{1,0},{2,3},{3,2},{4,5},{5,4},{6,7},{7,6},{8,9},{9,8},{10,11... | collective-permute-start | bytes 1179656 | tf_op jit(solution)/shard_map/ppermute | solution.py:271
  36.8 0.8 divide_multiply_fusion
  37.6 0.9 select_reduce_fusion
  38.5 0.7 mul.36
  39.1 0.7 pad_maximum_fusion.1
  39.8 1.8 %copy.18 = f32[24,768]{0,1:T(8,128)} copy(f32[24,768]{1,0:T(8,128)} %get-tuple-element.51) | data formatting | bytes 147456 | tf_op jit(solution)/shard_map/concatenate | solution.py:287
  41.6 4.4 %collective-permute-start.5 = (f32[24,768]{0,1:T(8,128)}, f32[24,768]{0,1:T(8,128)S(1)}, u32[]{:S(2)}, u32[]{:S(2)}) collective-permute-start(f32[24,768]{0,1:T(8,128)} %copy.18), channel_id=1, source_target_pairs={{0,252},{1,253},{2,254},{3,255},{4,0},{5,1},{6,2},{7,3},{8,4},{9,5... | collective-permute-start | bytes 221192 | tf_op jit(solution)/shard_map/ppermute | solution.py:271
  46.0 0.0 collective-permute-done.4.other_ref
  46.0 5.8 %next_scores_a.1 = (f32[384,1536]{1,0:T(8,128)S(1)}, f32[8,256]{1,0:T(8,128)S(1)}, bf16[384,1024]{1,0:T(8,128)(2,1)S(1)}) custom-call(bf16[192,1024]{1,0:T(8,128)(2,1)} %collective-permute-done.3.mine_ref, bf16[192,1024]{1,0:T(8,128)(2,1)} %collective-permute-done.4.other_ref, bf16[1536,1024]{1,0:T(8,128)(2,1)S(1)} %copy-done.1, ...), custom_call_target="tpu_custom_call" | custom-call | flops 1207959552 | bytes 7094272 | tf_op jit(solution)/shard_map/next_scores_a/pallas_call | solution.py:233
  51.8 0.0 copy-start.5
  51.9 1.4 %copy-done.5 = f32[384,1536]{1,0:T(8,128)} copy-done((f32[384,1536]{1,0:T(8,128)}, f32[384,1536]{1,0:T(8,128)S(1)}, u32[]{:S(2)}) %copy-start.5) | copy-done | bytes 2359320
  53.3 0.9 copy-done.22
  54.2 0.0 collective-permute-done.1.other_ref
  54.2 0.7 copy-done.19
  54.9 5.7 %next_scores_b.1 = (f32[384,1536]{1,0:T(8,128)S(1)}, f32[8,256]{1,0:T(8,128)S(1)}, bf16[384,1024]{1,0:T(8,128)(2,1)S(1)}) custom-call(bf16[192,1024]{1,0:T(8,128)(2,1)S(1)} %collective-permute-done.mine_ref, bf16[192,1024]{1,0:T(8,128)(2,1)} %collective-permute-done.1.other_ref, bf16[1536,1024]{1,0:T(8,128)(2,1)S(1)} %copy-done.1, f32[8,256]{1,0:T(8,128)S(1)} %copy-done.19, ...), custom_call_target="tpu_custom_call" | custom-call | flops 1207959552 | bytes 7102464 | tf_op jit(solution)/shard_map/next_scores_b/pallas_call | solution.py:233
  60.6 2.5 %collective-permute-start.6 = (f32[8,256]{1,0:T(8,128)S(1)}, f32[8,256]{1,0:T(8,128)S(1)}, u32[]{:S(2)}, u32[]{:S(2)}) collective-permute-start(f32[8,256]{1,0:T(8,128)S(1)} %get-tuple-element.28.refs_4_), channel_id=1, source_target_pairs={{0,2},{1,3},{2,0},{3,1},{4,6},{5,7},{6,4},{7,5},{8,10},{9,11},{10,... | collective-permute-start | bytes 24584 | tf_op jit(solution)/shard_map/ppermute | solution.py:271
  63.1 0.6 collective-permute-start.7
  63.7 0.4 collective-permute-start.8
  64.1 0.0 collective-permute-done.5
  64.1 8.1 %next_target.1.refs_1_ = f32[768,1536]{1,0:T(8,128)S(1)} custom-call(f32[768,24]{1,0:T(8,128)S(1)} %bitcast.7), custom_call_target="tpu_custom_call" | custom-call | flops 1769472000 | bytes 4792320 | tf_op jit(solution)/shard_map/next_target/pallas_call | solution.py:233
  72.2 0.0 collective-permute-done.6.refs_5_
  72.3 2.9 %next_grad_b.1 = (bf16[384,1536]{1,0:T(8,128)(2,1)S(1)}, bf16[192,1024]{1,0:T(8,128)(2,1)S(1)}, bf16[192,1024]{1,0:T(8,128)(2,1)}, f32[8,256]{1,0:T(8,128)S(1)}) custom-call(f32[384,1536]{1,0:T(8,128)S(1)} %get-tuple-element.27.refs_0_, f32[768,1536]{1,0:T(8,128)S(1)} %next_target.1.refs_1_, f32[768,24]{1,0:T(8,128)S(1)} %bitcast.8, ...), custom_call_target="tpu_custom_call" | custom-call | flops 1207959552 | bytes 12304384 | tf_op jit(solution)/shard_map/next_grad_b/pallas_call | solution.py:233
  75.2 0.7 copy-done.12
  75.9 0.6 copy-done.14
  76.5 1.1 copy-done.16
  77.6 0.5 collective-permute-start.14
  78.1 1.0 copy.17
  79.2 8.1 %own_target.1.refs_1_ = f32[768,1536]{1,0:T(8,128)S(1)} custom-call(f32[768,24]{1,0:T(8,128)S(1)} %bitcast.4), custom_call_target="tpu_custom_call" | custom-call | flops 1769472000 | bytes 4792320 | tf_op jit(solution)/shard_map/own_target/pallas_call | solution.py:233
  87.3 0.3 collective-permute-start.9
  87.6 0.0 copy-start.6
  87.6 1.8 %copy-done.6 = f32[384,1536]{1,0:T(8,128)S(1)} copy-done((f32[384,1536]{1,0:T(8,128)S(1)}, f32[384,1536]{1,0:T(8,128)}, u32[]{:S(2)}) %copy-start.6) | copy-done | bytes 2359320
  89.4 2.1 %next_grad_a.1 = (bf16[384,1536]{1,0:T(8,128)(2,1)S(1)}, bf16[192,1024]{1,0:T(8,128)(2,1)S(1)}, bf16[192,1024]{1,0:T(8,128)(2,1)S(1)}) custom-call(f32[384,1536]{1,0:T(8,128)S(1)} %copy-done.6, f32[768,1536]{1,0:T(8,128)S(1)} %copy-done.4, f32[768,24]{1,0:T(8,128)S(1)} %bitcast.9, bf16[1536,1024]{1,0:T(8,128)(2,1)S(1)} %copy-done.1, ...), custom_call_target="tpu_custom_call" | custom-call | flops 1207959552 | bytes 12279808 | tf_op jit(solution)/shard_map/next_grad_a/pallas_call | solution.py:233
  91.5 0.1 collective-permute-start.13
  91.6 2.7 %collective-permute-done.9.refs_5_ = f32[8,256]{1,0:T(8,128)S(1)} collective-permute-done((f32[8,256]{1,0:T(8,128)S(1)}, f32[8,256]{1,0:T(8,128)S(1)}, u32[]{:S(2)}, u32[]{:S(2)}) %collective-permute-start.9) | collective-permute-done | bytes 8224 | tf_op jit(solution)/shard_map/ppermute | solution.py:271
  94.3 2.2 %own_grad_b.1 = (bf16[384,1536]{1,0:T(8,128)(2,1)S(1)}, bf16[192,1024]{1,0:T(8,128)(2,1)S(1)}, bf16[192,1024]{1,0:T(8,128)(2,1)S(1)}) custom-call(f32[768,1536]{1,0:T(8,128)S(1)} %bitcast.3, f32[768,1536]{1,0:T(8,128)S(1)} %own_target.1.refs_1_, f32[768,24]{1,0:T(8,128)S(1)} %bitcast.5, bf16[1536,1024]{1,0:T(8,128)(2,1)S(1)} %copy-done.1, ...), custom_call_target="tpu_custom_call" | custom-call | flops 1207959552 | bytes 14639104 | tf_op jit(solution)/shard_map/own_grad_b/pallas_call | solution.py:233
  96.5 1.2 collective-permute-start.11
  97.7 1.1 add_convert_fusion.2
  98.8 2.6 %collective-permute-start.15 = (bf16[192,1024]{1,0:T(8,128)(2,1)S(1)}, bf16[192,1024]{1,0:T(8,128)(2,1)S(1)}, u32[]{:S(2)}, u32[]{:S(2)}) collective-permute-start(bf16[192,1024]{1,0:T(8,128)(2,1)S(1)} %add_convert_fusion.2), channel_id=1, source_target_pairs={{0,2},{1,3},{2,0},{3,1},{4,6},{5,7},{6,4},{7,5},{8,10},{9,11},{10,... | collective-permute-start | bytes 1179656 | tf_op jit(solution)/shard_map/ppermute | solution.py:271
  101.4 0.1 fusion.1
  101.5 2.2 %own_grad_a.1 = (bf16[384,1536]{1,0:T(8,128)(2,1)S(1)}, bf16[192,1024]{1,0:T(8,128)(2,1)S(1)}, bf16[192,1024]{1,0:T(8,128)(2,1)S(1)}) custom-call(f32[768,1536]{1,0:T(8,128)S(1)} %bitcast.3, f32[768,1536]{1,0:T(8,128)S(1)} %own_target.1.refs_1_, f32[768,24]{1,0:T(8,128)S(1)} %bitcast.6, bf16[1536,1024]{1,0:T(8,128)(2,1)S(1)} %copy-done.1, ...), custom_call_target="tpu_custom_call" | custom-call | flops 1207959552 | bytes 14639104 | tf_op jit(solution)/shard_map/own_grad_a/pallas_call | solution.py:233
  103.8 0.4 collective-permute-start.10
  104.2 0.1 add_convert_fusion.3
  104.3 0.6 collective-permute-start.12
  104.9 6.3 %collective-permute-done.15 = bf16[192,1024]{1,0:T(8,128)(2,1)S(1)} collective-permute-done((bf16[192,1024]{1,0:T(8,128)(2,1)S(1)}, bf16[192,1024]{1,0:T(8,128)(2,1)S(1)}, u32[]{:S(2)}, u32[]{:S(2)}) %collective-permute-start.15) | collective-permute-done | bytes 393248 | tf_op jit(solution)/shard_map/ppermute | solution.py:271
  111.1 0.2 add_convert_fusion.1
  111.3 0.1 collective-permute-start.16
  111.5 9.4 %passage_grad.1 = bf16[1536,1024]{1,0:T(8,128)(2,1)} custom-call(bf16[384,1536]{1,0:T(8,128)(2,1)S(1)} %copy-done.17, bf16[384,1536]{1,0:T(8,128)(2,1)S(1)} %get-tuple-element.40.refs_1_, bf16[384,1536]{1,0:T(8,128)(2,1)S(1)} %get-tuple-element.41.refs_2_, bf16[384,1536]{1,0:T(8,128)(2,1)S(1)} %get-tuple-element.42.refs_3_, ...), custom_call_target="tpu_custom_call" | custom-call | flops 4831838208 | bytes 11010048 | tf_op jit(solution)/shard_map/passage_grad/pallas_call | solution.py:233
  120.9 4.2 %collective-permute-done.16 = bf16[192,1024]{1,0:T(8,128)(2,1)S(1)} collective-permute-done((bf16[192,1024]{1,0:T(8,128)(2,1)S(1)}, bf16[192,1024]{1,0:T(8,128)(2,1)S(1)}, u32[]{:S(2)}, u32[]{:S(2)}) %collective-permute-start.16) | collective-permute-done | bytes 393248 | tf_op jit(solution)/shard_map/ppermute | solution.py:271
  125.0 1.0 add_convert_fusion
  (51 shorter events, 0.1 us)
Async XLA Ops:
  0.6 12.0 %copy-start.11 = (bf16[768,1024]{1,0:T(8,128)(2,1)S(1)}, bf16[768,1024]{1,0:T(8,128)(2,1)}, u32[]{:S(2)}) copy-start(bf16[768,1024]{1,0:T(8,128)(2,1)} %q_ref.1) | copy-start | bytes 4718596
  2.8 25.7 %collective-permute-start = (bf16[192,1024]{1,0:T(8,128)(2,1)}, bf16[192,1024]{1,0:T(8,128)(2,1)S(1)}, u32[]{:S(2)}, u32[]{:S(2)}) collective-permute-start(bf16[192,1024]{1,0:T(8,128)(2,1)} %get-tuple-element.49), channel_id=1, source_target_pairs={{0,252},{1,253},{2,254},{3,255},{4,0},{5,1},{6,2},{7,3},{8,4},{9,5... | collective-permute-start | bytes 1179656 | tf_op jit(solution)/shard_map/ppermute | solution.py:271
  12.6 1.9 %copy-start = (bf16[1536,1024]{1,0:T(8,128)(2,1)S(1)}, bf16[1536,1024]{1,0:T(8,128)(2,1)}, u32[]{:S(2)}) copy-start(bf16[1536,1024]{1,0:T(8,128)(2,1)} %refs_3_.7) | copy-start | bytes 9437188
  14.5 10.6 %copy-start.24 = (f32[768]{0:T(1024)S(1)}, f32[768]{0:T(1024)}, u32[]{:S(2)}) copy-start(f32[768]{0:T(1024)} %param.7) | copy-start | bytes 9220
  14.5 31.5 %copy-start.1 = (bf16[1536,1024]{1,0:T(8,128)(2,1)S(1)}, bf16[1536,1024]{1,0:T(8,128)(2,1)}, u32[]{:S(2)}) copy-start(bf16[1536,1024]{1,0:T(8,128)(2,1)} %refs_3_.7) | copy-start | bytes 9437188
  21.1 2.1 %copy-start.2 = (f32[768,1536]{1,0:T(8,128)}, f32[768,1536]{1,0:T(8,128)S(1)}, u32[]{:S(2)}) copy-start(f32[768,1536]{1,0:T(8,128)S(1)} %get-tuple-element.24.refs_0_) | copy-start | bytes 14155780
  23.3 1.1 copy-start.7
  24.4 21.6 %collective-permute-start.2 = (f32[8,256]{1,0:T(8,128)S(1)}, f32[8,256]{1,0:T(8,128)S(1)}, u32[]{:S(2)}, u32[]{:S(2)}) collective-permute-start(f32[8,256]{1,0:T(8,128)S(1)} %get-tuple-element.25.refs_4_), channel_id=1, source_target_pairs={{0,252},{1,253},{2,254},{3,255},{4,0},{5,1},{6,2},{7,3},{8,4},{9,5... | collective-permute-start | bytes 24584 | tf_op jit(solution)/shard_map/ppermute | solution.py:271
  24.9 9.9 %collective-permute-start.3 = (bf16[192,1024]{1,0:T(8,128)(2,1)}, bf16[192,1024]{1,0:T(8,128)(2,1)}, u32[]{:S(2)}, u32[]{:S(2)}) collective-permute-start(bf16[192,1024]{1,0:T(8,128)(2,1)} %get-tuple-element.48), channel_id=1, source_target_pairs={{0,252},{1,253},{2,254},{3,255},{4,0},{5,1},{6,2},{7,3},{8,4},{9,5... | collective-permute-start | bytes 1179656 | tf_op jit(solution)/shard_map/ppermute | solution.py:271
  28.5 25.7 %collective-permute-start.1 = (bf16[192,1024]{1,0:T(8,128)(2,1)S(1)}, bf16[192,1024]{1,0:T(8,128)(2,1)}, u32[]{:S(2)}, u32[]{:S(2)}) collective-permute-start(bf16[192,1024]{1,0:T(8,128)(2,1)S(1)} %collective-permute-done.mine_ref), channel_id=1, source_target_pairs={{0,1},{1,0},{2,3},{3,2},{4,5},{5,4},{6,7},{7,6},{8,9},{9,8},{10,11... | collective-permute-start | bytes 1179656 | tf_op jit(solution)/shard_map/ppermute | solution.py:271
  34.8 11.2 %collective-permute-start.4 = (bf16[192,1024]{1,0:T(8,128)(2,1)}, bf16[192,1024]{1,0:T(8,128)(2,1)}, u32[]{:S(2)}, u32[]{:S(2)}) collective-permute-start(bf16[192,1024]{1,0:T(8,128)(2,1)} %collective-permute-done.3.mine_ref), channel_id=1, source_target_pairs={{0,1},{1,0},{2,3},{3,2},{4,5},{5,4},{6,7},{7,6},{8,9},{9,8},{10,11... | collective-permute-start | bytes 1179656 | tf_op jit(solution)/shard_map/ppermute | solution.py:271
  41.6 22.5 %collective-permute-start.5 = (f32[24,768]{0,1:T(8,128)}, f32[24,768]{0,1:T(8,128)S(1)}, u32[]{:S(2)}, u32[]{:S(2)}) collective-permute-start(f32[24,768]{0,1:T(8,128)} %copy.18), channel_id=1, source_target_pairs={{0,252},{1,253},{2,254},{3,255},{4,0},{5,1},{6,2},{7,3},{8,4},{9,5... | collective-permute-start | bytes 221192 | tf_op jit(solution)/shard_map/ppermute | solution.py:271
  46.0 5.8 %copy-start.18 = (f32[8,256]{1,0:T(8,128)}, f32[8,256]{1,0:T(8,128)S(1)}, u32[]{:S(2)}) copy-start(f32[8,256]{1,0:T(8,128)S(1)} %collective-permute-done.2.before_ref) | copy-start | bytes 24580
  51.8 1.4 %copy-start.5 = (f32[384,1536]{1,0:T(8,128)}, f32[384,1536]{1,0:T(8,128)S(1)}, u32[]{:S(2)}) copy-start(f32[384,1536]{1,0:T(8,128)S(1)} %get-tuple-element.34.refs_0_) | copy-start | bytes 7077892
  53.3 0.9 copy-start.22
  54.2 0.7 copy-start.19
  60.6 11.6 %copy-start.20 = (bf16[384,1024]{1,0:T(8,128)(2,1)}, bf16[384,1024]{1,0:T(8,128)(2,1)S(1)}, u32[]{:S(2)}) copy-start(bf16[384,1024]{1,0:T(8,128)(2,1)S(1)} %get-tuple-element.43.refs_4_) | copy-start | bytes 2359300
  60.6 11.6 %collective-permute-start.6 = (f32[8,256]{1,0:T(8,128)S(1)}, f32[8,256]{1,0:T(8,128)S(1)}, u32[]{:S(2)}, u32[]{:S(2)}) collective-permute-start(f32[8,256]{1,0:T(8,128)S(1)} %get-tuple-element.28.refs_4_), channel_id=1, source_target_pairs={{0,2},{1,3},{2,0},{3,1},{4,6},{5,7},{6,4},{7,5},{8,10},{9,11},{10,... | collective-permute-start | bytes 24584 | tf_op jit(solution)/shard_map/ppermute | solution.py:271
  63.1 9.1 %collective-permute-start.7 = (f32[8,256]{1,0:T(8,128)S(1)}, f32[8,256]{1,0:T(8,128)S(1)}, u32[]{:S(2)}, u32[]{:S(2)}) collective-permute-start(f32[8,256]{1,0:T(8,128)S(1)} %get-tuple-element.28.refs_4_), channel_id=1, source_target_pairs={{0,1},{1,0},{2,3},{3,2},{4,5},{5,4},{6,7},{7,6},{8,9},{9,8},{10,11... | collective-permute-start | bytes 24584 | tf_op jit(solution)/shard_map/ppermute | solution.py:271
  63.7 8.5 %collective-permute-start.8 = (f32[8,256]{1,0:T(8,128)S(1)}, f32[8,256]{1,0:T(8,128)S(1)}, u32[]{:S(2)}, u32[]{:S(2)}) collective-permute-start(f32[8,256]{1,0:T(8,128)S(1)} %get-tuple-element.28.refs_4_), channel_id=1, source_target_pairs={{0,3},{1,2},{2,1},{3,0},{4,7},{5,6},{6,5},{7,4},{8,11},{9,10},{10,... | collective-permute-start | bytes 24584 | tf_op jit(solution)/shard_map/ppermute | solution.py:271
  64.1 8.2 %copy-start.9 = (f32[24,768]{0,1:T(8,128)}, f32[24,768]{0,1:T(8,128)S(1)}, u32[]{:S(2)}) copy-start(f32[24,768]{0,1:T(8,128)S(1)} %collective-permute-done.5) | copy-start | bytes 221188
  72.2 2.9 %copy-start.3 = (f32[768,1536]{1,0:T(8,128)}, f32[768,1536]{1,0:T(8,128)S(1)}, u32[]{:S(2)}) copy-start(f32[768,1536]{1,0:T(8,128)S(1)} %next_target.1.refs_1_) | copy-start | bytes 14155780
  75.2 0.7 copy-start.12
  75.9 0.6 copy-start.14
  76.5 1.1 copy-start.16
  77.6 20.2 %collective-permute-start.14 = (bf16[192,1024]{1,0:T(8,128)(2,1)}, bf16[192,1024]{1,0:T(8,128)(2,1)}, u32[]{:S(2)}, u32[]{:S(2)}) collective-permute-start(bf16[192,1024]{1,0:T(8,128)(2,1)} %get-tuple-element.38), channel_id=1, source_target_pairs={{0,1},{1,0},{2,3},{3,2},{4,5},{5,4},{6,7},{7,6},{8,9},{9,8},{10,11... | collective-permute-start | bytes 1179656 | tf_op jit(solution)/shard_map/ppermute | solution.py:271
  79.1 8.2 %copy-start.15 = (f32[8,256]{1,0:T(8,128)S(1)}, f32[8,256]{1,0:T(8,128)}, u32[]{:S(2)}) copy-start(f32[8,256]{1,0:T(8,128)} %copy-done.14) | copy-start | bytes 24580
  79.1 8.4 %copy-start.4 = (f32[768,1536]{1,0:T(8,128)S(1)}, f32[768,1536]{1,0:T(8,128)}, u32[]{:S(2)}) copy-start(f32[768,1536]{1,0:T(8,128)} %copy-done.3) | copy-start | bytes 14155780
  79.1 8.4 %copy-start.10 = (f32[24,768]{0,1:T(8,128)S(1)}, f32[24,768]{0,1:T(8,128)}, u32[]{:S(2)}) copy-start(f32[24,768]{0,1:T(8,128)} %copy-done.9) | copy-start | bytes 221188
  87.3 7.0 %collective-permute-start.9 = (f32[8,256]{1,0:T(8,128)S(1)}, f32[8,256]{1,0:T(8,128)S(1)}, u32[]{:S(2)}, u32[]{:S(2)}) collective-permute-start(f32[8,256]{1,0:T(8,128)S(1)} %copy-done.15), channel_id=1, source_target_pairs={{0,4},{1,5},{2,6},{3,7},{4,8},{5,9},{6,10},{7,11},{8,12},{9,13},{1... | collective-permute-start | bytes 24584 | tf_op jit(solution)/shard_map/ppermute | solution.py:271
  87.6 6.7 %slice-start = ((s8[4718592]{0:T(1024)(128)(4,1)}), s8[4194304]{0:T(1024)(128)(4,1)S(1)}, s32[]{:S(2)}) async-start(s8[4718592]{0:T(1024)(128)(4,1)} %bitcast.2), calls=%async_computation | async-start | bytes 8388608
  87.6 1.8 %copy-start.6 = (f32[384,1536]{1,0:T(8,128)S(1)}, f32[384,1536]{1,0:T(8,128)}, u32[]{:S(2)}) copy-start(f32[384,1536]{1,0:T(8,128)} %copy-done.5) | copy-start | bytes 7077892
  89.4 4.9 %slice-start.1 = ((s8[4718592]{0:T(1024)(128)(4,1)}), s8[524288]{0:T(1024)(128)(4,1)S(1)}, s32[]{:S(2)}) async-start(s8[4718592]{0:T(1024)(128)(4,1)} %bitcast.2), calls=%async_computation.1 | async-start | bytes 1048576
  91.5 13.4 %collective-permute-start.13 = (bf16[192,1024]{1,0:T(8,128)(2,1)S(1)}, bf16[192,1024]{1,0:T(8,128)(2,1)S(1)}, u32[]{:S(2)}, u32[]{:S(2)}) collective-permute-start(bf16[192,1024]{1,0:T(8,128)(2,1)S(1)} %get-tuple-element.36), channel_id=1, source_target_pairs={{0,1},{1,0},{2,3},{3,2},{4,5},{5,4},{6,7},{7,6},{8,9},{9,8},{10,11... | collective-permute-start | bytes 1179656 | tf_op jit(solution)/shard_map/ppermute | solution.py:271
  94.3 3.5 %copy-start.13 = (bf16[192,1024]{1,0:T(8,128)(2,1)S(1)}, bf16[192,1024]{1,0:T(8,128)(2,1)}, u32[]{:S(2)}) copy-start(bf16[192,1024]{1,0:T(8,128)(2,1)} %copy-done.12) | copy-start | bytes 1179652
  94.3 7.1 %copy-start.8 = (bf16[768,1024]{1,0:T(8,128)(2,1)S(1)}, bf16[768,1024]{1,0:T(8,128)(2,1)}, u32[]{:S(2)}) copy-start(bf16[768,1024]{1,0:T(8,128)(2,1)} %copy-done.7) | copy-start | bytes 4718596
  96.5 7.7 %collective-permute-start.11 = (bf16[192,1024]{1,0:T(8,128)(2,1)S(1)}, bf16[192,1024]{1,0:T(8,128)(2,1)S(1)}, u32[]{:S(2)}, u32[]{:S(2)}) collective-permute-start(bf16[192,1024]{1,0:T(8,128)(2,1)S(1)} %get-tuple-element.33), channel_id=1, source_target_pairs={{0,1},{1,0},{2,3},{3,2},{4,5},{5,4},{6,7},{7,6},{8,9},{9,8},{10,11... | collective-permute-start | bytes 1179656 | tf_op jit(solution)/shard_map/ppermute | solution.py:271
  98.8 12.3 %collective-permute-start.15 = (bf16[192,1024]{1,0:T(8,128)(2,1)S(1)}, bf16[192,1024]{1,0:T(8,128)(2,1)S(1)}, u32[]{:S(2)}, u32[]{:S(2)}) collective-permute-start(bf16[192,1024]{1,0:T(8,128)(2,1)S(1)} %add_convert_fusion.2), channel_id=1, source_target_pairs={{0,2},{1,3},{2,0},{3,1},{4,6},{5,7},{6,4},{7,5},{8,10},{9,11},{10,... | collective-permute-start | bytes 1179656 | tf_op jit(solution)/shard_map/ppermute | solution.py:271
  103.7 7.7 %copy-start.17 = (bf16[384,1536]{1,0:T(8,128)(2,1)S(1)}, bf16[384,1536]{1,0:T(8,128)(2,1)}, u32[]{:S(2)}) copy-start(bf16[384,1536]{1,0:T(8,128)(2,1)} %copy-done.16) | copy-start | bytes 3538948
  103.7 7.7 %copy-start.21 = (bf16[384,1024]{1,0:T(8,128)(2,1)S(1)}, bf16[384,1024]{1,0:T(8,128)(2,1)}, u32[]{:S(2)}) copy-start(bf16[384,1024]{1,0:T(8,128)(2,1)} %copy-done.20) | copy-start | bytes 2359300
  103.7 7.7 %copy-start.23 = (bf16[384,1024]{1,0:T(8,128)(2,1)S(1)}, bf16[384,1024]{1,0:T(8,128)(2,1)}, u32[]{:S(2)}) copy-start(bf16[384,1024]{1,0:T(8,128)(2,1)} %copy-done.22) | copy-start | bytes 2359300
  103.8 17.1 %collective-permute-start.10 = (bf16[192,1024]{1,0:T(8,128)(2,1)S(1)}, bf16[192,1024]{1,0:T(8,128)(2,1)S(1)}, u32[]{:S(2)}, u32[]{:S(2)}) collective-permute-start(bf16[192,1024]{1,0:T(8,128)(2,1)S(1)} %get-tuple-element.31), channel_id=1, source_target_pairs={{0,1},{1,0},{2,3},{3,2},{4,5},{5,4},{6,7},{7,6},{8,9},{9,8},{10,11... | collective-permute-start | bytes 1179656 | tf_op jit(solution)/shard_map/ppermute | solution.py:271
  104.3 16.6 %collective-permute-start.12 = (bf16[192,1024]{1,0:T(8,128)(2,1)S(1)}, bf16[192,1024]{1,0:T(8,128)(2,1)S(1)}, u32[]{:S(2)}, u32[]{:S(2)}) collective-permute-start(bf16[192,1024]{1,0:T(8,128)(2,1)S(1)} %add_convert_fusion.3), channel_id=1, source_target_pairs={{0,2},{1,3},{2,0},{3,1},{4,6},{5,7},{6,4},{7,5},{8,10},{9,11},{10,... | collective-permute-start | bytes 1179656 | tf_op jit(solution)/shard_map/ppermute | solution.py:271
  111.3 13.7 %collective-permute-start.16 = (bf16[192,1024]{1,0:T(8,128)(2,1)S(1)}, bf16[192,1024]{1,0:T(8,128)(2,1)S(1)}, u32[]{:S(2)}, u32[]{:S(2)}) collective-permute-start(bf16[192,1024]{1,0:T(8,128)(2,1)S(1)} %add_convert_fusion.1), channel_id=1, source_target_pairs={{0,4},{1,5},{2,6},{3,7},{4,8},{5,9},{6,10},{7,11},{8,12},{9,13},{1... | collective-permute-start | bytes 1179656 | tf_op jit(solution)/shard_map/ppermute | solution.py:271

commit v2 on v0

v2 whole, which is shorter than its diff:
```python
import functools
import math

import jax
import jax.numpy as jnp
from jax import lax
from jax.experimental import pallas as pl
from jax.experimental.pallas import tpu as pltpu
from jax.sharding import PartitionSpec as P

AXES = ("blk", "grp")
LANE = 128
LOG2E = 1.4426950408889634
IN_VMEM = pl.BlockSpec(memory_space=pltpu.VMEM)
TILE = 256
ROWS = 64
FEW = 4


def shape(dims, dtype):
    return jax.ShapeDtypeStruct(dims, dtype)


def reorder(x, group):
    half = x.shape[1] // 2
    parts = [x[:, :half], x[:, half:]]
    parts = [jnp.where(group % 2 == 1, pltpu.roll(part, half // 2, 1), part) for part in parts]
    swap = group >= 2
    return jnp.concatenate(
        [jnp.where(swap, parts[1], parts[0]), jnp.where(swap, parts[0], parts[1])], axis=1
    )


def fill_scores(scale, p_ref, q_ref, out_ref):
    for at in range(0, q_ref.shape[0], TILE):
        to = min(at + TILE, q_ref.shape[0])
        out_ref[:, at:to] = scale * lax.dot_general(
            p_ref[...], q_ref[at:to, :], (((1,), (1,)), ((), ())),
            preferred_element_type=jnp.float32,
        )


def exponentials(ref, floor=None):
    rows, cols = ref.shape
    fold = (ROWS // 8, 8, cols)

    def find(block, top):
        at = pl.multiple_of(block * ROWS, ROWS)
        return jnp.maximum(top, jnp.max(ref[pl.ds(at, ROWS), :].reshape(fold), axis=0))

    top = lax.fori_loop(0, rows // ROWS, find, jnp.full((8, cols), -jnp.inf, jnp.float32))
    top = jnp.max(top, axis=0, keepdims=True)
    if floor is not None:
        top = jnp.maximum(top, floor)

    def raised(block, total):
        at = pl.multiple_of(block * ROWS, ROWS)
        value = jnp.exp2(ref[pl.ds(at, ROWS), :] - top)
        ref[pl.ds(at, ROWS), :] = value
        return total + jnp.sum(value.reshape(fold), axis=0)

    total = lax.fori_loop(0, rows // ROWS, raised, jnp.zeros((8, cols), jnp.float32))
    return top, jnp.sum(total, axis=0, keepdims=True)


def own_kernel(scale, q_ref, p_ref, exp_ref, stat_ref):
    fill_scores(scale, p_ref, q_ref, exp_ref)
    top, total = exponentials(exp_ref)
    stat_ref[0:1, :] = top
    stat_ref[1:2, :] = total


def next_kernel(scale, *refs):
    pieces, p_ref, before_ref, exp_ref, stat_ref, rows_ref = refs[:6], *refs[6:]
    first_mine, first_other, cross_mine, cross_other, rest_mine, rest_other = pieces
    cut, left = first_mine.shape[0], rest_mine.shape[0] // 2
    at = 0
    for lead, rest, skip in (
        (first_mine, rest_mine, 0),
        (first_other, rest_other, 0),
        (cross_mine, rest_mine, left),
        (cross_other, rest_other, left),
    ):
        rows_ref[at : at + cut, :] = lead[...]
        rows_ref[at + cut : at + cut + left, :] = rest[skip : skip + left, :]
        at += cut + left
    fill_scores(scale, p_ref, rows_ref, exp_ref)
    before = reorder(before_ref[...], lax.axis_index("grp"))
    top, total = exponentials(exp_ref, before[0:1])
    stat_ref[0:1, :] = top
    stat_ref[1:2, :] = total + before[1:2] * jnp.exp2(before[0:1] - top)


def pack_kernel(width, ids_ref, logits_ref, coef_ref, own_ref, next_ref):
    device = lax.axis_index("blk") * 4 + lax.axis_index("grp")
    blocks = lax.axis_size("blk")
    before = (lax.axis_index("blk") + blocks - 1) % blocks * 4 + lax.axis_index("grp")
    ids = ids_ref[...]
    logits = logits_ref[...]
    power = jnp.exp(logits - jnp.max(logits, axis=0, keepdims=True))
    weights = coef_ref[...] * (power / jnp.sum(power, axis=0, keepdims=True))
    summed = jnp.zeros_like(weights)
    for k in range(8):
        summed = summed + jnp.where(ids == ids[k : k + 1], weights[k : k + 1], 0.0)
    for ref, at in ((own_ref, device), (next_ref, before)):
        place = ids - at * width
        inside = (place >= 0) & (place < width)
        places, count = [-1.0] * 8, jnp.zeros_like(coef_ref[...])
        values = [0.0] * 8
        for k in range(8):
            here = inside[k : k + 1]
            for r in range(k + 1):
                chosen = here & (count == r)
                places[r] = jnp.where(chosen, place[k : k + 1].astype(jnp.float32), places[r])
                values[r] = jnp.where(chosen, summed[k : k + 1], values[r])
            count = count + here.astype(jnp.float32)
        for r in range(8):
            ref[r : r + 1, :] = places[r]
            ref[8 + r : 9 + r, :] = values[r]
        ref[16:24, :] = jnp.broadcast_to(coef_ref[...], ids.shape)


def merge_stats(stat, cross, core, both):
    half = stat.shape[1] // 2
    quarter = half // 2

    def turned(x):
        return jnp.concatenate(
            [pltpu.roll(x[:, :half], quarter, 1), pltpu.roll(x[:, half:], quarter, 1)], axis=1
        )

    def crossed(x):
        return jnp.concatenate([x[:, half:], x[:, :half]], axis=1)

    parts = (stat, turned(core), crossed(cross), crossed(turned(both)))
    top = functools.reduce(jnp.maximum, [part[0:1] for part in parts])
    return top, sum(part[1:2] * jnp.exp2(part[0:1] - top) for part in parts)


def fill_grads(exp_ref, grad_ref, factor, ids, weights):
    rows, cols = exp_ref.shape
    lead = lax.broadcasted_iota(jnp.int32, (16, cols), 0)

    def fill(count):
        def step(block, carry):
            at = pl.multiple_of(block * 16, 16)
            place = (lead + block * 16).astype(jnp.float32)
            value = jnp.zeros((16, cols), jnp.float32)
            for k in range(count):
                value = jnp.where(ids[k : k + 1] == place, weights[k : k + 1], value)
            grad_ref[pl.ds(at, 16), :] = (factor * exp_ref[pl.ds(at, 16), :] - value).astype(
                jnp.bfloat16
            )
            return carry

        return step

    lax.fori_loop(0, rows // 16, fill(FEW), 0)
    more = ids[FEW:]
    low = jnp.min(jnp.where(more >= 0, more, float(rows))).astype(jnp.int32)
    high = jnp.max(more).astype(jnp.int32)
    lax.fori_loop(low // 16, jnp.where(high >= 0, high // 16 + 1, 0), fill(8), 0)


def query_product(grad_ref, p_ref, out):
    for at in range(0, p_ref.shape[1], TILE):
        out(
            at,
            lax.dot_general(
                grad_ref[...], p_ref[:, at : at + TILE], (((0,), (0,)), ((), ())),
                preferred_element_type=jnp.float32,
            ).astype(jnp.bfloat16),
        )


def next_grad_kernel(place, merge, exp_ref, pack_ref, p_ref, stat_ref, *refs):
    group = lax.axis_index("grp")
    if merge:
        cross_ref, core_ref, both_ref, grad_ref, mine_ref, other_ref, whole_ref = refs
        top, total = merge_stats(stat_ref[...], cross_ref[...], core_ref[...], both_ref[...])
        whole_ref[0:1, :] = top
        whole_ref[1:2, :] = total
    else:
        whole_ref, grad_ref, mine_ref, other_ref = refs
        top, total = whole_ref[0:1, :], whole_ref[1:2, :]
    quarter = mine_ref.shape[0]
    lanes = slice(place * 2 * quarter, (place + 1) * 2 * quarter)
    pack = reorder(pack_ref[...], group)[:, lanes]
    factor = pack[16:17] * (jnp.exp2(stat_ref[0:1, lanes] - top[:, lanes]) / total[:, lanes])
    fill_grads(exp_ref.at[:, lanes], grad_ref, factor, pack[0:8], pack[8:16])

    def put(at, part):
        mine_ref[:, at : at + TILE] = part[:quarter]
        other_ref[:, at : at + TILE] = part[quarter:]

    query_product(grad_ref, p_ref, put)


def own_grad_kernel(exp_ref, pack_ref, p_ref, stat_ref, whole_ref, grad_ref, *outs):
    *outs, rows_ref = outs
    group = lax.axis_index("grp")
    whole = reorder(whole_ref[...], group)
    factor = pack_ref[16:17, :] * (jnp.exp2(stat_ref[0:1, :] - whole[0:1]) / whole[1:2])
    fill_grads(exp_ref, grad_ref, factor, pack_ref[0:8, :], pack_ref[8:16, :])

    def put(at, part):
        rows_ref[:, at : at + TILE] = part

    query_product(grad_ref, p_ref, put)
    quarter = outs[0].shape[0]
    for slot in range(4):
        first = pl.multiple_of((group ^ slot) * quarter, quarter)
        outs[slot][...] = rows_ref[pl.ds(first, quarter), :]


def passage_kernel(count, half, *refs):
    grads, (rows_ref, next_ref, out_ref) = refs[:count], refs[count:]
    rows = (rows_ref, next_ref.at[half:, :], next_ref.at[:half, :])
    for at in range(0, out_ref.shape[1], TILE):
        out_ref[:, at : at + TILE] = sum(
            jnp.dot(
                grad_ref[...], rows_ref[:, at : at + TILE], preferred_element_type=jnp.float32
            )
            for grad_ref, rows_ref in zip(grads, rows)
        ).astype(jnp.bfloat16)


def take_kernel(pieces, q_ref, out_ref, sems):
    quarter = q_ref.shape[0] // 4
    group = lax.axis_index("grp")
    copies, at = [], 0
    for place, (slot, skip, rows) in enumerate(pieces):
        first = pl.multiple_of((group ^ slot) * quarter + skip, 16)
        copies.append(
            pltpu.make_async_copy(
                q_ref.at[pl.ds(first, rows)], out_ref.at[pl.ds(at, rows)], sems.at[place]
            )
        )
        at += rows
    for copy in copies:
        copy.start()
    for copy in copies:
        copy.wait()


def call(kernel, outs, ins, scratch=(), flops=0, name=None):
    size = sum(math.prod(o.shape) * o.dtype.itemsize for o in list(outs) + list(ins))
    return pl.pallas_call(
        kernel,
        out_shape=tuple(outs),
        in_specs=[IN_VMEM] * len(ins),
        out_specs=(IN_VMEM,) * len(outs),
        scratch_shapes=list(scratch),
        compiler_params=pltpu.CompilerParams(vmem_limit_bytes=16 * 2**20),
        cost_estimate=pl.CostEstimate(
            flops=int(flops), bytes_accessed=int(size), transcendentals=0
        ),
        name=name,
    )(*ins)


def per_device(queries, passages, loss_grad, teacher_logits, passage_ids):
    rows, depth = queries.shape
    width = passages.shape[0]
    quarter, half = rows // 4, rows // 2
    blocks, groups = lax.axis_size("blk"), lax.axis_size("grp")
    blk_index, grp_index = lax.axis_index("blk"), lax.axis_index("grp")
    f32, bf16 = jnp.float32, jnp.bfloat16
    score_scale = 3.0 / math.sqrt(depth)

    def along(by):
        return [
            (b * groups + g, (b + by) % blocks * groups + g)
            for b in range(blocks)
            for g in range(groups)
        ]

    def across(turn):
        return [
            (b * groups + g, b * groups + (g ^ turn))
            for b in range(blocks)
            for g in range(groups)
        ]

    def move(x, pairs):
        return lax.ppermute(x, AXES, pairs)

    stat = shape((8, rows), f32)
    piece = shape((quarter, depth), bf16)
    pack = shape((24, rows), f32)
    scale = score_scale * LOG2E

    cut = quarter * 2 // 3

    def take(pieces, name):
        return pl.pallas_call(
            functools.partial(take_kernel, pieces),
            out_shape=shape((sum(piece[2] for piece in pieces), depth), bf16),
            in_specs=[pl.BlockSpec(memory_space=pl.ANY)],
            out_specs=IN_VMEM,
            scratch_shapes=[pltpu.SemaphoreType.DMA((len(pieces),))],
            name=name,
        )(queries)

    first_out = take(((0, 0, cut),), "take_first")
    first_mine = move(first_out, along(-1))
    rest_out = take(((0, cut, quarter - cut), (2, cut, quarter - cut)), "take_rest")
    rest_mine = move(rest_out, along(-1))

    coef = (score_scale * loss_grad)[None, :]
    pack_own, pack_out = call(
        functools.partial(pack_kernel, width), [pack, pack],
        [passage_ids, teacher_logits, coef], flops=1e6, name="labels",
    )
    pack_next = move(pack_out, along(-1))
    exp_own, stat_own = call(
        functools.partial(own_kernel, scale),
        [shape((width, rows), f32), stat],
        [queries, passages],
        flops=2 * rows * width * depth,
        name="own_scores",
    )
    stat_before = move(stat_own, along(-1))
    first_mine, exp_own = lax.optimization_barrier((first_mine, exp_own))
    cross_mine = move(first_mine, across(2))
    first_other = move(first_mine, across(1))
    rest_other = move(rest_mine, across(1))
    cross_other = move(cross_mine, across(1))

    exp_next, stat_next, q_next = call(
        functools.partial(next_kernel, scale),
        [shape((width, rows), f32), stat, shape((rows, depth), bf16)],
        [first_mine, first_other, cross_mine, cross_other, rest_mine, rest_other]
        + [passages, stat_before],
        flops=2 * rows * width * depth,
        name="next_scores",
    )

    cross, core, both = (move(stat_next, across(turn)) for turn in (2, 1, 3))

    def next_grads(place, merge, stats, name):
        return call(
            functools.partial(next_grad_kernel, place, merge),
            [shape((width, half), bf16), piece, piece] + ([stat] if merge else []),
            [exp_next, pack_next, passages] + stats,
            flops=2 * half * width * depth,
            name=name,
        )

    g_b, nb_mine, nb_other, whole_next = next_grads(
        1, True, [stat_next, cross, core, both], "next_grad_b"
    )
    nb_in = move(nb_other, across(1))
    whole_own = move(whole_next, along(1))
    g_a, na_mine, na_other = next_grads(0, False, [stat_next, whole_next], "next_grad_a")
    na_in = move(na_other, across(1))
    nb = (nb_mine.astype(f32) + nb_in.astype(f32)).astype(bf16)
    nb, whole_own = lax.optimization_barrier((nb, whole_own))
    nb_cross = move(nb, across(2))
    g_own, oa_mine, oa_other, ob_mine, ob_other = call(
        own_grad_kernel,
        [shape((width, rows), bf16)] + [piece] * 4,
        [exp_own, pack_own, passages, stat_own, whole_own],
        [pltpu.VMEM((rows, depth), bf16)],
        flops=2 * rows * width * depth,
        name="own_grad",
    )
    ob = (ob_mine.astype(f32) + move(ob_other, across(1)).astype(f32)).astype(bf16)
    ob_cross = move(ob, across(2))
    oa_in = move(oa_other, across(1))
    sent = (na_mine.astype(f32) + na_in.astype(f32) + nb_cross.astype(f32)).astype(bf16)
    came = move(sent, along(1))
    (passage_grad,) = call(
        functools.partial(passage_kernel, 3, half),
        [shape((width, depth), bf16)],
        [g_own, g_b, g_a, queries, q_next],
        flops=4 * rows * width * depth,
        name="passage_grad",
    )
    query_grad = (
        oa_mine.astype(f32) + oa_in.astype(f32) + ob_cross.astype(f32) + came.astype(f32)
    ).astype(bf16)
    return query_grad, passage_grad


def solution(mesh):
    in_specs = (P("blk", None), P(("blk", "grp"), None), P("blk"), P(None, "blk"), P(None, "blk"))
    out_specs = (P(("blk", "grp"), None), P(("blk", "grp"), None))
    return jax.shard_map(
        per_device, mesh=mesh, in_specs=in_specs, out_specs=out_specs, check_vma=False
    )
```

time: 217 us -> 87 us (0.40); the launches traced: 214 us -> 87.1 us
  waiting for transfers between devices: 130 us -> 15.9 us
  Pallas kernels: 0 us -> 33.5 us
  starting transfers between devices: 2.77 us -> 34 us
  matrix products: 27.8 us -> 0 us
  blocking collectives: 16.5 us -> 0 us
  other arithmetic: 17.8 us -> 1.47 us
  between operations: 14.2 us -> 0.81 us
  local copies, waits for them, and re-layouts: 4.78 us -> 1.44 us
    ppermute x2 -> x19, waiting for transfers between devices: 128 us -> 15.9 us  [move(): return lax.ppermute(x, AXES, pairs)]
    pallas_call x0 -> x9, Pallas kernels: none -> 33.5 us  [the longest x7 30 us: call(): pl.pallas_call(kernel, out_shape=tuple(outs), in_specs=[IN_VMEM] * len(in...]
    ppermute x2 -> x19, starting transfers between devices: 2.74 us -> 34 us  [move(): return lax.ppermute(x, AXES, pairs)]
    dot_general x6 -> x0, matrix products: 27.8 us -> none  [the longest x2 10.2 us: grad_product(): lax.dot_general(grads, rows, (((0,), (0,)), ((), ())), preferred_element_...]
    convert_element_type x2 -> x4, other arithmetic: 13.1 us -> 1.47 us  [the longest x1 1.01 us: per_device(): query_grad = (oa_mine.astype(f32) + oa_in.astype(f32) + ob_cross.astype(f...]
    psum x1 -> x0, blocking collectives: 8.78 us -> none  [merge_rows(): whole_total = lax.psum(row_total * jnp.exp(row_top - whole_top), 'grp')]
    pmax x1 -> x0, blocking collectives: 7.76 us -> none  [merge_rows(): whole_top = lax.pmax(row_top, 'grp')]
    reduce_sum x3 -> x0, other arithmetic: 2.55 us -> none  [the longest x2 1.79 us: tile_stats(): tile_total = jnp.sum(jnp.exp(scores - tile_top[:, None]), axis=1)]
  transfers between devices with their start and end apart: 3 -> 19, of which waited for: 3 -> 8; matrix products, arithmetic and copies ran while one was open for 10% -> 1% of each run, Pallas kernels for 0% -> 33%
where the time goes in v2:
time: 87 us; the launch traced here: 87.1 us
  starting transfers between devices  34 us (39%)
  Pallas kernels  33.5 us (39%)
  waiting for transfers between devices  15.9 us (18%)
  other arithmetic  1.47 us (2%)
  local copies, waits for them, and re-layouts  1.44 us (2%)
    ppermute x19, starting transfers between devices, move(): return lax.ppermute(x, AXES, pairs)  34 us
    pallas_call x7, Pallas kernels, call(): pl.pallas_call(kernel, out_shape=tuple(outs), in_specs=[IN_VMEM] * len(in...  30 us
    ppermute x19, waiting for transfers between devices, move(): return lax.ppermute(x, AXES, pairs)  15.9 us
    pallas_call x2, Pallas kernels, take(): pl.pallas_call(functools.partial(take_kernel, pieces), out_shape=shape((s...  3.5 us
  transfers between devices with their start and end apart: 19, of which 8 were waited for; matrix products, arithmetic and copies ran while one was open for 1% of the time, Pallas kernels for 33%

profile of v2, /device:TPU:1, one launch (start us, length us, event | category | flops | bytes accessed | tf_op | source)
XLA Modules:
  0.0 87.1 jit_solution(18237129363613029345)
XLA Ops:
  0.6 0.0 copy-start
  0.6 1.8 %take_first.1 = bf16[128,1024]{1,0:T(8,128)(2,1)} custom-call(bf16[768,1024]{1,0:T(8,128)(2,1)} %refs_3_.1), custom_call_target="tpu_custom_call" | custom-call | tf_op jit(solution)/shard_map/take_first/pallas_call | solution.py:296
  2.5 9.9 %collective-permute-start = (bf16[128,1024]{1,0:T(8,128)(2,1)}, bf16[128,1024]{1,0:T(8,128)(2,1)S(1)}, u32[]{:S(2)}, u32[]{:S(2)}) collective-permute-start(bf16[128,1024]{1,0:T(8,128)(2,1)} %take_first.1), channel_id=1, source_target_pairs={{0,252},{1,253},{2,254},{3,255},{4,0},{5,1},{6,2},{7,3},{8,4},{9,5... | collective-permute-start | bytes 786440 | tf_op jit(solution)/shard_map/ppermute | solution.py:286
  12.3 1.7 %take_rest.1 = bf16[128,1024]{1,0:T(8,128)(2,1)} custom-call(bf16[768,1024]{1,0:T(8,128)(2,1)} %refs_3_.1), custom_call_target="tpu_custom_call" | custom-call | tf_op jit(solution)/shard_map/take_rest/pallas_call | solution.py:296
  14.0 0.5 collective-permute-start.4
  14.6 0.0 copy-done
  14.6 0.0 copy-start.1
  14.6 1.4 %copy-done.1 = bf16[768,1024]{1,0:T(8,128)(2,1)S(1)} copy-done((bf16[768,1024]{1,0:T(8,128)(2,1)S(1)}, bf16[768,1024]{1,0:T(8,128)(2,1)}, u32[]{:S(2)}) %copy-start.1) | copy-done | bytes 1572888
  16.0 0.0 copy-start.5
  16.0 0.0 copy-start.3
  16.0 0.0 copy-start.4
  16.0 4.0 %own_scores.1 = (f32[1536,768]{1,0:T(8,128)S(1)}, f32[8,768]{1,0:T(8,128)S(1)}) custom-call(bf16[768,1024]{1,0:T(8,128)(2,1)S(1)} %copy-done.1, bf16[1536,1024]{1,0:T(8,128)(2,1)S(1)} %copy-done), custom_call_target="tpu_custom_call" | custom-call | flops 2415919104 | bytes 9461760 | tf_op jit(solution)/shard_map/own_scores/pallas_call | solution.py:248
  19.9 0.0 collective-permute-done.refs_0_
  20.0 2.5 %collective-permute-start.2 = (bf16[128,1024]{1,0:T(8,128)(2,1)S(1)}, bf16[128,1024]{1,0:T(8,128)(2,1)S(1)}, u32[]{:S(2)}, u32[]{:S(2)}) collective-permute-start(bf16[128,1024]{1,0:T(8,128)(2,1)S(1)} %collective-permute-done.refs_0_), channel_id=1, source_target_pairs={{0,2},{1,3},{2,0},{3,1},{4,6},{5,7},{6,4},{7,5},{8,10},{9,11},{10,... | collective-permute-start | bytes 786440 | tf_op jit(solution)/shard_map/ppermute | solution.py:286
  22.5 1.5 %collective-permute-start.1 = (bf16[128,1024]{1,0:T(8,128)(2,1)S(1)}, bf16[128,1024]{1,0:T(8,128)(2,1)S(1)}, u32[]{:S(2)}, u32[]{:S(2)}) collective-permute-start(bf16[128,1024]{1,0:T(8,128)(2,1)S(1)} %collective-permute-done.refs_0_), channel_id=1, source_target_pairs={{0,1},{1,0},{2,3},{3,2},{4,5},{5,4},{6,7},{7,6},{8,9},{9,8},{10,11... | collective-permute-start | bytes 786440 | tf_op jit(solution)/shard_map/ppermute | solution.py:286
  24.0 0.0 collective-permute-done.4.refs_4_
  24.0 0.8 collective-permute-start.5
  24.8 3.3 %collective-permute-done.2.refs_2_ = bf16[128,1024]{1,0:T(8,128)(2,1)S(1)} collective-permute-done((bf16[128,1024]{1,0:T(8,128)(2,1)S(1)}, bf16[128,1024]{1,0:T(8,128)(2,1)S(1)}, u32[]{:S(2)}, u32[]{:S(2)}) %collective-permute-start.2) | collective-permute-done | bytes 262176 | tf_op jit(solution)/shard_map/ppermute | solution.py:286
  28.1 2.2 %collective-permute-start.3 = (bf16[128,1024]{1,0:T(8,128)(2,1)S(1)}, bf16[128,1024]{1,0:T(8,128)(2,1)S(1)}, u32[]{:S(2)}, u32[]{:S(2)}) collective-permute-start(bf16[128,1024]{1,0:T(8,128)(2,1)S(1)} %collective-permute-done.2.refs_2_), channel_id=1, source_target_pairs={{0,1},{1,0},{2,3},{3,2},{4,5},{5,4},{6,7},{7,6},{8,9},{9,8},{10,11... | collective-permute-start | bytes 786440 | tf_op jit(solution)/shard_map/ppermute | solution.py:286
  30.3 4.2 %collective-permute-start.6 = (f32[8,768]{1,0:T(8,128)S(1)}, f32[8,768]{1,0:T(8,128)S(1)}, u32[]{:S(2)}, u32[]{:S(2)}) collective-permute-start(f32[8,768]{1,0:T(8,128)S(1)} %get-tuple-element.28.stat_ref), channel_id=1, source_target_pairs={{0,252},{1,253},{2,254},{3,255},{4,0},{5,1},{6,2},{7,3},{8,4},{9,5... | collective-permute-start | bytes 73736 | tf_op jit(solution)/shard_map/ppermute | solution.py:286
  34.5 0.0 copy-done.5
  34.5 0.0 copy-done.3
  34.5 0.0 copy-done.4
  34.5 0.8 labels.1
  35.3 0.1 collective-permute-start.7
  35.4 0.1 collective-permute-done.6.refs_7_
  35.4 0.0 collective-permute-done.1.refs_1_
  35.5 0.0 collective-permute-done.5.refs_5_
  35.5 0.0 collective-permute-done.3.refs_3_
  35.5 4.0 %next_scores.1 = (f32[1536,768]{1,0:T(8,128)S(1)}, f32[8,768]{1,0:T(8,128)S(1)}, bf16[768,1024]{1,0:T(8,128)(2,1)S(1)}) custom-call(bf16[128,1024]{1,0:T(8,128)(2,1)S(1)} %collective-permute-done.refs_0_, bf16[128,1024]{1,0:T(8,128)(2,1)S(1)} %collective-permute-done.1.refs_1_, bf16[128,1024]{1,0:T(8,128)(2,1)S(1)} %collective-permute-done.2.refs_2_, ...), custom_call_target="tpu_custom_call" | custom-call | flops 2415919104 | bytes 11059200 | tf_op jit(solution)/shard_map/next_scores/pallas_call | solution.py:248
  39.4 2.6 %collective-permute-start.8 = (f32[8,768]{1,0:T(8,128)S(1)}, f32[8,768]{1,0:T(8,128)S(1)}, u32[]{:S(2)}, u32[]{:S(2)}) collective-permute-start(f32[8,768]{1,0:T(8,128)S(1)} %get-tuple-element.32.stat_ref), channel_id=1, source_target_pairs={{0,2},{1,3},{2,0},{3,1},{4,6},{5,7},{6,4},{7,5},{8,10},{9,11},{10,... | collective-permute-start | bytes 73736 | tf_op jit(solution)/shard_map/ppermute | solution.py:286
  42.0 1.1 %collective-permute-start.9 = (f32[8,768]{1,0:T(8,128)S(1)}, f32[8,768]{1,0:T(8,128)S(1)}, u32[]{:S(2)}, u32[]{:S(2)}) collective-permute-start(f32[8,768]{1,0:T(8,128)S(1)} %get-tuple-element.32.stat_ref), channel_id=1, source_target_pairs={{0,1},{1,0},{2,3},{3,2},{4,5},{5,4},{6,7},{7,6},{8,9},{9,8},{10,11... | collective-permute-start | bytes 73736 | tf_op jit(solution)/shard_map/ppermute | solution.py:286
  43.2 0.4 collective-permute-start.10
  43.5 0.0 collective-permute-done.7.pack_ref
  43.5 0.2 collective-permute-done.8.refs_0_
  43.7 0.3 collective-permute-done.9.refs_1_
  44.0 3.9 %collective-permute-done.10.refs_2_ = f32[8,768]{1,0:T(8,128)S(1)} collective-permute-done((f32[8,768]{1,0:T(8,128)S(1)}, f32[8,768]{1,0:T(8,128)S(1)}, u32[]{:S(2)}, u32[]{:S(2)}) %collective-permute-start.10) | collective-permute-done | bytes 24608 | tf_op jit(solution)/shard_map/ppermute | solution.py:286
  47.9 3.3 %next_grad_b.1 = (bf16[1536,384]{1,0:T(8,128)(2,1)S(1)}, bf16[192,1024]{1,0:T(8,128)(2,1)S(1)}, bf16[192,1024]{1,0:T(8,128)(2,1)S(1)}, f32[8,768]{1,0:T(8,128)S(1)}) custom-call(f32[1536,768]{1,0:T(8,128)S(1)} %get-tuple-element.30.exp_ref, f32[24,768]{1,0:T(8,128)S(1)} %collective-permute-done.7.pack_ref, bf16[1536,1024]{1,0:T(8,128)(2,1)S(1)} %copy-done, ...), custom_call_target="tpu_custom_call" | custom-call | flops 1207959552 | bytes 10027008 | tf_op jit(solution)/shard_map/next_grad_b/pallas_call | solution.py:248
  51.2 0.1 collective-permute-start.11
  51.3 1.2 %collective-permute-start.12 = (f32[8,768]{1,0:T(8,128)S(1)}, f32[8,768]{1,0:T(8,128)S(1)}, u32[]{:S(2)}, u32[]{:S(2)}) collective-permute-start(f32[8,768]{1,0:T(8,128)S(1)} %get-tuple-element.35.refs_0_), channel_id=1, source_target_pairs={{0,4},{1,5},{2,6},{3,7},{4,8},{5,9},{6,10},{7,11},{8,12},{9,13},{1... | collective-permute-start | bytes 73736 | tf_op jit(solution)/shard_map/ppermute | solution.py:286
  52.5 3.2 %next_grad_a.1 = (bf16[1536,384]{1,0:T(8,128)(2,1)S(1)}, bf16[192,1024]{1,0:T(8,128)(2,1)S(1)}, bf16[192,1024]{1,0:T(8,128)(2,1)S(1)}) custom-call(f32[1536,768]{1,0:T(8,128)S(1)} %get-tuple-element.30.exp_ref, f32[24,768]{1,0:T(8,128)S(1)} %collective-permute-done.7.pack_ref, bf16[1536,1024]{1,0:T(8,128)(2,1)S(1)} %copy-done, ...), custom_call_target="tpu_custom_call" | custom-call | flops 1207959552 | bytes 9953280 | tf_op jit(solution)/shard_map/next_grad_a/pallas_call | solution.py:248
  55.7 0.8 collective-permute-start.16
  56.5 0.0 collective-permute-done.11
  56.5 0.1 add_convert_fusion.3
  56.7 1.6 %collective-permute-done.12.whole_ref = f32[8,768]{1,0:T(8,128)S(1)} collective-permute-done((f32[8,768]{1,0:T(8,128)S(1)}, f32[8,768]{1,0:T(8,128)S(1)}, u32[]{:S(2)}, u32[]{:S(2)}) %collective-permute-start.12) | collective-permute-done | bytes 24608 | tf_op jit(solution)/shard_map/ppermute | solution.py:286
  58.3 1.6 %collective-permute-start.17 = (bf16[192,1024]{1,0:T(8,128)(2,1)S(1)}, bf16[192,1024]{1,0:T(8,128)(2,1)S(1)}, u32[]{:S(2)}, u32[]{:S(2)}) collective-permute-start(bf16[192,1024]{1,0:T(8,128)(2,1)S(1)} %add_convert_fusion.3), channel_id=1, source_target_pairs={{0,2},{1,3},{2,0},{3,1},{4,6},{5,7},{6,4},{7,5},{8,10},{9,11},{10,... | collective-permute-start | bytes 1179656 | tf_op jit(solution)/shard_map/ppermute | solution.py:286
  60.0 7.1 %own_grad.1 = (bf16[1536,768]{1,0:T(8,128)(2,1)S(1)}, bf16[192,1024]{1,0:T(8,128)(2,1)S(1)}, bf16[192,1024]{1,0:T(8,128)(2,1)S(1)}, bf16[192,1024]{1,0:T(8,128)(2,1)S(1)}, bf16[192,1024]{1,0:T(8,128)(2,1)S(1)}) custom-call(f32[1536,768]{1,0:T(8,128)S(1)} %get-tuple-element.26.exp_ref, f32[24,768]{1,0:T(8,128)S(1)} %get-tuple-element.27.pack_ref, ...), custom_call_target="tpu_custom_call" | custom-call | flops 2415919104 | bytes 11919360 | tf_op jit(solution)/shard_map/own_grad/pallas_call | solution.py:248
  67.1 0.0 copy-start.2
  67.1 4.0 %collective-permute-start.14 = (bf16[192,1024]{1,0:T(8,128)(2,1)S(1)}, bf16[192,1024]{1,0:T(8,128)(2,1)S(1)}, u32[]{:S(2)}, u32[]{:S(2)}) collective-permute-start(bf16[192,1024]{1,0:T(8,128)(2,1)S(1)} %get-tuple-element.40), channel_id=1, source_target_pairs={{0,1},{1,0},{2,3},{3,2},{4,5},{5,4},{6,7},{7,6},{8,9},{9,8},{10,11... | collective-permute-start | bytes 1179656 | tf_op jit(solution)/shard_map/ppermute | solution.py:286
  71.1 0.1 collective-permute-start.13
  71.2 0.0 collective-permute-done.16
  71.2 0.0 collective-permute-done.17
  71.2 0.2 add_convert_fusion.1
  71.4 0.1 collective-permute-start.18
  71.5 0.9 %collective-permute-done.14 = bf16[192,1024]{1,0:T(8,128)(2,1)S(1)} collective-permute-done((bf16[192,1024]{1,0:T(8,128)(2,1)S(1)}, bf16[192,1024]{1,0:T(8,128)(2,1)S(1)}, u32[]{:S(2)}, u32[]{:S(2)}) %collective-permute-start.14) | collective-permute-done | bytes 393248 | tf_op jit(solution)/shard_map/ppermute | solution.py:286
  72.5 0.1 add_convert_fusion.2
  72.6 0.3 collective-permute-start.15
  72.9 0.0 copy-done.2
  72.9 7.6 %passage_grad.1 = bf16[1536,1024]{1,0:T(8,128)(2,1)} custom-call(bf16[1536,768]{1,0:T(8,128)(2,1)S(1)} %get-tuple-element.44.refs_0_, bf16[1536,384]{1,0:T(8,128)(2,1)S(1)} %get-tuple-element.45.refs_1_, bf16[1536,384]{1,0:T(8,128)(2,1)S(1)} %get-tuple-element.46.refs_2_, bf16[768,1024]{1,0:T(8,128)(2,1)S(1)} %copy-done.2, ...), custom_call_target="tpu_custom_call" | custom-call | flops 4831838208 | bytes 11010048 | tf_op jit(solution)/shard_map/passage_grad/pallas_call | solution.py:248
  80.6 0.0 collective-permute-done.13
  80.6 5.5 %collective-permute-done.18 = bf16[192,1024]{1,0:T(8,128)(2,1)S(1)} collective-permute-done((bf16[192,1024]{1,0:T(8,128)(2,1)S(1)}, bf16[192,1024]{1,0:T(8,128)(2,1)S(1)}, u32[]{:S(2)}, u32[]{:S(2)}) %collective-permute-start.18) | collective-permute-done | bytes 393248 | tf_op jit(solution)/shard_map/ppermute | solution.py:286
  86.1 0.0 collective-permute-done.15
  86.1 1.0 %add_convert_fusion = bf16[192,1024]{1,0:T(8,128)(2,1)} fusion(bf16[192,1024]{1,0:T(8,128)(2,1)S(1)} %collective-permute-done.18, bf16[192,1024]{1,0:T(8,128)(2,1)S(1)} %collective-permute-done.15, bf16[192,1024]{1,0:T(8,128)(2,1)S(1)} %collective-permute-done.13, bf16[192,1024]{1,0:T(8,128)(2,1)S(1)} %get-tuple-element.37), kind=kLoop, calls=%fused_computation | loop fusion | flops 1572864 | bytes 1966080 | tf_op jit(solution)/shard_map/convert_element_type | solution.py:382
  (2 shorter events, 0.0 us)
Async XLA Ops:
  0.6 13.9 %copy-start = (bf16[1536,1024]{1,0:T(8,128)(2,1)S(1)}, bf16[1536,1024]{1,0:T(8,128)(2,1)}, u32[]{:S(2)}) copy-start(bf16[1536,1024]{1,0:T(8,128)(2,1)} %p_ref.7) | copy-start | bytes 9437188
  2.5 17.5 %collective-permute-start = (bf16[128,1024]{1,0:T(8,128)(2,1)}, bf16[128,1024]{1,0:T(8,128)(2,1)S(1)}, u32[]{:S(2)}, u32[]{:S(2)}) collective-permute-start(bf16[128,1024]{1,0:T(8,128)(2,1)} %take_first.1), channel_id=1, source_target_pairs={{0,252},{1,253},{2,254},{3,255},{4,0},{5,1},{6,2},{7,3},{8,4},{9,5... | collective-permute-start | bytes 786440 | tf_op jit(solution)/shard_map/ppermute | solution.py:286
  14.0 10.0 %collective-permute-start.4 = (bf16[128,1024]{1,0:T(8,128)(2,1)}, bf16[128,1024]{1,0:T(8,128)(2,1)S(1)}, u32[]{:S(2)}, u32[]{:S(2)}) collective-permute-start(bf16[128,1024]{1,0:T(8,128)(2,1)} %take_rest.1), channel_id=1, source_target_pairs={{0,252},{1,253},{2,254},{3,255},{4,0},{5,1},{6,2},{7,3},{8,4},{9,5... | collective-permute-start | bytes 786440 | tf_op jit(solution)/shard_map/ppermute | solution.py:286
  14.6 1.4 %copy-start.1 = (bf16[768,1024]{1,0:T(8,128)(2,1)S(1)}, bf16[768,1024]{1,0:T(8,128)(2,1)}, u32[]{:S(2)}) copy-start(bf16[768,1024]{1,0:T(8,128)(2,1)} %refs_3_.1) | copy-start | bytes 4718596
  16.0 18.5 %copy-start.5 = (f32[768]{0:T(1024)S(1)}, f32[768]{0:T(1024)}, u32[]{:S(2)}) copy-start(f32[768]{0:T(1024)} %param.7) | copy-start | bytes 9220
  16.0 18.5 %copy-start.3 = (s32[8,768]{1,0:T(8,128)S(1)}, s32[8,768]{1,0:T(8,128)}, u32[]{:S(2)}) copy-start(s32[8,768]{1,0:T(8,128)} %ids_ref.1) | copy-start | bytes 73732
  16.0 18.6 %copy-start.4 = (f32[8,768]{1,0:T(8,128)S(1)}, f32[8,768]{1,0:T(8,128)}, u32[]{:S(2)}) copy-start(f32[8,768]{1,0:T(8,128)} %logits_ref.1) | copy-start | bytes 73732
  20.0 8.2 %collective-permute-start.2 = (bf16[128,1024]{1,0:T(8,128)(2,1)S(1)}, bf16[128,1024]{1,0:T(8,128)(2,1)S(1)}, u32[]{:S(2)}, u32[]{:S(2)}) collective-permute-start(bf16[128,1024]{1,0:T(8,128)(2,1)S(1)} %collective-permute-done.refs_0_), channel_id=1, source_target_pairs={{0,2},{1,3},{2,0},{3,1},{4,6},{5,7},{6,4},{7,5},{8,10},{9,11},{10,... | collective-permute-start | bytes 786440 | tf_op jit(solution)/shard_map/ppermute | solution.py:286
  22.5 13.0 %collective-permute-start.1 = (bf16[128,1024]{1,0:T(8,128)(2,1)S(1)}, bf16[128,1024]{1,0:T(8,128)(2,1)S(1)}, u32[]{:S(2)}, u32[]{:S(2)}) collective-permute-start(bf16[128,1024]{1,0:T(8,128)(2,1)S(1)} %collective-permute-done.refs_0_), channel_id=1, source_target_pairs={{0,1},{1,0},{2,3},{3,2},{4,5},{5,4},{6,7},{7,6},{8,9},{9,8},{10,11... | collective-permute-start | bytes 786440 | tf_op jit(solution)/shard_map/ppermute | solution.py:286
  24.0 11.4 %collective-permute-start.5 = (bf16[128,1024]{1,0:T(8,128)(2,1)S(1)}, bf16[128,1024]{1,0:T(8,128)(2,1)S(1)}, u32[]{:S(2)}, u32[]{:S(2)}) collective-permute-start(bf16[128,1024]{1,0:T(8,128)(2,1)S(1)} %collective-permute-done.4.refs_4_), channel_id=1, source_target_pairs={{0,1},{1,0},{2,3},{3,2},{4,5},{5,4},{6,7},{7,6},{8,9},{9,8},{10,11... | collective-permute-start | bytes 786440 | tf_op jit(solution)/shard_map/ppermute | solution.py:286
  28.1 7.3 %collective-permute-start.3 = (bf16[128,1024]{1,0:T(8,128)(2,1)S(1)}, bf16[128,1024]{1,0:T(8,128)(2,1)S(1)}, u32[]{:S(2)}, u32[]{:S(2)}) collective-permute-start(bf16[128,1024]{1,0:T(8,128)(2,1)S(1)} %collective-permute-done.2.refs_2_), channel_id=1, source_target_pairs={{0,1},{1,0},{2,3},{3,2},{4,5},{5,4},{6,7},{7,6},{8,9},{9,8},{10,11... | collective-permute-start | bytes 786440 | tf_op jit(solution)/shard_map/ppermute | solution.py:286
  30.3 5.2 %collective-permute-start.6 = (f32[8,768]{1,0:T(8,128)S(1)}, f32[8,768]{1,0:T(8,128)S(1)}, u32[]{:S(2)}, u32[]{:S(2)}) collective-permute-start(f32[8,768]{1,0:T(8,128)S(1)} %get-tuple-element.28.stat_ref), channel_id=1, source_target_pairs={{0,252},{1,253},{2,254},{3,255},{4,0},{5,1},{6,2},{7,3},{8,4},{9,5... | collective-permute-start | bytes 73736 | tf_op jit(solution)/shard_map/ppermute | solution.py:286
  35.3 8.2 %collective-permute-start.7 = (f32[24,768]{1,0:T(8,128)S(1)}, f32[24,768]{1,0:T(8,128)S(1)}, u32[]{:S(2)}, u32[]{:S(2)}) collective-permute-start(f32[24,768]{1,0:T(8,128)S(1)} %get-tuple-element.31), channel_id=1, source_target_pairs={{0,252},{1,253},{2,254},{3,255},{4,0},{5,1},{6,2},{7,3},{8,4},{9,5... | collective-permute-start | bytes 221192 | tf_op jit(solution)/shard_map/ppermute | solution.py:286
  39.4 4.3 %collective-permute-start.8 = (f32[8,768]{1,0:T(8,128)S(1)}, f32[8,768]{1,0:T(8,128)S(1)}, u32[]{:S(2)}, u32[]{:S(2)}) collective-permute-start(f32[8,768]{1,0:T(8,128)S(1)} %get-tuple-element.32.stat_ref), channel_id=1, source_target_pairs={{0,2},{1,3},{2,0},{3,1},{4,6},{5,7},{6,4},{7,5},{8,10},{9,11},{10,... | collective-permute-start | bytes 73736 | tf_op jit(solution)/shard_map/ppermute | solution.py:286
  42.0 2.0 %collective-permute-start.9 = (f32[8,768]{1,0:T(8,128)S(1)}, f32[8,768]{1,0:T(8,128)S(1)}, u32[]{:S(2)}, u32[]{:S(2)}) collective-permute-start(f32[8,768]{1,0:T(8,128)S(1)} %get-tuple-element.32.stat_ref), channel_id=1, source_target_pairs={{0,1},{1,0},{2,3},{3,2},{4,5},{5,4},{6,7},{7,6},{8,9},{9,8},{10,11... | collective-permute-start | bytes 73736 | tf_op jit(solution)/shard_map/ppermute | solution.py:286
  43.2 4.8 %collective-permute-start.10 = (f32[8,768]{1,0:T(8,128)S(1)}, f32[8,768]{1,0:T(8,128)S(1)}, u32[]{:S(2)}, u32[]{:S(2)}) collective-permute-start(f32[8,768]{1,0:T(8,128)S(1)} %get-tuple-element.32.stat_ref), channel_id=1, source_target_pairs={{0,3},{1,2},{2,1},{3,0},{4,7},{5,6},{6,5},{7,4},{8,11},{9,10},{10,... | collective-permute-start | bytes 73736 | tf_op jit(solution)/shard_map/ppermute | solution.py:286
  51.2 5.3 %collective-permute-start.11 = (bf16[192,1024]{1,0:T(8,128)(2,1)S(1)}, bf16[192,1024]{1,0:T(8,128)(2,1)S(1)}, u32[]{:S(2)}, u32[]{:S(2)}) collective-permute-start(bf16[192,1024]{1,0:T(8,128)(2,1)S(1)} %get-tuple-element.34), channel_id=1, source_target_pairs={{0,1},{1,0},{2,3},{3,2},{4,5},{5,4},{6,7},{7,6},{8,9},{9,8},{10,11... | collective-permute-start | bytes 1179656 | tf_op jit(solution)/shard_map/ppermute | solution.py:286
  51.3 7.0 %collective-permute-start.12 = (f32[8,768]{1,0:T(8,128)S(1)}, f32[8,768]{1,0:T(8,128)S(1)}, u32[]{:S(2)}, u32[]{:S(2)}) collective-permute-start(f32[8,768]{1,0:T(8,128)S(1)} %get-tuple-element.35.refs_0_), channel_id=1, source_target_pairs={{0,4},{1,5},{2,6},{3,7},{4,8},{5,9},{6,10},{7,11},{8,12},{9,13},{1... | collective-permute-start | bytes 73736 | tf_op jit(solution)/shard_map/ppermute | solution.py:286
  55.7 15.5 %collective-permute-start.16 = (bf16[192,1024]{1,0:T(8,128)(2,1)S(1)}, bf16[192,1024]{1,0:T(8,128)(2,1)S(1)}, u32[]{:S(2)}, u32[]{:S(2)}) collective-permute-start(bf16[192,1024]{1,0:T(8,128)(2,1)S(1)} %get-tuple-element.42), channel_id=1, source_target_pairs={{0,1},{1,0},{2,3},{3,2},{4,5},{5,4},{6,7},{7,6},{8,9},{9,8},{10,11... | collective-permute-start | bytes 1179656 | tf_op jit(solution)/shard_map/ppermute | solution.py:286
  58.3 12.9 %collective-permute-start.17 = (bf16[192,1024]{1,0:T(8,128)(2,1)S(1)}, bf16[192,1024]{1,0:T(8,128)(2,1)S(1)}, u32[]{:S(2)}, u32[]{:S(2)}) collective-permute-start(bf16[192,1024]{1,0:T(8,128)(2,1)S(1)} %add_convert_fusion.3), channel_id=1, source_target_pairs={{0,2},{1,3},{2,0},{3,1},{4,6},{5,7},{6,4},{7,5},{8,10},{9,11},{10,... | collective-permute-start | bytes 1179656 | tf_op jit(solution)/shard_map/ppermute | solution.py:286
  67.1 5.8 %copy-start.2 = (bf16[768,1024]{1,0:T(8,128)(2,1)S(1)}, bf16[768,1024]{1,0:T(8,128)(2,1)}, u32[]{:S(2)}) copy-start(bf16[768,1024]{1,0:T(8,128)(2,1)} %refs_3_.1) | copy-start | bytes 4718596
  67.1 5.4 %collective-permute-start.14 = (bf16[192,1024]{1,0:T(8,128)(2,1)S(1)}, bf16[192,1024]{1,0:T(8,128)(2,1)S(1)}, u32[]{:S(2)}, u32[]{:S(2)}) collective-permute-start(bf16[192,1024]{1,0:T(8,128)(2,1)S(1)} %get-tuple-element.40), channel_id=1, source_target_pairs={{0,1},{1,0},{2,3},{3,2},{4,5},{5,4},{6,7},{7,6},{8,9},{9,8},{10,11... | collective-permute-start | bytes 1179656 | tf_op jit(solution)/shard_map/ppermute | solution.py:286
  71.1 9.4 %collective-permute-start.13 = (bf16[192,1024]{1,0:T(8,128)(2,1)S(1)}, bf16[192,1024]{1,0:T(8,128)(2,1)S(1)}, u32[]{:S(2)}, u32[]{:S(2)}) collective-permute-start(bf16[192,1024]{1,0:T(8,128)(2,1)S(1)} %get-tuple-element.38), channel_id=1, source_target_pairs={{0,1},{1,0},{2,3},{3,2},{4,5},{5,4},{6,7},{7,6},{8,9},{9,8},{10,11... | collective-permute-start | bytes 1179656 | tf_op jit(solution)/shard_map/ppermute | solution.py:286
  71.4 14.6 %collective-permute-start.18 = (bf16[192,1024]{1,0:T(8,128)(2,1)S(1)}, bf16[192,1024]{1,0:T(8,128)(2,1)S(1)}, u32[]{:S(2)}, u32[]{:S(2)}) collective-permute-start(bf16[192,1024]{1,0:T(8,128)(2,1)S(1)} %add_convert_fusion.1), channel_id=1, source_target_pairs={{0,4},{1,5},{2,6},{3,7},{4,8},{5,9},{6,10},{7,11},{8,12},{9,13},{1... | collective-permute-start | bytes 1179656 | tf_op jit(solution)/shard_map/ppermute | solution.py:286
  72.6 13.5 %collective-permute-start.15 = (bf16[192,1024]{1,0:T(8,128)(2,1)S(1)}, bf16[192,1024]{1,0:T(8,128)(2,1)S(1)}, u32[]{:S(2)}, u32[]{:S(2)}) collective-permute-start(bf16[192,1024]{1,0:T(8,128)(2,1)S(1)} %add_convert_fusion.2), channel_id=1, source_target_pairs={{0,2},{1,3},{2,0},{3,1},{4,6},{5,7},{6,4},{7,5},{8,10},{9,11},{10,... | collective-permute-start | bytes 1179656 | tf_op jit(solution)/shard_map/ppermute | solution.py:286

commit v3 on v2

--- a/solution.py
+++ b/solution.py
@@ -63,11 +63,28 @@
     return top, jnp.sum(total, axis=0, keepdims=True)
 
 
-def own_kernel(scale, q_ref, p_ref, exp_ref, stat_ref):
-    fill_scores(scale, p_ref, q_ref, exp_ref)
+def own_kernel(
+    scale, coef_scale, q_any, p_any, ids_ref, logits_ref, loss_ref,
+    exp_ref, stat_ref, pack_ref, sent_ref, q_ref, p_ref, sems,
+):
+    parts = sems.shape[0] - 1
+    size = p_ref.shape[0] // parts
+    copies = [pltpu.make_async_copy(q_any, q_ref, sems.at[parts])]
+    for part in range(parts):
+        rows = pl.ds(part * size, size)
+        copies.append(pltpu.make_async_copy(p_any.at[rows], p_ref.at[rows], sems.at[part]))
+    for copy in copies:
+        copy.start()
+    labels(coef_scale * loss_ref[...], ids_ref, logits_ref, pack_ref, sent_ref, p_ref.shape[0])
+    copies[0].wait()
+    for part in range(parts):
+        copies[1 + part].wait()
+        rows = pl.ds(part * size, size)
+        fill_scores(scale, p_ref.at[rows], q_ref, exp_ref.at[rows])
     top, total = exponentials(exp_ref)
-    stat_ref[0:1, :] = top
-    stat_ref[1:2, :] = total
+    for ref, at in ((stat_ref, 0), (sent_ref, 17)):
+        ref[at : at + 1, :] = top
+        ref[at + 1 : at + 2, :] = total
 
 
 def next_kernel(scale, *refs):
@@ -85,27 +102,27 @@
         rows_ref[at + cut : at + cut + left, :] = rest[skip : skip + left, :]
         at += cut + left
     fill_scores(scale, p_ref, rows_ref, exp_ref)
-    before = reorder(before_ref[...], lax.axis_index("grp"))
-    top, total = exponentials(exp_ref, before[0:1])
+    before = reorder(before_ref[16:24, :], lax.axis_index("grp"))
+    top, total = exponentials(exp_ref, before[1:2])
     stat_ref[0:1, :] = top
-    stat_ref[1:2, :] = total + before[1:2] * jnp.exp2(before[0:1] - top)
-
-
-def pack_kernel(width, ids_ref, logits_ref, coef_ref, own_ref, next_ref):
+    stat_ref[1:2, :] = total + before[2:3] * jnp.exp2(before[1:2] - top)
+
+
+def labels(coef, ids_ref, logits_ref, own_ref, next_ref, width):
     device = lax.axis_index("blk") * 4 + lax.axis_index("grp")
     blocks = lax.axis_size("blk")
     before = (lax.axis_index("blk") + blocks - 1) % blocks * 4 + lax.axis_index("grp")
     ids = ids_ref[...]
     logits = logits_ref[...]
     power = jnp.exp(logits - jnp.max(logits, axis=0, keepdims=True))
-    weights = coef_ref[...] * (power / jnp.sum(power, axis=0, keepdims=True))
+    weights = coef * (power / jnp.sum(power, axis=0, keepdims=True))
     summed = jnp.zeros_like(weights)
     for k in range(8):
         summed = summed + jnp.where(ids == ids[k : k + 1], weights[k : k + 1], 0.0)
     for ref, at in ((own_ref, device), (next_ref, before)):
         place = ids - at * width
         inside = (place >= 0) & (place < width)
-        places, count = [-1.0] * 8, jnp.zeros_like(coef_ref[...])
+        places, count = [-1.0] * 8, jnp.zeros_like(coef)
         values = [0.0] * 8
         for k in range(8):
             here = inside[k : k + 1]
@@ -117,7 +134,7 @@
         for r in range(8):
             ref[r : r + 1, :] = places[r]
             ref[8 + r : 9 + r, :] = values[r]
-        ref[16:24, :] = jnp.broadcast_to(coef_ref[...], ids.shape)
+        ref[16:24, :] = jnp.broadcast_to(coef, ids.shape)
 
 
 def merge_stats(stat, cross, core, both):
@@ -243,15 +260,16 @@
         copy.wait()
 
 
-def call(kernel, outs, ins, scratch=(), flops=0, name=None):
+def call(kernel, outs, ins, scratch=(), flops=0, name=None, anywhere=0):
     size = sum(math.prod(o.shape) * o.dtype.itemsize for o in list(outs) + list(ins))
     return pl.pallas_call(
         kernel,
         out_shape=tuple(outs),
-        in_specs=[IN_VMEM] * len(ins),
+        in_specs=[pl.BlockSpec(memory_space=pl.ANY)] * anywhere
+        + [IN_VMEM] * (len(ins) - anywhere),
         out_specs=(IN_VMEM,) * len(outs),
         scratch_shapes=list(scratch),
-        compiler_params=pltpu.CompilerParams(vmem_limit_bytes=16 * 2**20),
+        compiler_params=pltpu.CompilerParams(vmem_limit_bytes=24 * 2**20),
         cost_estimate=pl.CostEstimate(
             flops=int(flops), bytes_accessed=int(size), transcendentals=0
         ),
@@ -290,7 +308,7 @@
     pack = shape((24, rows), f32)
     scale = score_scale * LOG2E
 
-    cut = quarter * 2 // 3
+    cut = quarter * 7 // 12
 
     def take(pieces, name):
         return pl.pallas_call(
@@ -307,23 +325,26 @@
     rest_out = take(((0, cut, quarter - cut), (2, cut, quarter - cut)), "take_rest")
     rest_mine = move(rest_out, along(-1))
 
-    coef = (score_scale * loss_grad)[None, :]
-    pack_own, pack_out = call(
-        functools.partial(pack_kernel, width), [pack, pack],
-        [passage_ids, teacher_logits, coef], flops=1e6, name="labels",
-    )
-    pack_next = move(pack_out, along(-1))
-    exp_own, stat_own = call(
-        functools.partial(own_kernel, scale),
-        [shape((width, rows), f32), stat],
-        [queries, passages],
+    exp_own, stat_own, pack_own, pack_out = call(
+        functools.partial(own_kernel, scale, score_scale),
+        [shape((width, rows), f32), stat, pack, pack],
+        [queries, passages, passage_ids, teacher_logits, loss_grad[None, :]],
+        [
+            pltpu.VMEM((rows, depth), bf16),
+            pltpu.VMEM((width, depth), bf16),
+            pltpu.SemaphoreType.DMA((4,)),
+        ],
         flops=2 * rows * width * depth,
         name="own_scores",
-    )
-    stat_before = move(stat_own, along(-1))
-    first_mine, exp_own = lax.optimization_barrier((first_mine, exp_own))
+        anywhere=2,
+    )
+    pack_next = move(pack_out, along(-1))
+    first_mine, stat_own = lax.optimization_barrier((first_mine, stat_own))
     cross_mine = move(first_mine, across(2))
     first_other = move(first_mine, across(1))
+    rest_mine, first_other, pack_next = lax.optimization_barrier(
+        (rest_mine, first_other, pack_next)
+    )
     rest_other = move(rest_mine, across(1))
     cross_other = move(cross_mine, across(1))
 
@@ -331,7 +352,7 @@
         functools.partial(next_kernel, scale),
         [shape((width, rows), f32), stat, shape((rows, depth), bf16)],
         [first_mine, first_other, cross_mine, cross_other, rest_mine, rest_other]
-        + [passages, stat_before],
+        + [passages, pack_next],
         flops=2 * rows * width * depth,
         name="next_scores",
     )
@@ -352,11 +373,12 @@
     )
     nb_in = move(nb_other, across(1))
     whole_own = move(whole_next, along(1))
+    nb = (nb_mine.astype(f32) + nb_in.astype(f32)).astype(bf16)
+    nb, exp_next = lax.optimization_barrier((nb, exp_next))
+    whole_own, exp_next = lax.optimization_barrier((whole_own, exp_next))
+    nb_cross = move(nb, across(2))
     g_a, na_mine, na_other = next_grads(0, False, [stat_next, whole_next], "next_grad_a")
     na_in = move(na_other, across(1))
-    nb = (nb_mine.astype(f32) + nb_in.astype(f32)).astype(bf16)
-    nb, whole_own = lax.optimization_barrier((nb, whole_own))
-    nb_cross = move(nb, across(2))
     g_own, oa_mine, oa_other, ob_mine, ob_other = call(
         own_grad_kernel,
         [shape((width, rows), bf16)] + [piece] * 4,

time: 87 us -> 89.1 us (1.024)
  the two profiles are of different devices: /device:TPU:1 before, /device:TPU:26 now
where the time goes in v3:
time: 89.1 us; the launch traced here: 89.2 us
  Pallas kernels  36.9 us (41%)
  waiting for transfers between devices  26.4 us (30%)
  starting transfers between devices  22.2 us (25%)
  other arithmetic  1.47 us (2%)
  local copies, waits for them, and re-layouts  1.42 us (2%)
    pallas_call x6, Pallas kernels, call(): pl.pallas_call(kernel, out_shape=tuple(outs), in_specs=[pl.BlockSpec(memo...  33.3 us
    ppermute x18, waiting for transfers between devices, move(): return lax.ppermute(x, AXES, pairs)  26.4 us
    ppermute x18, starting transfers between devices, move(): return lax.ppermute(x, AXES, pairs)  22.2 us
    pallas_call x2, Pallas kernels, take(): pl.pallas_call(functools.partial(take_kernel, pieces), out_shape=shape((s...  3.53 us
  transfers between devices with their start and end apart: 18, of which 7 were waited for; matrix products, arithmetic and copies ran while one was open for 1% of the time, Pallas kernels for 31%

profile of v3, /device:TPU:26, one launch (start us, length us, event | category | flops | bytes accessed | tf_op | source)
XLA Modules:
  0.0 89.2 jit_solution(1360626967540234639)
XLA Ops:
  0.6 0.0 copy-start.4
  0.6 0.0 copy-start
  0.7 0.0 copy-start.2
  0.7 0.0 copy-start.3
  0.7 1.8 %take_first.1 = bf16[112,1024]{1,0:T(8,128)(2,1)} custom-call(bf16[768,1024]{1,0:T(8,128)(2,1)} %refs_3_.1), custom_call_target="tpu_custom_call" | custom-call | tf_op jit(solution)/shard_map/take_first/pallas_call | solution.py:314
  2.5 0.8 collective-permute-start
  3.3 1.7 %take_rest.1 = bf16[160,1024]{1,0:T(8,128)(2,1)} custom-call(bf16[768,1024]{1,0:T(8,128)(2,1)} %refs_3_.1), custom_call_target="tpu_custom_call" | custom-call | tf_op jit(solution)/shard_map/take_rest/pallas_call | solution.py:314
  5.0 0.5 collective-permute-start.1
  5.6 0.0 copy-done.4
  5.6 0.0 copy-done
  5.6 0.0 copy-done.2
  5.6 0.0 copy-done.3
  5.6 0.0 copy-start.1
  5.6 1.4 %copy-done.1 = bf16[768,1024]{1,0:T(8,128)(2,1)S(1)} copy-done((bf16[768,1024]{1,0:T(8,128)(2,1)S(1)}, bf16[768,1024]{1,0:T(8,128)(2,1)}, u32[]{:S(2)}) %copy-start.1) | copy-done | bytes 1572888
  7.0 6.0 %own_scores.1 = (f32[1536,768]{1,0:T(8,128)S(1)}, f32[8,768]{1,0:T(8,128)S(1)}, f32[24,768]{1,0:T(8,128)S(1)}, f32[24,768]{1,0:T(8,128)S(1)}) custom-call(bf16[768,1024]{1,0:T(8,128)(2,1)S(1)} %copy-done.1, bf16[1536,1024]{1,0:T(8,128)(2,1)S(1)} %copy-done, s32[8,768]{1,0:T(8,128)S(1)} %copy-done.2, f32[8,768]{1,0:T(8,128)S(1)} %copy-done.3, ...), custom_call_target="tpu_custom_call" | custom-call | flops 2415919104 | bytes 9661440 | tf_op jit(solution)/shard_map/own_scores/pallas_call | solution.py:265
  13.0 1.3 %collective-permute-done.refs_0_ = bf16[112,1024]{1,0:T(8,128)(2,1)S(1)} collective-permute-done((bf16[112,1024]{1,0:T(8,128)(2,1)}, bf16[112,1024]{1,0:T(8,128)(2,1)S(1)}, u32[]{:S(2)}, u32[]{:S(2)}) %collective-permute-start) | collective-permute-done | bytes 229408 | tf_op jit(solution)/shard_map/ppermute | solution.py:304
  14.3 0.0 collective-permute-start.2
  14.3 2.1 %collective-permute-start.4 = (bf16[112,1024]{1,0:T(8,128)(2,1)S(1)}, bf16[112,1024]{1,0:T(8,128)(2,1)S(1)}, u32[]{:S(2)}, u32[]{:S(2)}) collective-permute-start(bf16[112,1024]{1,0:T(8,128)(2,1)S(1)} %collective-permute-done.refs_0_), channel_id=1, source_target_pairs={{0,2},{1,3},{2,0},{3,1},{4,6},{5,7},{6,4},{7,5},{8,10},{9,11},{10,... | collective-permute-start | bytes 688136 | tf_op jit(solution)/shard_map/ppermute | solution.py:304
  16.4 0.0 collective-permute-start.3
  16.4 7.4 %collective-permute-done.3.refs_7_.pack_ref = f32[24,768]{1,0:T(8,128)S(1)} collective-permute-done((f32[24,768]{1,0:T(8,128)S(1)}, f32[24,768]{1,0:T(8,128)S(1)}, u32[]{:S(2)}, u32[]{:S(2)}) %collective-permute-start.3) | collective-permute-done | bytes 73760 | tf_op jit(solution)/shard_map/ppermute | solution.py:304
  23.8 0.0 collective-permute-done.1.refs_4_
  23.8 0.0 collective-permute-done.2.refs_1_
  23.8 0.0 collective-permute-start.6
  23.8 0.0 collective-permute-done.4.refs_2_
  23.8 0.5 collective-permute-start.5
  24.3 1.4 %collective-permute-done.5.refs_3_ = bf16[112,1024]{1,0:T(8,128)(2,1)S(1)} collective-permute-done((bf16[112,1024]{1,0:T(8,128)(2,1)S(1)}, bf16[112,1024]{1,0:T(8,128)(2,1)S(1)}, u32[]{:S(2)}, u32[]{:S(2)}) %collective-permute-start.5) | collective-permute-done | bytes 229408 | tf_op jit(solution)/shard_map/ppermute | solution.py:304
  25.8 0.0 collective-permute-done.6.refs_5_
  25.8 4.0 %next_scores.1 = (f32[1536,768]{1,0:T(8,128)S(1)}, f32[8,768]{1,0:T(8,128)S(1)}, bf16[768,1024]{1,0:T(8,128)(2,1)S(1)}) custom-call(bf16[112,1024]{1,0:T(8,128)(2,1)S(1)} %collective-permute-done.refs_0_, bf16[112,1024]{1,0:T(8,128)(2,1)S(1)} %collective-permute-done.2.refs_1_, bf16[112,1024]{1,0:T(8,128)(2,1)S(1)} %collective-permute-done.4.refs_2_, ...), custom_call_target="tpu_custom_call" | custom-call | flops 2415919104 | bytes 11108352 | tf_op jit(solution)/shard_map/next_scores/pallas_call | solution.py:265
  29.7 1.7 %collective-permute-start.7 = (f32[8,768]{1,0:T(8,128)S(1)}, f32[8,768]{1,0:T(8,128)S(1)}, u32[]{:S(2)}, u32[]{:S(2)}) collective-permute-start(f32[8,768]{1,0:T(8,128)S(1)} %get-tuple-element.40.stat_ref), channel_id=1, source_target_pairs={{0,2},{1,3},{2,0},{3,1},{4,6},{5,7},{6,4},{7,5},{8,10},{9,11},{10,... | collective-permute-start | bytes 73736 | tf_op jit(solution)/shard_map/ppermute | solution.py:304
  31.5 0.0 collective-permute-start.8
  31.5 2.0 %collective-permute-start.9 = (f32[8,768]{1,0:T(8,128)S(1)}, f32[8,768]{1,0:T(8,128)S(1)}, u32[]{:S(2)}, u32[]{:S(2)}) collective-permute-start(f32[8,768]{1,0:T(8,128)S(1)} %get-tuple-element.40.stat_ref), channel_id=1, source_target_pairs={{0,3},{1,2},{2,1},{3,0},{4,7},{5,6},{6,5},{7,4},{8,11},{9,10},{10,... | collective-permute-start | bytes 73736 | tf_op jit(solution)/shard_map/ppermute | solution.py:304
  33.5 1.7 %collective-permute-done.7.refs_0_ = f32[8,768]{1,0:T(8,128)S(1)} collective-permute-done((f32[8,768]{1,0:T(8,128)S(1)}, f32[8,768]{1,0:T(8,128)S(1)}, u32[]{:S(2)}, u32[]{:S(2)}) %collective-permute-start.7) | collective-permute-done | bytes 24608 | tf_op jit(solution)/shard_map/ppermute | solution.py:304
  35.2 0.0 collective-permute-done.8.refs_1_
  35.2 1.1 %collective-permute-done.9.refs_2_ = f32[8,768]{1,0:T(8,128)S(1)} collective-permute-done((f32[8,768]{1,0:T(8,128)S(1)}, f32[8,768]{1,0:T(8,128)S(1)}, u32[]{:S(2)}, u32[]{:S(2)}) %collective-permute-start.9) | collective-permute-done | bytes 24608 | tf_op jit(solution)/shard_map/ppermute | solution.py:304
  36.2 3.5 %next_grad_b.1 = (bf16[1536,384]{1,0:T(8,128)(2,1)S(1)}, bf16[192,1024]{1,0:T(8,128)(2,1)S(1)}, bf16[192,1024]{1,0:T(8,128)(2,1)S(1)}, f32[8,768]{1,0:T(8,128)S(1)}) custom-call(f32[1536,768]{1,0:T(8,128)S(1)} %get-tuple-element.50.exp_ref, f32[24,768]{1,0:T(8,128)S(1)} %collective-permute-done.3.refs_7_.pack_ref, bf16[1536,1024]{1,0:T(8,128)(2,1)S(1)} %copy-done, ...), custom_call_target="tpu_custom_call" | custom-call | flops 1207959552 | bytes 10027008 | tf_op jit(solution)/shard_map/next_grad_b/pallas_call | solution.py:265
  39.7 0.6 collective-permute-start.11
  40.3 5.6 %collective-permute-start.10 = (f32[8,768]{1,0:T(8,128)S(1)}, f32[8,768]{1,0:T(8,128)S(1)}, u32[]{:S(2)}, u32[]{:S(2)}) collective-permute-start(f32[8,768]{1,0:T(8,128)S(1)} %get-tuple-element.41.refs_0_), channel_id=1, source_target_pairs={{0,4},{1,5},{2,6},{3,7},{4,8},{5,9},{6,10},{7,11},{8,12},{9,13},{1... | collective-permute-start | bytes 73736 | tf_op jit(solution)/shard_map/ppermute | solution.py:304
  45.9 0.0 collective-permute-done.11
  45.9 0.1 add_convert_fusion.3
  46.1 2.2 %collective-permute-start.16 = (bf16[192,1024]{1,0:T(8,128)(2,1)S(1)}, bf16[192,1024]{1,0:T(8,128)(2,1)S(1)}, u32[]{:S(2)}, u32[]{:S(2)}) collective-permute-start(bf16[192,1024]{1,0:T(8,128)(2,1)S(1)} %add_convert_fusion.3), channel_id=1, source_target_pairs={{0,2},{1,3},{2,0},{3,1},{4,6},{5,7},{6,4},{7,5},{8,10},{9,11},{10,... | collective-permute-start | bytes 1179656 | tf_op jit(solution)/shard_map/ppermute | solution.py:304
  48.3 0.0 collective-permute-done.10.whole_ref
  48.3 3.2 %next_grad_a.1 = (bf16[1536,384]{1,0:T(8,128)(2,1)S(1)}, bf16[192,1024]{1,0:T(8,128)(2,1)S(1)}, bf16[192,1024]{1,0:T(8,128)(2,1)S(1)}) custom-call(f32[1536,768]{1,0:T(8,128)S(1)} %get-tuple-element.50.exp_ref, f32[24,768]{1,0:T(8,128)S(1)} %collective-permute-done.3.refs_7_.pack_ref, bf16[1536,1024]{1,0:T(8,128)(2,1)S(1)} %copy-done, ...), custom_call_target="tpu_custom_call" | custom-call | flops 1207959552 | bytes 9953280 | tf_op jit(solution)/shard_map/next_grad_a/pallas_call | solution.py:265
  51.5 0.1 collective-permute-start.15
  51.6 9.1 %own_grad.1 = (bf16[1536,768]{1,0:T(8,128)(2,1)S(1)}, bf16[192,1024]{1,0:T(8,128)(2,1)S(1)}, bf16[192,1024]{1,0:T(8,128)(2,1)S(1)}, bf16[192,1024]{1,0:T(8,128)(2,1)S(1)}, bf16[192,1024]{1,0:T(8,128)(2,1)S(1)}) custom-call(f32[1536,768]{1,0:T(8,128)S(1)} %get-tuple-element.30.exp_ref, f32[24,768]{1,0:T(8,128)S(1)} %get-tuple-element.31.pack_ref, ...), custom_call_target="tpu_custom_call" | custom-call | flops 2415919104 | bytes 11919360 | tf_op jit(solution)/shard_map/own_grad/pallas_call | solution.py:265
  60.7 0.1 collective-permute-start.13
  60.8 0.5 collective-permute-start.12
  61.3 0.0 collective-permute-done.16
  61.3 0.0 collective-permute-done.15
  61.4 0.2 add_convert_fusion.1
  61.6 5.1 %collective-permute-start.17 = (bf16[192,1024]{1,0:T(8,128)(2,1)S(1)}, bf16[192,1024]{1,0:T(8,128)(2,1)S(1)}, u32[]{:S(2)}, u32[]{:S(2)}) collective-permute-start(bf16[192,1024]{1,0:T(8,128)(2,1)S(1)} %add_convert_fusion.1), channel_id=1, source_target_pairs={{0,4},{1,5},{2,6},{3,7},{4,8},{5,9},{6,10},{7,11},{8,12},{9,13},{1... | collective-permute-start | bytes 1179656 | tf_op jit(solution)/shard_map/ppermute | solution.py:304
  66.7 0.0 collective-permute-done.13
  66.7 0.1 add_convert_fusion.2
  66.8 0.3 collective-permute-start.14
  67.1 7.5 %passage_grad.1 = bf16[1536,1024]{1,0:T(8,128)(2,1)} custom-call(bf16[1536,768]{1,0:T(8,128)(2,1)S(1)} %get-tuple-element.54.refs_0_, bf16[1536,384]{1,0:T(8,128)(2,1)S(1)} %get-tuple-element.55.refs_1_, bf16[1536,384]{1,0:T(8,128)(2,1)S(1)} %get-tuple-element.56.refs_2_, bf16[768,1024]{1,0:T(8,128)(2,1)S(1)} %copy-done.1, ...), custom_call_target="tpu_custom_call" | custom-call | flops 4831838208 | bytes 11010048 | tf_op jit(solution)/shard_map/passage_grad/pallas_call | solution.py:265
  74.7 0.0 collective-permute-done.12
  74.7 1.0 %collective-permute-done.17 = bf16[192,1024]{1,0:T(8,128)(2,1)S(1)} collective-permute-done((bf16[192,1024]{1,0:T(8,128)(2,1)S(1)}, bf16[192,1024]{1,0:T(8,128)(2,1)S(1)}, u32[]{:S(2)}, u32[]{:S(2)}) %collective-permute-start.17) | collective-permute-done | bytes 393248 | tf_op jit(solution)/shard_map/ppermute | solution.py:304
  75.7 12.5 %collective-permute-done.14 = bf16[192,1024]{1,0:T(8,128)(2,1)S(1)} collective-permute-done((bf16[192,1024]{1,0:T(8,128)(2,1)S(1)}, bf16[192,1024]{1,0:T(8,128)(2,1)S(1)}, u32[]{:S(2)}, u32[]{:S(2)}) %collective-permute-start.14) | collective-permute-done | bytes 393248 | tf_op jit(solution)/shard_map/ppermute | solution.py:304
  88.2 1.0 %add_convert_fusion = bf16[192,1024]{1,0:T(8,128)(2,1)} fusion(bf16[192,1024]{1,0:T(8,128)(2,1)S(1)} %collective-permute-done.17, bf16[192,1024]{1,0:T(8,128)(2,1)S(1)} %collective-permute-done.14, bf16[192,1024]{1,0:T(8,128)(2,1)S(1)} %collective-permute-done.12, bf16[192,1024]{1,0:T(8,128)(2,1)S(1)} %get-tuple-element.46), kind=kLoop, calls=%fused_computation | loop fusion | flops 1572864 | bytes 1966080 | tf_op jit(solution)/shard_map/convert_element_type | solution.py:404
  (1 shorter events, 0.0 us)
Async XLA Ops:
  0.6 4.9 %copy-start.4 = (f32[768]{0:T(1024)S(1)}, f32[768]{0:T(1024)}, u32[]{:S(2)}) copy-start(f32[768]{0:T(1024)} %param.7) | copy-start | bytes 9220
  0.6 4.9 %copy-start = (bf16[1536,1024]{1,0:T(8,128)(2,1)S(1)}, bf16[1536,1024]{1,0:T(8,128)(2,1)}, u32[]{:S(2)}) copy-start(bf16[1536,1024]{1,0:T(8,128)(2,1)} %p_ref.5) | copy-start | bytes 9437188
  0.7 4.9 %copy-start.2 = (s32[8,768]{1,0:T(8,128)S(1)}, s32[8,768]{1,0:T(8,128)}, u32[]{:S(2)}) copy-start(s32[8,768]{1,0:T(8,128)} %ids_ref.1) | copy-start | bytes 73732
  0.7 4.9 %copy-start.3 = (f32[8,768]{1,0:T(8,128)S(1)}, f32[8,768]{1,0:T(8,128)}, u32[]{:S(2)}) copy-start(f32[8,768]{1,0:T(8,128)} %logits_ref.1) | copy-start | bytes 73732
  2.5 11.8 %collective-permute-start = (bf16[112,1024]{1,0:T(8,128)(2,1)}, bf16[112,1024]{1,0:T(8,128)(2,1)S(1)}, u32[]{:S(2)}, u32[]{:S(2)}) collective-permute-start(bf16[112,1024]{1,0:T(8,128)(2,1)} %take_first.1), channel_id=1, source_target_pairs={{0,252},{1,253},{2,254},{3,255},{4,0},{5,1},{6,2},{7,3},{8,4},{9,5... | collective-permute-start | bytes 688136 | tf_op jit(solution)/shard_map/ppermute | solution.py:304
  5.0 18.8 %collective-permute-start.1 = (bf16[160,1024]{1,0:T(8,128)(2,1)}, bf16[160,1024]{1,0:T(8,128)(2,1)S(1)}, u32[]{:S(2)}, u32[]{:S(2)}) collective-permute-start(bf16[160,1024]{1,0:T(8,128)(2,1)} %take_rest.1), channel_id=1, source_target_pairs={{0,252},{1,253},{2,254},{3,255},{4,0},{5,1},{6,2},{7,3},{8,4},{9,5... | collective-permute-start | bytes 983048 | tf_op jit(solution)/shard_map/ppermute | solution.py:304
  5.6 1.4 %copy-start.1 = (bf16[768,1024]{1,0:T(8,128)(2,1)S(1)}, bf16[768,1024]{1,0:T(8,128)(2,1)}, u32[]{:S(2)}) copy-start(bf16[768,1024]{1,0:T(8,128)(2,1)} %refs_3_.1) | copy-start | bytes 4718596
  14.3 9.5 %collective-permute-start.2 = (bf16[112,1024]{1,0:T(8,128)(2,1)S(1)}, bf16[112,1024]{1,0:T(8,128)(2,1)S(1)}, u32[]{:S(2)}, u32[]{:S(2)}) collective-permute-start(bf16[112,1024]{1,0:T(8,128)(2,1)S(1)} %collective-permute-done.refs_0_), channel_id=1, source_target_pairs={{0,1},{1,0},{2,3},{3,2},{4,5},{5,4},{6,7},{7,6},{8,9},{9,8},{10,11... | collective-permute-start | bytes 688136 | tf_op jit(solution)/shard_map/ppermute | solution.py:304
  14.3 9.6 %collective-permute-start.4 = (bf16[112,1024]{1,0:T(8,128)(2,1)S(1)}, bf16[112,1024]{1,0:T(8,128)(2,1)S(1)}, u32[]{:S(2)}, u32[]{:S(2)}) collective-permute-start(bf16[112,1024]{1,0:T(8,128)(2,1)S(1)} %collective-permute-done.refs_0_), channel_id=1, source_target_pairs={{0,2},{1,3},{2,0},{3,1},{4,6},{5,7},{6,4},{7,5},{8,10},{9,11},{10,... | collective-permute-start | bytes 688136 | tf_op jit(solution)/shard_map/ppermute | solution.py:304
  16.4 7.4 %collective-permute-start.3 = (f32[24,768]{1,0:T(8,128)S(1)}, f32[24,768]{1,0:T(8,128)S(1)}, u32[]{:S(2)}, u32[]{:S(2)}) collective-permute-start(f32[24,768]{1,0:T(8,128)S(1)} %get-tuple-element.35), channel_id=1, source_target_pairs={{0,252},{1,253},{2,254},{3,255},{4,0},{5,1},{6,2},{7,3},{8,4},{9,5... | collective-permute-start | bytes 221192 | tf_op jit(solution)/shard_map/ppermute | solution.py:304
  23.8 2.0 %collective-permute-start.6 = (bf16[160,1024]{1,0:T(8,128)(2,1)S(1)}, bf16[160,1024]{1,0:T(8,128)(2,1)S(1)}, u32[]{:S(2)}, u32[]{:S(2)}) collective-permute-start(bf16[160,1024]{1,0:T(8,128)(2,1)S(1)} %collective-permute-done.1.refs_4_), channel_id=1, source_target_pairs={{0,1},{1,0},{2,3},{3,2},{4,5},{5,4},{6,7},{7,6},{8,9},{9,8},{10,11... | collective-permute-start | bytes 983048 | tf_op jit(solution)/shard_map/ppermute | solution.py:304
  23.8 1.9 %collective-permute-start.5 = (bf16[112,1024]{1,0:T(8,128)(2,1)S(1)}, bf16[112,1024]{1,0:T(8,128)(2,1)S(1)}, u32[]{:S(2)}, u32[]{:S(2)}) collective-permute-start(bf16[112,1024]{1,0:T(8,128)(2,1)S(1)} %collective-permute-done.4.refs_2_), channel_id=1, source_target_pairs={{0,1},{1,0},{2,3},{3,2},{4,5},{5,4},{6,7},{7,6},{8,9},{9,8},{10,11... | collective-permute-start | bytes 688136 | tf_op jit(solution)/shard_map/ppermute | solution.py:304
  29.7 5.4 %collective-permute-start.7 = (f32[8,768]{1,0:T(8,128)S(1)}, f32[8,768]{1,0:T(8,128)S(1)}, u32[]{:S(2)}, u32[]{:S(2)}) collective-permute-start(f32[8,768]{1,0:T(8,128)S(1)} %get-tuple-element.40.stat_ref), channel_id=1, source_target_pairs={{0,2},{1,3},{2,0},{3,1},{4,6},{5,7},{6,4},{7,5},{8,10},{9,11},{10,... | collective-permute-start | bytes 73736 | tf_op jit(solution)/shard_map/ppermute | solution.py:304
  31.5 3.7 %collective-permute-start.8 = (f32[8,768]{1,0:T(8,128)S(1)}, f32[8,768]{1,0:T(8,128)S(1)}, u32[]{:S(2)}, u32[]{:S(2)}) collective-permute-start(f32[8,768]{1,0:T(8,128)S(1)} %get-tuple-element.40.stat_ref), channel_id=1, source_target_pairs={{0,1},{1,0},{2,3},{3,2},{4,5},{5,4},{6,7},{7,6},{8,9},{9,8},{10,11... | collective-permute-start | bytes 73736 | tf_op jit(solution)/shard_map/ppermute | solution.py:304
  31.5 4.8 %collective-permute-start.9 = (f32[8,768]{1,0:T(8,128)S(1)}, f32[8,768]{1,0:T(8,128)S(1)}, u32[]{:S(2)}, u32[]{:S(2)}) collective-permute-start(f32[8,768]{1,0:T(8,128)S(1)} %get-tuple-element.40.stat_ref), channel_id=1, source_target_pairs={{0,3},{1,2},{2,1},{3,0},{4,7},{5,6},{6,5},{7,4},{8,11},{9,10},{10,... | collective-permute-start | bytes 73736 | tf_op jit(solution)/shard_map/ppermute | solution.py:304
  39.7 6.2 %collective-permute-start.11 = (bf16[192,1024]{1,0:T(8,128)(2,1)S(1)}, bf16[192,1024]{1,0:T(8,128)(2,1)S(1)}, u32[]{:S(2)}, u32[]{:S(2)}) collective-permute-start(bf16[192,1024]{1,0:T(8,128)(2,1)S(1)} %get-tuple-element.43), channel_id=1, source_target_pairs={{0,1},{1,0},{2,3},{3,2},{4,5},{5,4},{6,7},{7,6},{8,9},{9,8},{10,11... | collective-permute-start | bytes 1179656 | tf_op jit(solution)/shard_map/ppermute | solution.py:304
  40.3 7.9 %collective-permute-start.10 = (f32[8,768]{1,0:T(8,128)S(1)}, f32[8,768]{1,0:T(8,128)S(1)}, u32[]{:S(2)}, u32[]{:S(2)}) collective-permute-start(f32[8,768]{1,0:T(8,128)S(1)} %get-tuple-element.41.refs_0_), channel_id=1, source_target_pairs={{0,4},{1,5},{2,6},{3,7},{4,8},{5,9},{6,10},{7,11},{8,12},{9,13},{1... | collective-permute-start | bytes 73736 | tf_op jit(solution)/shard_map/ppermute | solution.py:304
  46.1 15.3 %collective-permute-start.16 = (bf16[192,1024]{1,0:T(8,128)(2,1)S(1)}, bf16[192,1024]{1,0:T(8,128)(2,1)S(1)}, u32[]{:S(2)}, u32[]{:S(2)}) collective-permute-start(bf16[192,1024]{1,0:T(8,128)(2,1)S(1)} %add_convert_fusion.3), channel_id=1, source_target_pairs={{0,2},{1,3},{2,0},{3,1},{4,6},{5,7},{6,4},{7,5},{8,10},{9,11},{10,... | collective-permute-start | bytes 1179656 | tf_op jit(solution)/shard_map/ppermute | solution.py:304
  51.5 9.9 %collective-permute-start.15 = (bf16[192,1024]{1,0:T(8,128)(2,1)S(1)}, bf16[192,1024]{1,0:T(8,128)(2,1)S(1)}, u32[]{:S(2)}, u32[]{:S(2)}) collective-permute-start(bf16[192,1024]{1,0:T(8,128)(2,1)S(1)} %get-tuple-element.52), channel_id=1, source_target_pairs={{0,1},{1,0},{2,3},{3,2},{4,5},{5,4},{6,7},{7,6},{8,9},{9,8},{10,11... | collective-permute-start | bytes 1179656 | tf_op jit(solution)/shard_map/ppermute | solution.py:304
  60.7 5.9 %collective-permute-start.13 = (bf16[192,1024]{1,0:T(8,128)(2,1)S(1)}, bf16[192,1024]{1,0:T(8,128)(2,1)S(1)}, u32[]{:S(2)}, u32[]{:S(2)}) collective-permute-start(bf16[192,1024]{1,0:T(8,128)(2,1)S(1)} %get-tuple-element.49), channel_id=1, source_target_pairs={{0,1},{1,0},{2,3},{3,2},{4,5},{5,4},{6,7},{7,6},{8,9},{9,8},{10,11... | collective-permute-start | bytes 1179656 | tf_op jit(solution)/shard_map/ppermute | solution.py:304
  60.8 13.8 %collective-permute-start.12 = (bf16[192,1024]{1,0:T(8,128)(2,1)S(1)}, bf16[192,1024]{1,0:T(8,128)(2,1)S(1)}, u32[]{:S(2)}, u32[]{:S(2)}) collective-permute-start(bf16[192,1024]{1,0:T(8,128)(2,1)S(1)} %get-tuple-element.47), channel_id=1, source_target_pairs={{0,1},{1,0},{2,3},{3,2},{4,5},{5,4},{6,7},{7,6},{8,9},{9,8},{10,11... | collective-permute-start | bytes 1179656 | tf_op jit(solution)/shard_map/ppermute | solution.py:304
  61.6 14.1 %collective-permute-start.17 = (bf16[192,1024]{1,0:T(8,128)(2,1)S(1)}, bf16[192,1024]{1,0:T(8,128)(2,1)S(1)}, u32[]{:S(2)}, u32[]{:S(2)}) collective-permute-start(bf16[192,1024]{1,0:T(8,128)(2,1)S(1)} %add_convert_fusion.1), channel_id=1, source_target_pairs={{0,4},{1,5},{2,6},{3,7},{4,8},{5,9},{6,10},{7,11},{8,12},{9,13},{1... | collective-permute-start | bytes 1179656 | tf_op jit(solution)/shard_map/ppermute | solution.py:304
  66.8 21.4 %collective-permute-start.14 = (bf16[192,1024]{1,0:T(8,128)(2,1)S(1)}, bf16[192,1024]{1,0:T(8,128)(2,1)S(1)}, u32[]{:S(2)}, u32[]{:S(2)}) collective-permute-start(bf16[192,1024]{1,0:T(8,128)(2,1)S(1)} %add_convert_fusion.2), channel_id=1, source_target_pairs={{0,2},{1,3},{2,0},{3,1},{4,6},{5,7},{6,4},{7,5},{8,10},{9,11},{10,... | collective-permute-start | bytes 1179656 | tf_op jit(solution)/shard_map/ppermute | solution.py:304

commit v4 on v3

--- a/solution.py
+++ b/solution.py
@@ -64,21 +64,34 @@
 
 
 def own_kernel(
-    scale, coef_scale, q_any, p_any, ids_ref, logits_ref, loss_ref,
+    scale, coef_scale, q_hbm, p_hbm, ids_ref, logits_ref, loss_ref,
     exp_ref, stat_ref, pack_ref, sent_ref, q_ref, p_ref, sems,
 ):
-    parts = sems.shape[0] - 1
-    size = p_ref.shape[0] // parts
-    copies = [pltpu.make_async_copy(q_any, q_ref, sems.at[parts])]
+    group = lax.axis_index("grp")
+    parts = sems.shape[0] - 4
+    quarter, size = q_ref.shape[0] // 4, p_ref.shape[0] // parts
+    copies = []
+    for slot in range(4):
+        first = pl.multiple_of((group ^ slot) * quarter, 16)
+        copies.append(
+            pltpu.make_async_copy(
+                q_hbm.at[pl.ds(first, quarter)],
+                q_ref.at[pl.ds(slot * quarter, quarter)],
+                sems.at[slot],
+            )
+        )
     for part in range(parts):
         rows = pl.ds(part * size, size)
-        copies.append(pltpu.make_async_copy(p_any.at[rows], p_ref.at[rows], sems.at[part]))
+        copies.append(pltpu.make_async_copy(p_hbm.at[rows], p_ref.at[rows], sems.at[4 + part]))
     for copy in copies:
         copy.start()
     labels(coef_scale * loss_ref[...], ids_ref, logits_ref, pack_ref, sent_ref, p_ref.shape[0])
-    copies[0].wait()
+    pack_ref[...] = reorder(pack_ref[...], group)
+    sent_ref[...] = reorder(sent_ref[...], group)
+    for copy in copies[:4]:
+        copy.wait()
     for part in range(parts):
-        copies[1 + part].wait()
+        copies[4 + part].wait()
         rows = pl.ds(part * size, size)
         fill_scores(scale, p_ref.at[rows], q_ref, exp_ref.at[rows])
     top, total = exponentials(exp_ref)
@@ -102,7 +115,7 @@
         rows_ref[at + cut : at + cut + left, :] = rest[skip : skip + left, :]
         at += cut + left
     fill_scores(scale, p_ref, rows_ref, exp_ref)
-    before = reorder(before_ref[16:24, :], lax.axis_index("grp"))
+    before = before_ref[16:24, :]
     top, total = exponentials(exp_ref, before[1:2])
     stat_ref[0:1, :] = top
     stat_ref[1:2, :] = total + before[2:3] * jnp.exp2(before[1:2] - top)
@@ -190,21 +203,15 @@
         )
 
 
-def next_grad_kernel(place, merge, exp_ref, pack_ref, p_ref, stat_ref, *refs):
-    group = lax.axis_index("grp")
-    if merge:
-        cross_ref, core_ref, both_ref, grad_ref, mine_ref, other_ref, whole_ref = refs
-        top, total = merge_stats(stat_ref[...], cross_ref[...], core_ref[...], both_ref[...])
-        whole_ref[0:1, :] = top
-        whole_ref[1:2, :] = total
-    else:
-        whole_ref, grad_ref, mine_ref, other_ref = refs
-        top, total = whole_ref[0:1, :], whole_ref[1:2, :]
+def grads_of(place, exp_ref, pack_ref, p_ref, stat_ref, whole_ref, grad_ref, mine_ref, other_ref):
     quarter = mine_ref.shape[0]
     lanes = slice(place * 2 * quarter, (place + 1) * 2 * quarter)
-    pack = reorder(pack_ref[...], group)[:, lanes]
-    factor = pack[16:17] * (jnp.exp2(stat_ref[0:1, lanes] - top[:, lanes]) / total[:, lanes])
-    fill_grads(exp_ref.at[:, lanes], grad_ref, factor, pack[0:8], pack[8:16])
+    factor = pack_ref[16:17, lanes] * (
+        jnp.exp2(stat_ref[0:1, lanes] - whole_ref[0:1, lanes]) / whole_ref[1:2, lanes]
+    )
+    fill_grads(
+        exp_ref.at[:, lanes], grad_ref, factor, pack_ref[0:8, lanes], pack_ref[8:16, lanes]
+    )
 
     def put(at, part):
         mine_ref[:, at : at + TILE] = part[:quarter]
@@ -213,26 +220,26 @@
     query_product(grad_ref, p_ref, put)
 
 
-def own_grad_kernel(exp_ref, pack_ref, p_ref, stat_ref, whole_ref, grad_ref, *outs):
-    *outs, rows_ref = outs
-    group = lax.axis_index("grp")
-    whole = reorder(whole_ref[...], group)
-    factor = pack_ref[16:17, :] * (jnp.exp2(stat_ref[0:1, :] - whole[0:1]) / whole[1:2])
-    fill_grads(exp_ref, grad_ref, factor, pack_ref[0:8, :], pack_ref[8:16, :])
-
-    def put(at, part):
-        rows_ref[:, at : at + TILE] = part
-
-    query_product(grad_ref, p_ref, put)
-    quarter = outs[0].shape[0]
-    for slot in range(4):
-        first = pl.multiple_of((group ^ slot) * quarter, quarter)
-        outs[slot][...] = rows_ref[pl.ds(first, quarter), :]
-
-
-def passage_kernel(count, half, *refs):
-    grads, (rows_ref, next_ref, out_ref) = refs[:count], refs[count:]
-    rows = (rows_ref, next_ref.at[half:, :], next_ref.at[:half, :])
+def first_grad_kernel(p_ref, exp_ref, pack_ref, stat_ref, cross_ref, core_ref, both_ref, *outs):
+    *outs, whole_ref = outs
+    top, total = merge_stats(stat_ref[...], cross_ref[...], core_ref[...], both_ref[...])
+    whole_ref[0:1, :] = top
+    whole_ref[1:2, :] = total
+    grads_of(1, exp_ref, pack_ref, p_ref, stat_ref, whole_ref, *outs)
+
+
+def grad_kernel(places, p_ref, *refs):
+    ins, outs = refs[: 4 * len(places)], refs[4 * len(places) :]
+    for n, place in enumerate(places):
+        exp_ref, pack_ref, stat_ref, whole_ref = ins[4 * n : 4 * n + 4]
+        grads_of(
+            place, exp_ref, pack_ref, p_ref, stat_ref, whole_ref, *outs[3 * n : 3 * n + 3]
+        )
+
+
+def passage_kernel(half, *refs):
+    grads, (own_ref, next_ref, out_ref) = refs[:4], refs[4:]
+    rows = [ref.at[at : at + half, :] for ref in (own_ref, next_ref) for at in (0, half)]
     for at in range(0, out_ref.shape[1], TILE):
         out_ref[:, at : at + TILE] = sum(
             jnp.dot(
@@ -265,7 +272,7 @@
     return pl.pallas_call(
         kernel,
         out_shape=tuple(outs),
-        in_specs=[pl.BlockSpec(memory_space=pl.ANY)] * anywhere
+        in_specs=[pl.BlockSpec(memory_space=pltpu.HBM)] * anywhere
         + [IN_VMEM] * (len(ins) - anywhere),
         out_specs=(IN_VMEM,) * len(outs),
         scratch_shapes=list(scratch),
@@ -325,21 +332,20 @@
     rest_out = take(((0, cut, quarter - cut), (2, cut, quarter - cut)), "take_rest")
     rest_mine = move(rest_out, along(-1))
 
-    exp_own, stat_own, pack_own, pack_out = call(
+    first_mine, loss_grad = lax.optimization_barrier((first_mine, loss_grad))
+    exp_own, stat_own, pack_own, pack_out, q_own = call(
         functools.partial(own_kernel, scale, score_scale),
-        [shape((width, rows), f32), stat, pack, pack],
+        [shape((width, rows), f32), stat, pack, pack, shape((rows, depth), bf16)],
         [queries, passages, passage_ids, teacher_logits, loss_grad[None, :]],
         [
-            pltpu.VMEM((rows, depth), bf16),
             pltpu.VMEM((width, depth), bf16),
-            pltpu.SemaphoreType.DMA((4,)),
+            pltpu.SemaphoreType.DMA((7,)),
         ],
         flops=2 * rows * width * depth,
         name="own_scores",
         anywhere=2,
     )
     pack_next = move(pack_out, along(-1))
-    first_mine, stat_own = lax.optimization_barrier((first_mine, stat_own))
     cross_mine = move(first_mine, across(2))
     first_other = move(first_mine, across(1))
     rest_mine, first_other, pack_next = lax.optimization_barrier(
@@ -359,43 +365,44 @@
 
     cross, core, both = (move(stat_next, across(turn)) for turn in (2, 1, 3))
 
-    def next_grads(place, merge, stats, name):
+    def grads(kernel, ins, count, more, name):
         return call(
-            functools.partial(next_grad_kernel, place, merge),
-            [shape((width, half), bf16), piece, piece] + ([stat] if merge else []),
-            [exp_next, pack_next, passages] + stats,
-            flops=2 * half * width * depth,
+            kernel,
+            [shape((width, half), bf16), piece, piece] * count + more,
+            [passages] + ins,
+            flops=2 * count * half * width * depth,
             name=name,
         )
 
-    g_b, nb_mine, nb_other, whole_next = next_grads(
-        1, True, [stat_next, cross, core, both], "next_grad_b"
+    g_b, nb_mine, nb_other, whole_next = grads(
+        first_grad_kernel, [exp_next, pack_next, stat_next, cross, core, both], 1, [stat],
+        "next_grad_b",
     )
     nb_in = move(nb_other, across(1))
     whole_own = move(whole_next, along(1))
     nb = (nb_mine.astype(f32) + nb_in.astype(f32)).astype(bf16)
     nb, exp_next = lax.optimization_barrier((nb, exp_next))
-    whole_own, exp_next = lax.optimization_barrier((whole_own, exp_next))
     nb_cross = move(nb, across(2))
-    g_a, na_mine, na_other = next_grads(0, False, [stat_next, whole_next], "next_grad_a")
+    of_next = [exp_next, pack_next, stat_next, whole_next]
+    of_own = [exp_own, pack_own, stat_own, whole_own]
+    g_a, na_mine, na_other, g_ob, ob_mine, ob_other = grads(
+        functools.partial(grad_kernel, (0, 1)), of_next + of_own, 2, [], "next_a_own_b"
+    )
     na_in = move(na_other, across(1))
-    g_own, oa_mine, oa_other, ob_mine, ob_other = call(
-        own_grad_kernel,
-        [shape((width, rows), bf16)] + [piece] * 4,
-        [exp_own, pack_own, passages, stat_own, whole_own],
-        [pltpu.VMEM((rows, depth), bf16)],
-        flops=2 * rows * width * depth,
-        name="own_grad",
-    )
-    ob = (ob_mine.astype(f32) + move(ob_other, across(1)).astype(f32)).astype(bf16)
+    ob_in = move(ob_other, across(1))
+    ob_mine, nb_cross = lax.optimization_barrier((ob_mine, nb_cross))
+    ob = (ob_mine.astype(f32) + ob_in.astype(f32)).astype(bf16)
     ob_cross = move(ob, across(2))
+    g_oa, oa_mine, oa_other = grads(
+        functools.partial(grad_kernel, (0,)), of_own, 1, [], "own_grad_a"
+    )
     oa_in = move(oa_other, across(1))
     sent = (na_mine.astype(f32) + na_in.astype(f32) + nb_cross.astype(f32)).astype(bf16)
     came = move(sent, along(1))
     (passage_grad,) = call(
-        functools.partial(passage_kernel, 3, half),
+        functools.partial(passage_kernel, half),
         [shape((width, depth), bf16)],
-        [g_own, g_b, g_a, queries, q_next],
+        [g_oa, g_ob, g_a, g_b, q_own, q_next],
         flops=4 * rows * width * depth,
         name="passage_grad",
     )

time: 89.1 us -> 93 us (1.044)
  the two profiles are of different devices: /device:TPU:26 before, /device:TPU:1 now
where the time goes in v4:
time: 93 us; the launch traced here: 92.9 us
  Pallas kernels  35.4 us (38%)
  starting transfers between devices  33.5 us (36%)
  waiting for transfers between devices  20.3 us (22%)
  other arithmetic  1.46 us (2%)
  local copies, waits for them, and re-layouts  1.42 us (2%)
    ppermute x18, starting transfers between devices, move(): return lax.ppermute(x, AXES, pairs)  33.5 us
    pallas_call x6, Pallas kernels, call(): pl.pallas_call(kernel, out_shape=tuple(outs), in_specs=[pl.BlockSpec(memo...  31.8 us
    ppermute x18, waiting for transfers between devices, move(): return lax.ppermute(x, AXES, pairs)  20.3 us
    pallas_call x2, Pallas kernels, take(): pl.pallas_call(functools.partial(take_kernel, pieces), out_shape=shape((s...  3.53 us
  transfers between devices with their start and end apart: 18, of which 9 were waited for; matrix products, arithmetic and copies ran while one was open for 0% of the time, Pallas kernels for 28%

profile of v4, /device:TPU:1, one launch (start us, length us, event | category | flops | bytes accessed | tf_op | source)
XLA Modules:
  0.0 92.9 jit_solution(12451146520031185210)
XLA Ops:
  0.6 0.0 copy-start.4
  0.6 0.0 copy-start
  0.7 0.0 copy-start.2
  0.7 0.0 copy-start.3
  0.7 1.8 %take_first.1 = bf16[112,1024]{1,0:T(8,128)(2,1)} custom-call(bf16[768,1024]{1,0:T(8,128)(2,1)} %q_ref.3), custom_call_target="tpu_custom_call" | custom-call | tf_op jit(solution)/shard_map/take_first/pallas_call | solution.py:321
  2.5 9.9 %collective-permute-start = (bf16[112,1024]{1,0:T(8,128)(2,1)}, bf16[112,1024]{1,0:T(8,128)(2,1)S(1)}, u32[]{:S(2)}, u32[]{:S(2)}) collective-permute-start(bf16[112,1024]{1,0:T(8,128)(2,1)} %take_first.1), channel_id=1, source_target_pairs={{0,252},{1,253},{2,254},{3,255},{4,0},{5,1},{6,2},{7,3},{8,4},{9,5... | collective-permute-start | bytes 688136 | tf_op jit(solution)/shard_map/ppermute | solution.py:311
  12.3 1.7 %take_rest.1 = bf16[160,1024]{1,0:T(8,128)(2,1)} custom-call(bf16[768,1024]{1,0:T(8,128)(2,1)} %q_ref.3), custom_call_target="tpu_custom_call" | custom-call | tf_op jit(solution)/shard_map/take_rest/pallas_call | solution.py:321
  14.1 0.5 collective-permute-start.1
  14.6 2.3 %collective-permute-done.refs_0_ = bf16[112,1024]{1,0:T(8,128)(2,1)S(1)} collective-permute-done((bf16[112,1024]{1,0:T(8,128)(2,1)}, bf16[112,1024]{1,0:T(8,128)(2,1)S(1)}, u32[]{:S(2)}, u32[]{:S(2)}) %collective-permute-start) | collective-permute-done | bytes 229408 | tf_op jit(solution)/shard_map/ppermute | solution.py:311
  16.9 2.5 %collective-permute-start.4 = (bf16[112,1024]{1,0:T(8,128)(2,1)S(1)}, bf16[112,1024]{1,0:T(8,128)(2,1)S(1)}, u32[]{:S(2)}, u32[]{:S(2)}) collective-permute-start(bf16[112,1024]{1,0:T(8,128)(2,1)S(1)} %collective-permute-done.refs_0_), channel_id=1, source_target_pairs={{0,2},{1,3},{2,0},{3,1},{4,6},{5,7},{6,4},{7,5},{8,10},{9,11},{10,... | collective-permute-start | bytes 688136 | tf_op jit(solution)/shard_map/ppermute | solution.py:311
  19.4 3.0 %collective-permute-start.2 = (bf16[112,1024]{1,0:T(8,128)(2,1)S(1)}, bf16[112,1024]{1,0:T(8,128)(2,1)S(1)}, u32[]{:S(2)}, u32[]{:S(2)}) collective-permute-start(bf16[112,1024]{1,0:T(8,128)(2,1)S(1)} %collective-permute-done.refs_0_), channel_id=1, source_target_pairs={{0,1},{1,0},{2,3},{3,2},{4,5},{5,4},{6,7},{7,6},{8,9},{9,8},{10,11... | collective-permute-start | bytes 688136 | tf_op jit(solution)/shard_map/ppermute | solution.py:311
  22.4 0.0 copy-done.4
  22.4 0.0 copy-done
  22.4 0.0 copy-done.2
  22.4 0.0 copy-done.3
  22.4 0.0 copy-start.1
  22.4 1.4 %copy-done.1 = bf16[768,1024]{1,0:T(8,128)(2,1)S(1)} copy-done((bf16[768,1024]{1,0:T(8,128)(2,1)S(1)}, bf16[768,1024]{1,0:T(8,128)(2,1)}, u32[]{:S(2)}) %copy-start.1) | copy-done | bytes 1572888
  23.8 6.8 %own_scores.1 = (f32[1536,768]{1,0:T(8,128)S(1)}, f32[8,768]{1,0:T(8,128)S(1)}, f32[24,768]{1,0:T(8,128)S(1)}, f32[24,768]{1,0:T(8,128)S(1)}, bf16[768,1024]{1,0:T(8,128)(2,1)S(1)}) custom-call(bf16[768,1024]{1,0:T(8,128)(2,1)S(1)} %copy-done.1, bf16[1536,1024]{1,0:T(8,128)(2,1)S(1)} %copy-done, s32[8,768]{1,0:T(8,128)S(1)} %copy-done.2, ...), custom_call_target="tpu_custom_call" | custom-call | flops 2415919104 | bytes 11234304 | tf_op jit(solution)/shard_map/own_scores/pallas_call | solution.py:272
  30.6 5.9 %collective-permute-start.3 = (f32[24,768]{1,0:T(8,128)S(1)}, f32[24,768]{1,0:T(8,128)S(1)}, u32[]{:S(2)}, u32[]{:S(2)}) collective-permute-start(f32[24,768]{1,0:T(8,128)S(1)} %get-tuple-element.37), channel_id=1, source_target_pairs={{0,252},{1,253},{2,254},{3,255},{4,0},{5,1},{6,2},{7,3},{8,4},{9,5... | collective-permute-start | bytes 221192 | tf_op jit(solution)/shard_map/ppermute | solution.py:311
  36.5 1.7 %collective-permute-done.3.refs_7_.pack_ref.refs_1_ = f32[24,768]{1,0:T(8,128)S(1)} collective-permute-done((f32[24,768]{1,0:T(8,128)S(1)}, f32[24,768]{1,0:T(8,128)S(1)}, u32[]{:S(2)}, u32[]{:S(2)}) %collective-permute-start.3) | collective-permute-done | bytes 73760 | tf_op jit(solution)/shard_map/ppermute | solution.py:311
  38.2 0.0 collective-permute-done.1.refs_4_
  38.2 0.0 collective-permute-done.2.refs_1_
  38.2 0.8 collective-permute-start.6
  39.0 0.0 collective-permute-done.4.refs_2_
  39.0 0.1 collective-permute-start.5
  39.1 1.5 %collective-permute-done.5.refs_3_ = bf16[112,1024]{1,0:T(8,128)(2,1)S(1)} collective-permute-done((bf16[112,1024]{1,0:T(8,128)(2,1)S(1)}, bf16[112,1024]{1,0:T(8,128)(2,1)S(1)}, u32[]{:S(2)}, u32[]{:S(2)}) %collective-permute-start.5) | collective-permute-done | bytes 229408 | tf_op jit(solution)/shard_map/ppermute | solution.py:311
  40.6 0.0 collective-permute-done.6.refs_5_
  40.6 4.0 %next_scores.1 = (f32[1536,768]{1,0:T(8,128)S(1)}, f32[8,768]{1,0:T(8,128)S(1)}, bf16[768,1024]{1,0:T(8,128)(2,1)S(1)}) custom-call(bf16[112,1024]{1,0:T(8,128)(2,1)S(1)} %collective-permute-done.refs_0_, bf16[112,1024]{1,0:T(8,128)(2,1)S(1)} %collective-permute-done.2.refs_1_, bf16[112,1024]{1,0:T(8,128)(2,1)S(1)} %collective-permute-done.4.refs_2_, ...), custom_call_target="tpu_custom_call" | custom-call | flops 2415919104 | bytes 11108352 | tf_op jit(solution)/shard_map/next_scores/pallas_call | solution.py:272
  44.5 2.1 %collective-permute-start.9 = (f32[8,768]{1,0:T(8,128)S(1)}, f32[8,768]{1,0:T(8,128)S(1)}, u32[]{:S(2)}, u32[]{:S(2)}) collective-permute-start(f32[8,768]{1,0:T(8,128)S(1)} %get-tuple-element.42.stat_ref.refs_2_), channel_id=1, source_target_pairs={{0,3},{1,2},{2,1},{3,0},{4,7},{5,6},{6,5},{7,4},{8,11},{9,10},{10,... | collective-permute-start | bytes 73736 | tf_op jit(solution)/shard_map/ppermute | solution.py:311
  46.6 0.1 collective-permute-start.8
  46.7 1.3 %collective-permute-start.7 = (f32[8,768]{1,0:T(8,128)S(1)}, f32[8,768]{1,0:T(8,128)S(1)}, u32[]{:S(2)}, u32[]{:S(2)}) collective-permute-start(f32[8,768]{1,0:T(8,128)S(1)} %get-tuple-element.42.stat_ref.refs_2_), channel_id=1, source_target_pairs={{0,2},{1,3},{2,0},{3,1},{4,6},{5,7},{6,4},{7,5},{8,10},{9,11},{10,... | collective-permute-start | bytes 73736 | tf_op jit(solution)/shard_map/ppermute | solution.py:311
  48.0 1.4 %collective-permute-done.9.both_ref = f32[8,768]{1,0:T(8,128)S(1)} collective-permute-done((f32[8,768]{1,0:T(8,128)S(1)}, f32[8,768]{1,0:T(8,128)S(1)}, u32[]{:S(2)}, u32[]{:S(2)}) %collective-permute-start.9) | collective-permute-done | bytes 24608 | tf_op jit(solution)/shard_map/ppermute | solution.py:311
  49.4 0.0 collective-permute-done.8.core_ref
  49.4 1.5 %collective-permute-done.7.cross_ref = f32[8,768]{1,0:T(8,128)S(1)} collective-permute-done((f32[8,768]{1,0:T(8,128)S(1)}, f32[8,768]{1,0:T(8,128)S(1)}, u32[]{:S(2)}, u32[]{:S(2)}) %collective-permute-start.7) | collective-permute-done | bytes 24608 | tf_op jit(solution)/shard_map/ppermute | solution.py:311
  50.9 3.3 %next_grad_b.1 = (bf16[1536,384]{1,0:T(8,128)(2,1)S(1)}, bf16[192,1024]{1,0:T(8,128)(2,1)S(1)}, bf16[192,1024]{1,0:T(8,128)(2,1)S(1)}, f32[8,768]{1,0:T(8,128)S(1)}) custom-call(bf16[1536,1024]{1,0:T(8,128)(2,1)S(1)} %copy-done, f32[1536,768]{1,0:T(8,128)S(1)} %get-tuple-element.48.exp_ref.refs_0_, ...), custom_call_target="tpu_custom_call" | custom-call | flops 1207959552 | bytes 10027008 | tf_op jit(solution)/shard_map/next_grad_b/pallas_call | solution.py:272
  54.2 1.6 %collective-permute-start.12 = (bf16[192,1024]{1,0:T(8,128)(2,1)S(1)}, bf16[192,1024]{1,0:T(8,128)(2,1)S(1)}, u32[]{:S(2)}, u32[]{:S(2)}) collective-permute-start(bf16[192,1024]{1,0:T(8,128)(2,1)S(1)} %get-tuple-element.47), channel_id=1, source_target_pairs={{0,1},{1,0},{2,3},{3,2},{4,5},{5,4},{6,7},{7,6},{8,9},{9,8},{10,11... | collective-permute-start | bytes 1179656 | tf_op jit(solution)/shard_map/ppermute | solution.py:311
  55.8 0.0 collective-permute-start.10
  55.8 1.3 %collective-permute-done.12 = bf16[192,1024]{1,0:T(8,128)(2,1)S(1)} collective-permute-done((bf16[192,1024]{1,0:T(8,128)(2,1)S(1)}, bf16[192,1024]{1,0:T(8,128)(2,1)S(1)}, u32[]{:S(2)}, u32[]{:S(2)}) %collective-permute-start.12) | collective-permute-done | bytes 393248 | tf_op jit(solution)/shard_map/ppermute | solution.py:311
  57.1 0.1 add_convert_fusion.3
  57.3 1.3 %collective-permute-start.13 = (bf16[192,1024]{1,0:T(8,128)(2,1)S(1)}, bf16[192,1024]{1,0:T(8,128)(2,1)S(1)}, u32[]{:S(2)}, u32[]{:S(2)}) collective-permute-start(bf16[192,1024]{1,0:T(8,128)(2,1)S(1)} %add_convert_fusion.3), channel_id=1, source_target_pairs={{0,2},{1,3},{2,0},{3,1},{4,6},{5,7},{6,4},{7,5},{8,10},{9,11},{10,... | collective-permute-start | bytes 1179656 | tf_op jit(solution)/shard_map/ppermute | solution.py:311
  58.6 4.3 %collective-permute-done.10.refs_3_.refs_7_ = f32[8,768]{1,0:T(8,128)S(1)} collective-permute-done((f32[8,768]{1,0:T(8,128)S(1)}, f32[8,768]{1,0:T(8,128)S(1)}, u32[]{:S(2)}, u32[]{:S(2)}) %collective-permute-start.10) | collective-permute-done | bytes 24608 | tf_op jit(solution)/shard_map/ppermute | solution.py:311
  62.9 6.3 %next_a_own_b.1 = (bf16[1536,384]{1,0:T(8,128)(2,1)S(1)}, bf16[192,1024]{1,0:T(8,128)(2,1)S(1)}, bf16[192,1024]{1,0:T(8,128)(2,1)S(1)}, bf16[1536,384]{1,0:T(8,1...) custom-call(bf16[1536,1024]{1,0:T(8,128)(2,1)S(1)} %copy-done, ...), custom_call_target="tpu_custom_call" | custom-call | flops 2415919104 | bytes 16760832 | tf_op jit(solution)/shard_map/next_a_own_b/pallas_call | solution.py:272
  69.2 1.1 %collective-permute-start.14 = (bf16[192,1024]{1,0:T(8,128)(2,1)S(1)}, bf16[192,1024]{1,0:T(8,128)(2,1)S(1)}, u32[]{:S(2)}, u32[]{:S(2)}) collective-permute-start(bf16[192,1024]{1,0:T(8,128)(2,1)S(1)} %get-tuple-element.52), channel_id=1, source_target_pairs={{0,1},{1,0},{2,3},{3,2},{4,5},{5,4},{6,7},{7,6},{8,9},{9,8},{10,11... | collective-permute-start | bytes 1179656 | tf_op jit(solution)/shard_map/ppermute | solution.py:311
  70.3 0.1 collective-permute-start.16
  70.4 3.1 %own_grad_a.1 = (bf16[1536,384]{1,0:T(8,128)(2,1)S(1)}, bf16[192,1024]{1,0:T(8,128)(2,1)S(1)}, bf16[192,1024]{1,0:T(8,128)(2,1)S(1)}) custom-call(bf16[1536,1024]{1,0:T(8,128)(2,1)S(1)} %copy-done, f32[1536,768]{1,0:T(8,128)S(1)} %get-tuple-element.33.refs_0_.refs_4_, f32[24,768]{1,0:T(8,128)S(1)} %get-tuple-element.34.refs_1_.refs_5_, ...), custom_call_target="tpu_custom_call" | custom-call | flops 1207959552 | bytes 9953280 | tf_op jit(solution)/shard_map/own_grad_a/pallas_call | solution.py:272
  73.6 0.5 collective-permute-start.11
  74.1 0.0 collective-permute-done.13
  74.1 0.0 collective-permute-done.14
  74.1 0.1 add_convert_fusion.2
  74.2 2.5 %collective-permute-start.15 = (bf16[192,1024]{1,0:T(8,128)(2,1)S(1)}, bf16[192,1024]{1,0:T(8,128)(2,1)S(1)}, u32[]{:S(2)}, u32[]{:S(2)}) collective-permute-start(bf16[192,1024]{1,0:T(8,128)(2,1)S(1)} %add_convert_fusion.2), channel_id=1, source_target_pairs={{0,2},{1,3},{2,0},{3,1},{4,6},{5,7},{6,4},{7,5},{8,10},{9,11},{10,... | collective-permute-start | bytes 1179656 | tf_op jit(solution)/shard_map/ppermute | solution.py:311
  76.8 0.0 collective-permute-done.16
  76.8 0.2 add_convert_fusion.1
  77.0 0.3 collective-permute-start.17
  77.3 8.4 %passage_grad.1 = bf16[1536,1024]{1,0:T(8,128)(2,1)} custom-call(bf16[1536,384]{1,0:T(8,128)(2,1)S(1)} %get-tuple-element.56.refs_0_, bf16[1536,384]{1,0:T(8,128)(2,1)S(1)} %get-tuple-element.57.refs_1_, bf16[1536,384]{1,0:T(8,128)(2,1)S(1)} %get-tuple-element.58.refs_2_, bf16[1536,384]{1,0:T(8,128)(2,1)S(1)} %get-tuple-element.59.refs_3_, ...), custom_call_target="tpu_custom_call" | custom-call | flops 4831838208 | bytes 11010048 | tf_op jit(solution)/shard_map/passage_grad/pallas_call | solution.py:272
  85.7 0.0 collective-permute-done.11
  85.7 0.9 collective-permute-done.15
  86.5 5.3 %collective-permute-done.17 = bf16[192,1024]{1,0:T(8,128)(2,1)S(1)} collective-permute-done((bf16[192,1024]{1,0:T(8,128)(2,1)S(1)}, bf16[192,1024]{1,0:T(8,128)(2,1)S(1)}, u32[]{:S(2)}, u32[]{:S(2)}) %collective-permute-start.17) | collective-permute-done | bytes 393248 | tf_op jit(solution)/shard_map/ppermute | solution.py:311
  91.9 1.0 %add_convert_fusion = bf16[192,1024]{1,0:T(8,128)(2,1)} fusion(bf16[192,1024]{1,0:T(8,128)(2,1)S(1)} %collective-permute-done.17, bf16[192,1024]{1,0:T(8,128)(2,1)S(1)} %collective-permute-done.15, bf16[192,1024]{1,0:T(8,128)(2,1)S(1)} %collective-permute-done.11, bf16[192,1024]{1,0:T(8,128)(2,1)S(1)} %get-tuple-element.44), kind=kLoop, calls=%fused_computation | loop fusion | flops 1572864 | bytes 1966080 | tf_op jit(solution)/shard_map/convert_element_type | solution.py:411
  (1 shorter events, 0.0 us)
Async XLA Ops:
  0.6 21.7 %copy-start.4 = (f32[768]{0:T(1024)S(1)}, f32[768]{0:T(1024)}, u32[]{:S(2)}) copy-start(f32[768]{0:T(1024)} %param.7) | copy-start | bytes 9220
  0.6 21.7 %copy-start = (bf16[1536,1024]{1,0:T(8,128)(2,1)S(1)}, bf16[1536,1024]{1,0:T(8,128)(2,1)}, u32[]{:S(2)}) copy-start(bf16[1536,1024]{1,0:T(8,128)(2,1)} %p_ref.5) | copy-start | bytes 9437188
  0.7 21.7 %copy-start.2 = (s32[8,768]{1,0:T(8,128)S(1)}, s32[8,768]{1,0:T(8,128)}, u32[]{:S(2)}) copy-start(s32[8,768]{1,0:T(8,128)} %ids_ref.1) | copy-start | bytes 73732
  0.7 21.7 %copy-start.3 = (f32[8,768]{1,0:T(8,128)S(1)}, f32[8,768]{1,0:T(8,128)}, u32[]{:S(2)}) copy-start(f32[8,768]{1,0:T(8,128)} %logits_ref.1) | copy-start | bytes 73732
  2.5 14.4 %collective-permute-start = (bf16[112,1024]{1,0:T(8,128)(2,1)}, bf16[112,1024]{1,0:T(8,128)(2,1)S(1)}, u32[]{:S(2)}, u32[]{:S(2)}) collective-permute-start(bf16[112,1024]{1,0:T(8,128)(2,1)} %take_first.1), channel_id=1, source_target_pairs={{0,252},{1,253},{2,254},{3,255},{4,0},{5,1},{6,2},{7,3},{8,4},{9,5... | collective-permute-start | bytes 688136 | tf_op jit(solution)/shard_map/ppermute | solution.py:311
  14.1 24.1 %collective-permute-start.1 = (bf16[160,1024]{1,0:T(8,128)(2,1)}, bf16[160,1024]{1,0:T(8,128)(2,1)S(1)}, u32[]{:S(2)}, u32[]{:S(2)}) collective-permute-start(bf16[160,1024]{1,0:T(8,128)(2,1)} %take_rest.1), channel_id=1, source_target_pairs={{0,252},{1,253},{2,254},{3,255},{4,0},{5,1},{6,2},{7,3},{8,4},{9,5... | collective-permute-start | bytes 983048 | tf_op jit(solution)/shard_map/ppermute | solution.py:311
  16.9 22.1 %collective-permute-start.4 = (bf16[112,1024]{1,0:T(8,128)(2,1)S(1)}, bf16[112,1024]{1,0:T(8,128)(2,1)S(1)}, u32[]{:S(2)}, u32[]{:S(2)}) collective-permute-start(bf16[112,1024]{1,0:T(8,128)(2,1)S(1)} %collective-permute-done.refs_0_), channel_id=1, source_target_pairs={{0,2},{1,3},{2,0},{3,1},{4,6},{5,7},{6,4},{7,5},{8,10},{9,11},{10,... | collective-permute-start | bytes 688136 | tf_op jit(solution)/shard_map/ppermute | solution.py:311
  19.4 18.8 %collective-permute-start.2 = (bf16[112,1024]{1,0:T(8,128)(2,1)S(1)}, bf16[112,1024]{1,0:T(8,128)(2,1)S(1)}, u32[]{:S(2)}, u32[]{:S(2)}) collective-permute-start(bf16[112,1024]{1,0:T(8,128)(2,1)S(1)} %collective-permute-done.refs_0_), channel_id=1, source_target_pairs={{0,1},{1,0},{2,3},{3,2},{4,5},{5,4},{6,7},{7,6},{8,9},{9,8},{10,11... | collective-permute-start | bytes 688136 | tf_op jit(solution)/shard_map/ppermute | solution.py:311
  22.4 1.4 %copy-start.1 = (bf16[768,1024]{1,0:T(8,128)(2,1)S(1)}, bf16[768,1024]{1,0:T(8,128)(2,1)}, u32[]{:S(2)}) copy-start(bf16[768,1024]{1,0:T(8,128)(2,1)} %q_ref.3) | copy-start | bytes 4718596
  30.6 7.6 %collective-permute-start.3 = (f32[24,768]{1,0:T(8,128)S(1)}, f32[24,768]{1,0:T(8,128)S(1)}, u32[]{:S(2)}, u32[]{:S(2)}) collective-permute-start(f32[24,768]{1,0:T(8,128)S(1)} %get-tuple-element.37), channel_id=1, source_target_pairs={{0,252},{1,253},{2,254},{3,255},{4,0},{5,1},{6,2},{7,3},{8,4},{9,5... | collective-permute-start | bytes 221192 | tf_op jit(solution)/shard_map/ppermute | solution.py:311
  38.2 2.4 %collective-permute-start.6 = (bf16[160,1024]{1,0:T(8,128)(2,1)S(1)}, bf16[160,1024]{1,0:T(8,128)(2,1)S(1)}, u32[]{:S(2)}, u32[]{:S(2)}) collective-permute-start(bf16[160,1024]{1,0:T(8,128)(2,1)S(1)} %collective-permute-done.1.refs_4_), channel_id=1, source_target_pairs={{0,1},{1,0},{2,3},{3,2},{4,5},{5,4},{6,7},{7,6},{8,9},{9,8},{10,11... | collective-permute-start | bytes 983048 | tf_op jit(solution)/shard_map/ppermute | solution.py:311
  39.0 1.6 %collective-permute-start.5 = (bf16[112,1024]{1,0:T(8,128)(2,1)S(1)}, bf16[112,1024]{1,0:T(8,128)(2,1)S(1)}, u32[]{:S(2)}, u32[]{:S(2)}) collective-permute-start(bf16[112,1024]{1,0:T(8,128)(2,1)S(1)} %collective-permute-done.4.refs_2_), channel_id=1, source_target_pairs={{0,1},{1,0},{2,3},{3,2},{4,5},{5,4},{6,7},{7,6},{8,9},{9,8},{10,11... | collective-permute-start | bytes 688136 | tf_op jit(solution)/shard_map/ppermute | solution.py:311
  44.5 4.8 %collective-permute-start.9 = (f32[8,768]{1,0:T(8,128)S(1)}, f32[8,768]{1,0:T(8,128)S(1)}, u32[]{:S(2)}, u32[]{:S(2)}) collective-permute-start(f32[8,768]{1,0:T(8,128)S(1)} %get-tuple-element.42.stat_ref.refs_2_), channel_id=1, source_target_pairs={{0,3},{1,2},{2,1},{3,0},{4,7},{5,6},{6,5},{7,4},{8,11},{9,10},{10,... | collective-permute-start | bytes 73736 | tf_op jit(solution)/shard_map/ppermute | solution.py:311
  46.6 2.8 %collective-permute-start.8 = (f32[8,768]{1,0:T(8,128)S(1)}, f32[8,768]{1,0:T(8,128)S(1)}, u32[]{:S(2)}, u32[]{:S(2)}) collective-permute-start(f32[8,768]{1,0:T(8,128)S(1)} %get-tuple-element.42.stat_ref.refs_2_), channel_id=1, source_target_pairs={{0,1},{1,0},{2,3},{3,2},{4,5},{5,4},{6,7},{7,6},{8,9},{9,8},{10,11... | collective-permute-start | bytes 73736 | tf_op jit(solution)/shard_map/ppermute | solution.py:311
  46.7 4.2 %collective-permute-start.7 = (f32[8,768]{1,0:T(8,128)S(1)}, f32[8,768]{1,0:T(8,128)S(1)}, u32[]{:S(2)}, u32[]{:S(2)}) collective-permute-start(f32[8,768]{1,0:T(8,128)S(1)} %get-tuple-element.42.stat_ref.refs_2_), channel_id=1, source_target_pairs={{0,2},{1,3},{2,0},{3,1},{4,6},{5,7},{6,4},{7,5},{8,10},{9,11},{10,... | collective-permute-start | bytes 73736 | tf_op jit(solution)/shard_map/ppermute | solution.py:311
  54.2 3.0 %collective-permute-start.12 = (bf16[192,1024]{1,0:T(8,128)(2,1)S(1)}, bf16[192,1024]{1,0:T(8,128)(2,1)S(1)}, u32[]{:S(2)}, u32[]{:S(2)}) collective-permute-start(bf16[192,1024]{1,0:T(8,128)(2,1)S(1)} %get-tuple-element.47), channel_id=1, source_target_pairs={{0,1},{1,0},{2,3},{3,2},{4,5},{5,4},{6,7},{7,6},{8,9},{9,8},{10,11... | collective-permute-start | bytes 1179656 | tf_op jit(solution)/shard_map/ppermute | solution.py:311
  55.8 7.1 %collective-permute-start.10 = (f32[8,768]{1,0:T(8,128)S(1)}, f32[8,768]{1,0:T(8,128)S(1)}, u32[]{:S(2)}, u32[]{:S(2)}) collective-permute-start(f32[8,768]{1,0:T(8,128)S(1)} %get-tuple-element.43.refs_3_), channel_id=1, source_target_pairs={{0,4},{1,5},{2,6},{3,7},{4,8},{5,9},{6,10},{7,11},{8,12},{9,13},{1... | collective-permute-start | bytes 73736 | tf_op jit(solution)/shard_map/ppermute | solution.py:311
  57.3 16.8 %collective-permute-start.13 = (bf16[192,1024]{1,0:T(8,128)(2,1)S(1)}, bf16[192,1024]{1,0:T(8,128)(2,1)S(1)}, u32[]{:S(2)}, u32[]{:S(2)}) collective-permute-start(bf16[192,1024]{1,0:T(8,128)(2,1)S(1)} %add_convert_fusion.3), channel_id=1, source_target_pairs={{0,2},{1,3},{2,0},{3,1},{4,6},{5,7},{6,4},{7,5},{8,10},{9,11},{10,... | collective-permute-start | bytes 1179656 | tf_op jit(solution)/shard_map/ppermute | solution.py:311
  69.2 4.9 %collective-permute-start.14 = (bf16[192,1024]{1,0:T(8,128)(2,1)S(1)}, bf16[192,1024]{1,0:T(8,128)(2,1)S(1)}, u32[]{:S(2)}, u32[]{:S(2)}) collective-permute-start(bf16[192,1024]{1,0:T(8,128)(2,1)S(1)} %get-tuple-element.52), channel_id=1, source_target_pairs={{0,1},{1,0},{2,3},{3,2},{4,5},{5,4},{6,7},{7,6},{8,9},{9,8},{10,11... | collective-permute-start | bytes 1179656 | tf_op jit(solution)/shard_map/ppermute | solution.py:311
  70.3 6.5 %collective-permute-start.16 = (bf16[192,1024]{1,0:T(8,128)(2,1)S(1)}, bf16[192,1024]{1,0:T(8,128)(2,1)S(1)}, u32[]{:S(2)}, u32[]{:S(2)}) collective-permute-start(bf16[192,1024]{1,0:T(8,128)(2,1)S(1)} %get-tuple-element.54), channel_id=1, source_target_pairs={{0,1},{1,0},{2,3},{3,2},{4,5},{5,4},{6,7},{7,6},{8,9},{9,8},{10,11... | collective-permute-start | bytes 1179656 | tf_op jit(solution)/shard_map/ppermute | solution.py:311
  73.6 12.1 %collective-permute-start.11 = (bf16[192,1024]{1,0:T(8,128)(2,1)S(1)}, bf16[192,1024]{1,0:T(8,128)(2,1)S(1)}, u32[]{:S(2)}, u32[]{:S(2)}) collective-permute-start(bf16[192,1024]{1,0:T(8,128)(2,1)S(1)} %get-tuple-element.45), channel_id=1, source_target_pairs={{0,1},{1,0},{2,3},{3,2},{4,5},{5,4},{6,7},{7,6},{8,9},{9,8},{10,11... | collective-permute-start | bytes 1179656 | tf_op jit(solution)/shard_map/ppermute | solution.py:311
  74.2 12.3 %collective-permute-start.15 = (bf16[192,1024]{1,0:T(8,128)(2,1)S(1)}, bf16[192,1024]{1,0:T(8,128)(2,1)S(1)}, u32[]{:S(2)}, u32[]{:S(2)}) collective-permute-start(bf16[192,1024]{1,0:T(8,128)(2,1)S(1)} %add_convert_fusion.2), channel_id=1, source_target_pairs={{0,2},{1,3},{2,0},{3,1},{4,6},{5,7},{6,4},{7,5},{8,10},{9,11},{10,... | collective-permute-start | bytes 1179656 | tf_op jit(solution)/shard_map/ppermute | solution.py:311
  77.0 14.9 %collective-permute-start.17 = (bf16[192,1024]{1,0:T(8,128)(2,1)S(1)}, bf16[192,1024]{1,0:T(8,128)(2,1)S(1)}, u32[]{:S(2)}, u32[]{:S(2)}) collective-permute-start(bf16[192,1024]{1,0:T(8,128)(2,1)S(1)} %add_convert_fusion.1), channel_id=1, source_target_pairs={{0,4},{1,5},{2,6},{3,7},{4,8},{5,9},{6,10},{7,11},{8,12},{9,13},{1... | collective-permute-start | bytes 1179656 | tf_op jit(solution)/shard_map/ppermute | solution.py:311

commit v5 on v4

--- a/solution.py
+++ b/solution.py
@@ -13,7 +13,8 @@
 LOG2E = 1.4426950408889634
 IN_VMEM = pl.BlockSpec(memory_space=pltpu.VMEM)
 TILE = 256
-ROWS = 64
+PARTS = 6
+STEPS = 3
 FEW = 4
 
 
@@ -31,45 +32,37 @@
     )
 
 
-def fill_scores(scale, p_ref, q_ref, out_ref):
-    for at in range(0, q_ref.shape[0], TILE):
-        to = min(at + TILE, q_ref.shape[0])
-        out_ref[:, at:to] = scale * lax.dot_general(
-            p_ref[...], q_ref[at:to, :], (((1,), (1,)), ((), ())),
+def scores(scale, p_ref, q_ref, exp_ref, stat_ref, before=None):
+    size = p_ref.shape[0] // PARTS
+    tops, totals = [], []
+    for part in range(PARTS):
+        rows = slice(part * size, (part + 1) * size)
+        values = scale * lax.dot_general(
+            p_ref[rows, :], q_ref[...], (((1,), (1,)), ((), ())),
             preferred_element_type=jnp.float32,
         )
-
-
-def exponentials(ref, floor=None):
-    rows, cols = ref.shape
-    fold = (ROWS // 8, 8, cols)
-
-    def find(block, top):
-        at = pl.multiple_of(block * ROWS, ROWS)
-        return jnp.maximum(top, jnp.max(ref[pl.ds(at, ROWS), :].reshape(fold), axis=0))
-
-    top = lax.fori_loop(0, rows // ROWS, find, jnp.full((8, cols), -jnp.inf, jnp.float32))
-    top = jnp.max(top, axis=0, keepdims=True)
-    if floor is not None:
-        top = jnp.maximum(top, floor)
-
-    def raised(block, total):
-        at = pl.multiple_of(block * ROWS, ROWS)
-        value = jnp.exp2(ref[pl.ds(at, ROWS), :] - top)
-        ref[pl.ds(at, ROWS), :] = value
-        return total + jnp.sum(value.reshape(fold), axis=0)
-
-    total = lax.fori_loop(0, rows // ROWS, raised, jnp.zeros((8, cols), jnp.float32))
-    return top, jnp.sum(total, axis=0, keepdims=True)
+        fold = (size // 8, 8, values.shape[1])
+        top = jnp.max(jnp.max(values.reshape(fold), axis=0), axis=0, keepdims=True)
+        values = jnp.exp2(values - top)
+        exp_ref[rows, :] = values
+        total = jnp.sum(jnp.sum(values.reshape(fold), axis=0), axis=0, keepdims=True)
+        stat_ref[2 + part : 3 + part, :] = top
+        tops.append(top)
+        totals.append(total)
+    if before is not None:
+        tops.append(before[0:1])
+        totals.append(before[1:2])
+    whole = functools.reduce(jnp.maximum, tops)
+    stat_ref[0:1, :] = whole
+    stat_ref[1:2, :] = sum(total * jnp.exp2(top - whole) for top, total in zip(tops, totals))
 
 
 def own_kernel(
-    scale, coef_scale, q_hbm, p_hbm, ids_ref, logits_ref, loss_ref,
-    exp_ref, stat_ref, pack_ref, sent_ref, q_ref, p_ref, sems,
+    scale, coef_scale, q_hbm, p_ref, ids_ref, logits_ref, loss_ref,
+    exp_ref, stat_ref, pack_ref, sent_ref, q_ref, sems,
 ):
     group = lax.axis_index("grp")
-    parts = sems.shape[0] - 4
-    quarter, size = q_ref.shape[0] // 4, p_ref.shape[0] // parts
+    quarter = q_ref.shape[0] // 4
     copies = []
     for slot in range(4):
         first = pl.multiple_of((group ^ slot) * quarter, 16)
@@ -80,24 +73,14 @@
                 sems.at[slot],
             )
         )
-    for part in range(parts):
-        rows = pl.ds(part * size, size)
-        copies.append(pltpu.make_async_copy(p_hbm.at[rows], p_ref.at[rows], sems.at[4 + part]))
     for copy in copies:
         copy.start()
     labels(coef_scale * loss_ref[...], ids_ref, logits_ref, pack_ref, sent_ref, p_ref.shape[0])
     pack_ref[...] = reorder(pack_ref[...], group)
     sent_ref[...] = reorder(sent_ref[...], group)
-    for copy in copies[:4]:
+    for copy in copies:
         copy.wait()
-    for part in range(parts):
-        copies[4 + part].wait()
-        rows = pl.ds(part * size, size)
-        fill_scores(scale, p_ref.at[rows], q_ref, exp_ref.at[rows])
-    top, total = exponentials(exp_ref)
-    for ref, at in ((stat_ref, 0), (sent_ref, 17)):
-        ref[at : at + 1, :] = top
-        ref[at + 1 : at + 2, :] = total
+    scores(scale, p_ref, q_ref, exp_ref, stat_ref)
 
 
 def next_kernel(scale, *refs):
@@ -114,11 +97,7 @@
         rows_ref[at : at + cut, :] = lead[...]
         rows_ref[at + cut : at + cut + left, :] = rest[skip : skip + left, :]
         at += cut + left
-    fill_scores(scale, p_ref, rows_ref, exp_ref)
-    before = before_ref[16:24, :]
-    top, total = exponentials(exp_ref, before[1:2])
-    stat_ref[0:1, :] = top
-    stat_ref[1:2, :] = total + before[2:3] * jnp.exp2(before[1:2] - top)
+    scores(scale, p_ref, rows_ref, exp_ref, stat_ref, before_ref[...])
 
 
 def labels(coef, ids_ref, logits_ref, own_ref, next_ref, width):
@@ -167,73 +146,82 @@
     return top, sum(part[1:2] * jnp.exp2(part[0:1] - top) for part in parts)
 
 
-def fill_grads(exp_ref, grad_ref, factor, ids, weights):
-    rows, cols = exp_ref.shape
-    lead = lax.broadcasted_iota(jnp.int32, (16, cols), 0)
-
-    def fill(count):
-        def step(block, carry):
-            at = pl.multiple_of(block * 16, 16)
-            place = (lead + block * 16).astype(jnp.float32)
-            value = jnp.zeros((16, cols), jnp.float32)
-            for k in range(count):
-                value = jnp.where(ids[k : k + 1] == place, weights[k : k + 1], value)
-            grad_ref[pl.ds(at, 16), :] = (factor * exp_ref[pl.ds(at, 16), :] - value).astype(
-                jnp.bfloat16
-            )
-            return carry
-
-        return step
-
-    lax.fori_loop(0, rows // 16, fill(FEW), 0)
-    more = ids[FEW:]
-    low = jnp.min(jnp.where(more >= 0, more, float(rows))).astype(jnp.int32)
-    high = jnp.max(more).astype(jnp.int32)
-    lax.fori_loop(low // 16, jnp.where(high >= 0, high // 16 + 1, 0), fill(8), 0)
-
-
-def query_product(grad_ref, p_ref, out):
-    for at in range(0, p_ref.shape[1], TILE):
-        out(
-            at,
-            lax.dot_general(
-                grad_ref[...], p_ref[:, at : at + TILE], (((0,), (0,)), ((), ())),
-                preferred_element_type=jnp.float32,
-            ).astype(jnp.bfloat16),
-        )
-
-
-def grads_of(place, exp_ref, pack_ref, p_ref, stat_ref, whole_ref, grad_ref, mine_ref, other_ref):
+def fill_grads(block, count, exp_ref, grad_ref, factor, ids, weights):
+    cols = exp_ref.shape[1]
+    rows = pl.ds(block * 16, 16)
+    place = lax.broadcasted_iota(jnp.int32, (16, cols), 0) + block * 16
+    place = place.astype(jnp.float32)
+    value = jnp.zeros((16, cols), jnp.float32)
+    for k in range(count):
+        value = jnp.where(ids[k : k + 1] == place, weights[k : k + 1], value)
+    grad_ref[rows, :] = (factor * exp_ref[rows, :] - value).astype(jnp.bfloat16)
+
+
+def grads_of(
+    place, exp_ref, pack_ref, p_ref, stat_ref, whole_ref, grad_ref, mine_ref, other_ref,
+    total_ref,
+):
     quarter = mine_ref.shape[0]
     lanes = slice(place * 2 * quarter, (place + 1) * 2 * quarter)
-    factor = pack_ref[16:17, lanes] * (
-        jnp.exp2(stat_ref[0:1, lanes] - whole_ref[0:1, lanes]) / whole_ref[1:2, lanes]
-    )
-    fill_grads(
-        exp_ref.at[:, lanes], grad_ref, factor, pack_ref[0:8, lanes], pack_ref[8:16, lanes]
-    )
-
-    def put(at, part):
-        mine_ref[:, at : at + TILE] = part[:quarter]
-        other_ref[:, at : at + TILE] = part[quarter:]
-
-    query_product(grad_ref, p_ref, put)
+    whole = whole_ref[0:2, lanes]
+    coef = pack_ref[16:17, lanes] / whole[1:2]
+    factors = coef * jnp.exp2(stat_ref[2 : 2 + PARTS, lanes] - whole[0:1])
+    ids, weights = pack_ref[0:8, lanes], pack_ref[8:16, lanes]
+    exps = exp_ref.at[:, lanes]
+    rows = exp_ref.shape[0]
+    more = ids[FEW:]
+    low = jnp.min(jnp.where(more >= 0, more, float(rows))).astype(jnp.int32) // 16
+    high = jnp.max(more).astype(jnp.int32)
+    high = jnp.where(high >= 0, high // 16 + 1, 0)
+    size = rows // STEPS
+    for step in range(STEPS):
+        first, last = step * size // 16, (step + 1) * size // 16
+        for block in range(first, last):
+            part = block * 16 * PARTS // rows
+            fill_grads(
+                block, FEW, exps, grad_ref, factors[part : part + 1], ids, weights
+            )
+
+        def again(block, carry):
+            part = block // (rows // PARTS // 16)
+            factor = factors[0:1]
+            for n in range(1, PARTS):
+                factor = jnp.where(part == n, factors[n : n + 1], factor)
+            fill_grads(block, 8, exps, grad_ref, factor, ids, weights)
+            return carry
+
+        lax.fori_loop(jnp.maximum(low, first), jnp.minimum(high, last), again, 0)
+        taken = slice(step * size, (step + 1) * size)
+        for at in range(0, p_ref.shape[1], TILE):
+            cols = slice(at, at + TILE)
+            part = lax.dot_general(
+                grad_ref[taken, :], p_ref[taken, cols], (((0,), (0,)), ((), ())),
+                preferred_element_type=jnp.float32,
+            )
+            if step > 0:
+                part = total_ref[:, cols] + part
+            if step < STEPS - 1:
+                total_ref[:, cols] = part
+            else:
+                mine_ref[:, cols] = part[:quarter].astype(jnp.bfloat16)
+                other_ref[:, cols] = part[quarter:].astype(jnp.bfloat16)
 
 
 def first_grad_kernel(p_ref, exp_ref, pack_ref, stat_ref, cross_ref, core_ref, both_ref, *outs):
-    *outs, whole_ref = outs
+    *outs, whole_ref, total_ref = outs
     top, total = merge_stats(stat_ref[...], cross_ref[...], core_ref[...], both_ref[...])
     whole_ref[0:1, :] = top
     whole_ref[1:2, :] = total
-    grads_of(1, exp_ref, pack_ref, p_ref, stat_ref, whole_ref, *outs)
+    grads_of(1, exp_ref, pack_ref, p_ref, stat_ref, whole_ref, *outs, total_ref)
 
 
 def grad_kernel(places, p_ref, *refs):
-    ins, outs = refs[: 4 * len(places)], refs[4 * len(places) :]
+    ins, outs, total_ref = refs[: 4 * len(places)], refs[4 * len(places) : -1], refs[-1]
     for n, place in enumerate(places):
         exp_ref, pack_ref, stat_ref, whole_ref = ins[4 * n : 4 * n + 4]
         grads_of(
-            place, exp_ref, pack_ref, p_ref, stat_ref, whole_ref, *outs[3 * n : 3 * n + 3]
+            place, exp_ref, pack_ref, p_ref, stat_ref, whole_ref, *outs[3 * n : 3 * n + 3],
+            total_ref,
         )
 
 
@@ -332,33 +320,34 @@
     rest_out = take(((0, cut, quarter - cut), (2, cut, quarter - cut)), "take_rest")
     rest_mine = move(rest_out, along(-1))
 
-    first_mine, loss_grad = lax.optimization_barrier((first_mine, loss_grad))
     exp_own, stat_own, pack_own, pack_out, q_own = call(
         functools.partial(own_kernel, scale, score_scale),
         [shape((width, rows), f32), stat, pack, pack, shape((rows, depth), bf16)],
-        [queries, passages, passage_ids, teacher_logits, loss_grad[None, :]],
+        [pltpu.with_memory_space_constraint(queries, pltpu.HBM), passages, passage_ids, teacher_logits, loss_grad[None, :]],
         [
-            pltpu.VMEM((width, depth), bf16),
-            pltpu.SemaphoreType.DMA((7,)),
+            pltpu.SemaphoreType.DMA((4,)),
         ],
         flops=2 * rows * width * depth,
         name="own_scores",
-        anywhere=2,
-    )
-    pack_next = move(pack_out, along(-1))
+        anywhere=1,
+    )
+    stat_before = move(stat_own, along(-1))
+    first_mine, stat_own = lax.optimization_barrier((first_mine, stat_own))
     cross_mine = move(first_mine, across(2))
     first_other = move(first_mine, across(1))
-    rest_mine, first_other, pack_next = lax.optimization_barrier(
-        (rest_mine, first_other, pack_next)
+    rest_mine, first_other, stat_before = lax.optimization_barrier(
+        (rest_mine, first_other, stat_before)
     )
     rest_other = move(rest_mine, across(1))
+    rest_mine, pack_out = lax.optimization_barrier((rest_mine, pack_out))
+    pack_next = move(pack_out, along(-1))
     cross_other = move(cross_mine, across(1))
 
     exp_next, stat_next, q_next = call(
         functools.partial(next_kernel, scale),
         [shape((width, rows), f32), stat, shape((rows, depth), bf16)],
         [first_mine, first_other, cross_mine, cross_other, rest_mine, rest_other]
-        + [passages, pack_next],
+        + [passages, stat_before],
         flops=2 * rows * width * depth,
         name="next_scores",
     )
@@ -370,6 +359,7 @@
             kernel,
             [shape((width, half), bf16), piece, piece] * count + more,
             [passages] + ins,
+            [pltpu.VMEM((half, depth), f32)],
             flops=2 * count * half * width * depth,
             name=name,
         )
@@ -382,23 +372,24 @@
     whole_own = move(whole_next, along(1))
     nb = (nb_mine.astype(f32) + nb_in.astype(f32)).astype(bf16)
     nb, exp_next = lax.optimization_barrier((nb, exp_next))
+    whole_own, exp_next = lax.optimization_barrier((whole_own, exp_next))
     nb_cross = move(nb, across(2))
-    of_next = [exp_next, pack_next, stat_next, whole_next]
+    g_a, na_mine, na_other = grads(
+        functools.partial(grad_kernel, (0,)), [exp_next, pack_next, stat_next, whole_next], 1, [],
+        "next_grad_a",
+    )
+    na_in = move(na_other, across(1))
     of_own = [exp_own, pack_own, stat_own, whole_own]
-    g_a, na_mine, na_other, g_ob, ob_mine, ob_other = grads(
-        functools.partial(grad_kernel, (0, 1)), of_next + of_own, 2, [], "next_a_own_b"
-    )
-    na_in = move(na_other, across(1))
+    g_ob, ob_mine, ob_other, g_oa, oa_mine, oa_other = grads(
+        functools.partial(grad_kernel, (1, 0)), of_own + of_own, 2, [], "own_grad"
+    )
     ob_in = move(ob_other, across(1))
+    oa_in = move(oa_other, across(1))
     ob_mine, nb_cross = lax.optimization_barrier((ob_mine, nb_cross))
     ob = (ob_mine.astype(f32) + ob_in.astype(f32)).astype(bf16)
-    ob_cross = move(ob, across(2))
-    g_oa, oa_mine, oa_other = grads(
-        functools.partial(grad_kernel, (0,)), of_own, 1, [], "own_grad_a"
-    )
-    oa_in = move(oa_other, across(1))
+    came_across = move(ob, across(2))
     sent = (na_mine.astype(f32) + na_in.astype(f32) + nb_cross.astype(f32)).astype(bf16)
-    came = move(sent, along(1))
+    came_along = move(sent, along(1))
     (passage_grad,) = call(
         functools.partial(passage_kernel, half),
         [shape((width, depth), bf16)],
@@ -407,7 +398,10 @@
         name="passage_grad",
     )
     query_grad = (
-        oa_mine.astype(f32) + oa_in.astype(f32) + ob_cross.astype(f32) + came.astype(f32)
+        oa_mine.astype(f32)
+        + oa_in.astype(f32)
+        + came_along.astype(f32)
+        + came_across.astype(f32)
     ).astype(bf16)
     return query_grad, passage_grad
 

time: 93 us -> 85.7 us (0.922)
  Pallas kernels: 35.4 us -> 30.4 us
  waiting for transfers between devices: 20.3 us -> 16.9 us
  starting transfers between devices: 33.5 us -> 36.7 us
  local copies, waits for them, and re-layouts: 1.42 us -> 0.02 us
    pallas_call x6, Pallas kernels: 31.8 us -> 26.9 us  [call(): pl.pallas_call(kernel, out_shape=tuple(outs), in_specs=[pl.BlockSpec(memo...]
    ppermute x18 -> x19, waiting for transfers between devices: 20.3 us -> 16.9 us  [move(): return lax.ppermute(x, AXES, pairs)]
    ppermute x18 -> x19, starting transfers between devices: 33.5 us -> 36.7 us  [move(): return lax.ppermute(x, AXES, pairs)]
    unnamed x10 -> x8, local copies, waits for them, and re-layouts: 1.42 us -> 0.02 us
  transfers between devices with their start and end apart: 18 -> 19, of which waited for: 9 -> 8; matrix products, arithmetic and copies ran while one was open for 0% -> 1% of each run, Pallas kernels for 28% -> 30%
where the time goes in v5:
time: 85.7 us; the launch traced here: 86.3 us
  starting transfers between devices  36.7 us (43%)
  Pallas kernels  30.4 us (35%)
  waiting for transfers between devices  16.9 us (20%)
  other arithmetic  1.46 us (2%)
    ppermute x19, starting transfers between devices, move(): return lax.ppermute(x, AXES, pairs)  36.7 us
    pallas_call x6, Pallas kernels, call(): pl.pallas_call(kernel, out_shape=tuple(outs), in_specs=[pl.BlockSpec(memo...  26.9 us
    ppermute x19, waiting for transfers between devices, move(): return lax.ppermute(x, AXES, pairs)  16.9 us
    pallas_call x2, Pallas kernels, take(): pl.pallas_call(functools.partial(take_kernel, pieces), out_shape=shape((s...  3.53 us
  transfers between devices with their start and end apart: 19, of which 8 were waited for; matrix products, arithmetic and copies ran while one was open for 1% of the time, Pallas kernels for 30%

profile of v5, /device:TPU:1, one launch (start us, length us, event | category | flops | bytes accessed | tf_op | source)
XLA Modules:
  0.0 86.3 jit_solution(15287193070353671560)
XLA Ops:
  0.6 0.0 copy-start.3
  0.6 0.0 copy-start
  0.7 0.0 copy-start.2
  0.7 0.0 copy-start.1
  0.7 1.8 %take_first.1 = bf16[112,1024]{1,0:T(8,128)(2,1)} custom-call(bf16[768,1024]{1,0:T(8,128)(2,1)} %q_ref.3), custom_call_target="tpu_custom_call" | custom-call | tf_op jit(solution)/shard_map/take_first/pallas_call | solution.py:309
  2.5 9.9 %collective-permute-start = (bf16[112,1024]{1,0:T(8,128)(2,1)}, bf16[112,1024]{1,0:T(8,128)(2,1)S(1)}, u32[]{:S(2)}, u32[]{:S(2)}) collective-permute-start(bf16[112,1024]{1,0:T(8,128)(2,1)} %take_first.1), channel_id=1, source_target_pairs={{0,252},{1,253},{2,254},{3,255},{4,0},{5,1},{6,2},{7,3},{8,4},{9,5... | collective-permute-start | bytes 688136 | tf_op jit(solution)/shard_map/ppermute | solution.py:299
  12.3 1.7 %take_rest.1 = bf16[160,1024]{1,0:T(8,128)(2,1)} custom-call(bf16[768,1024]{1,0:T(8,128)(2,1)} %q_ref.3), custom_call_target="tpu_custom_call" | custom-call | tf_op jit(solution)/shard_map/take_rest/pallas_call | solution.py:309
  14.1 0.5 collective-permute-start.1
  14.6 0.0 copy-done.3
  14.6 0.0 copy-done
  14.6 0.0 copy-done.2
  14.6 0.0 copy-done.1
  14.6 5.3 %own_scores.1 = (f32[1536,768]{1,0:T(8,128)S(1)}, f32[8,768]{1,0:T(8,128)S(1)}, f32[24,768]{1,0:T(8,128)S(1)}, f32[24,768]{1,0:T(8,128)S(1)}, bf16[768,1024]{1,0:T(8,128)(2,1)S(1)}) custom-call(bf16[768,1024]{1,0:T(8,128)(2,1)} %q_ref.3, bf16[1536,1024]{1,0:T(8,128)(2,1)S(1)} %copy-done, s32[8,768]{1,0:T(8,128)S(1)} %copy-done.1, f32[8,768]{1,0:T(8,128)S(1)} %copy-done.2, ...), custom_call_target="tpu_custom_call" | custom-call | flops 2415919104 | bytes 11234304 | tf_op jit(solution)/shard_map/own_scores/pallas_call | solution.py:260
  19.9 0.0 collective-permute-done.refs_0_
  19.9 1.3 %collective-permute-start.2 = (bf16[112,1024]{1,0:T(8,128)(2,1)S(1)}, bf16[112,1024]{1,0:T(8,128)(2,1)S(1)}, u32[]{:S(2)}, u32[]{:S(2)}) collective-permute-start(bf16[112,1024]{1,0:T(8,128)(2,1)S(1)} %collective-permute-done.refs_0_), channel_id=1, source_target_pairs={{0,1},{1,0},{2,3},{3,2},{4,5},{5,4},{6,7},{7,6},{8,9},{9,8},{10,11... | collective-permute-start | bytes 688136 | tf_op jit(solution)/shard_map/ppermute | solution.py:299
  21.3 2.5 %collective-permute-start.4 = (bf16[112,1024]{1,0:T(8,128)(2,1)S(1)}, bf16[112,1024]{1,0:T(8,128)(2,1)S(1)}, u32[]{:S(2)}, u32[]{:S(2)}) collective-permute-start(bf16[112,1024]{1,0:T(8,128)(2,1)S(1)} %collective-permute-done.refs_0_), channel_id=1, source_target_pairs={{0,2},{1,3},{2,0},{3,1},{4,6},{5,7},{6,4},{7,5},{8,10},{9,11},{10,... | collective-permute-start | bytes 688136 | tf_op jit(solution)/shard_map/ppermute | solution.py:299
  23.7 4.0 %collective-permute-start.3 = (f32[8,768]{1,0:T(8,128)S(1)}, f32[8,768]{1,0:T(8,128)S(1)}, u32[]{:S(2)}, u32[]{:S(2)}) collective-permute-start(f32[8,768]{1,0:T(8,128)S(1)} %get-tuple-element.39.refs_2_.refs_6_), channel_id=1, source_target_pairs={{0,252},{1,253},{2,254},{3,255},{4,0},{5,1},{6,2},{7,3},{8,4},{9,5... | collective-permute-start | bytes 73736 | tf_op jit(solution)/shard_map/ppermute | solution.py:299
  27.8 0.9 %collective-permute-done.3.refs_7_ = f32[8,768]{1,0:T(8,128)S(1)} collective-permute-done((f32[8,768]{1,0:T(8,128)S(1)}, f32[8,768]{1,0:T(8,128)S(1)}, u32[]{:S(2)}, u32[]{:S(2)}) %collective-permute-start.3) | collective-permute-done | bytes 24608 | tf_op jit(solution)/shard_map/ppermute | solution.py:299
  28.7 0.0 collective-permute-done.1.refs_4_
  28.7 0.0 collective-permute-done.2.refs_1_
  28.7 1.1 %collective-permute-start.6 = (bf16[160,1024]{1,0:T(8,128)(2,1)S(1)}, bf16[160,1024]{1,0:T(8,128)(2,1)S(1)}, u32[]{:S(2)}, u32[]{:S(2)}) collective-permute-start(bf16[160,1024]{1,0:T(8,128)(2,1)S(1)} %collective-permute-done.1.refs_4_), channel_id=1, source_target_pairs={{0,1},{1,0},{2,3},{3,2},{4,5},{5,4},{6,7},{7,6},{8,9},{9,8},{10,11... | collective-permute-start | bytes 983048 | tf_op jit(solution)/shard_map/ppermute | solution.py:299
  29.9 0.4 collective-permute-done.4.refs_2_
  30.2 0.8 collective-permute-start.5
  31.1 5.2 %collective-permute-start.7 = (f32[24,768]{1,0:T(8,128)S(1)}, f32[24,768]{1,0:T(8,128)S(1)}, u32[]{:S(2)}, u32[]{:S(2)}) collective-permute-start(f32[24,768]{1,0:T(8,128)S(1)} %get-tuple-element.47), channel_id=1, source_target_pairs={{0,252},{1,253},{2,254},{3,255},{4,0},{5,1},{6,2},{7,3},{8,4},{9,5... | collective-permute-start | bytes 221192 | tf_op jit(solution)/shard_map/ppermute | solution.py:299
  36.2 0.0 collective-permute-done.5.refs_3_
  36.2 0.0 collective-permute-done.6.refs_5_
  36.2 3.2 %next_scores.1 = (f32[1536,768]{1,0:T(8,128)S(1)}, f32[8,768]{1,0:T(8,128)S(1)}, bf16[768,1024]{1,0:T(8,128)(2,1)S(1)}) custom-call(bf16[112,1024]{1,0:T(8,128)(2,1)S(1)} %collective-permute-done.refs_0_, bf16[112,1024]{1,0:T(8,128)(2,1)S(1)} %collective-permute-done.2.refs_1_, bf16[112,1024]{1,0:T(8,128)(2,1)S(1)} %collective-permute-done.4.refs_2_, ...), custom_call_target="tpu_custom_call" | custom-call | flops 2415919104 | bytes 11059200 | tf_op jit(solution)/shard_map/next_scores/pallas_call | solution.py:260
  39.4 2.6 %collective-permute-start.10 = (f32[8,768]{1,0:T(8,128)S(1)}, f32[8,768]{1,0:T(8,128)S(1)}, u32[]{:S(2)}, u32[]{:S(2)}) collective-permute-start(f32[8,768]{1,0:T(8,128)S(1)} %get-tuple-element.48.stat_ref.refs_2_), channel_id=1, source_target_pairs={{0,3},{1,2},{2,1},{3,0},{4,7},{5,6},{6,5},{7,4},{8,11},{9,10},{10,... | collective-permute-start | bytes 73736 | tf_op jit(solution)/shard_map/ppermute | solution.py:299
  42.0 1.2 %collective-permute-start.8 = (f32[8,768]{1,0:T(8,128)S(1)}, f32[8,768]{1,0:T(8,128)S(1)}, u32[]{:S(2)}, u32[]{:S(2)}) collective-permute-start(f32[8,768]{1,0:T(8,128)S(1)} %get-tuple-element.48.stat_ref.refs_2_), channel_id=1, source_target_pairs={{0,2},{1,3},{2,0},{3,1},{4,6},{5,7},{6,4},{7,5},{8,10},{9,11},{10,... | collective-permute-start | bytes 73736 | tf_op jit(solution)/shard_map/ppermute | solution.py:299
  43.3 0.1 collective-permute-start.9
  43.4 0.0 collective-permute-done.7.pack_ref.refs_1_
  43.4 1.7 %collective-permute-done.10.both_ref = f32[8,768]{1,0:T(8,128)S(1)} collective-permute-done((f32[8,768]{1,0:T(8,128)S(1)}, f32[8,768]{1,0:T(8,128)S(1)}, u32[]{:S(2)}, u32[]{:S(2)}) %collective-permute-start.10) | collective-permute-done | bytes 24608 | tf_op jit(solution)/shard_map/ppermute | solution.py:299
  45.0 1.2 %collective-permute-done.8.cross_ref = f32[8,768]{1,0:T(8,128)S(1)} collective-permute-done((f32[8,768]{1,0:T(8,128)S(1)}, f32[8,768]{1,0:T(8,128)S(1)}, u32[]{:S(2)}, u32[]{:S(2)}) %collective-permute-start.8) | collective-permute-done | bytes 24608 | tf_op jit(solution)/shard_map/ppermute | solution.py:299
  46.2 0.0 collective-permute-done.9.core_ref
  46.2 2.5 %next_grad_b.1 = (bf16[1536,384]{1,0:T(8,128)(2,1)S(1)}, bf16[192,1024]{1,0:T(8,128)(2,1)S(1)}, bf16[192,1024]{1,0:T(8,128)(2,1)S(1)}, f32[8,768]{1,0:T(8,128)S(1)}) custom-call(bf16[1536,1024]{1,0:T(8,128)(2,1)S(1)} %copy-done, f32[1536,768]{1,0:T(8,128)S(1)} %get-tuple-element.56.exp_ref.refs_0_, f32[24,768]{1,0:T(8,128)S(1)} %collective-permute-done.7.pack_ref.refs_1_, ...), custom_call_target="tpu_custom_call" | custom-call | flops 1207959552 | bytes 10027008 | tf_op jit(solution)/shard_map/next_grad_b/pallas_call | solution.py:260
  48.7 1.1 %collective-permute-start.12 = (bf16[192,1024]{1,0:T(8,128)(2,1)S(1)}, bf16[192,1024]{1,0:T(8,128)(2,1)S(1)}, u32[]{:S(2)}, u32[]{:S(2)}) collective-permute-start(bf16[192,1024]{1,0:T(8,128)(2,1)S(1)} %get-tuple-element.51), channel_id=1, source_target_pairs={{0,1},{1,0},{2,3},{3,2},{4,5},{5,4},{6,7},{7,6},{8,9},{9,8},{10,11... | collective-permute-start | bytes 1179656 | tf_op jit(solution)/shard_map/ppermute | solution.py:299
  49.8 0.0 collective-permute-start.11
  49.8 1.3 %collective-permute-done.12 = bf16[192,1024]{1,0:T(8,128)(2,1)S(1)} collective-permute-done((bf16[192,1024]{1,0:T(8,128)(2,1)S(1)}, bf16[192,1024]{1,0:T(8,128)(2,1)S(1)}, u32[]{:S(2)}, u32[]{:S(2)}) %collective-permute-start.12) | collective-permute-done | bytes 393248 | tf_op jit(solution)/shard_map/ppermute | solution.py:299
  51.1 0.1 add_convert_fusion.3
  51.3 5.5 %collective-permute-done.11.refs_3_.refs_7_ = f32[8,768]{1,0:T(8,128)S(1)} collective-permute-done((f32[8,768]{1,0:T(8,128)S(1)}, f32[8,768]{1,0:T(8,128)S(1)}, u32[]{:S(2)}, u32[]{:S(2)}) %collective-permute-start.11) | collective-permute-done | bytes 24608 | tf_op jit(solution)/shard_map/ppermute | solution.py:299
  56.8 1.2 %collective-permute-start.15 = (bf16[192,1024]{1,0:T(8,128)(2,1)S(1)}, bf16[192,1024]{1,0:T(8,128)(2,1)S(1)}, u32[]{:S(2)}, u32[]{:S(2)}) collective-permute-start(bf16[192,1024]{1,0:T(8,128)(2,1)S(1)} %add_convert_fusion.3), channel_id=1, source_target_pairs={{0,2},{1,3},{2,0},{3,1},{4,6},{5,7},{6,4},{7,5},{8,10},{9,11},{10,... | collective-permute-start | bytes 1179656 | tf_op jit(solution)/shard_map/ppermute | solution.py:299
  58.0 2.4 %next_grad_a.1 = (bf16[1536,384]{1,0:T(8,128)(2,1)S(1)}, bf16[192,1024]{1,0:T(8,128)(2,1)S(1)}, bf16[192,1024]{1,0:T(8,128)(2,1)S(1)}) custom-call(bf16[1536,1024]{1,0:T(8,128)(2,1)S(1)} %copy-done, f32[1536,768]{1,0:T(8,128)S(1)} %get-tuple-element.56.exp_ref.refs_0_, f32[24,768]{1,0:T(8,128)S(1)} %collective-permute-done.7.pack_ref.refs_1_, ...), custom_call_target="tpu_custom_call" | custom-call | flops 1207959552 | bytes 9953280 | tf_op jit(solution)/shard_map/next_grad_a/pallas_call | solution.py:260
  60.5 1.5 %collective-permute-start.14 = (bf16[192,1024]{1,0:T(8,128)(2,1)S(1)}, bf16[192,1024]{1,0:T(8,128)(2,1)S(1)}, u32[]{:S(2)}, u32[]{:S(2)}) collective-permute-start(bf16[192,1024]{1,0:T(8,128)(2,1)S(1)} %get-tuple-element.58), channel_id=1, source_target_pairs={{0,1},{1,0},{2,3},{3,2},{4,5},{5,4},{6,7},{7,6},{8,9},{9,8},{10,11... | collective-permute-start | bytes 1179656 | tf_op jit(solution)/shard_map/ppermute | solution.py:299
  62.0 5.0 %own_grad.1 = (bf16[1536,384]{1,0:T(8,128)(2,1)S(1)}, bf16[192,1024]{1,0:T(8,128)(2,1)S(1)}, bf16[192,1024]{1,0:T(8,128)(2,1)S(1)}, bf16[1536,384]{1,0:T(8,128)(...) custom-call(bf16[1536,1024]{1,0:T(8,128)(2,1)S(1)} %copy-done, ...), custom_call_target="tpu_custom_call" | custom-call | flops 2415919104 | bytes 16760832 | tf_op jit(solution)/shard_map/own_grad/pallas_call | solution.py:260
  67.0 3.4 %collective-permute-start.17 = (bf16[192,1024]{1,0:T(8,128)(2,1)S(1)}, bf16[192,1024]{1,0:T(8,128)(2,1)S(1)}, u32[]{:S(2)}, u32[]{:S(2)}) collective-permute-start(bf16[192,1024]{1,0:T(8,128)(2,1)S(1)} %get-tuple-element.63), channel_id=1, source_target_pairs={{0,1},{1,0},{2,3},{3,2},{4,5},{5,4},{6,7},{7,6},{8,9},{9,8},{10,11... | collective-permute-start | bytes 1179656 | tf_op jit(solution)/shard_map/ppermute | solution.py:299
  70.4 0.1 collective-permute-start.13
  70.5 0.0 collective-permute-done.15
  70.5 0.0 collective-permute-done.14
  70.5 0.2 add_convert_fusion.2
  70.7 0.1 collective-permute-start.16
  70.8 0.9 %collective-permute-done.17 = bf16[192,1024]{1,0:T(8,128)(2,1)S(1)} collective-permute-done((bf16[192,1024]{1,0:T(8,128)(2,1)S(1)}, bf16[192,1024]{1,0:T(8,128)(2,1)S(1)}, u32[]{:S(2)}, u32[]{:S(2)}) %collective-permute-start.17) | collective-permute-done | bytes 393248 | tf_op jit(solution)/shard_map/ppermute | solution.py:299
  71.7 0.1 add_convert_fusion.1
  71.9 0.1 collective-permute-start.18
  72.0 8.4 %passage_grad.1 = bf16[1536,1024]{1,0:T(8,128)(2,1)} custom-call(bf16[1536,384]{1,0:T(8,128)(2,1)S(1)} %get-tuple-element.64.refs_0_, bf16[1536,384]{1,0:T(8,128)(2,1)S(1)} %get-tuple-element.65.refs_1_, bf16[1536,384]{1,0:T(8,128)(2,1)S(1)} %get-tuple-element.66.refs_2_, bf16[1536,384]{1,0:T(8,128)(2,1)S(1)} %get-tuple-element.67.refs_3_, ...), custom_call_target="tpu_custom_call" | custom-call | flops 4831838208 | bytes 11010048 | tf_op jit(solution)/shard_map/passage_grad/pallas_call | solution.py:260
  80.4 0.0 collective-permute-done.13
  80.4 4.9 %collective-permute-done.16 = bf16[192,1024]{1,0:T(8,128)(2,1)S(1)} collective-permute-done((bf16[192,1024]{1,0:T(8,128)(2,1)S(1)}, bf16[192,1024]{1,0:T(8,128)(2,1)S(1)}, u32[]{:S(2)}, u32[]{:S(2)}) %collective-permute-start.16) | collective-permute-done | bytes 393248 | tf_op jit(solution)/shard_map/ppermute | solution.py:299
  85.3 0.0 collective-permute-done.18
  85.3 1.0 %add_convert_fusion = bf16[192,1024]{1,0:T(8,128)(2,1)} fusion(bf16[192,1024]{1,0:T(8,128)(2,1)S(1)} %collective-permute-done.18, bf16[192,1024]{1,0:T(8,128)(2,1)S(1)} %collective-permute-done.16, bf16[192,1024]{1,0:T(8,128)(2,1)S(1)} %collective-permute-done.13, bf16[192,1024]{1,0:T(8,128)(2,1)S(1)} %get-tuple-element.54), kind=kLoop, calls=%fused_computation | loop fusion | flops 1572864 | bytes 1966080 | tf_op jit(solution)/shard_map/convert_element_type | solution.py:405
  (1 shorter events, 0.0 us)
Async XLA Ops:
  0.6 14.0 %copy-start.3 = (f32[768]{0:T(1024)S(1)}, f32[768]{0:T(1024)}, u32[]{:S(2)}) copy-start(f32[768]{0:T(1024)} %param.7) | copy-start | bytes 9220
  0.6 14.0 %copy-start = (bf16[1536,1024]{1,0:T(8,128)(2,1)S(1)}, bf16[1536,1024]{1,0:T(8,128)(2,1)}, u32[]{:S(2)}) copy-start(bf16[1536,1024]{1,0:T(8,128)(2,1)} %p_ref.7) | copy-start | bytes 9437188
  0.7 14.0 %copy-start.2 = (f32[8,768]{1,0:T(8,128)S(1)}, f32[8,768]{1,0:T(8,128)}, u32[]{:S(2)}) copy-start(f32[8,768]{1,0:T(8,128)} %logits_ref.1) | copy-start | bytes 73732
  0.7 14.0 %copy-start.1 = (s32[8,768]{1,0:T(8,128)S(1)}, s32[8,768]{1,0:T(8,128)}, u32[]{:S(2)}) copy-start(s32[8,768]{1,0:T(8,128)} %ids_ref.1) | copy-start | bytes 73732
  2.5 17.5 %collective-permute-start = (bf16[112,1024]{1,0:T(8,128)(2,1)}, bf16[112,1024]{1,0:T(8,128)(2,1)S(1)}, u32[]{:S(2)}, u32[]{:S(2)}) collective-permute-start(bf16[112,1024]{1,0:T(8,128)(2,1)} %take_first.1), channel_id=1, source_target_pairs={{0,252},{1,253},{2,254},{3,255},{4,0},{5,1},{6,2},{7,3},{8,4},{9,5... | collective-permute-start | bytes 688136 | tf_op jit(solution)/shard_map/ppermute | solution.py:299
  14.1 14.7 %collective-permute-start.1 = (bf16[160,1024]{1,0:T(8,128)(2,1)}, bf16[160,1024]{1,0:T(8,128)(2,1)S(1)}, u32[]{:S(2)}, u32[]{:S(2)}) collective-permute-start(bf16[160,1024]{1,0:T(8,128)(2,1)} %take_rest.1), channel_id=1, source_target_pairs={{0,252},{1,253},{2,254},{3,255},{4,0},{5,1},{6,2},{7,3},{8,4},{9,5... | collective-permute-start | bytes 983048 | tf_op jit(solution)/shard_map/ppermute | solution.py:299
  19.9 8.8 %collective-permute-start.2 = (bf16[112,1024]{1,0:T(8,128)(2,1)S(1)}, bf16[112,1024]{1,0:T(8,128)(2,1)S(1)}, u32[]{:S(2)}, u32[]{:S(2)}) collective-permute-start(bf16[112,1024]{1,0:T(8,128)(2,1)S(1)} %collective-permute-done.refs_0_), channel_id=1, source_target_pairs={{0,1},{1,0},{2,3},{3,2},{4,5},{5,4},{6,7},{7,6},{8,9},{9,8},{10,11... | collective-permute-start | bytes 688136 | tf_op jit(solution)/shard_map/ppermute | solution.py:299
  21.3 9.0 %collective-permute-start.4 = (bf16[112,1024]{1,0:T(8,128)(2,1)S(1)}, bf16[112,1024]{1,0:T(8,128)(2,1)S(1)}, u32[]{:S(2)}, u32[]{:S(2)}) collective-permute-start(bf16[112,1024]{1,0:T(8,128)(2,1)S(1)} %collective-permute-done.refs_0_), channel_id=1, source_target_pairs={{0,2},{1,3},{2,0},{3,1},{4,6},{5,7},{6,4},{7,5},{8,10},{9,11},{10,... | collective-permute-start | bytes 688136 | tf_op jit(solution)/shard_map/ppermute | solution.py:299
  23.7 5.0 %collective-permute-start.3 = (f32[8,768]{1,0:T(8,128)S(1)}, f32[8,768]{1,0:T(8,128)S(1)}, u32[]{:S(2)}, u32[]{:S(2)}) collective-permute-start(f32[8,768]{1,0:T(8,128)S(1)} %get-tuple-element.39.refs_2_.refs_6_), channel_id=1, source_target_pairs={{0,252},{1,253},{2,254},{3,255},{4,0},{5,1},{6,2},{7,3},{8,4},{9,5... | collective-permute-start | bytes 73736 | tf_op jit(solution)/shard_map/ppermute | solution.py:299
  28.7 7.5 %collective-permute-start.6 = (bf16[160,1024]{1,0:T(8,128)(2,1)S(1)}, bf16[160,1024]{1,0:T(8,128)(2,1)S(1)}, u32[]{:S(2)}, u32[]{:S(2)}) collective-permute-start(bf16[160,1024]{1,0:T(8,128)(2,1)S(1)} %collective-permute-done.1.refs_4_), channel_id=1, source_target_pairs={{0,1},{1,0},{2,3},{3,2},{4,5},{5,4},{6,7},{7,6},{8,9},{9,8},{10,11... | collective-permute-start | bytes 983048 | tf_op jit(solution)/shard_map/ppermute | solution.py:299
  30.2 6.0 %collective-permute-start.5 = (bf16[112,1024]{1,0:T(8,128)(2,1)S(1)}, bf16[112,1024]{1,0:T(8,128)(2,1)S(1)}, u32[]{:S(2)}, u32[]{:S(2)}) collective-permute-start(bf16[112,1024]{1,0:T(8,128)(2,1)S(1)} %collective-permute-done.4.refs_2_), channel_id=1, source_target_pairs={{0,1},{1,0},{2,3},{3,2},{4,5},{5,4},{6,7},{7,6},{8,9},{9,8},{10,11... | collective-permute-start | bytes 688136 | tf_op jit(solution)/shard_map/ppermute | solution.py:299
  31.1 12.3 %collective-permute-start.7 = (f32[24,768]{1,0:T(8,128)S(1)}, f32[24,768]{1,0:T(8,128)S(1)}, u32[]{:S(2)}, u32[]{:S(2)}) collective-permute-start(f32[24,768]{1,0:T(8,128)S(1)} %get-tuple-element.47), channel_id=1, source_target_pairs={{0,252},{1,253},{2,254},{3,255},{4,0},{5,1},{6,2},{7,3},{8,4},{9,5... | collective-permute-start | bytes 221192 | tf_op jit(solution)/shard_map/ppermute | solution.py:299
  39.4 5.6 %collective-permute-start.10 = (f32[8,768]{1,0:T(8,128)S(1)}, f32[8,768]{1,0:T(8,128)S(1)}, u32[]{:S(2)}, u32[]{:S(2)}) collective-permute-start(f32[8,768]{1,0:T(8,128)S(1)} %get-tuple-element.48.stat_ref.refs_2_), channel_id=1, source_target_pairs={{0,3},{1,2},{2,1},{3,0},{4,7},{5,6},{6,5},{7,4},{8,11},{9,10},{10,... | collective-permute-start | bytes 73736 | tf_op jit(solution)/shard_map/ppermute | solution.py:299
  42.0 4.2 %collective-permute-start.8 = (f32[8,768]{1,0:T(8,128)S(1)}, f32[8,768]{1,0:T(8,128)S(1)}, u32[]{:S(2)}, u32[]{:S(2)}) collective-permute-start(f32[8,768]{1,0:T(8,128)S(1)} %get-tuple-element.48.stat_ref.refs_2_), channel_id=1, source_target_pairs={{0,2},{1,3},{2,0},{3,1},{4,6},{5,7},{6,4},{7,5},{8,10},{9,11},{10,... | collective-permute-start | bytes 73736 | tf_op jit(solution)/shard_map/ppermute | solution.py:299
  43.3 2.9 %collective-permute-start.9 = (f32[8,768]{1,0:T(8,128)S(1)}, f32[8,768]{1,0:T(8,128)S(1)}, u32[]{:S(2)}, u32[]{:S(2)}) collective-permute-start(f32[8,768]{1,0:T(8,128)S(1)} %get-tuple-element.48.stat_ref.refs_2_), channel_id=1, source_target_pairs={{0,1},{1,0},{2,3},{3,2},{4,5},{5,4},{6,7},{7,6},{8,9},{9,8},{10,11... | collective-permute-start | bytes 73736 | tf_op jit(solution)/shard_map/ppermute | solution.py:299
  48.7 2.4 %collective-permute-start.12 = (bf16[192,1024]{1,0:T(8,128)(2,1)S(1)}, bf16[192,1024]{1,0:T(8,128)(2,1)S(1)}, u32[]{:S(2)}, u32[]{:S(2)}) collective-permute-start(bf16[192,1024]{1,0:T(8,128)(2,1)S(1)} %get-tuple-element.51), channel_id=1, source_target_pairs={{0,1},{1,0},{2,3},{3,2},{4,5},{5,4},{6,7},{7,6},{8,9},{9,8},{10,11... | collective-permute-start | bytes 1179656 | tf_op jit(solution)/shard_map/ppermute | solution.py:299
  49.8 7.0 %collective-permute-start.11 = (f32[8,768]{1,0:T(8,128)S(1)}, f32[8,768]{1,0:T(8,128)S(1)}, u32[]{:S(2)}, u32[]{:S(2)}) collective-permute-start(f32[8,768]{1,0:T(8,128)S(1)} %get-tuple-element.49.refs_3_), channel_id=1, source_target_pairs={{0,4},{1,5},{2,6},{3,7},{4,8},{5,9},{6,10},{7,11},{8,12},{9,13},{1... | collective-permute-start | bytes 73736 | tf_op jit(solution)/shard_map/ppermute | solution.py:299
  56.8 13.7 %collective-permute-start.15 = (bf16[192,1024]{1,0:T(8,128)(2,1)S(1)}, bf16[192,1024]{1,0:T(8,128)(2,1)S(1)}, u32[]{:S(2)}, u32[]{:S(2)}) collective-permute-start(bf16[192,1024]{1,0:T(8,128)(2,1)S(1)} %add_convert_fusion.3), channel_id=1, source_target_pairs={{0,2},{1,3},{2,0},{3,1},{4,6},{5,7},{6,4},{7,5},{8,10},{9,11},{10,... | collective-permute-start | bytes 1179656 | tf_op jit(solution)/shard_map/ppermute | solution.py:299
  60.5 10.0 %collective-permute-start.14 = (bf16[192,1024]{1,0:T(8,128)(2,1)S(1)}, bf16[192,1024]{1,0:T(8,128)(2,1)S(1)}, u32[]{:S(2)}, u32[]{:S(2)}) collective-permute-start(bf16[192,1024]{1,0:T(8,128)(2,1)S(1)} %get-tuple-element.58), channel_id=1, source_target_pairs={{0,1},{1,0},{2,3},{3,2},{4,5},{5,4},{6,7},{7,6},{8,9},{9,8},{10,11... | collective-permute-start | bytes 1179656 | tf_op jit(solution)/shard_map/ppermute | solution.py:299
  67.0 4.7 %collective-permute-start.17 = (bf16[192,1024]{1,0:T(8,128)(2,1)S(1)}, bf16[192,1024]{1,0:T(8,128)(2,1)S(1)}, u32[]{:S(2)}, u32[]{:S(2)}) collective-permute-start(bf16[192,1024]{1,0:T(8,128)(2,1)S(1)} %get-tuple-element.63), channel_id=1, source_target_pairs={{0,1},{1,0},{2,3},{3,2},{4,5},{5,4},{6,7},{7,6},{8,9},{9,8},{10,11... | collective-permute-start | bytes 1179656 | tf_op jit(solution)/shard_map/ppermute | solution.py:299
  70.4 10.0 %collective-permute-start.13 = (bf16[192,1024]{1,0:T(8,128)(2,1)S(1)}, bf16[192,1024]{1,0:T(8,128)(2,1)S(1)}, u32[]{:S(2)}, u32[]{:S(2)}) collective-permute-start(bf16[192,1024]{1,0:T(8,128)(2,1)S(1)} %get-tuple-element.55), channel_id=1, source_target_pairs={{0,1},{1,0},{2,3},{3,2},{4,5},{5,4},{6,7},{7,6},{8,9},{9,8},{10,11... | collective-permute-start | bytes 1179656 | tf_op jit(solution)/shard_map/ppermute | solution.py:299
  70.7 14.6 %collective-permute-start.16 = (bf16[192,1024]{1,0:T(8,128)(2,1)S(1)}, bf16[192,1024]{1,0:T(8,128)(2,1)S(1)}, u32[]{:S(2)}, u32[]{:S(2)}) collective-permute-start(bf16[192,1024]{1,0:T(8,128)(2,1)S(1)} %add_convert_fusion.2), channel_id=1, source_target_pairs={{0,4},{1,5},{2,6},{3,7},{4,8},{5,9},{6,10},{7,11},{8,12},{9,13},{1... | collective-permute-start | bytes 1179656 | tf_op jit(solution)/shard_map/ppermute | solution.py:299
  71.9 13.4 %collective-permute-start.18 = (bf16[192,1024]{1,0:T(8,128)(2,1)S(1)}, bf16[192,1024]{1,0:T(8,128)(2,1)S(1)}, u32[]{:S(2)}, u32[]{:S(2)}) collective-permute-start(bf16[192,1024]{1,0:T(8,128)(2,1)S(1)} %add_convert_fusion.1), channel_id=1, source_target_pairs={{0,2},{1,3},{2,0},{3,1},{4,6},{5,7},{6,4},{7,5},{8,10},{9,11},{10,... | collective-permute-start | bytes 1179656 | tf_op jit(solution)/shard_map/ppermute | solution.py:299

commit v6 on v5

--- a/solution.py
+++ b/solution.py
@@ -32,7 +32,7 @@
     )
 
 
-def scores(scale, p_ref, q_ref, exp_ref, stat_ref, before=None):
+def scores(scale, p_ref, q_ref, exp_ref, stat_ref):
     size = p_ref.shape[0] // PARTS
     tops, totals = [], []
     for part in range(PARTS):
@@ -49,9 +49,6 @@
         stat_ref[2 + part : 3 + part, :] = top
         tops.append(top)
         totals.append(total)
-    if before is not None:
-        tops.append(before[0:1])
-        totals.append(before[1:2])
     whole = functools.reduce(jnp.maximum, tops)
     stat_ref[0:1, :] = whole
     stat_ref[1:2, :] = sum(total * jnp.exp2(top - whole) for top, total in zip(tops, totals))
@@ -83,21 +80,22 @@
     scores(scale, p_ref, q_ref, exp_ref, stat_ref)
 
 
-def next_kernel(scale, *refs):
-    pieces, p_ref, before_ref, exp_ref, stat_ref, rows_ref = refs[:6], *refs[6:]
-    first_mine, first_other, cross_mine, cross_other, rest_mine, rest_other = pieces
-    cut, left = first_mine.shape[0], rest_mine.shape[0] // 2
-    at = 0
-    for lead, rest, skip in (
-        (first_mine, rest_mine, 0),
-        (first_other, rest_other, 0),
-        (cross_mine, rest_mine, left),
-        (cross_other, rest_other, left),
-    ):
-        rows_ref[at : at + cut, :] = lead[...]
-        rows_ref[at + cut : at + cut + left, :] = rest[skip : skip + left, :]
-        at += cut + left
-    scores(scale, p_ref, rows_ref, exp_ref, stat_ref, before_ref[...])
+def next_kernel(scale, place, mine_ref, other_ref, p_ref, *refs):
+    exp_ref, stat_ref, rows_ref = refs[-3:]
+    quarter = mine_ref.shape[0]
+    half = 2 * quarter
+    rows_ref[:quarter, :] = mine_ref[...]
+    rows_ref[quarter:, :] = other_ref[...]
+    if place == 1:
+        known_ref, before_ref = refs[:2]
+        stat_ref[:, :half] = known_ref[:, :half]
+    scores(scale, p_ref, rows_ref, exp_ref, stat_ref.at[:, place * half : (place + 1) * half])
+    if place == 1:
+        top = jnp.maximum(stat_ref[0:1, :], before_ref[0:1, :])
+        stat_ref[1:2, :] = stat_ref[1:2, :] * jnp.exp2(stat_ref[0:1, :] - top) + before_ref[
+            1:2, :
+        ] * jnp.exp2(before_ref[0:1, :] - top)
+        stat_ref[0:1, :] = top
 
 
 def labels(coef, ids_ref, logits_ref, own_ref, next_ref, width):
@@ -167,7 +165,7 @@
     coef = pack_ref[16:17, lanes] / whole[1:2]
     factors = coef * jnp.exp2(stat_ref[2 : 2 + PARTS, lanes] - whole[0:1])
     ids, weights = pack_ref[0:8, lanes], pack_ref[8:16, lanes]
-    exps = exp_ref.at[:, lanes]
+    exps = exp_ref if exp_ref.shape[1] == 2 * quarter else exp_ref.at[:, lanes]
     rows = exp_ref.shape[0]
     more = ids[FEW:]
     low = jnp.min(jnp.where(more >= 0, more, float(rows))).astype(jnp.int32) // 16
@@ -226,8 +224,8 @@
 
 
 def passage_kernel(half, *refs):
-    grads, (own_ref, next_ref, out_ref) = refs[:4], refs[4:]
-    rows = [ref.at[at : at + half, :] for ref in (own_ref, next_ref) for at in (0, half)]
+    grads, (own_ref, *rows, out_ref) = refs[:4], refs[4:]
+    rows = [own_ref.at[at : at + half, :] for at in (0, half)] + rows
     for at in range(0, out_ref.shape[1], TILE):
         out_ref[:, at : at + TILE] = sum(
             jnp.dot(
@@ -237,22 +235,12 @@
         ).astype(jnp.bfloat16)
 
 
-def take_kernel(pieces, q_ref, out_ref, sems):
-    quarter = q_ref.shape[0] // 4
-    group = lax.axis_index("grp")
-    copies, at = [], 0
-    for place, (slot, skip, rows) in enumerate(pieces):
-        first = pl.multiple_of((group ^ slot) * quarter + skip, 16)
-        copies.append(
-            pltpu.make_async_copy(
-                q_ref.at[pl.ds(first, rows)], out_ref.at[pl.ds(at, rows)], sems.at[place]
-            )
-        )
-        at += rows
-    for copy in copies:
-        copy.start()
-    for copy in copies:
-        copy.wait()
+def take_kernel(slot, q_ref, out_ref, sem):
+    quarter = out_ref.shape[0]
+    first = pl.multiple_of((lax.axis_index("grp") ^ slot) * quarter, 16)
+    copy = pltpu.make_async_copy(q_ref.at[pl.ds(first, quarter)], out_ref, sem)
+    copy.start()
+    copy.wait()
 
 
 def call(kernel, outs, ins, scratch=(), flops=0, name=None, anywhere=0):
@@ -303,22 +291,18 @@
     pack = shape((24, rows), f32)
     scale = score_scale * LOG2E
 
-    cut = quarter * 7 // 12
-
-    def take(pieces, name):
+    def take(slot, name):
         return pl.pallas_call(
-            functools.partial(take_kernel, pieces),
-            out_shape=shape((sum(piece[2] for piece in pieces), depth), bf16),
+            functools.partial(take_kernel, slot),
+            out_shape=piece,
             in_specs=[pl.BlockSpec(memory_space=pl.ANY)],
             out_specs=IN_VMEM,
-            scratch_shapes=[pltpu.SemaphoreType.DMA((len(pieces),))],
+            scratch_shapes=[pltpu.SemaphoreType.DMA(())],
             name=name,
         )(queries)
 
-    first_out = take(((0, 0, cut),), "take_first")
-    first_mine = move(first_out, along(-1))
-    rest_out = take(((0, cut, quarter - cut), (2, cut, quarter - cut)), "take_rest")
-    rest_mine = move(rest_out, along(-1))
+    a_mine = move(take(0, "take_a"), along(-1))
+    b_mine = move(take(2, "take_b"), along(-1))
 
     exp_own, stat_own, pack_own, pack_out, q_own = call(
         functools.partial(own_kernel, scale, score_scale),
@@ -332,24 +316,25 @@
         anywhere=1,
     )
     stat_before = move(stat_own, along(-1))
-    first_mine, stat_own = lax.optimization_barrier((first_mine, stat_own))
-    cross_mine = move(first_mine, across(2))
-    first_other = move(first_mine, across(1))
-    rest_mine, first_other, stat_before = lax.optimization_barrier(
-        (rest_mine, first_other, stat_before)
-    )
-    rest_other = move(rest_mine, across(1))
-    rest_mine, pack_out = lax.optimization_barrier((rest_mine, pack_out))
+    a_mine, stat_own = lax.optimization_barrier((a_mine, stat_own))
+    a_other = move(a_mine, across(1))
+
+    def next_scores(place, ins, name):
+        return call(
+            functools.partial(next_kernel, scale, place),
+            [shape((width, half), f32), stat, shape((half, depth), bf16)],
+            ins,
+            flops=2 * half * width * depth,
+            name=name,
+        )
+
+    exp_a, stat_a, q_a = next_scores(0, [a_mine, a_other, passages], "next_scores_a")
+    b_mine, stat_before = lax.optimization_barrier((b_mine, stat_before))
+    b_other = move(b_mine, across(1))
+    b_mine, pack_out = lax.optimization_barrier((b_mine, pack_out))
     pack_next = move(pack_out, along(-1))
-    cross_other = move(cross_mine, across(1))
-
-    exp_next, stat_next, q_next = call(
-        functools.partial(next_kernel, scale),
-        [shape((width, rows), f32), stat, shape((rows, depth), bf16)],
-        [first_mine, first_other, cross_mine, cross_other, rest_mine, rest_other]
-        + [passages, stat_before],
-        flops=2 * rows * width * depth,
-        name="next_scores",
+    exp_b, stat_next, q_b = next_scores(
+        1, [b_mine, b_other, passages, stat_a, stat_before], "next_scores_b"
     )
 
     cross, core, both = (move(stat_next, across(turn)) for turn in (2, 1, 3))
@@ -365,17 +350,16 @@
         )
 
     g_b, nb_mine, nb_other, whole_next = grads(
-        first_grad_kernel, [exp_next, pack_next, stat_next, cross, core, both], 1, [stat],
+        first_grad_kernel, [exp_b, pack_next, stat_next, cross, core, both], 1, [stat],
         "next_grad_b",
     )
     nb_in = move(nb_other, across(1))
     whole_own = move(whole_next, along(1))
     nb = (nb_mine.astype(f32) + nb_in.astype(f32)).astype(bf16)
-    nb, exp_next = lax.optimization_barrier((nb, exp_next))
-    whole_own, exp_next = lax.optimization_barrier((whole_own, exp_next))
+    nb, exp_a = lax.optimization_barrier((nb, exp_a))
     nb_cross = move(nb, across(2))
     g_a, na_mine, na_other = grads(
-        functools.partial(grad_kernel, (0,)), [exp_next, pack_next, stat_next, whole_next], 1, [],
+        functools.partial(grad_kernel, (0,)), [exp_a, pack_next, stat_next, whole_next], 1, [],
         "next_grad_a",
     )
     na_in = move(na_other, across(1))
@@ -393,7 +377,7 @@
     (passage_grad,) = call(
         functools.partial(passage_kernel, half),
         [shape((width, depth), bf16)],
-        [g_oa, g_ob, g_a, g_b, q_own, q_next],
+        [g_oa, g_ob, g_a, g_b, q_own, q_a, q_b],
         flops=4 * rows * width * depth,
         name="passage_grad",
     )

time: 85.7 us -> 88.1 us (1.028); the launches traced: 86.3 us -> 87.6 us
  starting transfers between devices: 36.7 us -> 32.7 us
  Pallas kernels: 30.4 us -> 33.1 us
  local copies, waits for them, and re-layouts: 0.02 us -> 1.48 us
  waiting for transfers between devices: 16.9 us -> 18 us
    ppermute x19 -> x17, starting transfers between devices: 36.7 us -> 32.7 us  [move(): return lax.ppermute(x, AXES, pairs)]
    pallas_call x6 -> x7, Pallas kernels: 26.9 us -> 29.4 us  [call(): pl.pallas_call(kernel, out_shape=tuple(outs), in_specs=[pl.BlockSpec(memo...]
    unnamed x8, local copies, waits for them, and re-layouts: 0.02 us -> 1.48 us
    ppermute x19 -> x17, waiting for transfers between devices: 16.9 us -> 18 us  [move(): return lax.ppermute(x, AXES, pairs)]
  transfers between devices with their start and end apart: 19 -> 17, of which waited for: 8 -> 7; matrix products, arithmetic and copies ran while one was open for 1% -> 0% of each run, Pallas kernels for 30% -> 33%
where the time goes in v6:
time: 88.1 us; the launch traced here: 87.6 us
  Pallas kernels  33.1 us (38%)
  starting transfers between devices  32.7 us (37%)
  waiting for transfers between devices  18 us (20%)
  local copies, waits for them, and re-layouts  1.48 us (2%)
  other arithmetic  1.46 us (2%)
    ppermute x17, starting transfers between devices, move(): return lax.ppermute(x, AXES, pairs)  32.7 us
    pallas_call x7, Pallas kernels, call(): pl.pallas_call(kernel, out_shape=tuple(outs), in_specs=[pl.BlockSpec(memo...  29.4 us
    ppermute x17, waiting for transfers between devices, move(): return lax.ppermute(x, AXES, pairs)  18 us
    pallas_call x2, Pallas kernels, take(): pl.pallas_call(functools.partial(take_kernel, slot), out_shape=piece, in_...  3.66 us
  transfers between devices with their start and end apart: 17, of which 7 were waited for; matrix products, arithmetic and copies ran while one was open for 0% of the time, Pallas kernels for 33%

profile of v6, /device:TPU:1, one launch (start us, length us, event | category | flops | bytes accessed | tf_op | source)
XLA Modules:
  0.0 87.6 jit_solution(12644463219963925274)
XLA Ops:
  0.6 0.0 copy-start.3
  0.6 0.0 copy-start
  0.6 1.9 %take_a.1 = bf16[192,1024]{1,0:T(8,128)(2,1)} custom-call(bf16[768,1024]{1,0:T(8,128)(2,1)} %q_ref.3), custom_call_target="tpu_custom_call" | custom-call | tf_op jit(solution)/shard_map/take_a/pallas_call | solution.py:295
  2.6 9.9 %collective-permute-start = (bf16[192,1024]{1,0:T(8,128)(2,1)}, bf16[192,1024]{1,0:T(8,128)(2,1)S(1)}, u32[]{:S(2)}, u32[]{:S(2)}) collective-permute-start(bf16[192,1024]{1,0:T(8,128)(2,1)} %take_a.1), channel_id=1, source_target_pairs={{0,252},{1,253},{2,254},{3,255},{4,0},{5,1},{6,2},{7,3},{8,4},{9,5... | collective-permute-start | bytes 1179656 | tf_op jit(solution)/shard_map/ppermute | solution.py:287
  12.4 1.7 %take_b.1 = bf16[192,1024]{1,0:T(8,128)(2,1)} custom-call(bf16[768,1024]{1,0:T(8,128)(2,1)} %q_ref.3), custom_call_target="tpu_custom_call" | custom-call | tf_op jit(solution)/shard_map/take_b/pallas_call | solution.py:295
  14.2 0.5 collective-permute-start.1
  14.7 0.0 copy-done.3
  14.7 0.0 copy-done
  14.7 0.0 copy-start.1
  14.7 0.7 copy-done.1
  15.5 0.0 copy-start.2
  15.5 0.7 copy-done.2
  16.2 5.3 %own_scores.1 = (f32[1536,768]{1,0:T(8,128)S(1)}, f32[8,768]{1,0:T(8,128)S(1)}, f32[24,768]{1,0:T(8,128)S(1)}, f32[24,768]{1,0:T(8,128)S(1)}, bf16[768,1024]{1,0:T(8,128)(2,1)S(1)}) custom-call(bf16[768,1024]{1,0:T(8,128)(2,1)} %q_ref.3, bf16[1536,1024]{1,0:T(8,128)(2,1)S(1)} %copy-done, s32[8,768]{1,0:T(8,128)S(1)} %copy-done.1, f32[8,768]{1,0:T(8,128)S(1)} %copy-done.2, ...), custom_call_target="tpu_custom_call" | custom-call | flops 2415919104 | bytes 11234304 | tf_op jit(solution)/shard_map/own_scores/pallas_call | solution.py:248
  21.5 0.0 collective-permute-done.mine_ref
  21.5 1.7 %collective-permute-start.4 = (bf16[192,1024]{1,0:T(8,128)(2,1)S(1)}, bf16[192,1024]{1,0:T(8,128)(2,1)S(1)}, u32[]{:S(2)}, u32[]{:S(2)}) collective-permute-start(bf16[192,1024]{1,0:T(8,128)(2,1)S(1)} %collective-permute-done.mine_ref), channel_id=1, source_target_pairs={{0,1},{1,0},{2,3},{3,2},{4,5},{5,4},{6,7},{7,6},{8,9},{9,8},{10,11... | collective-permute-start | bytes 1179656 | tf_op jit(solution)/shard_map/ppermute | solution.py:287
  23.2 6.3 %collective-permute-start.2 = (f32[8,768]{1,0:T(8,128)S(1)}, f32[8,768]{1,0:T(8,128)S(1)}, u32[]{:S(2)}, u32[]{:S(2)}) collective-permute-start(f32[8,768]{1,0:T(8,128)S(1)} %get-tuple-element.39.refs_2_.refs_6_), channel_id=1, source_target_pairs={{0,252},{1,253},{2,254},{3,255},{4,0},{5,1},{6,2},{7,3},{8,4},{9,5... | collective-permute-start | bytes 73736 | tf_op jit(solution)/shard_map/ppermute | solution.py:287
  29.5 0.9 %collective-permute-done.2.refs_1_ = f32[8,768]{1,0:T(8,128)S(1)} collective-permute-done((f32[8,768]{1,0:T(8,128)S(1)}, f32[8,768]{1,0:T(8,128)S(1)}, u32[]{:S(2)}, u32[]{:S(2)}) %collective-permute-start.2) | collective-permute-done | bytes 24608 | tf_op jit(solution)/shard_map/ppermute | solution.py:287
  30.5 0.0 collective-permute-done.1.mine_ref
  30.5 0.9 collective-permute-start.3
  31.3 6.2 %collective-permute-start.5 = (f32[24,768]{1,0:T(8,128)S(1)}, f32[24,768]{1,0:T(8,128)S(1)}, u32[]{:S(2)}, u32[]{:S(2)}) collective-permute-start(f32[24,768]{1,0:T(8,128)S(1)} %get-tuple-element.47), channel_id=1, source_target_pairs={{0,252},{1,253},{2,254},{3,255},{4,0},{5,1},{6,2},{7,3},{8,4},{9,5... | collective-permute-start | bytes 221192 | tf_op jit(solution)/shard_map/ppermute | solution.py:287
  37.6 0.0 collective-permute-done.4.other_ref
  37.6 1.9 %next_scores_a.1 = (f32[1536,384]{1,0:T(8,128)S(1)}, f32[8,768]{1,0:T(8,128)S(1)}, bf16[384,1024]{1,0:T(8,128)(2,1)S(1)}) custom-call(bf16[192,1024]{1,0:T(8,128)(2,1)S(1)} %collective-permute-done.mine_ref, bf16[192,1024]{1,0:T(8,128)(2,1)S(1)} %collective-permute-done.4.other_ref, bf16[1536,1024]{1,0:T(8,128)(2,1)S(1)} %copy-done), custom_call_target="tpu_custom_call" | custom-call | flops 1207959552 | bytes 7102464 | tf_op jit(solution)/shard_map/next_scores_a/pallas_call | solution.py:248
  39.5 0.0 collective-permute-done.3.other_ref
  39.5 1.9 %next_scores_b.1 = (f32[1536,384]{1,0:T(8,128)S(1)}, f32[8,768]{1,0:T(8,128)S(1)}, bf16[384,1024]{1,0:T(8,128)(2,1)S(1)}) custom-call(bf16[192,1024]{1,0:T(8,128)(2,1)S(1)} %collective-permute-done.1.mine_ref, bf16[192,1024]{1,0:T(8,128)(2,1)S(1)} %collective-permute-done.3.other_ref, bf16[1536,1024]{1,0:T(8,128)(2,1)S(1)} %copy-done, ...), custom_call_target="tpu_custom_call" | custom-call | flops 1207959552 | bytes 7151616 | tf_op jit(solution)/shard_map/next_scores_b/pallas_call | solution.py:248
  41.5 2.5 %collective-permute-start.6 = (f32[8,768]{1,0:T(8,128)S(1)}, f32[8,768]{1,0:T(8,128)S(1)}, u32[]{:S(2)}, u32[]{:S(2)}) collective-permute-start(f32[8,768]{1,0:T(8,128)S(1)} %get-tuple-element.48.stat_ref.refs_2_), channel_id=1, source_target_pairs={{0,2},{1,3},{2,0},{3,1},{4,6},{5,7},{6,4},{7,5},{8,10},{9,11},{10,... | collective-permute-start | bytes 73736 | tf_op jit(solution)/shard_map/ppermute | solution.py:287
  44.0 0.6 collective-permute-start.7
  44.6 0.4 collective-permute-start.8
  45.0 0.0 collective-permute-done.5.pack_ref.refs_1_
  45.0 0.8 collective-permute-done.6.cross_ref
  45.8 0.0 collective-permute-done.7.core_ref
  45.8 3.6 %collective-permute-done.8.both_ref = f32[8,768]{1,0:T(8,128)S(1)} collective-permute-done((f32[8,768]{1,0:T(8,128)S(1)}, f32[8,768]{1,0:T(8,128)S(1)}, u32[]{:S(2)}, u32[]{:S(2)}) %collective-permute-start.8) | collective-permute-done | bytes 24608 | tf_op jit(solution)/shard_map/ppermute | solution.py:287
  49.3 2.5 %next_grad_b.1 = (bf16[1536,384]{1,0:T(8,128)(2,1)S(1)}, bf16[192,1024]{1,0:T(8,128)(2,1)S(1)}, bf16[192,1024]{1,0:T(8,128)(2,1)S(1)}, f32[8,768]{1,0:T(8,128)S(1)}) custom-call(bf16[1536,1024]{1,0:T(8,128)(2,1)S(1)} %copy-done, f32[1536,384]{1,0:T(8,128)S(1)} %get-tuple-element.46.exp_ref, f32[24,768]{1,0:T(8,128)S(1)} %collective-permute-done.5.pack_ref.refs_1_, ...), custom_call_target="tpu_custom_call" | custom-call | flops 1207959552 | bytes 7667712 | tf_op jit(solution)/shard_map/next_grad_b/pallas_call | solution.py:248
  51.9 0.1 collective-permute-start.11
  52.0 1.7 %collective-permute-done.11 = bf16[192,1024]{1,0:T(8,128)(2,1)S(1)} collective-permute-done((bf16[192,1024]{1,0:T(8,128)(2,1)S(1)}, bf16[192,1024]{1,0:T(8,128)(2,1)S(1)}, u32[]{:S(2)}, u32[]{:S(2)}) %collective-permute-start.11) | collective-permute-done | bytes 393248 | tf_op jit(solution)/shard_map/ppermute | solution.py:287
  53.7 0.1 add_convert_fusion.3
  53.8 0.6 collective-permute-start.13
  54.4 2.5 %next_grad_a.1 = (bf16[1536,384]{1,0:T(8,128)(2,1)S(1)}, bf16[192,1024]{1,0:T(8,128)(2,1)S(1)}, bf16[192,1024]{1,0:T(8,128)(2,1)S(1)}) custom-call(bf16[1536,1024]{1,0:T(8,128)(2,1)S(1)} %copy-done, f32[1536,384]{1,0:T(8,128)S(1)} %get-tuple-element.55.refs_0_, f32[24,768]{1,0:T(8,128)S(1)} %collective-permute-done.5.pack_ref.refs_1_, ...), custom_call_target="tpu_custom_call" | custom-call | flops 1207959552 | bytes 7593984 | tf_op jit(solution)/shard_map/next_grad_a/pallas_call | solution.py:248
  56.9 0.5 collective-permute-start.12
  57.4 0.0 collective-permute-start.9
  57.4 6.9 %collective-permute-done.9.refs_3_.refs_7_ = f32[8,768]{1,0:T(8,128)S(1)} collective-permute-done((f32[8,768]{1,0:T(8,128)S(1)}, f32[8,768]{1,0:T(8,128)S(1)}, u32[]{:S(2)}, u32[]{:S(2)}) %collective-permute-start.9) | collective-permute-done | bytes 24608 | tf_op jit(solution)/shard_map/ppermute | solution.py:287
  64.3 6.8 %own_grad.1 = (bf16[1536,384]{1,0:T(8,128)(2,1)S(1)}, bf16[192,1024]{1,0:T(8,128)(2,1)S(1)}, bf16[192,1024]{1,0:T(8,128)(2,1)S(1)}, bf16[1536,384]{1,0:T(8,128)(...) custom-call(bf16[1536,1024]{1,0:T(8,128)(2,1)S(1)} %copy-done, ...), custom_call_target="tpu_custom_call" | custom-call | flops 2415919104 | bytes 16760832 | tf_op jit(solution)/shard_map/own_grad/pallas_call | solution.py:248
  71.1 0.4 collective-permute-start.15
  71.5 0.2 collective-permute-start.10
  71.7 0.0 collective-permute-done.13
  71.7 0.0 collective-permute-done.12
  71.7 0.2 add_convert_fusion.2
  71.9 0.1 collective-permute-start.14
  72.0 0.9 %collective-permute-done.15 = bf16[192,1024]{1,0:T(8,128)(2,1)S(1)} collective-permute-done((bf16[192,1024]{1,0:T(8,128)(2,1)S(1)}, bf16[192,1024]{1,0:T(8,128)(2,1)S(1)}, u32[]{:S(2)}, u32[]{:S(2)}) %collective-permute-start.15) | collective-permute-done | bytes 393248 | tf_op jit(solution)/shard_map/ppermute | solution.py:287
  72.9 0.1 add_convert_fusion.1
  73.0 1.9 %collective-permute-start.16 = (bf16[192,1024]{1,0:T(8,128)(2,1)S(1)}, bf16[192,1024]{1,0:T(8,128)(2,1)S(1)}, u32[]{:S(2)}, u32[]{:S(2)}) collective-permute-start(bf16[192,1024]{1,0:T(8,128)(2,1)S(1)} %add_convert_fusion.1), channel_id=1, source_target_pairs={{0,2},{1,3},{2,0},{3,1},{4,6},{5,7},{6,4},{7,5},{8,10},{9,11},{10,... | collective-permute-start | bytes 1179656 | tf_op jit(solution)/shard_map/ppermute | solution.py:287
  74.9 8.4 %passage_grad.1 = bf16[1536,1024]{1,0:T(8,128)(2,1)} custom-call(bf16[1536,384]{1,0:T(8,128)(2,1)S(1)} %get-tuple-element.63.refs_0_, bf16[1536,384]{1,0:T(8,128)(2,1)S(1)} %get-tuple-element.64.refs_1_, bf16[1536,384]{1,0:T(8,128)(2,1)S(1)} %get-tuple-element.65.refs_2_, bf16[1536,384]{1,0:T(8,128)(2,1)S(1)} %get-tuple-element.66.refs_3_, ...), custom_call_target="tpu_custom_call" | custom-call | flops 4831838208 | bytes 11010048 | tf_op jit(solution)/shard_map/passage_grad/pallas_call | solution.py:248
  83.4 0.0 collective-permute-done.10
  83.4 3.2 %collective-permute-done.14 = bf16[192,1024]{1,0:T(8,128)(2,1)S(1)} collective-permute-done((bf16[192,1024]{1,0:T(8,128)(2,1)S(1)}, bf16[192,1024]{1,0:T(8,128)(2,1)S(1)}, u32[]{:S(2)}, u32[]{:S(2)}) %collective-permute-start.14) | collective-permute-done | bytes 393248 | tf_op jit(solution)/shard_map/ppermute | solution.py:287
  86.6 0.0 collective-permute-done.16
  86.6 1.0 %add_convert_fusion = bf16[192,1024]{1,0:T(8,128)(2,1)} fusion(bf16[192,1024]{1,0:T(8,128)(2,1)S(1)} %collective-permute-done.16, bf16[192,1024]{1,0:T(8,128)(2,1)S(1)} %collective-permute-done.14, bf16[192,1024]{1,0:T(8,128)(2,1)S(1)} %collective-permute-done.10, bf16[192,1024]{1,0:T(8,128)(2,1)S(1)} %get-tuple-element.50), kind=kLoop, calls=%fused_computation | loop fusion | flops 1572864 | bytes 1966080 | tf_op jit(solution)/shard_map/convert_element_type | solution.py:389
  (1 shorter events, 0.0 us)
Async XLA Ops:
  0.6 14.1 %copy-start.3 = (f32[768]{0:T(1024)S(1)}, f32[768]{0:T(1024)}, u32[]{:S(2)}) copy-start(f32[768]{0:T(1024)} %param.7) | copy-start | bytes 9220
  0.6 14.1 %copy-start = (bf16[1536,1024]{1,0:T(8,128)(2,1)S(1)}, bf16[1536,1024]{1,0:T(8,128)(2,1)}, u32[]{:S(2)}) copy-start(bf16[1536,1024]{1,0:T(8,128)(2,1)} %p_ref.11) | copy-start | bytes 9437188
  2.6 18.9 %collective-permute-start = (bf16[192,1024]{1,0:T(8,128)(2,1)}, bf16[192,1024]{1,0:T(8,128)(2,1)S(1)}, u32[]{:S(2)}, u32[]{:S(2)}) collective-permute-start(bf16[192,1024]{1,0:T(8,128)(2,1)} %take_a.1), channel_id=1, source_target_pairs={{0,252},{1,253},{2,254},{3,255},{4,0},{5,1},{6,2},{7,3},{8,4},{9,5... | collective-permute-start | bytes 1179656 | tf_op jit(solution)/shard_map/ppermute | solution.py:287
  14.2 16.3 %collective-permute-start.1 = (bf16[192,1024]{1,0:T(8,128)(2,1)}, bf16[192,1024]{1,0:T(8,128)(2,1)S(1)}, u32[]{:S(2)}, u32[]{:S(2)}) collective-permute-start(bf16[192,1024]{1,0:T(8,128)(2,1)} %take_b.1), channel_id=1, source_target_pairs={{0,252},{1,253},{2,254},{3,255},{4,0},{5,1},{6,2},{7,3},{8,4},{9,5... | collective-permute-start | bytes 1179656 | tf_op jit(solution)/shard_map/ppermute | solution.py:287
  14.7 0.7 copy-start.1
  15.5 0.7 copy-start.2
  21.5 16.1 %collective-permute-start.4 = (bf16[192,1024]{1,0:T(8,128)(2,1)S(1)}, bf16[192,1024]{1,0:T(8,128)(2,1)S(1)}, u32[]{:S(2)}, u32[]{:S(2)}) collective-permute-start(bf16[192,1024]{1,0:T(8,128)(2,1)S(1)} %collective-permute-done.mine_ref), channel_id=1, source_target_pairs={{0,1},{1,0},{2,3},{3,2},{4,5},{5,4},{6,7},{7,6},{8,9},{9,8},{10,11... | collective-permute-start | bytes 1179656 | tf_op jit(solution)/shard_map/ppermute | solution.py:287
  23.2 7.3 %collective-permute-start.2 = (f32[8,768]{1,0:T(8,128)S(1)}, f32[8,768]{1,0:T(8,128)S(1)}, u32[]{:S(2)}, u32[]{:S(2)}) collective-permute-start(f32[8,768]{1,0:T(8,128)S(1)} %get-tuple-element.39.refs_2_.refs_6_), channel_id=1, source_target_pairs={{0,252},{1,253},{2,254},{3,255},{4,0},{5,1},{6,2},{7,3},{8,4},{9,5... | collective-permute-start | bytes 73736 | tf_op jit(solution)/shard_map/ppermute | solution.py:287
  30.5 9.1 %collective-permute-start.3 = (bf16[192,1024]{1,0:T(8,128)(2,1)S(1)}, bf16[192,1024]{1,0:T(8,128)(2,1)S(1)}, u32[]{:S(2)}, u32[]{:S(2)}) collective-permute-start(bf16[192,1024]{1,0:T(8,128)(2,1)S(1)} %collective-permute-done.1.mine_ref), channel_id=1, source_target_pairs={{0,1},{1,0},{2,3},{3,2},{4,5},{5,4},{6,7},{7,6},{8,9},{9,8},{10,11... | collective-permute-start | bytes 1179656 | tf_op jit(solution)/shard_map/ppermute | solution.py:287
  31.3 13.7 %collective-permute-start.5 = (f32[24,768]{1,0:T(8,128)S(1)}, f32[24,768]{1,0:T(8,128)S(1)}, u32[]{:S(2)}, u32[]{:S(2)}) collective-permute-start(f32[24,768]{1,0:T(8,128)S(1)} %get-tuple-element.47), channel_id=1, source_target_pairs={{0,252},{1,253},{2,254},{3,255},{4,0},{5,1},{6,2},{7,3},{8,4},{9,5... | collective-permute-start | bytes 221192 | tf_op jit(solution)/shard_map/ppermute | solution.py:287
  41.5 4.3 %collective-permute-start.6 = (f32[8,768]{1,0:T(8,128)S(1)}, f32[8,768]{1,0:T(8,128)S(1)}, u32[]{:S(2)}, u32[]{:S(2)}) collective-permute-start(f32[8,768]{1,0:T(8,128)S(1)} %get-tuple-element.48.stat_ref.refs_2_), channel_id=1, source_target_pairs={{0,2},{1,3},{2,0},{3,1},{4,6},{5,7},{6,4},{7,5},{8,10},{9,11},{10,... | collective-permute-start | bytes 73736 | tf_op jit(solution)/shard_map/ppermute | solution.py:287
  44.0 1.7 %collective-permute-start.7 = (f32[8,768]{1,0:T(8,128)S(1)}, f32[8,768]{1,0:T(8,128)S(1)}, u32[]{:S(2)}, u32[]{:S(2)}) collective-permute-start(f32[8,768]{1,0:T(8,128)S(1)} %get-tuple-element.48.stat_ref.refs_2_), channel_id=1, source_target_pairs={{0,1},{1,0},{2,3},{3,2},{4,5},{5,4},{6,7},{7,6},{8,9},{9,8},{10,11... | collective-permute-start | bytes 73736 | tf_op jit(solution)/shard_map/ppermute | solution.py:287
  44.6 4.8 %collective-permute-start.8 = (f32[8,768]{1,0:T(8,128)S(1)}, f32[8,768]{1,0:T(8,128)S(1)}, u32[]{:S(2)}, u32[]{:S(2)}) collective-permute-start(f32[8,768]{1,0:T(8,128)S(1)} %get-tuple-element.48.stat_ref.refs_2_), channel_id=1, source_target_pairs={{0,3},{1,2},{2,1},{3,0},{4,7},{5,6},{6,5},{7,4},{8,11},{9,10},{10,... | collective-permute-start | bytes 73736 | tf_op jit(solution)/shard_map/ppermute | solution.py:287
  51.9 1.8 %collective-permute-start.11 = (bf16[192,1024]{1,0:T(8,128)(2,1)S(1)}, bf16[192,1024]{1,0:T(8,128)(2,1)S(1)}, u32[]{:S(2)}, u32[]{:S(2)}) collective-permute-start(bf16[192,1024]{1,0:T(8,128)(2,1)S(1)} %get-tuple-element.53), channel_id=1, source_target_pairs={{0,1},{1,0},{2,3},{3,2},{4,5},{5,4},{6,7},{7,6},{8,9},{9,8},{10,11... | collective-permute-start | bytes 1179656 | tf_op jit(solution)/shard_map/ppermute | solution.py:287
  53.8 17.8 %collective-permute-start.13 = (bf16[192,1024]{1,0:T(8,128)(2,1)S(1)}, bf16[192,1024]{1,0:T(8,128)(2,1)S(1)}, u32[]{:S(2)}, u32[]{:S(2)}) collective-permute-start(bf16[192,1024]{1,0:T(8,128)(2,1)S(1)} %add_convert_fusion.3), channel_id=1, source_target_pairs={{0,2},{1,3},{2,0},{3,1},{4,6},{5,7},{6,4},{7,5},{8,10},{9,11},{10,... | collective-permute-start | bytes 1179656 | tf_op jit(solution)/shard_map/ppermute | solution.py:287
  56.9 14.7 %collective-permute-start.12 = (bf16[192,1024]{1,0:T(8,128)(2,1)S(1)}, bf16[192,1024]{1,0:T(8,128)(2,1)S(1)}, u32[]{:S(2)}, u32[]{:S(2)}) collective-permute-start(bf16[192,1024]{1,0:T(8,128)(2,1)S(1)} %get-tuple-element.57), channel_id=1, source_target_pairs={{0,1},{1,0},{2,3},{3,2},{4,5},{5,4},{6,7},{7,6},{8,9},{9,8},{10,11... | collective-permute-start | bytes 1179656 | tf_op jit(solution)/shard_map/ppermute | solution.py:287
  57.4 6.9 %collective-permute-start.9 = (f32[8,768]{1,0:T(8,128)S(1)}, f32[8,768]{1,0:T(8,128)S(1)}, u32[]{:S(2)}, u32[]{:S(2)}) collective-permute-start(f32[8,768]{1,0:T(8,128)S(1)} %get-tuple-element.49.refs_3_), channel_id=1, source_target_pairs={{0,4},{1,5},{2,6},{3,7},{4,8},{5,9},{6,10},{7,11},{8,12},{9,13},{1... | collective-permute-start | bytes 73736 | tf_op jit(solution)/shard_map/ppermute | solution.py:287
  71.1 1.8 %collective-permute-start.15 = (bf16[192,1024]{1,0:T(8,128)(2,1)S(1)}, bf16[192,1024]{1,0:T(8,128)(2,1)S(1)}, u32[]{:S(2)}, u32[]{:S(2)}) collective-permute-start(bf16[192,1024]{1,0:T(8,128)(2,1)S(1)} %get-tuple-element.62), channel_id=1, source_target_pairs={{0,1},{1,0},{2,3},{3,2},{4,5},{5,4},{6,7},{7,6},{8,9},{9,8},{10,11... | collective-permute-start | bytes 1179656 | tf_op jit(solution)/shard_map/ppermute | solution.py:287
  71.5 11.9 %collective-permute-start.10 = (bf16[192,1024]{1,0:T(8,128)(2,1)S(1)}, bf16[192,1024]{1,0:T(8,128)(2,1)S(1)}, u32[]{:S(2)}, u32[]{:S(2)}) collective-permute-start(bf16[192,1024]{1,0:T(8,128)(2,1)S(1)} %get-tuple-element.51), channel_id=1, source_target_pairs={{0,1},{1,0},{2,3},{3,2},{4,5},{5,4},{6,7},{7,6},{8,9},{9,8},{10,11... | collective-permute-start | bytes 1179656 | tf_op jit(solution)/shard_map/ppermute | solution.py:287
  71.9 14.7 %collective-permute-start.14 = (bf16[192,1024]{1,0:T(8,128)(2,1)S(1)}, bf16[192,1024]{1,0:T(8,128)(2,1)S(1)}, u32[]{:S(2)}, u32[]{:S(2)}) collective-permute-start(bf16[192,1024]{1,0:T(8,128)(2,1)S(1)} %add_convert_fusion.2), channel_id=1, source_target_pairs={{0,4},{1,5},{2,6},{3,7},{4,8},{5,9},{6,10},{7,11},{8,12},{9,13},{1... | collective-permute-start | bytes 1179656 | tf_op jit(solution)/shard_map/ppermute | solution.py:287
  73.0 13.6 %collective-permute-start.16 = (bf16[192,1024]{1,0:T(8,128)(2,1)S(1)}, bf16[192,1024]{1,0:T(8,128)(2,1)S(1)}, u32[]{:S(2)}, u32[]{:S(2)}) collective-permute-start(bf16[192,1024]{1,0:T(8,128)(2,1)S(1)} %add_convert_fusion.1), channel_id=1, source_target_pairs={{0,2},{1,3},{2,0},{3,1},{4,6},{5,7},{6,4},{7,5},{8,10},{9,11},{10,... | collective-permute-start | bytes 1179656 | tf_op jit(solution)/shard_map/ppermute | solution.py:287

commit v7 on v6

--- a/solution.py
+++ b/solution.py
@@ -354,19 +354,20 @@
         "next_grad_b",
     )
     nb_in = move(nb_other, across(1))
+    nb = (nb_mine.astype(f32) + nb_in.astype(f32)).astype(bf16)
+    nb, exp_a, whole_next = lax.optimization_barrier((nb, exp_a, whole_next))
     whole_own = move(whole_next, along(1))
-    nb = (nb_mine.astype(f32) + nb_in.astype(f32)).astype(bf16)
-    nb, exp_a = lax.optimization_barrier((nb, exp_a))
     nb_cross = move(nb, across(2))
     g_a, na_mine, na_other = grads(
         functools.partial(grad_kernel, (0,)), [exp_a, pack_next, stat_next, whole_next], 1, [],
         "next_grad_a",
     )
-    na_in = move(na_other, across(1))
     of_own = [exp_own, pack_own, stat_own, whole_own]
     g_ob, ob_mine, ob_other, g_oa, oa_mine, oa_other = grads(
         functools.partial(grad_kernel, (1, 0)), of_own + of_own, 2, [], "own_grad"
     )
+    na_other, ob_other = lax.optimization_barrier((na_other, ob_other))
+    na_in = move(na_other, across(1))
     ob_in = move(ob_other, across(1))
     oa_in = move(oa_other, across(1))
     ob_mine, nb_cross = lax.optimization_barrier((ob_mine, nb_cross))

time: 88.1 us -> 87.7 us (level)
  starting transfers between devices: 32.7 us -> 35.1 us
  Pallas kernels: 33.1 us -> 31.3 us
  waiting for transfers between devices: 18 us -> 17.1 us
    ppermute x17, starting transfers between devices: 32.7 us -> 35.1 us  [move(): return lax.ppermute(x, AXES, pairs)]
    pallas_call x7, Pallas kernels: 29.4 us -> 27.6 us  [call(): pl.pallas_call(kernel, out_shape=tuple(outs), in_specs=[pl.BlockSpec(memo...]
    ppermute x17, waiting for transfers between devices: 18 us -> 17.1 us  [move(): return lax.ppermute(x, AXES, pairs)]
  transfers between devices with their start and end apart: 17 -> 17, of which waited for: 7 -> 9; matrix products, arithmetic and copies ran while one was open for 0% -> 0% of each run, Pallas kernels for 33% -> 31%
where the time goes in v7:
time: 87.7 us; the launch traced here: 87.2 us
  starting transfers between devices  35.1 us (40%)
  Pallas kernels  31.3 us (36%)
  waiting for transfers between devices  17.1 us (19%)
  local copies, waits for them, and re-layouts  1.48 us (2%)
  other arithmetic  1.47 us (2%)
    ppermute x17, starting transfers between devices, move(): return lax.ppermute(x, AXES, pairs)  35.1 us
    pallas_call x7, Pallas kernels, call(): pl.pallas_call(kernel, out_shape=tuple(outs), in_specs=[pl.BlockSpec(memo...  27.6 us
    ppermute x17, waiting for transfers between devices, move(): return lax.ppermute(x, AXES, pairs)  17.1 us
    pallas_call x2, Pallas kernels, take(): pl.pallas_call(functools.partial(take_kernel, slot), out_shape=piece, in_...  3.66 us
  transfers between devices with their start and end apart: 17, of which 9 were waited for; matrix products, arithmetic and copies ran while one was open for 0% of the time, Pallas kernels for 31%

profile of v7, /device:TPU:1, one launch (start us, length us, event | category | flops | bytes accessed | tf_op | source)
XLA Modules:
  0.0 87.2 jit_solution(12491338648095670153)
XLA Ops:
  0.6 0.0 copy-start.3
  0.6 0.0 copy-start
  0.6 1.9 %take_a.1 = bf16[192,1024]{1,0:T(8,128)(2,1)} custom-call(bf16[768,1024]{1,0:T(8,128)(2,1)} %q_ref.3), custom_call_target="tpu_custom_call" | custom-call | tf_op jit(solution)/shard_map/take_a/pallas_call | solution.py:295
  2.6 9.9 %collective-permute-start = (bf16[192,1024]{1,0:T(8,128)(2,1)}, bf16[192,1024]{1,0:T(8,128)(2,1)S(1)}, u32[]{:S(2)}, u32[]{:S(2)}) collective-permute-start(bf16[192,1024]{1,0:T(8,128)(2,1)} %take_a.1), channel_id=1, source_target_pairs={{0,252},{1,253},{2,254},{3,255},{4,0},{5,1},{6,2},{7,3},{8,4},{9,5... | collective-permute-start | bytes 1179656 | tf_op jit(solution)/shard_map/ppermute | solution.py:287
  12.4 1.7 %take_b.1 = bf16[192,1024]{1,0:T(8,128)(2,1)} custom-call(bf16[768,1024]{1,0:T(8,128)(2,1)} %q_ref.3), custom_call_target="tpu_custom_call" | custom-call | tf_op jit(solution)/shard_map/take_b/pallas_call | solution.py:295
  14.2 0.5 collective-permute-start.1
  14.7 0.0 copy-done.3
  14.7 0.0 copy-done
  14.7 0.0 copy-start.1
  14.7 0.7 copy-done.1
  15.5 0.0 copy-start.2
  15.5 0.7 copy-done.2
  16.2 5.3 %own_scores.1 = (f32[1536,768]{1,0:T(8,128)S(1)}, f32[8,768]{1,0:T(8,128)S(1)}, f32[24,768]{1,0:T(8,128)S(1)}, f32[24,768]{1,0:T(8,128)S(1)}, bf16[768,1024]{1,0:T(8,128)(2,1)S(1)}) custom-call(bf16[768,1024]{1,0:T(8,128)(2,1)} %q_ref.3, bf16[1536,1024]{1,0:T(8,128)(2,1)S(1)} %copy-done, s32[8,768]{1,0:T(8,128)S(1)} %copy-done.1, f32[8,768]{1,0:T(8,128)S(1)} %copy-done.2, ...), custom_call_target="tpu_custom_call" | custom-call | flops 2415919104 | bytes 11234304 | tf_op jit(solution)/shard_map/own_scores/pallas_call | solution.py:248
  21.5 0.0 collective-permute-done.mine_ref
  21.5 1.7 %collective-permute-start.4 = (bf16[192,1024]{1,0:T(8,128)(2,1)S(1)}, bf16[192,1024]{1,0:T(8,128)(2,1)S(1)}, u32[]{:S(2)}, u32[]{:S(2)}) collective-permute-start(bf16[192,1024]{1,0:T(8,128)(2,1)S(1)} %collective-permute-done.mine_ref), channel_id=1, source_target_pairs={{0,1},{1,0},{2,3},{3,2},{4,5},{5,4},{6,7},{7,6},{8,9},{9,8},{10,11... | collective-permute-start | bytes 1179656 | tf_op jit(solution)/shard_map/ppermute | solution.py:287
  23.2 6.3 %collective-permute-start.2 = (f32[8,768]{1,0:T(8,128)S(1)}, f32[8,768]{1,0:T(8,128)S(1)}, u32[]{:S(2)}, u32[]{:S(2)}) collective-permute-start(f32[8,768]{1,0:T(8,128)S(1)} %get-tuple-element.42.refs_2_.refs_6_), channel_id=1, source_target_pairs={{0,252},{1,253},{2,254},{3,255},{4,0},{5,1},{6,2},{7,3},{8,4},{9,5... | collective-permute-start | bytes 73736 | tf_op jit(solution)/shard_map/ppermute | solution.py:287
  29.5 0.9 %collective-permute-done.2.refs_1_ = f32[8,768]{1,0:T(8,128)S(1)} collective-permute-done((f32[8,768]{1,0:T(8,128)S(1)}, f32[8,768]{1,0:T(8,128)S(1)}, u32[]{:S(2)}, u32[]{:S(2)}) %collective-permute-start.2) | collective-permute-done | bytes 24608 | tf_op jit(solution)/shard_map/ppermute | solution.py:287
  30.5 0.0 collective-permute-done.1.mine_ref
  30.5 0.9 collective-permute-start.3
  31.3 6.2 %collective-permute-start.5 = (f32[24,768]{1,0:T(8,128)S(1)}, f32[24,768]{1,0:T(8,128)S(1)}, u32[]{:S(2)}, u32[]{:S(2)}) collective-permute-start(f32[24,768]{1,0:T(8,128)S(1)} %get-tuple-element.50), channel_id=1, source_target_pairs={{0,252},{1,253},{2,254},{3,255},{4,0},{5,1},{6,2},{7,3},{8,4},{9,5... | collective-permute-start | bytes 221192 | tf_op jit(solution)/shard_map/ppermute | solution.py:287
  37.6 0.0 collective-permute-done.4.other_ref
  37.6 1.9 %next_scores_a.1 = (f32[1536,384]{1,0:T(8,128)S(1)}, f32[8,768]{1,0:T(8,128)S(1)}, bf16[384,1024]{1,0:T(8,128)(2,1)S(1)}) custom-call(bf16[192,1024]{1,0:T(8,128)(2,1)S(1)} %collective-permute-done.mine_ref, bf16[192,1024]{1,0:T(8,128)(2,1)S(1)} %collective-permute-done.4.other_ref, bf16[1536,1024]{1,0:T(8,128)(2,1)S(1)} %copy-done), custom_call_target="tpu_custom_call" | custom-call | flops 1207959552 | bytes 7102464 | tf_op jit(solution)/shard_map/next_scores_a/pallas_call | solution.py:248
  39.5 0.0 collective-permute-done.3.other_ref
  39.5 2.0 %next_scores_b.1 = (f32[1536,384]{1,0:T(8,128)S(1)}, f32[8,768]{1,0:T(8,128)S(1)}, bf16[384,1024]{1,0:T(8,128)(2,1)S(1)}) custom-call(bf16[192,1024]{1,0:T(8,128)(2,1)S(1)} %collective-permute-done.1.mine_ref, bf16[192,1024]{1,0:T(8,128)(2,1)S(1)} %collective-permute-done.3.other_ref, bf16[1536,1024]{1,0:T(8,128)(2,1)S(1)} %copy-done, ...), custom_call_target="tpu_custom_call" | custom-call | flops 1207959552 | bytes 7151616 | tf_op jit(solution)/shard_map/next_scores_b/pallas_call | solution.py:248
  41.5 2.7 %collective-permute-start.8 = (f32[8,768]{1,0:T(8,128)S(1)}, f32[8,768]{1,0:T(8,128)S(1)}, u32[]{:S(2)}, u32[]{:S(2)}) collective-permute-start(f32[8,768]{1,0:T(8,128)S(1)} %get-tuple-element.51.stat_ref.refs_2_), channel_id=1, source_target_pairs={{0,3},{1,2},{2,1},{3,0},{4,7},{5,6},{6,5},{7,4},{8,11},{9,10},{10,... | collective-permute-start | bytes 73736 | tf_op jit(solution)/shard_map/ppermute | solution.py:287
  44.2 0.2 collective-permute-start.7
  44.4 0.5 collective-permute-start.6
  45.0 0.0 collective-permute-done.5.pack_ref.refs_1_
  45.0 1.4 %collective-permute-done.8.both_ref = f32[8,768]{1,0:T(8,128)S(1)} collective-permute-done((f32[8,768]{1,0:T(8,128)S(1)}, f32[8,768]{1,0:T(8,128)S(1)}, u32[]{:S(2)}, u32[]{:S(2)}) %collective-permute-start.8) | collective-permute-done | bytes 24608 | tf_op jit(solution)/shard_map/ppermute | solution.py:287
  46.3 0.0 collective-permute-done.7.core_ref
  46.4 2.3 %collective-permute-done.6.cross_ref = f32[8,768]{1,0:T(8,128)S(1)} collective-permute-done((f32[8,768]{1,0:T(8,128)S(1)}, f32[8,768]{1,0:T(8,128)S(1)}, u32[]{:S(2)}, u32[]{:S(2)}) %collective-permute-start.6) | collective-permute-done | bytes 24608 | tf_op jit(solution)/shard_map/ppermute | solution.py:287
  48.6 2.5 %next_grad_b.1 = (bf16[1536,384]{1,0:T(8,128)(2,1)S(1)}, bf16[192,1024]{1,0:T(8,128)(2,1)S(1)}, bf16[192,1024]{1,0:T(8,128)(2,1)S(1)}, f32[8,768]{1,0:T(8,128)S(1)}) custom-call(bf16[1536,1024]{1,0:T(8,128)(2,1)S(1)} %copy-done, f32[1536,384]{1,0:T(8,128)S(1)} %get-tuple-element.49.exp_ref, f32[24,768]{1,0:T(8,128)S(1)} %collective-permute-done.5.pack_ref.refs_1_, ...), custom_call_target="tpu_custom_call" | custom-call | flops 1207959552 | bytes 7667712 | tf_op jit(solution)/shard_map/next_grad_b/pallas_call | solution.py:248
  51.1 1.6 %collective-permute-start.9 = (bf16[192,1024]{1,0:T(8,128)(2,1)S(1)}, bf16[192,1024]{1,0:T(8,128)(2,1)S(1)}, u32[]{:S(2)}, u32[]{:S(2)}) collective-permute-start(bf16[192,1024]{1,0:T(8,128)(2,1)S(1)} %get-tuple-element.53), channel_id=1, source_target_pairs={{0,1},{1,0},{2,3},{3,2},{4,5},{5,4},{6,7},{7,6},{8,9},{9,8},{10,11... | collective-permute-start | bytes 1179656 | tf_op jit(solution)/shard_map/ppermute | solution.py:287
  52.7 1.3 %collective-permute-done.9 = bf16[192,1024]{1,0:T(8,128)(2,1)S(1)} collective-permute-done((bf16[192,1024]{1,0:T(8,128)(2,1)S(1)}, bf16[192,1024]{1,0:T(8,128)(2,1)S(1)}, u32[]{:S(2)}, u32[]{:S(2)}) %collective-permute-start.9) | collective-permute-done | bytes 393248 | tf_op jit(solution)/shard_map/ppermute | solution.py:287
  54.0 0.1 add_convert_fusion.3
  54.1 0.1 collective-permute-start.10
  54.2 0.6 collective-permute-start.13
  54.8 2.5 %next_grad_a.1 = (bf16[1536,384]{1,0:T(8,128)(2,1)S(1)}, bf16[192,1024]{1,0:T(8,128)(2,1)S(1)}, bf16[192,1024]{1,0:T(8,128)(2,1)S(1)}) custom-call(bf16[1536,1024]{1,0:T(8,128)(2,1)S(1)} %copy-done, f32[1536,384]{1,0:T(8,128)S(1)} %get-tuple-element.59.refs_0_, f32[24,768]{1,0:T(8,128)S(1)} %collective-permute-done.5.pack_ref.refs_1_, ...), custom_call_target="tpu_custom_call" | custom-call | flops 1207959552 | bytes 7593984 | tf_op jit(solution)/shard_map/next_grad_a/pallas_call | solution.py:248
  57.3 3.9 %collective-permute-done.10.refs_3_.refs_7_ = f32[8,768]{1,0:T(8,128)S(1)} collective-permute-done((f32[8,768]{1,0:T(8,128)S(1)}, f32[8,768]{1,0:T(8,128)S(1)}, u32[]{:S(2)}, u32[]{:S(2)}) %collective-permute-start.10) | collective-permute-done | bytes 24608 | tf_op jit(solution)/shard_map/ppermute | solution.py:287
  61.2 5.0 %own_grad.1 = (bf16[1536,384]{1,0:T(8,128)(2,1)S(1)}, bf16[192,1024]{1,0:T(8,128)(2,1)S(1)}, bf16[192,1024]{1,0:T(8,128)(2,1)S(1)}, bf16[1536,384]{1,0:T(8,128)(...) custom-call(bf16[1536,1024]{1,0:T(8,128)(2,1)S(1)} %copy-done, ...), custom_call_target="tpu_custom_call" | custom-call | flops 2415919104 | bytes 16760832 | tf_op jit(solution)/shard_map/own_grad/pallas_call | solution.py:248
  66.3 3.2 %collective-permute-start.15 = (bf16[192,1024]{1,0:T(8,128)(2,1)S(1)}, bf16[192,1024]{1,0:T(8,128)(2,1)S(1)}, u32[]{:S(2)}, u32[]{:S(2)}) collective-permute-start(bf16[192,1024]{1,0:T(8,128)(2,1)S(1)} %get-tuple-element.68), channel_id=1, source_target_pairs={{0,1},{1,0},{2,3},{3,2},{4,5},{5,4},{6,7},{7,6},{8,9},{9,8},{10,11... | collective-permute-start | bytes 1179656 | tf_op jit(solution)/shard_map/ppermute | solution.py:287
  69.5 0.1 collective-permute-start.12
  69.6 0.4 collective-permute-start.11
  70.0 0.0 collective-permute-done.13
  70.0 0.8 collective-permute-done.15
  70.8 0.1 add_convert_fusion.1
  70.9 0.1 collective-permute-start.16
  71.0 0.3 collective-permute-done.12
  71.4 0.2 add_convert_fusion.2
  71.6 0.1 collective-permute-start.14
  71.7 8.5 %passage_grad.1 = bf16[1536,1024]{1,0:T(8,128)(2,1)} custom-call(bf16[1536,384]{1,0:T(8,128)(2,1)S(1)} %get-tuple-element.69.refs_0_, bf16[1536,384]{1,0:T(8,128)(2,1)S(1)} %get-tuple-element.70.refs_1_, bf16[1536,384]{1,0:T(8,128)(2,1)S(1)} %get-tuple-element.71.refs_2_, bf16[1536,384]{1,0:T(8,128)(2,1)S(1)} %get-tuple-element.72.refs_3_, ...), custom_call_target="tpu_custom_call" | custom-call | flops 4831838208 | bytes 11010048 | tf_op jit(solution)/shard_map/passage_grad/pallas_call | solution.py:248
  80.1 0.0 collective-permute-done.11
  80.1 2.7 %collective-permute-done.16 = bf16[192,1024]{1,0:T(8,128)(2,1)S(1)} collective-permute-done((bf16[192,1024]{1,0:T(8,128)(2,1)S(1)}, bf16[192,1024]{1,0:T(8,128)(2,1)S(1)}, u32[]{:S(2)}, u32[]{:S(2)}) %collective-permute-start.16) | collective-permute-done | bytes 393248 | tf_op jit(solution)/shard_map/ppermute | solution.py:287
  82.9 3.3 %collective-permute-done.14 = bf16[192,1024]{1,0:T(8,128)(2,1)S(1)} collective-permute-done((bf16[192,1024]{1,0:T(8,128)(2,1)S(1)}, bf16[192,1024]{1,0:T(8,128)(2,1)S(1)}, u32[]{:S(2)}, u32[]{:S(2)}) %collective-permute-start.14) | collective-permute-done | bytes 393248 | tf_op jit(solution)/shard_map/ppermute | solution.py:287
  86.2 1.0 %add_convert_fusion = bf16[192,1024]{1,0:T(8,128)(2,1)} fusion(bf16[192,1024]{1,0:T(8,128)(2,1)S(1)} %collective-permute-done.16, bf16[192,1024]{1,0:T(8,128)(2,1)S(1)} %collective-permute-done.14, bf16[192,1024]{1,0:T(8,128)(2,1)S(1)} %collective-permute-done.11, bf16[192,1024]{1,0:T(8,128)(2,1)S(1)} %get-tuple-element.57), kind=kLoop, calls=%fused_computation | loop fusion | flops 1572864 | bytes 1966080 | tf_op jit(solution)/shard_map/convert_element_type | solution.py:390
  (1 shorter events, 0.0 us)
Async XLA Ops:
  0.6 14.1 %copy-start.3 = (f32[768]{0:T(1024)S(1)}, f32[768]{0:T(1024)}, u32[]{:S(2)}) copy-start(f32[768]{0:T(1024)} %param.7) | copy-start | bytes 9220
  0.6 14.1 %copy-start = (bf16[1536,1024]{1,0:T(8,128)(2,1)S(1)}, bf16[1536,1024]{1,0:T(8,128)(2,1)}, u32[]{:S(2)}) copy-start(bf16[1536,1024]{1,0:T(8,128)(2,1)} %p_ref.11) | copy-start | bytes 9437188
  2.6 18.9 %collective-permute-start = (bf16[192,1024]{1,0:T(8,128)(2,1)}, bf16[192,1024]{1,0:T(8,128)(2,1)S(1)}, u32[]{:S(2)}, u32[]{:S(2)}) collective-permute-start(bf16[192,1024]{1,0:T(8,128)(2,1)} %take_a.1), channel_id=1, source_target_pairs={{0,252},{1,253},{2,254},{3,255},{4,0},{5,1},{6,2},{7,3},{8,4},{9,5... | collective-permute-start | bytes 1179656 | tf_op jit(solution)/shard_map/ppermute | solution.py:287
  14.2 16.3 %collective-permute-start.1 = (bf16[192,1024]{1,0:T(8,128)(2,1)}, bf16[192,1024]{1,0:T(8,128)(2,1)S(1)}, u32[]{:S(2)}, u32[]{:S(2)}) collective-permute-start(bf16[192,1024]{1,0:T(8,128)(2,1)} %take_b.1), channel_id=1, source_target_pairs={{0,252},{1,253},{2,254},{3,255},{4,0},{5,1},{6,2},{7,3},{8,4},{9,5... | collective-permute-start | bytes 1179656 | tf_op jit(solution)/shard_map/ppermute | solution.py:287
  14.7 0.7 copy-start.1
  15.5 0.7 copy-start.2
  21.5 16.1 %collective-permute-start.4 = (bf16[192,1024]{1,0:T(8,128)(2,1)S(1)}, bf16[192,1024]{1,0:T(8,128)(2,1)S(1)}, u32[]{:S(2)}, u32[]{:S(2)}) collective-permute-start(bf16[192,1024]{1,0:T(8,128)(2,1)S(1)} %collective-permute-done.mine_ref), channel_id=1, source_target_pairs={{0,1},{1,0},{2,3},{3,2},{4,5},{5,4},{6,7},{7,6},{8,9},{9,8},{10,11... | collective-permute-start | bytes 1179656 | tf_op jit(solution)/shard_map/ppermute | solution.py:287
  23.2 7.3 %collective-permute-start.2 = (f32[8,768]{1,0:T(8,128)S(1)}, f32[8,768]{1,0:T(8,128)S(1)}, u32[]{:S(2)}, u32[]{:S(2)}) collective-permute-start(f32[8,768]{1,0:T(8,128)S(1)} %get-tuple-element.42.refs_2_.refs_6_), channel_id=1, source_target_pairs={{0,252},{1,253},{2,254},{3,255},{4,0},{5,1},{6,2},{7,3},{8,4},{9,5... | collective-permute-start | bytes 73736 | tf_op jit(solution)/shard_map/ppermute | solution.py:287
  30.5 9.1 %collective-permute-start.3 = (bf16[192,1024]{1,0:T(8,128)(2,1)S(1)}, bf16[192,1024]{1,0:T(8,128)(2,1)S(1)}, u32[]{:S(2)}, u32[]{:S(2)}) collective-permute-start(bf16[192,1024]{1,0:T(8,128)(2,1)S(1)} %collective-permute-done.1.mine_ref), channel_id=1, source_target_pairs={{0,1},{1,0},{2,3},{3,2},{4,5},{5,4},{6,7},{7,6},{8,9},{9,8},{10,11... | collective-permute-start | bytes 1179656 | tf_op jit(solution)/shard_map/ppermute | solution.py:287
  31.3 13.6 %collective-permute-start.5 = (f32[24,768]{1,0:T(8,128)S(1)}, f32[24,768]{1,0:T(8,128)S(1)}, u32[]{:S(2)}, u32[]{:S(2)}) collective-permute-start(f32[24,768]{1,0:T(8,128)S(1)} %get-tuple-element.50), channel_id=1, source_target_pairs={{0,252},{1,253},{2,254},{3,255},{4,0},{5,1},{6,2},{7,3},{8,4},{9,5... | collective-permute-start | bytes 221192 | tf_op jit(solution)/shard_map/ppermute | solution.py:287
  41.5 4.8 %collective-permute-start.8 = (f32[8,768]{1,0:T(8,128)S(1)}, f32[8,768]{1,0:T(8,128)S(1)}, u32[]{:S(2)}, u32[]{:S(2)}) collective-permute-start(f32[8,768]{1,0:T(8,128)S(1)} %get-tuple-element.51.stat_ref.refs_2_), channel_id=1, source_target_pairs={{0,3},{1,2},{2,1},{3,0},{4,7},{5,6},{6,5},{7,4},{8,11},{9,10},{10,... | collective-permute-start | bytes 73736 | tf_op jit(solution)/shard_map/ppermute | solution.py:287
  44.2 2.1 %collective-permute-start.7 = (f32[8,768]{1,0:T(8,128)S(1)}, f32[8,768]{1,0:T(8,128)S(1)}, u32[]{:S(2)}, u32[]{:S(2)}) collective-permute-start(f32[8,768]{1,0:T(8,128)S(1)} %get-tuple-element.51.stat_ref.refs_2_), channel_id=1, source_target_pairs={{0,1},{1,0},{2,3},{3,2},{4,5},{5,4},{6,7},{7,6},{8,9},{9,8},{10,11... | collective-permute-start | bytes 73736 | tf_op jit(solution)/shard_map/ppermute | solution.py:287
  44.4 4.2 %collective-permute-start.6 = (f32[8,768]{1,0:T(8,128)S(1)}, f32[8,768]{1,0:T(8,128)S(1)}, u32[]{:S(2)}, u32[]{:S(2)}) collective-permute-start(f32[8,768]{1,0:T(8,128)S(1)} %get-tuple-element.51.stat_ref.refs_2_), channel_id=1, source_target_pairs={{0,2},{1,3},{2,0},{3,1},{4,6},{5,7},{6,4},{7,5},{8,10},{9,11},{10,... | collective-permute-start | bytes 73736 | tf_op jit(solution)/shard_map/ppermute | solution.py:287
  51.1 2.9 %collective-permute-start.9 = (bf16[192,1024]{1,0:T(8,128)(2,1)S(1)}, bf16[192,1024]{1,0:T(8,128)(2,1)S(1)}, u32[]{:S(2)}, u32[]{:S(2)}) collective-permute-start(bf16[192,1024]{1,0:T(8,128)(2,1)S(1)} %get-tuple-element.53), channel_id=1, source_target_pairs={{0,1},{1,0},{2,3},{3,2},{4,5},{5,4},{6,7},{7,6},{8,9},{9,8},{10,11... | collective-permute-start | bytes 1179656 | tf_op jit(solution)/shard_map/ppermute | solution.py:287
  54.1 7.1 %collective-permute-start.10 = (f32[8,768]{1,0:T(8,128)S(1)}, f32[8,768]{1,0:T(8,128)S(1)}, u32[]{:S(2)}, u32[]{:S(2)}) collective-permute-start(f32[8,768]{1,0:T(8,128)S(1)} %get-tuple-element.56.refs_3_), channel_id=1, source_target_pairs={{0,4},{1,5},{2,6},{3,7},{4,8},{5,9},{6,10},{7,11},{8,12},{9,13},{1... | collective-permute-start | bytes 73736 | tf_op jit(solution)/shard_map/ppermute | solution.py:287
  54.2 15.7 %collective-permute-start.13 = (bf16[192,1024]{1,0:T(8,128)(2,1)S(1)}, bf16[192,1024]{1,0:T(8,128)(2,1)S(1)}, u32[]{:S(2)}, u32[]{:S(2)}) collective-permute-start(bf16[192,1024]{1,0:T(8,128)(2,1)S(1)} %add_convert_fusion.3), channel_id=1, source_target_pairs={{0,2},{1,3},{2,0},{3,1},{4,6},{5,7},{6,4},{7,5},{8,10},{9,11},{10,... | collective-permute-start | bytes 1179656 | tf_op jit(solution)/shard_map/ppermute | solution.py:287
  66.3 4.6 %collective-permute-start.15 = (bf16[192,1024]{1,0:T(8,128)(2,1)S(1)}, bf16[192,1024]{1,0:T(8,128)(2,1)S(1)}, u32[]{:S(2)}, u32[]{:S(2)}) collective-permute-start(bf16[192,1024]{1,0:T(8,128)(2,1)S(1)} %get-tuple-element.68), channel_id=1, source_target_pairs={{0,1},{1,0},{2,3},{3,2},{4,5},{5,4},{6,7},{7,6},{8,9},{9,8},{10,11... | collective-permute-start | bytes 1179656 | tf_op jit(solution)/shard_map/ppermute | solution.py:287
  69.5 1.9 %collective-permute-start.12 = (bf16[192,1024]{1,0:T(8,128)(2,1)S(1)}, bf16[192,1024]{1,0:T(8,128)(2,1)S(1)}, u32[]{:S(2)}, u32[]{:S(2)}) collective-permute-start(bf16[192,1024]{1,0:T(8,128)(2,1)S(1)} %get-tuple-element.63), channel_id=1, source_target_pairs={{0,1},{1,0},{2,3},{3,2},{4,5},{5,4},{6,7},{7,6},{8,9},{9,8},{10,11... | collective-permute-start | bytes 1179656 | tf_op jit(solution)/shard_map/ppermute | solution.py:287
  69.6 10.6 %collective-permute-start.11 = (bf16[192,1024]{1,0:T(8,128)(2,1)S(1)}, bf16[192,1024]{1,0:T(8,128)(2,1)S(1)}, u32[]{:S(2)}, u32[]{:S(2)}) collective-permute-start(bf16[192,1024]{1,0:T(8,128)(2,1)S(1)} %get-tuple-element.58), channel_id=1, source_target_pairs={{0,1},{1,0},{2,3},{3,2},{4,5},{5,4},{6,7},{7,6},{8,9},{9,8},{10,11... | collective-permute-start | bytes 1179656 | tf_op jit(solution)/shard_map/ppermute | solution.py:287
  70.9 11.9 %collective-permute-start.16 = (bf16[192,1024]{1,0:T(8,128)(2,1)S(1)}, bf16[192,1024]{1,0:T(8,128)(2,1)S(1)}, u32[]{:S(2)}, u32[]{:S(2)}) collective-permute-start(bf16[192,1024]{1,0:T(8,128)(2,1)S(1)} %add_convert_fusion.1), channel_id=1, source_target_pairs={{0,2},{1,3},{2,0},{3,1},{4,6},{5,7},{6,4},{7,5},{8,10},{9,11},{10,... | collective-permute-start | bytes 1179656 | tf_op jit(solution)/shard_map/ppermute | solution.py:287
  71.6 14.6 %collective-permute-start.14 = (bf16[192,1024]{1,0:T(8,128)(2,1)S(1)}, bf16[192,1024]{1,0:T(8,128)(2,1)S(1)}, u32[]{:S(2)}, u32[]{:S(2)}) collective-permute-start(bf16[192,1024]{1,0:T(8,128)(2,1)S(1)} %add_convert_fusion.2), channel_id=1, source_target_pairs={{0,4},{1,5},{2,6},{3,7},{4,8},{5,9},{6,10},{7,11},{8,12},{9,13},{1... | collective-permute-start | bytes 1179656 | tf_op jit(solution)/shard_map/ppermute | solution.py:287

commit v8 on v7

--- a/solution.py
+++ b/solution.py
@@ -166,6 +166,7 @@
     factors = coef * jnp.exp2(stat_ref[2 : 2 + PARTS, lanes] - whole[0:1])
     ids, weights = pack_ref[0:8, lanes], pack_ref[8:16, lanes]
     exps = exp_ref if exp_ref.shape[1] == 2 * quarter else exp_ref.at[:, lanes]
+    grad_ref = grad_ref.at[:, lanes]
     rows = exp_ref.shape[0]
     more = ids[FEW:]
     low = jnp.min(jnp.where(more >= 0, more, float(rows))).astype(jnp.int32) // 16
@@ -214,24 +215,24 @@
 
 
 def grad_kernel(places, p_ref, *refs):
-    ins, outs, total_ref = refs[: 4 * len(places)], refs[4 * len(places) : -1], refs[-1]
+    exp_ref, pack_ref, stat_ref, whole_ref = refs[:4]
+    grad_ref, *outs, total_ref = refs[-2 - 2 * len(places) :]
     for n, place in enumerate(places):
-        exp_ref, pack_ref, stat_ref, whole_ref = ins[4 * n : 4 * n + 4]
         grads_of(
-            place, exp_ref, pack_ref, p_ref, stat_ref, whole_ref, *outs[3 * n : 3 * n + 3],
-            total_ref,
-        )
-
-
-def passage_kernel(half, *refs):
-    grads, (own_ref, *rows, out_ref) = refs[:4], refs[4:]
-    rows = [own_ref.at[at : at + half, :] for at in (0, half)] + rows
+            place, exp_ref, pack_ref, p_ref, stat_ref, whole_ref, grad_ref,
+            *outs[2 * n : 2 * n + 2], total_ref,
+        )
+
+
+def passage_kernel(own_grad_ref, next_grad_ref, own_ref, a_ref, b_ref, out_ref, rows_ref):
+    half = a_ref.shape[0]
+    rows_ref[:half, :] = a_ref[...]
+    rows_ref[half:, :] = b_ref[...]
     for at in range(0, out_ref.shape[1], TILE):
-        out_ref[:, at : at + TILE] = sum(
-            jnp.dot(
-                grad_ref[...], rows_ref[:, at : at + TILE], preferred_element_type=jnp.float32
-            )
-            for grad_ref, rows_ref in zip(grads, rows)
+        cols = slice(at, at + TILE)
+        out_ref[:, cols] = (
+            jnp.dot(own_grad_ref[...], own_ref[:, cols], preferred_element_type=jnp.float32)
+            + jnp.dot(next_grad_ref[...], rows_ref[:, cols], preferred_element_type=jnp.float32)
         ).astype(jnp.bfloat16)
 
 
@@ -243,11 +244,12 @@
     copy.wait()
 
 
-def call(kernel, outs, ins, scratch=(), flops=0, name=None, anywhere=0):
+def call(kernel, outs, ins, scratch=(), flops=0, name=None, anywhere=0, aliases=None):
     size = sum(math.prod(o.shape) * o.dtype.itemsize for o in list(outs) + list(ins))
     return pl.pallas_call(
         kernel,
         out_shape=tuple(outs),
+        input_output_aliases=aliases or {},
         in_specs=[pl.BlockSpec(memory_space=pltpu.HBM)] * anywhere
         + [IN_VMEM] * (len(ins) - anywhere),
         out_specs=(IN_VMEM,) * len(outs),
@@ -339,17 +341,18 @@
 
     cross, core, both = (move(stat_next, across(turn)) for turn in (2, 1, 3))
 
-    def grads(kernel, ins, count, more, name):
+    def grads(kernel, ins, count, more, name, aliases=None):
         return call(
             kernel,
-            [shape((width, half), bf16), piece, piece] * count + more,
+            [shape((width, rows), bf16)] + [piece, piece] * count + more,
             [passages] + ins,
             [pltpu.VMEM((half, depth), f32)],
             flops=2 * count * half * width * depth,
             name=name,
-        )
-
-    g_b, nb_mine, nb_other, whole_next = grads(
+            aliases=aliases,
+        )
+
+    g_next, nb_mine, nb_other, whole_next = grads(
         first_grad_kernel, [exp_b, pack_next, stat_next, cross, core, both], 1, [stat],
         "next_grad_b",
     )
@@ -357,28 +360,29 @@
     nb = (nb_mine.astype(f32) + nb_in.astype(f32)).astype(bf16)
     nb, exp_a, whole_next = lax.optimization_barrier((nb, exp_a, whole_next))
     whole_own = move(whole_next, along(1))
-    nb_cross = move(nb, across(2))
-    g_a, na_mine, na_other = grads(
-        functools.partial(grad_kernel, (0,)), [exp_a, pack_next, stat_next, whole_next], 1, [],
-        "next_grad_a",
+    nb_came = move(nb, along(1))
+    g_next, na_mine, na_other = grads(
+        functools.partial(grad_kernel, (0,)),
+        [exp_a, pack_next, stat_next, whole_next, g_next], 1, [], "next_grad_a", {5: 0},
     )
     of_own = [exp_own, pack_own, stat_own, whole_own]
-    g_ob, ob_mine, ob_other, g_oa, oa_mine, oa_other = grads(
-        functools.partial(grad_kernel, (1, 0)), of_own + of_own, 2, [], "own_grad"
+    g_own, ob_mine, ob_other, oa_mine, oa_other = grads(
+        functools.partial(grad_kernel, (1, 0)), of_own, 2, [], "own_grad"
     )
     na_other, ob_other = lax.optimization_barrier((na_other, ob_other))
     na_in = move(na_other, across(1))
     ob_in = move(ob_other, across(1))
     oa_in = move(oa_other, across(1))
-    ob_mine, nb_cross = lax.optimization_barrier((ob_mine, nb_cross))
-    ob = (ob_mine.astype(f32) + ob_in.astype(f32)).astype(bf16)
+    ob_mine, nb_came = lax.optimization_barrier((ob_mine, nb_came))
+    ob = (ob_mine.astype(f32) + ob_in.astype(f32) + nb_came.astype(f32)).astype(bf16)
     came_across = move(ob, across(2))
-    sent = (na_mine.astype(f32) + na_in.astype(f32) + nb_cross.astype(f32)).astype(bf16)
+    sent = (na_mine.astype(f32) + na_in.astype(f32)).astype(bf16)
     came_along = move(sent, along(1))
     (passage_grad,) = call(
-        functools.partial(passage_kernel, half),
+        passage_kernel,
         [shape((width, depth), bf16)],
-        [g_oa, g_ob, g_a, g_b, q_own, q_a, q_b],
+        [g_own, g_next, q_own, q_a, q_b],
+        [pltpu.VMEM((rows, depth), bf16)],
         flops=4 * rows * width * depth,
         name="passage_grad",
     )

time: 87.7 us -> 86.1 us (0.982); the launches traced: 87.2 us -> 87 us
  starting transfers between devices: 35.1 us -> 32.6 us
  Pallas kernels: 31.3 us -> 32.5 us
  waiting for transfers between devices: 17.1 us -> 18.2 us
    ppermute x17, starting transfers between devices: 35.1 us -> 32.6 us  [move(): return lax.ppermute(x, AXES, pairs)]
    pallas_call x7, Pallas kernels: 27.6 us -> 28.8 us  [call(): pl.pallas_call(kernel, out_shape=tuple(outs), input_output_aliases=aliase...]
    ppermute x17, waiting for transfers between devices: 17.1 us -> 18.2 us  [move(): return lax.ppermute(x, AXES, pairs)]
  transfers between devices with their start and end apart: 17 -> 17, of which waited for: 9 -> 8; matrix products, arithmetic and copies ran while one was open for 0% -> 0% of each run, Pallas kernels for 31% -> 32%
where the time goes in v8:
time: 86.1 us; the launch traced here: 87 us
  starting transfers between devices  32.6 us (38%)
  Pallas kernels  32.5 us (38%)
  waiting for transfers between devices  18.2 us (21%)
  local copies, waits for them, and re-layouts  1.48 us (2%)
  other arithmetic  1.46 us (2%)
    ppermute x17, starting transfers between devices, move(): return lax.ppermute(x, AXES, pairs)  32.6 us
    pallas_call x7, Pallas kernels, call(): pl.pallas_call(kernel, out_shape=tuple(outs), input_output_aliases=aliase...  28.8 us
    ppermute x17, waiting for transfers between devices, move(): return lax.ppermute(x, AXES, pairs)  18.2 us
    pallas_call x2, Pallas kernels, take(): pl.pallas_call(functools.partial(take_kernel, slot), out_shape=piece, in_...  3.66 us
  transfers between devices with their start and end apart: 17, of which 8 were waited for; matrix products, arithmetic and copies ran while one was open for 0% of the time, Pallas kernels for 32%

profile of v8, /device:TPU:1, one launch (start us, length us, event | category | flops | bytes accessed | tf_op | source)
XLA Modules:
  0.0 87.0 jit_solution(12153017773070341645)
XLA Ops:
  0.6 0.0 copy-start.3
  0.6 0.0 copy-start
  0.6 1.9 %take_a.1 = bf16[192,1024]{1,0:T(8,128)(2,1)} custom-call(bf16[768,1024]{1,0:T(8,128)(2,1)} %q_ref.3), custom_call_target="tpu_custom_call" | custom-call | tf_op jit(solution)/shard_map/take_a/pallas_call | solution.py:297
  2.6 9.9 %collective-permute-start = (bf16[192,1024]{1,0:T(8,128)(2,1)}, bf16[192,1024]{1,0:T(8,128)(2,1)S(1)}, u32[]{:S(2)}, u32[]{:S(2)}) collective-permute-start(bf16[192,1024]{1,0:T(8,128)(2,1)} %take_a.1), channel_id=1, source_target_pairs={{0,252},{1,253},{2,254},{3,255},{4,0},{5,1},{6,2},{7,3},{8,4},{9,5... | collective-permute-start | bytes 1179656 | tf_op jit(solution)/shard_map/ppermute | solution.py:289
  12.4 1.7 %take_b.1 = bf16[192,1024]{1,0:T(8,128)(2,1)} custom-call(bf16[768,1024]{1,0:T(8,128)(2,1)} %q_ref.3), custom_call_target="tpu_custom_call" | custom-call | tf_op jit(solution)/shard_map/take_b/pallas_call | solution.py:297
  14.2 0.5 collective-permute-start.1
  14.7 0.0 copy-done.3
  14.7 0.0 copy-done
  14.7 0.0 copy-start.1
  14.7 0.7 copy-done.1
  15.5 0.0 copy-start.2
  15.5 0.7 copy-done.2
  16.2 5.2 %own_scores.1 = (f32[1536,768]{1,0:T(8,128)S(1)}, f32[8,768]{1,0:T(8,128)S(1)}, f32[24,768]{1,0:T(8,128)S(1)}, f32[24,768]{1,0:T(8,128)S(1)}, bf16[768,1024]{1,0:T(8,128)(2,1)S(1)}) custom-call(bf16[768,1024]{1,0:T(8,128)(2,1)} %q_ref.3, bf16[1536,1024]{1,0:T(8,128)(2,1)S(1)} %copy-done, s32[8,768]{1,0:T(8,128)S(1)} %copy-done.1, f32[8,768]{1,0:T(8,128)S(1)} %copy-done.2, ...), custom_call_target="tpu_custom_call" | custom-call | flops 2415919104 | bytes 11234304 | tf_op jit(solution)/shard_map/own_scores/pallas_call | solution.py:249
  21.4 0.0 collective-permute-done.mine_ref
  21.4 1.8 %collective-permute-start.4 = (bf16[192,1024]{1,0:T(8,128)(2,1)S(1)}, bf16[192,1024]{1,0:T(8,128)(2,1)S(1)}, u32[]{:S(2)}, u32[]{:S(2)}) collective-permute-start(bf16[192,1024]{1,0:T(8,128)(2,1)S(1)} %collective-permute-done.mine_ref), channel_id=1, source_target_pairs={{0,1},{1,0},{2,3},{3,2},{4,5},{5,4},{6,7},{7,6},{8,9},{9,8},{10,11... | collective-permute-start | bytes 1179656 | tf_op jit(solution)/shard_map/ppermute | solution.py:289
  23.2 6.3 %collective-permute-start.2 = (f32[8,768]{1,0:T(8,128)S(1)}, f32[8,768]{1,0:T(8,128)S(1)}, u32[]{:S(2)}, u32[]{:S(2)}) collective-permute-start(f32[8,768]{1,0:T(8,128)S(1)} %get-tuple-element.41.refs_2_), channel_id=1, source_target_pairs={{0,252},{1,253},{2,254},{3,255},{4,0},{5,1},{6,2},{7,3},{8,4},{9,5... | collective-permute-start | bytes 73736 | tf_op jit(solution)/shard_map/ppermute | solution.py:289
  29.5 0.9 %collective-permute-done.2.refs_1_ = f32[8,768]{1,0:T(8,128)S(1)} collective-permute-done((f32[8,768]{1,0:T(8,128)S(1)}, f32[8,768]{1,0:T(8,128)S(1)}, u32[]{:S(2)}, u32[]{:S(2)}) %collective-permute-start.2) | collective-permute-done | bytes 24608 | tf_op jit(solution)/shard_map/ppermute | solution.py:289
  30.5 0.0 collective-permute-done.1.mine_ref
  30.5 0.9 collective-permute-start.3
  31.3 6.2 %collective-permute-start.5 = (f32[24,768]{1,0:T(8,128)S(1)}, f32[24,768]{1,0:T(8,128)S(1)}, u32[]{:S(2)}, u32[]{:S(2)}) collective-permute-start(f32[24,768]{1,0:T(8,128)S(1)} %get-tuple-element.49), channel_id=1, source_target_pairs={{0,252},{1,253},{2,254},{3,255},{4,0},{5,1},{6,2},{7,3},{8,4},{9,5... | collective-permute-start | bytes 221192 | tf_op jit(solution)/shard_map/ppermute | solution.py:289
  37.6 0.0 collective-permute-done.4.other_ref
  37.6 1.9 %next_scores_a.1 = (f32[1536,384]{1,0:T(8,128)S(1)}, f32[8,768]{1,0:T(8,128)S(1)}, bf16[384,1024]{1,0:T(8,128)(2,1)S(1)}) custom-call(bf16[192,1024]{1,0:T(8,128)(2,1)S(1)} %collective-permute-done.mine_ref, bf16[192,1024]{1,0:T(8,128)(2,1)S(1)} %collective-permute-done.4.other_ref, bf16[1536,1024]{1,0:T(8,128)(2,1)S(1)} %copy-done), custom_call_target="tpu_custom_call" | custom-call | flops 1207959552 | bytes 7102464 | tf_op jit(solution)/shard_map/next_scores_a/pallas_call | solution.py:249
  39.5 0.0 collective-permute-done.3.other_ref
  39.5 2.0 %next_scores_b.1 = (f32[1536,384]{1,0:T(8,128)S(1)}, f32[8,768]{1,0:T(8,128)S(1)}, bf16[384,1024]{1,0:T(8,128)(2,1)S(1)}) custom-call(bf16[192,1024]{1,0:T(8,128)(2,1)S(1)} %collective-permute-done.1.mine_ref, bf16[192,1024]{1,0:T(8,128)(2,1)S(1)} %collective-permute-done.3.other_ref, bf16[1536,1024]{1,0:T(8,128)(2,1)S(1)} %copy-done, ...), custom_call_target="tpu_custom_call" | custom-call | flops 1207959552 | bytes 7151616 | tf_op jit(solution)/shard_map/next_scores_b/pallas_call | solution.py:249
  41.5 2.7 %collective-permute-start.8 = (f32[8,768]{1,0:T(8,128)S(1)}, f32[8,768]{1,0:T(8,128)S(1)}, u32[]{:S(2)}, u32[]{:S(2)}) collective-permute-start(f32[8,768]{1,0:T(8,128)S(1)} %get-tuple-element.50.stat_ref.refs_2_), channel_id=1, source_target_pairs={{0,3},{1,2},{2,1},{3,0},{4,7},{5,6},{6,5},{7,4},{8,11},{9,10},{10,... | collective-permute-start | bytes 73736 | tf_op jit(solution)/shard_map/ppermute | solution.py:289
  44.2 0.2 collective-permute-start.7
  44.4 0.5 collective-permute-start.6
  45.0 0.0 collective-permute-done.5.pack_ref.refs_1_
  45.0 1.4 %collective-permute-done.8.both_ref = f32[8,768]{1,0:T(8,128)S(1)} collective-permute-done((f32[8,768]{1,0:T(8,128)S(1)}, f32[8,768]{1,0:T(8,128)S(1)}, u32[]{:S(2)}, u32[]{:S(2)}) %collective-permute-start.8) | collective-permute-done | bytes 24608 | tf_op jit(solution)/shard_map/ppermute | solution.py:289
  46.3 0.0 collective-permute-done.7.core_ref
  46.3 2.3 %collective-permute-done.6.cross_ref = f32[8,768]{1,0:T(8,128)S(1)} collective-permute-done((f32[8,768]{1,0:T(8,128)S(1)}, f32[8,768]{1,0:T(8,128)S(1)}, u32[]{:S(2)}, u32[]{:S(2)}) %collective-permute-start.6) | collective-permute-done | bytes 24608 | tf_op jit(solution)/shard_map/ppermute | solution.py:289
  48.6 2.5 %next_grad_b.1 = (bf16[1536,768]{1,0:T(8,128)(2,1)S(1)}, bf16[192,1024]{1,0:T(8,128)(2,1)S(1)}, bf16[192,1024]{1,0:T(8,128)(2,1)S(1)}, f32[8,768]{1,0:T(8,128)S(1)}) custom-call(bf16[1536,1024]{1,0:T(8,128)(2,1)S(1)} %copy-done, f32[1536,384]{1,0:T(8,128)S(1)} %get-tuple-element.48.exp_ref, f32[24,768]{1,0:T(8,128)S(1)} %collective-permute-done.5.pack_ref.refs_1_, ...), custom_call_target="tpu_custom_call" | custom-call | flops 1207959552 | bytes 8847360 | tf_op jit(solution)/shard_map/next_grad_b/pallas_call | solution.py:249
  51.1 1.6 %collective-permute-start.9 = (bf16[192,1024]{1,0:T(8,128)(2,1)S(1)}, bf16[192,1024]{1,0:T(8,128)(2,1)S(1)}, u32[]{:S(2)}, u32[]{:S(2)}) collective-permute-start(bf16[192,1024]{1,0:T(8,128)(2,1)S(1)} %get-tuple-element.52), channel_id=1, source_target_pairs={{0,1},{1,0},{2,3},{3,2},{4,5},{5,4},{6,7},{7,6},{8,9},{9,8},{10,11... | collective-permute-start | bytes 1179656 | tf_op jit(solution)/shard_map/ppermute | solution.py:289
  52.7 1.3 %collective-permute-done.9 = bf16[192,1024]{1,0:T(8,128)(2,1)S(1)} collective-permute-done((bf16[192,1024]{1,0:T(8,128)(2,1)S(1)}, bf16[192,1024]{1,0:T(8,128)(2,1)S(1)}, u32[]{:S(2)}, u32[]{:S(2)}) %collective-permute-start.9) | collective-permute-done | bytes 393248 | tf_op jit(solution)/shard_map/ppermute | solution.py:289
  54.0 0.1 add_convert_fusion.3
  54.2 0.1 collective-permute-start.10
  54.3 0.1 collective-permute-start.14
  54.3 2.5 %next_grad_a.1 = (bf16[1536,768]{1,0:T(8,128)(2,1)S(1)}, bf16[192,1024]{1,0:T(8,128)(2,1)S(1)}, bf16[192,1024]{1,0:T(8,128)(2,1)S(1)}) custom-call(bf16[1536,1024]{1,0:T(8,128)(2,1)S(1)} %copy-done, f32[1536,384]{1,0:T(8,128)S(1)} %get-tuple-element.58.refs_0_, ...), custom_call_target="tpu_custom_call", output_to_operand_aliasing={{0}: (5, {})} | custom-call | flops 1207959552 | bytes 11132928 | tf_op jit(solution)/shard_map/next_grad_a/pallas_call | solution.py:249
  56.9 4.3 %collective-permute-done.10.refs_3_ = f32[8,768]{1,0:T(8,128)S(1)} collective-permute-done((f32[8,768]{1,0:T(8,128)S(1)}, f32[8,768]{1,0:T(8,128)S(1)}, u32[]{:S(2)}, u32[]{:S(2)}) %collective-permute-start.10) | collective-permute-done | bytes 24608 | tf_op jit(solution)/shard_map/ppermute | solution.py:289
  61.1 7.9 %own_grad.1 = (bf16[1536,768]{1,0:T(8,128)(2,1)S(1)}, bf16[192,1024]{1,0:T(8,128)(2,1)S(1)}, bf16[192,1024]{1,0:T(8,128)(2,1)S(1)}, bf16[192,1024]{1,0:T(8,128)(2,1)S(1)}, bf16[192,1024]{1,0:T(8,128)(2,1)S(1)}) custom-call(bf16[1536,1024]{1,0:T(8,128)(2,1)S(1)} %copy-done, f32[1536,768]{1,0:T(8,128)S(1)} %get-tuple-element.38.refs_0_, ...), custom_call_target="tpu_custom_call" | custom-call | flops 2415919104 | bytes 11919360 | tf_op jit(solution)/shard_map/own_grad/pallas_call | solution.py:249
  69.1 0.7 collective-permute-start.12
  69.8 0.1 collective-permute-start.15
  69.9 0.4 collective-permute-start.11
  70.3 0.0 collective-permute-done.14
  70.3 0.8 collective-permute-done.12
  71.2 0.1 add_convert_fusion.2
  71.3 0.1 collective-permute-start.13
  71.4 0.3 collective-permute-done.15
  71.7 0.2 add_convert_fusion.1
  71.9 0.5 collective-permute-start.16
  72.4 6.8 %passage_grad.1 = bf16[1536,1024]{1,0:T(8,128)(2,1)} custom-call(bf16[1536,768]{1,0:T(8,128)(2,1)S(1)} %get-tuple-element.69.own_grad_ref, bf16[1536,768]{1,0:T(8,128)(2,1)S(1)} %get-tuple-element.70.next_grad_ref, bf16[768,1024]{1,0:T(8,128)(2,1)S(1)} %get-tuple-element.71.own_ref, bf16[384,1024]{1,0:T(8,128)(2,1)S(1)} %get-tuple-element.72.a_ref, ...), custom_call_target="tpu_custom_call" | custom-call | flops 4831838208 | bytes 11010048 | tf_op jit(solution)/shard_map/passage_grad/pallas_call | solution.py:249
  79.2 0.0 collective-permute-done.11
  79.2 6.8 %collective-permute-done.13 = bf16[192,1024]{1,0:T(8,128)(2,1)S(1)} collective-permute-done((bf16[192,1024]{1,0:T(8,128)(2,1)S(1)}, bf16[192,1024]{1,0:T(8,128)(2,1)S(1)}, u32[]{:S(2)}, u32[]{:S(2)}) %collective-permute-start.13) | collective-permute-done | bytes 393248 | tf_op jit(solution)/shard_map/ppermute | solution.py:289
  86.0 0.0 collective-permute-done.16
  86.0 1.0 %add_convert_fusion = bf16[192,1024]{1,0:T(8,128)(2,1)} fusion(bf16[192,1024]{1,0:T(8,128)(2,1)S(1)} %collective-permute-done.16, bf16[192,1024]{1,0:T(8,128)(2,1)S(1)} %collective-permute-done.13, bf16[192,1024]{1,0:T(8,128)(2,1)S(1)} %collective-permute-done.11, bf16[192,1024]{1,0:T(8,128)(2,1)S(1)} %get-tuple-element.56), kind=kLoop, calls=%fused_computation | loop fusion | flops 1572864 | bytes 1966080 | tf_op jit(solution)/shard_map/convert_element_type | solution.py:394
  (1 shorter events, 0.0 us)
Async XLA Ops:
  0.6 14.1 %copy-start.3 = (f32[768]{0:T(1024)S(1)}, f32[768]{0:T(1024)}, u32[]{:S(2)}) copy-start(f32[768]{0:T(1024)} %param.7) | copy-start | bytes 9220
  0.6 14.1 %copy-start = (bf16[1536,1024]{1,0:T(8,128)(2,1)S(1)}, bf16[1536,1024]{1,0:T(8,128)(2,1)}, u32[]{:S(2)}) copy-start(bf16[1536,1024]{1,0:T(8,128)(2,1)} %p_ref.11) | copy-start | bytes 9437188
  2.6 18.9 %collective-permute-start = (bf16[192,1024]{1,0:T(8,128)(2,1)}, bf16[192,1024]{1,0:T(8,128)(2,1)S(1)}, u32[]{:S(2)}, u32[]{:S(2)}) collective-permute-start(bf16[192,1024]{1,0:T(8,128)(2,1)} %take_a.1), channel_id=1, source_target_pairs={{0,252},{1,253},{2,254},{3,255},{4,0},{5,1},{6,2},{7,3},{8,4},{9,5... | collective-permute-start | bytes 1179656 | tf_op jit(solution)/shard_map/ppermute | solution.py:289
  14.2 16.3 %collective-permute-start.1 = (bf16[192,1024]{1,0:T(8,128)(2,1)}, bf16[192,1024]{1,0:T(8,128)(2,1)S(1)}, u32[]{:S(2)}, u32[]{:S(2)}) collective-permute-start(bf16[192,1024]{1,0:T(8,128)(2,1)} %take_b.1), channel_id=1, source_target_pairs={{0,252},{1,253},{2,254},{3,255},{4,0},{5,1},{6,2},{7,3},{8,4},{9,5... | collective-permute-start | bytes 1179656 | tf_op jit(solution)/shard_map/ppermute | solution.py:289
  14.7 0.7 copy-start.1
  15.5 0.7 copy-start.2
  21.4 16.2 %collective-permute-start.4 = (bf16[192,1024]{1,0:T(8,128)(2,1)S(1)}, bf16[192,1024]{1,0:T(8,128)(2,1)S(1)}, u32[]{:S(2)}, u32[]{:S(2)}) collective-permute-start(bf16[192,1024]{1,0:T(8,128)(2,1)S(1)} %collective-permute-done.mine_ref), channel_id=1, source_target_pairs={{0,1},{1,0},{2,3},{3,2},{4,5},{5,4},{6,7},{7,6},{8,9},{9,8},{10,11... | collective-permute-start | bytes 1179656 | tf_op jit(solution)/shard_map/ppermute | solution.py:289
  23.2 7.3 %collective-permute-start.2 = (f32[8,768]{1,0:T(8,128)S(1)}, f32[8,768]{1,0:T(8,128)S(1)}, u32[]{:S(2)}, u32[]{:S(2)}) collective-permute-start(f32[8,768]{1,0:T(8,128)S(1)} %get-tuple-element.41.refs_2_), channel_id=1, source_target_pairs={{0,252},{1,253},{2,254},{3,255},{4,0},{5,1},{6,2},{7,3},{8,4},{9,5... | collective-permute-start | bytes 73736 | tf_op jit(solution)/shard_map/ppermute | solution.py:289
  30.5 9.1 %collective-permute-start.3 = (bf16[192,1024]{1,0:T(8,128)(2,1)S(1)}, bf16[192,1024]{1,0:T(8,128)(2,1)S(1)}, u32[]{:S(2)}, u32[]{:S(2)}) collective-permute-start(bf16[192,1024]{1,0:T(8,128)(2,1)S(1)} %collective-permute-done.1.mine_ref), channel_id=1, source_target_pairs={{0,1},{1,0},{2,3},{3,2},{4,5},{5,4},{6,7},{7,6},{8,9},{9,8},{10,11... | collective-permute-start | bytes 1179656 | tf_op jit(solution)/shard_map/ppermute | solution.py:289
  31.3 13.6 %collective-permute-start.5 = (f32[24,768]{1,0:T(8,128)S(1)}, f32[24,768]{1,0:T(8,128)S(1)}, u32[]{:S(2)}, u32[]{:S(2)}) collective-permute-start(f32[24,768]{1,0:T(8,128)S(1)} %get-tuple-element.49), channel_id=1, source_target_pairs={{0,252},{1,253},{2,254},{3,255},{4,0},{5,1},{6,2},{7,3},{8,4},{9,5... | collective-permute-start | bytes 221192 | tf_op jit(solution)/shard_map/ppermute | solution.py:289
  41.5 4.8 %collective-permute-start.8 = (f32[8,768]{1,0:T(8,128)S(1)}, f32[8,768]{1,0:T(8,128)S(1)}, u32[]{:S(2)}, u32[]{:S(2)}) collective-permute-start(f32[8,768]{1,0:T(8,128)S(1)} %get-tuple-element.50.stat_ref.refs_2_), channel_id=1, source_target_pairs={{0,3},{1,2},{2,1},{3,0},{4,7},{5,6},{6,5},{7,4},{8,11},{9,10},{10,... | collective-permute-start | bytes 73736 | tf_op jit(solution)/shard_map/ppermute | solution.py:289
  44.2 2.1 %collective-permute-start.7 = (f32[8,768]{1,0:T(8,128)S(1)}, f32[8,768]{1,0:T(8,128)S(1)}, u32[]{:S(2)}, u32[]{:S(2)}) collective-permute-start(f32[8,768]{1,0:T(8,128)S(1)} %get-tuple-element.50.stat_ref.refs_2_), channel_id=1, source_target_pairs={{0,1},{1,0},{2,3},{3,2},{4,5},{5,4},{6,7},{7,6},{8,9},{9,8},{10,11... | collective-permute-start | bytes 73736 | tf_op jit(solution)/shard_map/ppermute | solution.py:289
  44.4 4.2 %collective-permute-start.6 = (f32[8,768]{1,0:T(8,128)S(1)}, f32[8,768]{1,0:T(8,128)S(1)}, u32[]{:S(2)}, u32[]{:S(2)}) collective-permute-start(f32[8,768]{1,0:T(8,128)S(1)} %get-tuple-element.50.stat_ref.refs_2_), channel_id=1, source_target_pairs={{0,2},{1,3},{2,0},{3,1},{4,6},{5,7},{6,4},{7,5},{8,10},{9,11},{10,... | collective-permute-start | bytes 73736 | tf_op jit(solution)/shard_map/ppermute | solution.py:289
  51.1 2.9 %collective-permute-start.9 = (bf16[192,1024]{1,0:T(8,128)(2,1)S(1)}, bf16[192,1024]{1,0:T(8,128)(2,1)S(1)}, u32[]{:S(2)}, u32[]{:S(2)}) collective-permute-start(bf16[192,1024]{1,0:T(8,128)(2,1)S(1)} %get-tuple-element.52), channel_id=1, source_target_pairs={{0,1},{1,0},{2,3},{3,2},{4,5},{5,4},{6,7},{7,6},{8,9},{9,8},{10,11... | collective-permute-start | bytes 1179656 | tf_op jit(solution)/shard_map/ppermute | solution.py:289
  54.2 7.0 %collective-permute-start.10 = (f32[8,768]{1,0:T(8,128)S(1)}, f32[8,768]{1,0:T(8,128)S(1)}, u32[]{:S(2)}, u32[]{:S(2)}) collective-permute-start(f32[8,768]{1,0:T(8,128)S(1)} %get-tuple-element.55.refs_3_), channel_id=1, source_target_pairs={{0,4},{1,5},{2,6},{3,7},{4,8},{5,9},{6,10},{7,11},{8,12},{9,13},{1... | collective-permute-start | bytes 73736 | tf_op jit(solution)/shard_map/ppermute | solution.py:289
  54.3 16.1 %collective-permute-start.14 = (bf16[192,1024]{1,0:T(8,128)(2,1)S(1)}, bf16[192,1024]{1,0:T(8,128)(2,1)S(1)}, u32[]{:S(2)}, u32[]{:S(2)}) collective-permute-start(bf16[192,1024]{1,0:T(8,128)(2,1)S(1)} %add_convert_fusion.3), channel_id=1, source_target_pairs={{0,4},{1,5},{2,6},{3,7},{4,8},{5,9},{6,10},{7,11},{8,12},{9,13},{1... | collective-permute-start | bytes 1179656 | tf_op jit(solution)/shard_map/ppermute | solution.py:289
  69.1 2.1 %collective-permute-start.12 = (bf16[192,1024]{1,0:T(8,128)(2,1)S(1)}, bf16[192,1024]{1,0:T(8,128)(2,1)S(1)}, u32[]{:S(2)}, u32[]{:S(2)}) collective-permute-start(bf16[192,1024]{1,0:T(8,128)(2,1)S(1)} %get-tuple-element.63), channel_id=1, source_target_pairs={{0,1},{1,0},{2,3},{3,2},{4,5},{5,4},{6,7},{7,6},{8,9},{9,8},{10,11... | collective-permute-start | bytes 1179656 | tf_op jit(solution)/shard_map/ppermute | solution.py:289
  69.8 1.9 %collective-permute-start.15 = (bf16[192,1024]{1,0:T(8,128)(2,1)S(1)}, bf16[192,1024]{1,0:T(8,128)(2,1)S(1)}, u32[]{:S(2)}, u32[]{:S(2)}) collective-permute-start(bf16[192,1024]{1,0:T(8,128)(2,1)S(1)} %get-tuple-element.67), channel_id=1, source_target_pairs={{0,1},{1,0},{2,3},{3,2},{4,5},{5,4},{6,7},{7,6},{8,9},{9,8},{10,11... | collective-permute-start | bytes 1179656 | tf_op jit(solution)/shard_map/ppermute | solution.py:289
  69.9 9.3 %collective-permute-start.11 = (bf16[192,1024]{1,0:T(8,128)(2,1)S(1)}, bf16[192,1024]{1,0:T(8,128)(2,1)S(1)}, u32[]{:S(2)}, u32[]{:S(2)}) collective-permute-start(bf16[192,1024]{1,0:T(8,128)(2,1)S(1)} %get-tuple-element.57), channel_id=1, source_target_pairs={{0,1},{1,0},{2,3},{3,2},{4,5},{5,4},{6,7},{7,6},{8,9},{9,8},{10,11... | collective-permute-start | bytes 1179656 | tf_op jit(solution)/shard_map/ppermute | solution.py:289
  71.3 14.7 %collective-permute-start.13 = (bf16[192,1024]{1,0:T(8,128)(2,1)S(1)}, bf16[192,1024]{1,0:T(8,128)(2,1)S(1)}, u32[]{:S(2)}, u32[]{:S(2)}) collective-permute-start(bf16[192,1024]{1,0:T(8,128)(2,1)S(1)} %add_convert_fusion.2), channel_id=1, source_target_pairs={{0,4},{1,5},{2,6},{3,7},{4,8},{5,9},{6,10},{7,11},{8,12},{9,13},{1... | collective-permute-start | bytes 1179656 | tf_op jit(solution)/shard_map/ppermute | solution.py:289
  71.9 14.0 %collective-permute-start.16 = (bf16[192,1024]{1,0:T(8,128)(2,1)S(1)}, bf16[192,1024]{1,0:T(8,128)(2,1)S(1)}, u32[]{:S(2)}, u32[]{:S(2)}) collective-permute-start(bf16[192,1024]{1,0:T(8,128)(2,1)S(1)} %add_convert_fusion.1), channel_id=1, source_target_pairs={{0,2},{1,3},{2,0},{3,1},{4,6},{5,7},{6,4},{7,5},{8,10},{9,11},{10,... | collective-permute-start | bytes 1179656 | tf_op jit(solution)/shard_map/ppermute | solution.py:289

commit v9 on v8

--- a/solution.py
+++ b/solution.py
@@ -127,21 +127,19 @@
         ref[16:24, :] = jnp.broadcast_to(coef, ids.shape)
 
 
-def merge_stats(stat, cross, core, both):
-    half = stat.shape[1] // 2
-    quarter = half // 2
-
-    def turned(x):
-        return jnp.concatenate(
-            [pltpu.roll(x[:, :half], quarter, 1), pltpu.roll(x[:, half:], quarter, 1)], axis=1
-        )
-
-    def crossed(x):
-        return jnp.concatenate([x[:, half:], x[:, :half]], axis=1)
-
-    parts = (stat, turned(core), crossed(cross), crossed(turned(both)))
-    top = functools.reduce(jnp.maximum, [part[0:1] for part in parts])
-    return top, sum(part[1:2] * jnp.exp2(part[0:1] - top) for part in parts)
+def merge_stats(ref, came, out_ref):
+    top = jnp.maximum(ref[0:1, :], came[0:1])
+    out_ref[1:2, :] = ref[1:2, :] * jnp.exp2(ref[0:1, :] - top) + came[1:2] * jnp.exp2(
+        came[0:1] - top
+    )
+    out_ref[0:1, :] = top
+
+
+def chip_stats_kernel(stat_ref, core_ref, out_ref):
+    half = core_ref.shape[1] // 2
+    core = core_ref[...]
+    turned = [pltpu.roll(core[:, at : at + half], half // 2, 1) for at in (0, half)]
+    merge_stats(stat_ref, jnp.concatenate(turned, axis=1), out_ref)
 
 
 def fill_grads(block, count, exp_ref, grad_ref, factor, ids, weights):
@@ -206,11 +204,13 @@
                 other_ref[:, cols] = part[quarter:].astype(jnp.bfloat16)
 
 
-def first_grad_kernel(p_ref, exp_ref, pack_ref, stat_ref, cross_ref, core_ref, both_ref, *outs):
+def first_grad_kernel(p_ref, exp_ref, pack_ref, stat_ref, chip_ref, cross_ref, *outs):
     *outs, whole_ref, total_ref = outs
-    top, total = merge_stats(stat_ref[...], cross_ref[...], core_ref[...], both_ref[...])
-    whole_ref[0:1, :] = top
-    whole_ref[1:2, :] = total
+    half = cross_ref.shape[1] // 2
+    cross = cross_ref[...]
+    merge_stats(
+        chip_ref, jnp.concatenate([cross[:, half:], cross[:, :half]], axis=1), whole_ref
+    )
     grads_of(1, exp_ref, pack_ref, p_ref, stat_ref, whole_ref, *outs, total_ref)
 
 
@@ -339,7 +339,10 @@
         1, [b_mine, b_other, passages, stat_a, stat_before], "next_scores_b"
     )
 
-    cross, core, both = (move(stat_next, across(turn)) for turn in (2, 1, 3))
+    (stat_chip,) = call(
+        chip_stats_kernel, [stat], [stat_next, move(stat_next, across(1))], name="chip_stats"
+    )
+    cross = move(stat_chip, across(2))
 
     def grads(kernel, ins, count, more, name, aliases=None):
         return call(
@@ -353,7 +356,7 @@
         )
 
     g_next, nb_mine, nb_other, whole_next = grads(
-        first_grad_kernel, [exp_b, pack_next, stat_next, cross, core, both], 1, [stat],
+        first_grad_kernel, [exp_b, pack_next, stat_next, stat_chip, cross], 1, [stat],
         "next_grad_b",
     )
     nb_in = move(nb_other, across(1))
@@ -376,6 +379,7 @@
     ob_mine, nb_came = lax.optimization_barrier((ob_mine, nb_came))
     ob = (ob_mine.astype(f32) + ob_in.astype(f32) + nb_came.astype(f32)).astype(bf16)
     came_across = move(ob, across(2))
+    ob, na_in = lax.optimization_barrier((ob, na_in))
     sent = (na_mine.astype(f32) + na_in.astype(f32)).astype(bf16)
     came_along = move(sent, along(1))
     (passage_grad,) = call(

time: 86.1 us -> 86.7 us (level); the launches traced: 87 us -> 85.3 us
  Pallas kernels: 32.5 us -> 29.4 us
  starting transfers between devices: 32.6 us -> 35.6 us
  waiting for transfers between devices: 18.2 us -> 16.6 us
    pallas_call x7 -> x8, Pallas kernels: 28.8 us -> 25.8 us  [call(): pl.pallas_call(kernel, out_shape=tuple(outs), input_output_aliases=aliase...]
    ppermute x17 -> x16, starting transfers between devices: 32.6 us -> 35.6 us  [move(): return lax.ppermute(x, AXES, pairs)]
    ppermute x17 -> x16, waiting for transfers between devices: 18.2 us -> 16.6 us  [move(): return lax.ppermute(x, AXES, pairs)]
  transfers between devices with their start and end apart: 17 -> 16, of which waited for: 8 -> 7; matrix products, arithmetic and copies ran while one was open for 0% -> 0% of each run, Pallas kernels for 32% -> 29%
where the time goes in v9:
time: 86.7 us; the launch traced here: 85.3 us
  starting transfers between devices  35.6 us (41%)
  Pallas kernels  29.4 us (34%)
  waiting for transfers between devices  16.6 us (19%)
  local copies, waits for them, and re-layouts  1.48 us (2%)
  other arithmetic  1.47 us (2%)
    ppermute x16, starting transfers between devices, move(): return lax.ppermute(x, AXES, pairs)  35.6 us
    pallas_call x8, Pallas kernels, call(): pl.pallas_call(kernel, out_shape=tuple(outs), input_output_aliases=aliase...  25.8 us
    ppermute x16, waiting for transfers between devices, move(): return lax.ppermute(x, AXES, pairs)  16.6 us
    pallas_call x2, Pallas kernels, take(): pl.pallas_call(functools.partial(take_kernel, slot), out_shape=piece, in_...  3.66 us
  transfers between devices with their start and end apart: 16, of which 7 were waited for; matrix products, arithmetic and copies ran while one was open for 0% of the time, Pallas kernels for 29%

profile of v9, /device:TPU:1, one launch (start us, length us, event | category | flops | bytes accessed | tf_op | source)
XLA Modules:
  0.0 85.3 jit_solution(900309920459925465)
XLA Ops:
  0.6 0.0 copy-start.3
  0.6 0.0 copy-start
  0.6 1.9 %take_a.1 = bf16[192,1024]{1,0:T(8,128)(2,1)} custom-call(bf16[768,1024]{1,0:T(8,128)(2,1)} %q_ref.3), custom_call_target="tpu_custom_call" | custom-call | tf_op jit(solution)/shard_map/take_a/pallas_call | solution.py:297
  2.6 9.9 %collective-permute-start = (bf16[192,1024]{1,0:T(8,128)(2,1)}, bf16[192,1024]{1,0:T(8,128)(2,1)S(1)}, u32[]{:S(2)}, u32[]{:S(2)}) collective-permute-start(bf16[192,1024]{1,0:T(8,128)(2,1)} %take_a.1), channel_id=1, source_target_pairs={{0,252},{1,253},{2,254},{3,255},{4,0},{5,1},{6,2},{7,3},{8,4},{9,5... | collective-permute-start | bytes 1179656 | tf_op jit(solution)/shard_map/ppermute | solution.py:289
  12.4 1.7 %take_b.1 = bf16[192,1024]{1,0:T(8,128)(2,1)} custom-call(bf16[768,1024]{1,0:T(8,128)(2,1)} %q_ref.3), custom_call_target="tpu_custom_call" | custom-call | tf_op jit(solution)/shard_map/take_b/pallas_call | solution.py:297
  14.2 0.5 collective-permute-start.1
  14.7 0.0 copy-done.3
  14.7 0.0 copy-done
  14.7 0.0 copy-start.1
  14.7 0.7 copy-done.1
  15.5 0.0 copy-start.2
  15.5 0.7 copy-done.2
  16.2 5.2 %own_scores.1 = (f32[1536,768]{1,0:T(8,128)S(1)}, f32[8,768]{1,0:T(8,128)S(1)}, f32[24,768]{1,0:T(8,128)S(1)}, f32[24,768]{1,0:T(8,128)S(1)}, bf16[768,1024]{1,0:T(8,128)(2,1)S(1)}) custom-call(bf16[768,1024]{1,0:T(8,128)(2,1)} %q_ref.3, bf16[1536,1024]{1,0:T(8,128)(2,1)S(1)} %copy-done, s32[8,768]{1,0:T(8,128)S(1)} %copy-done.1, f32[8,768]{1,0:T(8,128)S(1)} %copy-done.2, ...), custom_call_target="tpu_custom_call" | custom-call | flops 2415919104 | bytes 11234304 | tf_op jit(solution)/shard_map/own_scores/pallas_call | solution.py:249
  21.4 0.0 collective-permute-done.mine_ref
  21.4 1.8 %collective-permute-start.4 = (bf16[192,1024]{1,0:T(8,128)(2,1)S(1)}, bf16[192,1024]{1,0:T(8,128)(2,1)S(1)}, u32[]{:S(2)}, u32[]{:S(2)}) collective-permute-start(bf16[192,1024]{1,0:T(8,128)(2,1)S(1)} %collective-permute-done.mine_ref), channel_id=1, source_target_pairs={{0,1},{1,0},{2,3},{3,2},{4,5},{5,4},{6,7},{7,6},{8,9},{9,8},{10,11... | collective-permute-start | bytes 1179656 | tf_op jit(solution)/shard_map/ppermute | solution.py:289
  23.2 6.3 %collective-permute-start.2 = (f32[8,768]{1,0:T(8,128)S(1)}, f32[8,768]{1,0:T(8,128)S(1)}, u32[]{:S(2)}, u32[]{:S(2)}) collective-permute-start(f32[8,768]{1,0:T(8,128)S(1)} %get-tuple-element.42.refs_2_), channel_id=1, source_target_pairs={{0,252},{1,253},{2,254},{3,255},{4,0},{5,1},{6,2},{7,3},{8,4},{9,5... | collective-permute-start | bytes 73736 | tf_op jit(solution)/shard_map/ppermute | solution.py:289
  29.5 0.9 %collective-permute-done.2.refs_1_ = f32[8,768]{1,0:T(8,128)S(1)} collective-permute-done((f32[8,768]{1,0:T(8,128)S(1)}, f32[8,768]{1,0:T(8,128)S(1)}, u32[]{:S(2)}, u32[]{:S(2)}) %collective-permute-start.2) | collective-permute-done | bytes 24608 | tf_op jit(solution)/shard_map/ppermute | solution.py:289
  30.5 0.0 collective-permute-done.1.mine_ref
  30.5 0.9 %collective-permute-start.3 = (bf16[192,1024]{1,0:T(8,128)(2,1)S(1)}, bf16[192,1024]{1,0:T(8,128)(2,1)S(1)}, u32[]{:S(2)}, u32[]{:S(2)}) collective-permute-start(bf16[192,1024]{1,0:T(8,128)(2,1)S(1)} %collective-permute-done.1.mine_ref), channel_id=1, source_target_pairs={{0,1},{1,0},{2,3},{3,2},{4,5},{5,4},{6,7},{7,6},{8,9},{9,8},{10,11... | collective-permute-start | bytes 1179656 | tf_op jit(solution)/shard_map/ppermute | solution.py:289
  31.3 6.2 %collective-permute-start.5 = (f32[24,768]{1,0:T(8,128)S(1)}, f32[24,768]{1,0:T(8,128)S(1)}, u32[]{:S(2)}, u32[]{:S(2)}) collective-permute-start(f32[24,768]{1,0:T(8,128)S(1)} %get-tuple-element.50), channel_id=1, source_target_pairs={{0,252},{1,253},{2,254},{3,255},{4,0},{5,1},{6,2},{7,3},{8,4},{9,5... | collective-permute-start | bytes 221192 | tf_op jit(solution)/shard_map/ppermute | solution.py:289
  37.6 0.0 collective-permute-done.4.other_ref
  37.6 1.9 %next_scores_a.1 = (f32[1536,384]{1,0:T(8,128)S(1)}, f32[8,768]{1,0:T(8,128)S(1)}, bf16[384,1024]{1,0:T(8,128)(2,1)S(1)}) custom-call(bf16[192,1024]{1,0:T(8,128)(2,1)S(1)} %collective-permute-done.mine_ref, bf16[192,1024]{1,0:T(8,128)(2,1)S(1)} %collective-permute-done.4.other_ref, bf16[1536,1024]{1,0:T(8,128)(2,1)S(1)} %copy-done), custom_call_target="tpu_custom_call" | custom-call | flops 1207959552 | bytes 7102464 | tf_op jit(solution)/shard_map/next_scores_a/pallas_call | solution.py:249
  39.5 0.0 collective-permute-done.3.other_ref
  39.5 2.0 %next_scores_b.1 = (f32[1536,384]{1,0:T(8,128)S(1)}, f32[8,768]{1,0:T(8,128)S(1)}, bf16[384,1024]{1,0:T(8,128)(2,1)S(1)}) custom-call(bf16[192,1024]{1,0:T(8,128)(2,1)S(1)} %collective-permute-done.1.mine_ref, bf16[192,1024]{1,0:T(8,128)(2,1)S(1)} %collective-permute-done.3.other_ref, bf16[1536,1024]{1,0:T(8,128)(2,1)S(1)} %copy-done, ...), custom_call_target="tpu_custom_call" | custom-call | flops 1207959552 | bytes 7151616 | tf_op jit(solution)/shard_map/next_scores_b/pallas_call | solution.py:249
  41.5 0.4 collective-permute-start.6
  41.9 0.9 %collective-permute-done.6.core_ref = f32[8,768]{1,0:T(8,128)S(1)} collective-permute-done((f32[8,768]{1,0:T(8,128)S(1)}, f32[8,768]{1,0:T(8,128)S(1)}, u32[]{:S(2)}, u32[]{:S(2)}) %collective-permute-start.6) | collective-permute-done | bytes 24608 | tf_op jit(solution)/shard_map/ppermute | solution.py:289
  42.8 0.1 chip_stats.1.chip_ref
  42.9 2.7 %collective-permute-start.7 = (f32[8,768]{1,0:T(8,128)S(1)}, f32[8,768]{1,0:T(8,128)S(1)}, u32[]{:S(2)}, u32[]{:S(2)}) collective-permute-start(f32[8,768]{1,0:T(8,128)S(1)} %chip_stats.1.chip_ref), channel_id=1, source_target_pairs={{0,2},{1,3},{2,0},{3,1},{4,6},{5,7},{6,4},{7,5},{8,10},{9,11},{10,... | collective-permute-start | bytes 73736 | tf_op jit(solution)/shard_map/ppermute | solution.py:289
  45.6 0.0 collective-permute-done.5.pack_ref.refs_1_
  45.6 1.7 %collective-permute-done.7.cross_ref = f32[8,768]{1,0:T(8,128)S(1)} collective-permute-done((f32[8,768]{1,0:T(8,128)S(1)}, f32[8,768]{1,0:T(8,128)S(1)}, u32[]{:S(2)}, u32[]{:S(2)}) %collective-permute-start.7) | collective-permute-done | bytes 24608 | tf_op jit(solution)/shard_map/ppermute | solution.py:289
  47.3 2.5 %next_grad_b.1 = (bf16[1536,768]{1,0:T(8,128)(2,1)S(1)}, bf16[192,1024]{1,0:T(8,128)(2,1)S(1)}, bf16[192,1024]{1,0:T(8,128)(2,1)S(1)}, f32[8,768]{1,0:T(8,128)S(1)}) custom-call(bf16[1536,1024]{1,0:T(8,128)(2,1)S(1)} %copy-done, f32[1536,384]{1,0:T(8,128)S(1)} %get-tuple-element.49.exp_ref, f32[24,768]{1,0:T(8,128)S(1)} %collective-permute-done.5.pack_ref.refs_1_, ...), custom_call_target="tpu_custom_call" | custom-call | flops 1207959552 | bytes 8822784 | tf_op jit(solution)/shard_map/next_grad_b/pallas_call | solution.py:249
  49.8 1.5 %collective-permute-start.8 = (bf16[192,1024]{1,0:T(8,128)(2,1)S(1)}, bf16[192,1024]{1,0:T(8,128)(2,1)S(1)}, u32[]{:S(2)}, u32[]{:S(2)}) collective-permute-start(bf16[192,1024]{1,0:T(8,128)(2,1)S(1)} %get-tuple-element.53), channel_id=1, source_target_pairs={{0,1},{1,0},{2,3},{3,2},{4,5},{5,4},{6,7},{7,6},{8,9},{9,8},{10,11... | collective-permute-start | bytes 1179656 | tf_op jit(solution)/shard_map/ppermute | solution.py:289
  51.3 1.3 %collective-permute-done.8 = bf16[192,1024]{1,0:T(8,128)(2,1)S(1)} collective-permute-done((bf16[192,1024]{1,0:T(8,128)(2,1)S(1)}, bf16[192,1024]{1,0:T(8,128)(2,1)S(1)}, u32[]{:S(2)}, u32[]{:S(2)}) %collective-permute-start.8) | collective-permute-done | bytes 393248 | tf_op jit(solution)/shard_map/ppermute | solution.py:289
  52.7 0.1 add_convert_fusion.3
  52.8 0.1 collective-permute-start.9
  52.9 0.1 collective-permute-start.11
  53.0 2.5 %next_grad_a.1 = (bf16[1536,768]{1,0:T(8,128)(2,1)S(1)}, bf16[192,1024]{1,0:T(8,128)(2,1)S(1)}, bf16[192,1024]{1,0:T(8,128)(2,1)S(1)}) custom-call(bf16[1536,1024]{1,0:T(8,128)(2,1)S(1)} %copy-done, f32[1536,384]{1,0:T(8,128)S(1)} %get-tuple-element.59.refs_0_, ...), custom_call_target="tpu_custom_call", output_to_operand_aliasing={{0}: (5, {})} | custom-call | flops 1207959552 | bytes 11132928 | tf_op jit(solution)/shard_map/next_grad_a/pallas_call | solution.py:249
  55.5 4.3 %collective-permute-done.9.refs_3_ = f32[8,768]{1,0:T(8,128)S(1)} collective-permute-done((f32[8,768]{1,0:T(8,128)S(1)}, f32[8,768]{1,0:T(8,128)S(1)}, u32[]{:S(2)}, u32[]{:S(2)}) %collective-permute-start.9) | collective-permute-done | bytes 24608 | tf_op jit(solution)/shard_map/ppermute | solution.py:289
  59.8 4.8 %own_grad.1 = (bf16[1536,768]{1,0:T(8,128)(2,1)S(1)}, bf16[192,1024]{1,0:T(8,128)(2,1)S(1)}, bf16[192,1024]{1,0:T(8,128)(2,1)S(1)}, bf16[192,1024]{1,0:T(8,128)(2,1)S(1)}, bf16[192,1024]{1,0:T(8,128)(2,1)S(1)}) custom-call(bf16[1536,1024]{1,0:T(8,128)(2,1)S(1)} %copy-done, f32[1536,768]{1,0:T(8,128)S(1)} %get-tuple-element.39.refs_0_, ...), custom_call_target="tpu_custom_call" | custom-call | flops 2415919104 | bytes 11919360 | tf_op jit(solution)/shard_map/own_grad/pallas_call | solution.py:249
  64.6 2.0 %collective-permute-start.12 = (bf16[192,1024]{1,0:T(8,128)(2,1)S(1)}, bf16[192,1024]{1,0:T(8,128)(2,1)S(1)}, u32[]{:S(2)}, u32[]{:S(2)}) collective-permute-start(bf16[192,1024]{1,0:T(8,128)(2,1)S(1)} %get-tuple-element.67), channel_id=1, source_target_pairs={{0,1},{1,0},{2,3},{3,2},{4,5},{5,4},{6,7},{7,6},{8,9},{9,8},{10,11... | collective-permute-start | bytes 1179656 | tf_op jit(solution)/shard_map/ppermute | solution.py:289
  66.6 0.1 collective-permute-start.13
  66.7 0.4 collective-permute-start.10
  67.1 0.9 %collective-permute-done.11 = bf16[192,1024]{1,0:T(8,128)(2,1)S(1)} collective-permute-done((bf16[192,1024]{1,0:T(8,128)(2,1)S(1)}, bf16[192,1024]{1,0:T(8,128)(2,1)S(1)}, u32[]{:S(2)}, u32[]{:S(2)}) %collective-permute-start.11) | collective-permute-done | bytes 393248 | tf_op jit(solution)/shard_map/ppermute | solution.py:289
  68.0 0.0 collective-permute-done.12
  68.0 0.2 add_convert_fusion.2
  68.2 2.6 %collective-permute-start.15 = (bf16[192,1024]{1,0:T(8,128)(2,1)S(1)}, bf16[192,1024]{1,0:T(8,128)(2,1)S(1)}, u32[]{:S(2)}, u32[]{:S(2)}) collective-permute-start(bf16[192,1024]{1,0:T(8,128)(2,1)S(1)} %add_convert_fusion.2), channel_id=1, source_target_pairs={{0,2},{1,3},{2,0},{3,1},{4,6},{5,7},{6,4},{7,5},{8,10},{9,11},{10,... | collective-permute-start | bytes 1179656 | tf_op jit(solution)/shard_map/ppermute | solution.py:289
  70.8 0.0 collective-permute-done.13
  70.8 0.1 add_convert_fusion.1
  70.9 0.1 collective-permute-start.14
  71.0 6.8 %passage_grad.1 = bf16[1536,1024]{1,0:T(8,128)(2,1)} custom-call(bf16[1536,768]{1,0:T(8,128)(2,1)S(1)} %get-tuple-element.71.own_grad_ref, bf16[1536,768]{1,0:T(8,128)(2,1)S(1)} %get-tuple-element.72.next_grad_ref, bf16[768,1024]{1,0:T(8,128)(2,1)S(1)} %get-tuple-element.73.own_ref, bf16[384,1024]{1,0:T(8,128)(2,1)S(1)} %get-tuple-element.74.a_ref, ...), custom_call_target="tpu_custom_call" | custom-call | flops 4831838208 | bytes 11010048 | tf_op jit(solution)/shard_map/passage_grad/pallas_call | solution.py:249
  77.8 0.0 collective-permute-done.10
  77.8 6.5 %collective-permute-done.14 = bf16[192,1024]{1,0:T(8,128)(2,1)S(1)} collective-permute-done((bf16[192,1024]{1,0:T(8,128)(2,1)S(1)}, bf16[192,1024]{1,0:T(8,128)(2,1)S(1)}, u32[]{:S(2)}, u32[]{:S(2)}) %collective-permute-start.14) | collective-permute-done | bytes 393248 | tf_op jit(solution)/shard_map/ppermute | solution.py:289
  84.3 0.0 collective-permute-done.15
  84.3 1.0 %add_convert_fusion = bf16[192,1024]{1,0:T(8,128)(2,1)} fusion(bf16[192,1024]{1,0:T(8,128)(2,1)S(1)} %collective-permute-done.15, bf16[192,1024]{1,0:T(8,128)(2,1)S(1)} %collective-permute-done.14, bf16[192,1024]{1,0:T(8,128)(2,1)S(1)} %collective-permute-done.10, bf16[192,1024]{1,0:T(8,128)(2,1)S(1)} %get-tuple-element.57), kind=kLoop, calls=%fused_computation | loop fusion | flops 1572864 | bytes 1966080 | tf_op jit(solution)/shard_map/convert_element_type | solution.py:398
  (1 shorter events, 0.0 us)
Async XLA Ops:
  0.6 14.1 %copy-start.3 = (f32[768]{0:T(1024)S(1)}, f32[768]{0:T(1024)}, u32[]{:S(2)}) copy-start(f32[768]{0:T(1024)} %param.7) | copy-start | bytes 9220
  0.6 14.1 %copy-start = (bf16[1536,1024]{1,0:T(8,128)(2,1)S(1)}, bf16[1536,1024]{1,0:T(8,128)(2,1)}, u32[]{:S(2)}) copy-start(bf16[1536,1024]{1,0:T(8,128)(2,1)} %p_ref.11) | copy-start | bytes 9437188
  2.6 18.9 %collective-permute-start = (bf16[192,1024]{1,0:T(8,128)(2,1)}, bf16[192,1024]{1,0:T(8,128)(2,1)S(1)}, u32[]{:S(2)}, u32[]{:S(2)}) collective-permute-start(bf16[192,1024]{1,0:T(8,128)(2,1)} %take_a.1), channel_id=1, source_target_pairs={{0,252},{1,253},{2,254},{3,255},{4,0},{5,1},{6,2},{7,3},{8,4},{9,5... | collective-permute-start | bytes 1179656 | tf_op jit(solution)/shard_map/ppermute | solution.py:289
  14.2 16.3 %collective-permute-start.1 = (bf16[192,1024]{1,0:T(8,128)(2,1)}, bf16[192,1024]{1,0:T(8,128)(2,1)S(1)}, u32[]{:S(2)}, u32[]{:S(2)}) collective-permute-start(bf16[192,1024]{1,0:T(8,128)(2,1)} %take_b.1), channel_id=1, source_target_pairs={{0,252},{1,253},{2,254},{3,255},{4,0},{5,1},{6,2},{7,3},{8,4},{9,5... | collective-permute-start | bytes 1179656 | tf_op jit(solution)/shard_map/ppermute | solution.py:289
  14.7 0.7 copy-start.1
  15.5 0.7 copy-start.2
  21.4 16.2 %collective-permute-start.4 = (bf16[192,1024]{1,0:T(8,128)(2,1)S(1)}, bf16[192,1024]{1,0:T(8,128)(2,1)S(1)}, u32[]{:S(2)}, u32[]{:S(2)}) collective-permute-start(bf16[192,1024]{1,0:T(8,128)(2,1)S(1)} %collective-permute-done.mine_ref), channel_id=1, source_target_pairs={{0,1},{1,0},{2,3},{3,2},{4,5},{5,4},{6,7},{7,6},{8,9},{9,8},{10,11... | collective-permute-start | bytes 1179656 | tf_op jit(solution)/shard_map/ppermute | solution.py:289
  23.2 7.3 %collective-permute-start.2 = (f32[8,768]{1,0:T(8,128)S(1)}, f32[8,768]{1,0:T(8,128)S(1)}, u32[]{:S(2)}, u32[]{:S(2)}) collective-permute-start(f32[8,768]{1,0:T(8,128)S(1)} %get-tuple-element.42.refs_2_), channel_id=1, source_target_pairs={{0,252},{1,253},{2,254},{3,255},{4,0},{5,1},{6,2},{7,3},{8,4},{9,5... | collective-permute-start | bytes 73736 | tf_op jit(solution)/shard_map/ppermute | solution.py:289
  30.5 9.1 %collective-permute-start.3 = (bf16[192,1024]{1,0:T(8,128)(2,1)S(1)}, bf16[192,1024]{1,0:T(8,128)(2,1)S(1)}, u32[]{:S(2)}, u32[]{:S(2)}) collective-permute-start(bf16[192,1024]{1,0:T(8,128)(2,1)S(1)} %collective-permute-done.1.mine_ref), channel_id=1, source_target_pairs={{0,1},{1,0},{2,3},{3,2},{4,5},{5,4},{6,7},{7,6},{8,9},{9,8},{10,11... | collective-permute-start | bytes 1179656 | tf_op jit(solution)/shard_map/ppermute | solution.py:289
  31.3 14.3 %collective-permute-start.5 = (f32[24,768]{1,0:T(8,128)S(1)}, f32[24,768]{1,0:T(8,128)S(1)}, u32[]{:S(2)}, u32[]{:S(2)}) collective-permute-start(f32[24,768]{1,0:T(8,128)S(1)} %get-tuple-element.50), channel_id=1, source_target_pairs={{0,252},{1,253},{2,254},{3,255},{4,0},{5,1},{6,2},{7,3},{8,4},{9,5... | collective-permute-start | bytes 221192 | tf_op jit(solution)/shard_map/ppermute | solution.py:289
  41.5 1.3 %collective-permute-start.6 = (f32[8,768]{1,0:T(8,128)S(1)}, f32[8,768]{1,0:T(8,128)S(1)}, u32[]{:S(2)}, u32[]{:S(2)}) collective-permute-start(f32[8,768]{1,0:T(8,128)S(1)} %get-tuple-element.51.stat_ref.refs_2_), channel_id=1, source_target_pairs={{0,1},{1,0},{2,3},{3,2},{4,5},{5,4},{6,7},{7,6},{8,9},{9,8},{10,11... | collective-permute-start | bytes 73736 | tf_op jit(solution)/shard_map/ppermute | solution.py:289
  42.9 4.4 %collective-permute-start.7 = (f32[8,768]{1,0:T(8,128)S(1)}, f32[8,768]{1,0:T(8,128)S(1)}, u32[]{:S(2)}, u32[]{:S(2)}) collective-permute-start(f32[8,768]{1,0:T(8,128)S(1)} %chip_stats.1.chip_ref), channel_id=1, source_target_pairs={{0,2},{1,3},{2,0},{3,1},{4,6},{5,7},{6,4},{7,5},{8,10},{9,11},{10,... | collective-permute-start | bytes 73736 | tf_op jit(solution)/shard_map/ppermute | solution.py:289
  49.8 2.9 %collective-permute-start.8 = (bf16[192,1024]{1,0:T(8,128)(2,1)S(1)}, bf16[192,1024]{1,0:T(8,128)(2,1)S(1)}, u32[]{:S(2)}, u32[]{:S(2)}) collective-permute-start(bf16[192,1024]{1,0:T(8,128)(2,1)S(1)} %get-tuple-element.53), channel_id=1, source_target_pairs={{0,1},{1,0},{2,3},{3,2},{4,5},{5,4},{6,7},{7,6},{8,9},{9,8},{10,11... | collective-permute-start | bytes 1179656 | tf_op jit(solution)/shard_map/ppermute | solution.py:289
  52.8 7.0 %collective-permute-start.9 = (f32[8,768]{1,0:T(8,128)S(1)}, f32[8,768]{1,0:T(8,128)S(1)}, u32[]{:S(2)}, u32[]{:S(2)}) collective-permute-start(f32[8,768]{1,0:T(8,128)S(1)} %get-tuple-element.56.refs_3_), channel_id=1, source_target_pairs={{0,4},{1,5},{2,6},{3,7},{4,8},{5,9},{6,10},{7,11},{8,12},{9,13},{1... | collective-permute-start | bytes 73736 | tf_op jit(solution)/shard_map/ppermute | solution.py:289
  52.9 15.1 %collective-permute-start.11 = (bf16[192,1024]{1,0:T(8,128)(2,1)S(1)}, bf16[192,1024]{1,0:T(8,128)(2,1)S(1)}, u32[]{:S(2)}, u32[]{:S(2)}) collective-permute-start(bf16[192,1024]{1,0:T(8,128)(2,1)S(1)} %add_convert_fusion.3), channel_id=1, source_target_pairs={{0,4},{1,5},{2,6},{3,7},{4,8},{5,9},{6,10},{7,11},{8,12},{9,13},{1... | collective-permute-start | bytes 1179656 | tf_op jit(solution)/shard_map/ppermute | solution.py:289
  64.6 3.4 %collective-permute-start.12 = (bf16[192,1024]{1,0:T(8,128)(2,1)S(1)}, bf16[192,1024]{1,0:T(8,128)(2,1)S(1)}, u32[]{:S(2)}, u32[]{:S(2)}) collective-permute-start(bf16[192,1024]{1,0:T(8,128)(2,1)S(1)} %get-tuple-element.67), channel_id=1, source_target_pairs={{0,1},{1,0},{2,3},{3,2},{4,5},{5,4},{6,7},{7,6},{8,9},{9,8},{10,11... | collective-permute-start | bytes 1179656 | tf_op jit(solution)/shard_map/ppermute | solution.py:289
  66.6 4.2 %collective-permute-start.13 = (bf16[192,1024]{1,0:T(8,128)(2,1)S(1)}, bf16[192,1024]{1,0:T(8,128)(2,1)S(1)}, u32[]{:S(2)}, u32[]{:S(2)}) collective-permute-start(bf16[192,1024]{1,0:T(8,128)(2,1)S(1)} %get-tuple-element.69), channel_id=1, source_target_pairs={{0,1},{1,0},{2,3},{3,2},{4,5},{5,4},{6,7},{7,6},{8,9},{9,8},{10,11... | collective-permute-start | bytes 1179656 | tf_op jit(solution)/shard_map/ppermute | solution.py:289
  66.7 11.1 %collective-permute-start.10 = (bf16[192,1024]{1,0:T(8,128)(2,1)S(1)}, bf16[192,1024]{1,0:T(8,128)(2,1)S(1)}, u32[]{:S(2)}, u32[]{:S(2)}) collective-permute-start(bf16[192,1024]{1,0:T(8,128)(2,1)S(1)} %get-tuple-element.58), channel_id=1, source_target_pairs={{0,1},{1,0},{2,3},{3,2},{4,5},{5,4},{6,7},{7,6},{8,9},{9,8},{10,11... | collective-permute-start | bytes 1179656 | tf_op jit(solution)/shard_map/ppermute | solution.py:289
  68.2 16.1 %collective-permute-start.15 = (bf16[192,1024]{1,0:T(8,128)(2,1)S(1)}, bf16[192,1024]{1,0:T(8,128)(2,1)S(1)}, u32[]{:S(2)}, u32[]{:S(2)}) collective-permute-start(bf16[192,1024]{1,0:T(8,128)(2,1)S(1)} %add_convert_fusion.2), channel_id=1, source_target_pairs={{0,2},{1,3},{2,0},{3,1},{4,6},{5,7},{6,4},{7,5},{8,10},{9,11},{10,... | collective-permute-start | bytes 1179656 | tf_op jit(solution)/shard_map/ppermute | solution.py:289
  70.9 13.4 %collective-permute-start.14 = (bf16[192,1024]{1,0:T(8,128)(2,1)S(1)}, bf16[192,1024]{1,0:T(8,128)(2,1)S(1)}, u32[]{:S(2)}, u32[]{:S(2)}) collective-permute-start(bf16[192,1024]{1,0:T(8,128)(2,1)S(1)} %add_convert_fusion.1), channel_id=1, source_target_pairs={{0,4},{1,5},{2,6},{3,7},{4,8},{5,9},{6,10},{7,11},{8,12},{9,13},{1... | collective-permute-start | bytes 1179656 | tf_op jit(solution)/shard_map/ppermute | solution.py:289

commit v10 on v9

--- a/solution.py
+++ b/solution.py
@@ -379,7 +379,6 @@
     ob_mine, nb_came = lax.optimization_barrier((ob_mine, nb_came))
     ob = (ob_mine.astype(f32) + ob_in.astype(f32) + nb_came.astype(f32)).astype(bf16)
     came_across = move(ob, across(2))
-    ob, na_in = lax.optimization_barrier((ob, na_in))
     sent = (na_mine.astype(f32) + na_in.astype(f32)).astype(bf16)
     came_along = move(sent, along(1))
     (passage_grad,) = call(

time: 86.7 us -> 85.8 us (0.990); the launches traced: 85.3 us -> 86.2 us
  starting transfers between devices: 35.6 us -> 37.2 us
    ppermute x16, starting transfers between devices: 35.6 us -> 37.2 us  [move(): return lax.ppermute(x, AXES, pairs)]
  transfers between devices with their start and end apart: 16 -> 16, of which waited for: 7 -> 8; matrix products, arithmetic and copies ran while one was open for 0% -> 0% of each run, Pallas kernels for 29% -> 29%
where the time goes in v10:
time: 85.8 us; the launch traced here: 86.2 us
  starting transfers between devices  37.2 us (43%)
  Pallas kernels  29.4 us (34%)
  waiting for transfers between devices  15.8 us (18%)
  local copies, waits for them, and re-layouts  1.48 us (2%)
  other arithmetic  1.46 us (2%)
    ppermute x16, starting transfers between devices, move(): return lax.ppermute(x, AXES, pairs)  37.2 us
    pallas_call x8, Pallas kernels, call(): pl.pallas_call(kernel, out_shape=tuple(outs), input_output_aliases=aliase...  25.8 us
    ppermute x16, waiting for transfers between devices, move(): return lax.ppermute(x, AXES, pairs)  15.8 us
    pallas_call x2, Pallas kernels, take(): pl.pallas_call(functools.partial(take_kernel, slot), out_shape=piece, in_...  3.66 us
  transfers between devices with their start and end apart: 16, of which 8 were waited for; matrix products, arithmetic and copies ran while one was open for 0% of the time, Pallas kernels for 29%

profile of v10, /device:TPU:1, one launch (start us, length us, event | category | flops | bytes accessed | tf_op | source)
XLA Modules:
  0.0 86.2 jit_solution(18249908415885814245)
XLA Ops:
  0.6 0.0 copy-start.3
  0.6 0.0 copy-start
  0.6 1.9 %take_a.1 = bf16[192,1024]{1,0:T(8,128)(2,1)} custom-call(bf16[768,1024]{1,0:T(8,128)(2,1)} %q_ref.3), custom_call_target="tpu_custom_call" | custom-call | tf_op jit(solution)/shard_map/take_a/pallas_call | solution.py:297
  2.6 9.9 %collective-permute-start = (bf16[192,1024]{1,0:T(8,128)(2,1)}, bf16[192,1024]{1,0:T(8,128)(2,1)S(1)}, u32[]{:S(2)}, u32[]{:S(2)}) collective-permute-start(bf16[192,1024]{1,0:T(8,128)(2,1)} %take_a.1), channel_id=1, source_target_pairs={{0,252},{1,253},{2,254},{3,255},{4,0},{5,1},{6,2},{7,3},{8,4},{9,5... | collective-permute-start | bytes 1179656 | tf_op jit(solution)/shard_map/ppermute | solution.py:289
  12.4 1.7 %take_b.1 = bf16[192,1024]{1,0:T(8,128)(2,1)} custom-call(bf16[768,1024]{1,0:T(8,128)(2,1)} %q_ref.3), custom_call_target="tpu_custom_call" | custom-call | tf_op jit(solution)/shard_map/take_b/pallas_call | solution.py:297
  14.2 0.5 collective-permute-start.1
  14.7 0.0 copy-done.3
  14.7 0.0 copy-done
  14.7 0.0 copy-start.1
  14.7 0.7 copy-done.1
  15.5 0.0 copy-start.2
  15.5 0.7 copy-done.2
  16.2 5.2 %own_scores.1 = (f32[1536,768]{1,0:T(8,128)S(1)}, f32[8,768]{1,0:T(8,128)S(1)}, f32[24,768]{1,0:T(8,128)S(1)}, f32[24,768]{1,0:T(8,128)S(1)}, bf16[768,1024]{1,0:T(8,128)(2,1)S(1)}) custom-call(bf16[768,1024]{1,0:T(8,128)(2,1)} %q_ref.3, bf16[1536,1024]{1,0:T(8,128)(2,1)S(1)} %copy-done, s32[8,768]{1,0:T(8,128)S(1)} %copy-done.1, f32[8,768]{1,0:T(8,128)S(1)} %copy-done.2, ...), custom_call_target="tpu_custom_call" | custom-call | flops 2415919104 | bytes 11234304 | tf_op jit(solution)/shard_map/own_scores/pallas_call | solution.py:249
  21.4 0.0 collective-permute-done.mine_ref
  21.4 1.8 %collective-permute-start.4 = (bf16[192,1024]{1,0:T(8,128)(2,1)S(1)}, bf16[192,1024]{1,0:T(8,128)(2,1)S(1)}, u32[]{:S(2)}, u32[]{:S(2)}) collective-permute-start(bf16[192,1024]{1,0:T(8,128)(2,1)S(1)} %collective-permute-done.mine_ref), channel_id=1, source_target_pairs={{0,1},{1,0},{2,3},{3,2},{4,5},{5,4},{6,7},{7,6},{8,9},{9,8},{10,11... | collective-permute-start | bytes 1179656 | tf_op jit(solution)/shard_map/ppermute | solution.py:289
  23.2 6.3 %collective-permute-start.2 = (f32[8,768]{1,0:T(8,128)S(1)}, f32[8,768]{1,0:T(8,128)S(1)}, u32[]{:S(2)}, u32[]{:S(2)}) collective-permute-start(f32[8,768]{1,0:T(8,128)S(1)} %get-tuple-element.41.refs_2_), channel_id=1, source_target_pairs={{0,252},{1,253},{2,254},{3,255},{4,0},{5,1},{6,2},{7,3},{8,4},{9,5... | collective-permute-start | bytes 73736 | tf_op jit(solution)/shard_map/ppermute | solution.py:289
  29.5 0.9 %collective-permute-done.2.refs_1_ = f32[8,768]{1,0:T(8,128)S(1)} collective-permute-done((f32[8,768]{1,0:T(8,128)S(1)}, f32[8,768]{1,0:T(8,128)S(1)}, u32[]{:S(2)}, u32[]{:S(2)}) %collective-permute-start.2) | collective-permute-done | bytes 24608 | tf_op jit(solution)/shard_map/ppermute | solution.py:289
  30.5 0.0 collective-permute-done.1.mine_ref
  30.5 0.9 collective-permute-start.3
  31.3 6.2 %collective-permute-start.5 = (f32[24,768]{1,0:T(8,128)S(1)}, f32[24,768]{1,0:T(8,128)S(1)}, u32[]{:S(2)}, u32[]{:S(2)}) collective-permute-start(f32[24,768]{1,0:T(8,128)S(1)} %get-tuple-element.49), channel_id=1, source_target_pairs={{0,252},{1,253},{2,254},{3,255},{4,0},{5,1},{6,2},{7,3},{8,4},{9,5... | collective-permute-start | bytes 221192 | tf_op jit(solution)/shard_map/ppermute | solution.py:289
  37.6 0.0 collective-permute-done.4.other_ref
  37.6 1.9 %next_scores_a.1 = (f32[1536,384]{1,0:T(8,128)S(1)}, f32[8,768]{1,0:T(8,128)S(1)}, bf16[384,1024]{1,0:T(8,128)(2,1)S(1)}) custom-call(bf16[192,1024]{1,0:T(8,128)(2,1)S(1)} %collective-permute-done.mine_ref, bf16[192,1024]{1,0:T(8,128)(2,1)S(1)} %collective-permute-done.4.other_ref, bf16[1536,1024]{1,0:T(8,128)(2,1)S(1)} %copy-done), custom_call_target="tpu_custom_call" | custom-call | flops 1207959552 | bytes 7102464 | tf_op jit(solution)/shard_map/next_scores_a/pallas_call | solution.py:249
  39.5 0.0 collective-permute-done.3.other_ref
  39.5 2.0 %next_scores_b.1 = (f32[1536,384]{1,0:T(8,128)S(1)}, f32[8,768]{1,0:T(8,128)S(1)}, bf16[384,1024]{1,0:T(8,128)(2,1)S(1)}) custom-call(bf16[192,1024]{1,0:T(8,128)(2,1)S(1)} %collective-permute-done.1.mine_ref, bf16[192,1024]{1,0:T(8,128)(2,1)S(1)} %collective-permute-done.3.other_ref, bf16[1536,1024]{1,0:T(8,128)(2,1)S(1)} %copy-done, ...), custom_call_target="tpu_custom_call" | custom-call | flops 1207959552 | bytes 7151616 | tf_op jit(solution)/shard_map/next_scores_b/pallas_call | solution.py:249
  41.5 0.4 collective-permute-start.6
  41.9 0.9 %collective-permute-done.6.core_ref = f32[8,768]{1,0:T(8,128)S(1)} collective-permute-done((f32[8,768]{1,0:T(8,128)S(1)}, f32[8,768]{1,0:T(8,128)S(1)}, u32[]{:S(2)}, u32[]{:S(2)}) %collective-permute-start.6) | collective-permute-done | bytes 24608 | tf_op jit(solution)/shard_map/ppermute | solution.py:289
  42.8 0.1 chip_stats.1.chip_ref
  42.9 2.7 %collective-permute-start.7 = (f32[8,768]{1,0:T(8,128)S(1)}, f32[8,768]{1,0:T(8,128)S(1)}, u32[]{:S(2)}, u32[]{:S(2)}) collective-permute-start(f32[8,768]{1,0:T(8,128)S(1)} %chip_stats.1.chip_ref), channel_id=1, source_target_pairs={{0,2},{1,3},{2,0},{3,1},{4,6},{5,7},{6,4},{7,5},{8,10},{9,11},{10,... | collective-permute-start | bytes 73736 | tf_op jit(solution)/shard_map/ppermute | solution.py:289
  45.6 0.0 collective-permute-done.5.pack_ref.refs_1_
  45.6 1.7 %collective-permute-done.7.cross_ref = f32[8,768]{1,0:T(8,128)S(1)} collective-permute-done((f32[8,768]{1,0:T(8,128)S(1)}, f32[8,768]{1,0:T(8,128)S(1)}, u32[]{:S(2)}, u32[]{:S(2)}) %collective-permute-start.7) | collective-permute-done | bytes 24608 | tf_op jit(solution)/shard_map/ppermute | solution.py:289
  47.3 2.5 %next_grad_b.1 = (bf16[1536,768]{1,0:T(8,128)(2,1)S(1)}, bf16[192,1024]{1,0:T(8,128)(2,1)S(1)}, bf16[192,1024]{1,0:T(8,128)(2,1)S(1)}, f32[8,768]{1,0:T(8,128)S(1)}) custom-call(bf16[1536,1024]{1,0:T(8,128)(2,1)S(1)} %copy-done, f32[1536,384]{1,0:T(8,128)S(1)} %get-tuple-element.48.exp_ref, f32[24,768]{1,0:T(8,128)S(1)} %collective-permute-done.5.pack_ref.refs_1_, ...), custom_call_target="tpu_custom_call" | custom-call | flops 1207959552 | bytes 8822784 | tf_op jit(solution)/shard_map/next_grad_b/pallas_call | solution.py:249
  49.9 1.5 %collective-permute-start.8 = (bf16[192,1024]{1,0:T(8,128)(2,1)S(1)}, bf16[192,1024]{1,0:T(8,128)(2,1)S(1)}, u32[]{:S(2)}, u32[]{:S(2)}) collective-permute-start(bf16[192,1024]{1,0:T(8,128)(2,1)S(1)} %get-tuple-element.52), channel_id=1, source_target_pairs={{0,1},{1,0},{2,3},{3,2},{4,5},{5,4},{6,7},{7,6},{8,9},{9,8},{10,11... | collective-permute-start | bytes 1179656 | tf_op jit(solution)/shard_map/ppermute | solution.py:289
  51.3 1.3 %collective-permute-done.8 = bf16[192,1024]{1,0:T(8,128)(2,1)S(1)} collective-permute-done((bf16[192,1024]{1,0:T(8,128)(2,1)S(1)}, bf16[192,1024]{1,0:T(8,128)(2,1)S(1)}, u32[]{:S(2)}, u32[]{:S(2)}) %collective-permute-start.8) | collective-permute-done | bytes 393248 | tf_op jit(solution)/shard_map/ppermute | solution.py:289
  52.7 0.1 add_convert_fusion.3
  52.8 0.1 collective-permute-start.9
  52.9 0.1 collective-permute-start.13
  53.0 2.5 %next_grad_a.1 = (bf16[1536,768]{1,0:T(8,128)(2,1)S(1)}, bf16[192,1024]{1,0:T(8,128)(2,1)S(1)}, bf16[192,1024]{1,0:T(8,128)(2,1)S(1)}) custom-call(bf16[1536,1024]{1,0:T(8,128)(2,1)S(1)} %copy-done, f32[1536,384]{1,0:T(8,128)S(1)} %get-tuple-element.58.refs_0_, ...), custom_call_target="tpu_custom_call", output_to_operand_aliasing={{0}: (5, {})} | custom-call | flops 1207959552 | bytes 11132928 | tf_op jit(solution)/shard_map/next_grad_a/pallas_call | solution.py:249
  55.5 4.3 %collective-permute-done.9.refs_3_ = f32[8,768]{1,0:T(8,128)S(1)} collective-permute-done((f32[8,768]{1,0:T(8,128)S(1)}, f32[8,768]{1,0:T(8,128)S(1)}, u32[]{:S(2)}, u32[]{:S(2)}) %collective-permute-start.9) | collective-permute-done | bytes 24608 | tf_op jit(solution)/shard_map/ppermute | solution.py:289
  59.8 4.8 %own_grad.1 = (bf16[1536,768]{1,0:T(8,128)(2,1)S(1)}, bf16[192,1024]{1,0:T(8,128)(2,1)S(1)}, bf16[192,1024]{1,0:T(8,128)(2,1)S(1)}, bf16[192,1024]{1,0:T(8,128)(2,1)S(1)}, bf16[192,1024]{1,0:T(8,128)(2,1)S(1)}) custom-call(bf16[1536,1024]{1,0:T(8,128)(2,1)S(1)} %copy-done, f32[1536,768]{1,0:T(8,128)S(1)} %get-tuple-element.38.refs_0_, ...), custom_call_target="tpu_custom_call" | custom-call | flops 2415919104 | bytes 11919360 | tf_op jit(solution)/shard_map/own_grad/pallas_call | solution.py:249
  64.6 4.5 %collective-permute-start.11 = (bf16[192,1024]{1,0:T(8,128)(2,1)S(1)}, bf16[192,1024]{1,0:T(8,128)(2,1)S(1)}, u32[]{:S(2)}, u32[]{:S(2)}) collective-permute-start(bf16[192,1024]{1,0:T(8,128)(2,1)S(1)} %get-tuple-element.63), channel_id=1, source_target_pairs={{0,1},{1,0},{2,3},{3,2},{4,5},{5,4},{6,7},{7,6},{8,9},{9,8},{10,11... | collective-permute-start | bytes 1179656 | tf_op jit(solution)/shard_map/ppermute | solution.py:289
  69.1 0.1 collective-permute-start.14
  69.2 0.4 collective-permute-start.10
  69.6 0.0 collective-permute-done.13
  69.6 0.8 collective-permute-done.11
  70.4 0.1 add_convert_fusion.2
  70.5 0.1 collective-permute-start.12
  70.6 0.3 collective-permute-done.14
  71.0 0.2 add_convert_fusion.1
  71.2 1.8 %collective-permute-start.15 = (bf16[192,1024]{1,0:T(8,128)(2,1)S(1)}, bf16[192,1024]{1,0:T(8,128)(2,1)S(1)}, u32[]{:S(2)}, u32[]{:S(2)}) collective-permute-start(bf16[192,1024]{1,0:T(8,128)(2,1)S(1)} %add_convert_fusion.1), channel_id=1, source_target_pairs={{0,2},{1,3},{2,0},{3,1},{4,6},{5,7},{6,4},{7,5},{8,10},{9,11},{10,... | collective-permute-start | bytes 1179656 | tf_op jit(solution)/shard_map/ppermute | solution.py:289
  73.0 6.8 %passage_grad.1 = bf16[1536,1024]{1,0:T(8,128)(2,1)} custom-call(bf16[1536,768]{1,0:T(8,128)(2,1)S(1)} %get-tuple-element.69.own_grad_ref, bf16[1536,768]{1,0:T(8,128)(2,1)S(1)} %get-tuple-element.70.next_grad_ref, bf16[768,1024]{1,0:T(8,128)(2,1)S(1)} %get-tuple-element.71.own_ref, bf16[384,1024]{1,0:T(8,128)(2,1)S(1)} %get-tuple-element.72.a_ref, ...), custom_call_target="tpu_custom_call" | custom-call | flops 4831838208 | bytes 11010048 | tf_op jit(solution)/shard_map/passage_grad/pallas_call | solution.py:249
  79.8 0.0 collective-permute-done.10
  79.8 5.4 %collective-permute-done.12 = bf16[192,1024]{1,0:T(8,128)(2,1)S(1)} collective-permute-done((bf16[192,1024]{1,0:T(8,128)(2,1)S(1)}, bf16[192,1024]{1,0:T(8,128)(2,1)S(1)}, u32[]{:S(2)}, u32[]{:S(2)}) %collective-permute-start.12) | collective-permute-done | bytes 393248 | tf_op jit(solution)/shard_map/ppermute | solution.py:289
  85.2 0.0 collective-permute-done.15
  85.2 1.0 %add_convert_fusion = bf16[192,1024]{1,0:T(8,128)(2,1)} fusion(bf16[192,1024]{1,0:T(8,128)(2,1)S(1)} %collective-permute-done.15, bf16[192,1024]{1,0:T(8,128)(2,1)S(1)} %collective-permute-done.12, bf16[192,1024]{1,0:T(8,128)(2,1)S(1)} %collective-permute-done.10, bf16[192,1024]{1,0:T(8,128)(2,1)S(1)} %get-tuple-element.56), kind=kLoop, calls=%fused_computation | loop fusion | flops 1572864 | bytes 1966080 | tf_op jit(solution)/shard_map/convert_element_type | solution.py:397
  (1 shorter events, 0.0 us)
Async XLA Ops:
  0.6 14.1 %copy-start.3 = (f32[768]{0:T(1024)S(1)}, f32[768]{0:T(1024)}, u32[]{:S(2)}) copy-start(f32[768]{0:T(1024)} %param.7) | copy-start | bytes 9220
  0.6 14.1 %copy-start = (bf16[1536,1024]{1,0:T(8,128)(2,1)S(1)}, bf16[1536,1024]{1,0:T(8,128)(2,1)}, u32[]{:S(2)}) copy-start(bf16[1536,1024]{1,0:T(8,128)(2,1)} %p_ref.11) | copy-start | bytes 9437188
  2.6 18.9 %collective-permute-start = (bf16[192,1024]{1,0:T(8,128)(2,1)}, bf16[192,1024]{1,0:T(8,128)(2,1)S(1)}, u32[]{:S(2)}, u32[]{:S(2)}) collective-permute-start(bf16[192,1024]{1,0:T(8,128)(2,1)} %take_a.1), channel_id=1, source_target_pairs={{0,252},{1,253},{2,254},{3,255},{4,0},{5,1},{6,2},{7,3},{8,4},{9,5... | collective-permute-start | bytes 1179656 | tf_op jit(solution)/shard_map/ppermute | solution.py:289
  14.2 16.3 %collective-permute-start.1 = (bf16[192,1024]{1,0:T(8,128)(2,1)}, bf16[192,1024]{1,0:T(8,128)(2,1)S(1)}, u32[]{:S(2)}, u32[]{:S(2)}) collective-permute-start(bf16[192,1024]{1,0:T(8,128)(2,1)} %take_b.1), channel_id=1, source_target_pairs={{0,252},{1,253},{2,254},{3,255},{4,0},{5,1},{6,2},{7,3},{8,4},{9,5... | collective-permute-start | bytes 1179656 | tf_op jit(solution)/shard_map/ppermute | solution.py:289
  14.7 0.7 copy-start.1
  15.5 0.7 copy-start.2
  21.4 16.2 %collective-permute-start.4 = (bf16[192,1024]{1,0:T(8,128)(2,1)S(1)}, bf16[192,1024]{1,0:T(8,128)(2,1)S(1)}, u32[]{:S(2)}, u32[]{:S(2)}) collective-permute-start(bf16[192,1024]{1,0:T(8,128)(2,1)S(1)} %collective-permute-done.mine_ref), channel_id=1, source_target_pairs={{0,1},{1,0},{2,3},{3,2},{4,5},{5,4},{6,7},{7,6},{8,9},{9,8},{10,11... | collective-permute-start | bytes 1179656 | tf_op jit(solution)/shard_map/ppermute | solution.py:289
  23.2 7.3 %collective-permute-start.2 = (f32[8,768]{1,0:T(8,128)S(1)}, f32[8,768]{1,0:T(8,128)S(1)}, u32[]{:S(2)}, u32[]{:S(2)}) collective-permute-start(f32[8,768]{1,0:T(8,128)S(1)} %get-tuple-element.41.refs_2_), channel_id=1, source_target_pairs={{0,252},{1,253},{2,254},{3,255},{4,0},{5,1},{6,2},{7,3},{8,4},{9,5... | collective-permute-start | bytes 73736 | tf_op jit(solution)/shard_map/ppermute | solution.py:289
  30.5 9.1 %collective-permute-start.3 = (bf16[192,1024]{1,0:T(8,128)(2,1)S(1)}, bf16[192,1024]{1,0:T(8,128)(2,1)S(1)}, u32[]{:S(2)}, u32[]{:S(2)}) collective-permute-start(bf16[192,1024]{1,0:T(8,128)(2,1)S(1)} %collective-permute-done.1.mine_ref), channel_id=1, source_target_pairs={{0,1},{1,0},{2,3},{3,2},{4,5},{5,4},{6,7},{7,6},{8,9},{9,8},{10,11... | collective-permute-start | bytes 1179656 | tf_op jit(solution)/shard_map/ppermute | solution.py:289
  31.3 14.3 %collective-permute-start.5 = (f32[24,768]{1,0:T(8,128)S(1)}, f32[24,768]{1,0:T(8,128)S(1)}, u32[]{:S(2)}, u32[]{:S(2)}) collective-permute-start(f32[24,768]{1,0:T(8,128)S(1)} %get-tuple-element.49), channel_id=1, source_target_pairs={{0,252},{1,253},{2,254},{3,255},{4,0},{5,1},{6,2},{7,3},{8,4},{9,5... | collective-permute-start | bytes 221192 | tf_op jit(solution)/shard_map/ppermute | solution.py:289
  41.5 1.3 %collective-permute-start.6 = (f32[8,768]{1,0:T(8,128)S(1)}, f32[8,768]{1,0:T(8,128)S(1)}, u32[]{:S(2)}, u32[]{:S(2)}) collective-permute-start(f32[8,768]{1,0:T(8,128)S(1)} %get-tuple-element.50.stat_ref.refs_2_), channel_id=1, source_target_pairs={{0,1},{1,0},{2,3},{3,2},{4,5},{5,4},{6,7},{7,6},{8,9},{9,8},{10,11... | collective-permute-start | bytes 73736 | tf_op jit(solution)/shard_map/ppermute | solution.py:289
  42.9 4.4 %collective-permute-start.7 = (f32[8,768]{1,0:T(8,128)S(1)}, f32[8,768]{1,0:T(8,128)S(1)}, u32[]{:S(2)}, u32[]{:S(2)}) collective-permute-start(f32[8,768]{1,0:T(8,128)S(1)} %chip_stats.1.chip_ref), channel_id=1, source_target_pairs={{0,2},{1,3},{2,0},{3,1},{4,6},{5,7},{6,4},{7,5},{8,10},{9,11},{10,... | collective-permute-start | bytes 73736 | tf_op jit(solution)/shard_map/ppermute | solution.py:289
  49.9 2.8 %collective-permute-start.8 = (bf16[192,1024]{1,0:T(8,128)(2,1)S(1)}, bf16[192,1024]{1,0:T(8,128)(2,1)S(1)}, u32[]{:S(2)}, u32[]{:S(2)}) collective-permute-start(bf16[192,1024]{1,0:T(8,128)(2,1)S(1)} %get-tuple-element.52), channel_id=1, source_target_pairs={{0,1},{1,0},{2,3},{3,2},{4,5},{5,4},{6,7},{7,6},{8,9},{9,8},{10,11... | collective-permute-start | bytes 1179656 | tf_op jit(solution)/shard_map/ppermute | solution.py:289
  52.8 7.0 %collective-permute-start.9 = (f32[8,768]{1,0:T(8,128)S(1)}, f32[8,768]{1,0:T(8,128)S(1)}, u32[]{:S(2)}, u32[]{:S(2)}) collective-permute-start(f32[8,768]{1,0:T(8,128)S(1)} %get-tuple-element.55.refs_3_), channel_id=1, source_target_pairs={{0,4},{1,5},{2,6},{3,7},{4,8},{5,9},{6,10},{7,11},{8,12},{9,13},{1... | collective-permute-start | bytes 73736 | tf_op jit(solution)/shard_map/ppermute | solution.py:289
  52.9 16.7 %collective-permute-start.13 = (bf16[192,1024]{1,0:T(8,128)(2,1)S(1)}, bf16[192,1024]{1,0:T(8,128)(2,1)S(1)}, u32[]{:S(2)}, u32[]{:S(2)}) collective-permute-start(bf16[192,1024]{1,0:T(8,128)(2,1)S(1)} %add_convert_fusion.3), channel_id=1, source_target_pairs={{0,4},{1,5},{2,6},{3,7},{4,8},{5,9},{6,10},{7,11},{8,12},{9,13},{1... | collective-permute-start | bytes 1179656 | tf_op jit(solution)/shard_map/ppermute | solution.py:289
  64.6 5.8 %collective-permute-start.11 = (bf16[192,1024]{1,0:T(8,128)(2,1)S(1)}, bf16[192,1024]{1,0:T(8,128)(2,1)S(1)}, u32[]{:S(2)}, u32[]{:S(2)}) collective-permute-start(bf16[192,1024]{1,0:T(8,128)(2,1)S(1)} %get-tuple-element.63), channel_id=1, source_target_pairs={{0,1},{1,0},{2,3},{3,2},{4,5},{5,4},{6,7},{7,6},{8,9},{9,8},{10,11... | collective-permute-start | bytes 1179656 | tf_op jit(solution)/shard_map/ppermute | solution.py:289
  69.1 1.9 %collective-permute-start.14 = (bf16[192,1024]{1,0:T(8,128)(2,1)S(1)}, bf16[192,1024]{1,0:T(8,128)(2,1)S(1)}, u32[]{:S(2)}, u32[]{:S(2)}) collective-permute-start(bf16[192,1024]{1,0:T(8,128)(2,1)S(1)} %get-tuple-element.67), channel_id=1, source_target_pairs={{0,1},{1,0},{2,3},{3,2},{4,5},{5,4},{6,7},{7,6},{8,9},{9,8},{10,11... | collective-permute-start | bytes 1179656 | tf_op jit(solution)/shard_map/ppermute | solution.py:289
  69.2 10.7 %collective-permute-start.10 = (bf16[192,1024]{1,0:T(8,128)(2,1)S(1)}, bf16[192,1024]{1,0:T(8,128)(2,1)S(1)}, u32[]{:S(2)}, u32[]{:S(2)}) collective-permute-start(bf16[192,1024]{1,0:T(8,128)(2,1)S(1)} %get-tuple-element.57), channel_id=1, source_target_pairs={{0,1},{1,0},{2,3},{3,2},{4,5},{5,4},{6,7},{7,6},{8,9},{9,8},{10,11... | collective-permute-start | bytes 1179656 | tf_op jit(solution)/shard_map/ppermute | solution.py:289
  70.5 14.7 %collective-permute-start.12 = (bf16[192,1024]{1,0:T(8,128)(2,1)S(1)}, bf16[192,1024]{1,0:T(8,128)(2,1)S(1)}, u32[]{:S(2)}, u32[]{:S(2)}) collective-permute-start(bf16[192,1024]{1,0:T(8,128)(2,1)S(1)} %add_convert_fusion.2), channel_id=1, source_target_pairs={{0,4},{1,5},{2,6},{3,7},{4,8},{5,9},{6,10},{7,11},{8,12},{9,13},{1... | collective-permute-start | bytes 1179656 | tf_op jit(solution)/shard_map/ppermute | solution.py:289
  71.2 14.0 %collective-permute-start.15 = (bf16[192,1024]{1,0:T(8,128)(2,1)S(1)}, bf16[192,1024]{1,0:T(8,128)(2,1)S(1)}, u32[]{:S(2)}, u32[]{:S(2)}) collective-permute-start(bf16[192,1024]{1,0:T(8,128)(2,1)S(1)} %add_convert_fusion.1), channel_id=1, source_target_pairs={{0,2},{1,3},{2,0},{3,1},{4,6},{5,7},{6,4},{7,5},{8,10},{9,11},{10,... | collective-permute-start | bytes 1179656 | tf_op jit(solution)/shard_map/ppermute | solution.py:289
